TPU v7x, 32 devices: a whole 2x2x4 slice. The times are simulated.
32 devices in a mesh: dp: 16 (over z, x, core), tensor: 2 (over y).
Axes of the slice: x: 2, y: 2, z: 4, core: 2. Of those that a mesh axis runs over, the one named last changes fastest.
Arguments:
- tokens: bfloat16 [32768, 768], P('dp'), may hold values from -6 to 6
- cotangent: bfloat16 [32768, 768], P('dp'), may hold values from -6 to 6
- buckets: int32 [64], P('dp'), may hold values from 0 to 1, as said below
- lengths: int32 [64, 4], P('dp'), may hold values from 0 to 512, as said below
- qkv_weight: bfloat16 [2, 3, 768, 768], P(None, None, 'dp', 'tensor'), may hold values from -0.3125 to 0.3125
- qv_bias: float32 [2, 2, 768], P(None, None, 'tensor'), may hold values from -1.5 to 1.5
- out_weight: bfloat16 [2, 768, 768], P(None, 'dp', 'tensor'), may hold values from -0.875 to 0.875
- ffn_in_weight: bfloat16 [2, 768, 3072], P(None, 'dp', 'tensor'), may hold values from -0.21875 to 0.21875
- ffn_in_bias: float32 [2, 3072], P(None, 'tensor'), may hold values from -1.5 to 1.5
- ffn_out_weight: bfloat16 [2, 768, 3072], P(None, 'dp', 'tensor'), may hold values from -0.109375 to 0.109375
- out_bias: float32 [2, 2, 768], replicated, may hold values from -1.5 to 1.5
- norm_gain: float32 [2, 2, 768], replicated, may hold values from 0.5 to 1.5
- norm_bias: float32 [2, 2, 768], replicated, may hold values from -1.5 to 1.5
Outputs:
- layer_one: bfloat16 [32768, 768], P('dp')
- layer_two: bfloat16 [32768, 768], P('dp')
- token_grad: float32 [32768, 768], P('dp')
- qkv_grad: float32 [2, 3, 768, 768], P(None, None, 'dp', 'tensor')
- qv_bias_grad: float32 [2, 2, 768], P(None, None, 'tensor')
- out_weight_grad: float32 [2, 768, 768], P(None, 'dp', 'tensor')
- ffn_in_weight_grad: float32 [2, 768, 3072], P(None, 'dp', 'tensor')
- ffn_in_bias_grad: float32 [2, 3072], P(None, 'tensor')
- ffn_out_weight_grad: float32 [2, 768, 3072], P(None, 'dp', 'tensor')
- out_bias_grad: float32 [2, 2, 768], replicated
- norm_gain_grad: float32 [2, 2, 768], replicated
- norm_bias_grad: float32 [2, 2, 768], replicated
Inputs may be any that keep to these rules, and one draw needn't show every extreme that they name: `buckets`: 0 marks a slab of four sequences of 128 slots, 1 a slab of one sequence of 512 slots; some slab of every draw has bucket 1. `lengths`: for a slab of bucket 0, each of the four entries is its sequence's live length, from 32 to 128. For bucket 1, the first entry is the live length, from 128 to 512, and the other three are 0. Some slab of bucket 1 has length 512.
All inputs are finite; a program needn't handle non-finite values.
Results may differ from a plain program's by a relative error of at most 0.038.
Values may be sent and summed in bfloat16 or wider, within the bound.
No kernel may reach another device: no remote copies, remote signals or barrier semaphores. Data moves between devices by JAX's collectives and lax.ppermute only.
A program may use at most 256 MiB of HBM per device.

v0:
```python
import jax
import jax.numpy as jnp
from jax import lax
from jax.sharding import PartitionSpec as P

HEAD_DIM = 64
SLABS_MB = 2


norm_eps = 1e-06
big_negative = -1e30
root_half = 0.7071067811865476
inv_root_tau = 0.3989422804014327


def layer_norm(residual, norm_gain, norm_shift):
    centered = residual - jnp.mean(residual, axis=-1, keepdims=True)
    inv_spread = lax.rsqrt(jnp.mean(centered * centered, axis=-1, keepdims=True) + norm_eps)
    normed = centered * inv_spread
    return (normed * norm_gain + norm_shift, normed, inv_spread)


def norm_back(gradient, normed, inv_spread, norm_gain):
    scaled = gradient * norm_gain
    inner = jnp.mean(scaled * normed, axis=-1, keepdims=True)
    return inv_spread * (scaled - jnp.mean(scaled, axis=-1, keepdims=True) - normed * inner)


def gelu_value(inputs):
    return 0.5 * inputs * (1.0 + lax.erf(inputs * root_half))


def gelu_slope(inputs):
    return 0.5 * (1.0 + lax.erf(inputs * root_half)) + inputs * inv_root_tau * jnp.exp(
        -0.5 * inputs * inputs
    )


def slab_mask(bucket, slab_lengths, row_count):
    segment_width = jnp.where(bucket == 0, row_count // 4, row_count).astype(jnp.int32)
    positions = jnp.arange(row_count, dtype=jnp.int32)
    segment = positions // segment_width
    offset = positions - segment * segment_width
    choices_four = jnp.arange(4, dtype=jnp.int32)
    segment_length = jnp.sum(
        jnp.where(segment[:, None] == choices_four[None, :], slab_lengths[None, :], 0), axis=1
    )
    return (segment[:, None] == segment[None, :]) & (offset[None, :] < segment_length[None, :])


def attend(query_rows, key_rows, value_rows, visible):
    score_scale = query_rows.shape[-1] ** (-0.5)
    raw_scores = jnp.einsum(
        "gqhe,gkhe->ghqk", query_rows, key_rows, preferred_element_type=jnp.float32
    )
    scores = jnp.where(visible[:, None], raw_scores * score_scale, big_negative)
    row_max = jnp.max(scores, axis=-1, keepdims=True)
    row_total = jnp.sum(jnp.exp(scores - row_max), axis=-1, keepdims=True)
    logsum = row_max + jnp.log(row_total)
    probs_low = jnp.exp(scores - logsum).astype(jnp.bfloat16)
    mixed = jnp.einsum("ghqk,gkhe->gqhe", probs_low, value_rows, preferred_element_type=jnp.float32)
    return (mixed.astype(jnp.bfloat16), logsum[..., 0])


def attend_back(query_rows, key_rows, value_rows, visible, logsum, mixed_grad):
    score_scale = query_rows.shape[-1] ** (-0.5)
    raw_scores = jnp.einsum(
        "gqhe,gkhe->ghqk", query_rows, key_rows, preferred_element_type=jnp.float32
    )
    scores = jnp.where(visible[:, None], raw_scores * score_scale, big_negative)
    probs = jnp.exp(scores - logsum[..., None])
    probs_grad = jnp.einsum(
        "gqhe,gkhe->ghqk", mixed_grad, value_rows, preferred_element_type=jnp.float32
    )
    row_delta = jnp.sum(probs * probs_grad, axis=-1, keepdims=True)
    raw_grad = (probs * (probs_grad - row_delta) * score_scale).astype(jnp.bfloat16)
    query_grad = jnp.einsum(
        "ghqk,gkhe->gqhe", raw_grad, key_rows, preferred_element_type=jnp.float32
    )
    key_grad = jnp.einsum(
        "ghqk,gqhe->gkhe", raw_grad, query_rows, preferred_element_type=jnp.float32
    )
    value_grad = jnp.einsum(
        "ghqk,gqhe->gkhe",
        probs.astype(jnp.bfloat16),
        mixed_grad,
        preferred_element_type=jnp.float32,
    )
    return (
        query_grad.astype(jnp.bfloat16),
        key_grad.astype(jnp.bfloat16),
        value_grad.astype(jnp.bfloat16),
    )


def to_groups(tensor, group_count):
    row_count, head_count, head_size = tensor.shape
    return tensor.reshape(group_count, row_count // group_count, head_count, head_size)


def from_groups(tensor):
    return tensor.reshape(-1, tensor.shape[2], tensor.shape[3])


def grouped_forward(query_rows, key_rows, value_rows, visible):
    group_count = visible.shape[0]
    mixed, logsum = attend(
        to_groups(query_rows, group_count),
        to_groups(key_rows, group_count),
        to_groups(value_rows, group_count),
        visible,
    )
    return (from_groups(mixed), jnp.transpose(logsum, (1, 0, 2)).reshape(logsum.shape[1], -1))


def grouped_backward(query_rows, key_rows, value_rows, visible, logsum, mixed_grad):
    group_count = visible.shape[0]
    head_count, row_count = logsum.shape
    grouped_lse = jnp.transpose(
        logsum.reshape(head_count, group_count, row_count // group_count), (1, 0, 2)
    )
    gradients = attend_back(
        to_groups(query_rows, group_count),
        to_groups(key_rows, group_count),
        to_groups(value_rows, group_count),
        visible,
        grouped_lse,
        to_groups(mixed_grad, group_count),
    )
    return tuple((from_groups(member) for member in gradients))


def slab_forward(query_rows, key_rows, value_rows, bucket, slab_lengths):
    row_count = query_rows.shape[0]
    visible = slab_mask(bucket, slab_lengths, row_count)[None]
    return grouped_forward(query_rows, key_rows, value_rows, visible)


def slab_backward(query_rows, key_rows, value_rows, bucket, slab_lengths, logsum, mixed_grad):
    row_count = query_rows.shape[0]
    visible = slab_mask(bucket, slab_lengths, row_count)[None]
    return grouped_backward(query_rows, key_rows, value_rows, visible, logsum, mixed_grad)


def micro_forward(query_rows, key_rows, value_rows, bucket_rows, length_rows):
    slab_count = bucket_rows.shape[0]
    slab_rows = query_rows.shape[0] // slab_count
    mixed_parts = []
    logsum_parts = []
    for slab_index in range(slab_count):
        start = slab_index * slab_rows
        finish = start + slab_rows
        mixed, logsum = slab_forward(
            query_rows[start:finish],
            key_rows[start:finish],
            value_rows[start:finish],
            bucket_rows[slab_index],
            length_rows[slab_index],
        )
        mixed_parts.append(mixed)
        logsum_parts.append(logsum)
    return (jnp.concatenate(mixed_parts, axis=0), jnp.concatenate(logsum_parts, axis=1))


def micro_backward(query_rows, key_rows, value_rows, bucket_rows, length_rows, logsum, mixed_grad):
    slab_count = bucket_rows.shape[0]
    slab_rows = query_rows.shape[0] // slab_count
    query_parts = []
    key_parts = []
    value_parts = []
    for slab_index in range(slab_count):
        start = slab_index * slab_rows
        finish = start + slab_rows
        query_grad, key_grad, value_grad = slab_backward(
            query_rows[start:finish],
            key_rows[start:finish],
            value_rows[start:finish],
            bucket_rows[slab_index],
            length_rows[slab_index],
            logsum[:, start:finish],
            mixed_grad[start:finish],
        )
        query_parts.append(query_grad)
        key_parts.append(key_grad)
        value_parts.append(value_grad)
    return (
        jnp.concatenate(query_parts, axis=0),
        jnp.concatenate(key_parts, axis=0),
        jnp.concatenate(value_parts, axis=0),
    )


def gather_forward(qkv_weight, out_weight, ffn_in_weight, ffn_out_weight, layer_index):
    return (
        lax.all_gather(qkv_weight[layer_index], "dp", axis=1, tiled=True),
        lax.all_gather(out_weight[layer_index], "dp", axis=0, tiled=True),
        lax.all_gather(ffn_in_weight[layer_index], "dp", axis=0, tiled=True),
        lax.all_gather(ffn_out_weight[layer_index], "dp", axis=0, tiled=True),
    )


def gather_backward(qkv_weight, out_weight, ffn_in_weight, ffn_out_weight, layer_index):
    return (
        lax.all_gather(qkv_weight[layer_index], "dp", axis=1, tiled=True),
        lax.all_gather(out_weight[layer_index], "dp", axis=0, tiled=True),
        lax.all_gather(ffn_in_weight[layer_index], "dp", axis=0, tiled=True),
        lax.all_gather(ffn_out_weight[layer_index], "dp", axis=0, tiled=True),
    )


def layer_forward(inputs, whole, smalls, bucket_rows, length_rows):
    qkv_whole, out_whole, in_whole, down_whole = whole
    query_bias, ffn_bias, branch_bias, norm_gain, norm_shift = smalls
    row_count = inputs.shape[0]
    head_count = qkv_whole.shape[2] // HEAD_DIM
    projected = jnp.einsum("sd,cde->cse", inputs, qkv_whole, preferred_element_type=jnp.float32)
    query_rows = (
        (projected[0] + query_bias[0]).astype(jnp.bfloat16).reshape(row_count, head_count, HEAD_DIM)
    )
    key_rows = projected[1].astype(jnp.bfloat16).reshape(row_count, head_count, HEAD_DIM)
    value_rows = (
        (projected[2] + query_bias[1]).astype(jnp.bfloat16).reshape(row_count, head_count, HEAD_DIM)
    )
    mixed, logsum = micro_forward(query_rows, key_rows, value_rows, bucket_rows, length_rows)
    mixed = mixed.reshape(row_count, -1)
    attention_part = jnp.einsum("se,de->sd", mixed, out_whole, preferred_element_type=jnp.float32)
    attention_out = lax.psum(attention_part, "tensor") + branch_bias[0]
    hidden, normed_one, spread_one = layer_norm(
        inputs.astype(jnp.float32) + attention_out, norm_gain[0], norm_shift[0]
    )
    hidden_low = hidden.astype(jnp.bfloat16)
    pre_gelu = jnp.dot(hidden_low, in_whole, preferred_element_type=jnp.float32) + ffn_bias
    activated = gelu_value(pre_gelu).astype(jnp.bfloat16)
    down_part = jnp.einsum("sf,df->sd", activated, down_whole, preferred_element_type=jnp.float32)
    ffn_out = (
        lax.psum(down_part.astype(jnp.bfloat16), "tensor").astype(jnp.float32) + branch_bias[1]
    )
    result, normed_two, spread_two = layer_norm(
        hidden_low.astype(jnp.float32) + ffn_out, norm_gain[1], norm_shift[1]
    )
    kept = (
        inputs,
        query_rows,
        key_rows,
        value_rows,
        logsum,
        mixed,
        normed_one,
        spread_one,
        hidden_low,
        pre_gelu,
        normed_two,
        spread_two,
    )
    return (result.astype(jnp.bfloat16), kept)


def layer_backward(gradient, kept, whole, smalls, bucket_rows, length_rows):
    qkv_whole, out_whole, in_whole, down_whole = whole
    query_bias, ffn_bias, branch_bias, norm_gain, norm_shift = smalls
    (
        inputs,
        query_rows,
        key_rows,
        value_rows,
        logsum,
        mixed,
        normed_one,
        spread_one,
        hidden_low,
        pre_gelu,
        normed_two,
        spread_two,
    ) = kept
    row_count = inputs.shape[0]
    head_count = query_rows.shape[1]
    gain_two = jnp.sum(gradient * normed_two, axis=0)
    shift_two = jnp.sum(gradient, axis=0)
    resid_two_grad = norm_back(gradient, normed_two, spread_two, norm_gain[1])
    branch_grad = resid_two_grad.astype(jnp.bfloat16)
    bias_two = jnp.sum(branch_grad.astype(jnp.float32), axis=0)
    activated = gelu_value(pre_gelu).astype(jnp.bfloat16)
    down_term = jnp.einsum("sd,sf->df", branch_grad, activated, preferred_element_type=jnp.float32)
    activated_grad = jnp.dot(branch_grad, down_whole, preferred_element_type=jnp.float32)
    pre_grad = (activated_grad * gelu_slope(pre_gelu)).astype(jnp.bfloat16)
    ffn_bias_term = jnp.sum(pre_grad.astype(jnp.float32), axis=0)
    in_term = jnp.einsum("sd,sf->df", hidden_low, pre_grad, preferred_element_type=jnp.float32)
    hidden_part = jnp.einsum("sf,df->sd", pre_grad, in_whole, preferred_element_type=jnp.float32)
    hidden_grad = (
        lax.psum(hidden_part.astype(jnp.bfloat16), "tensor").astype(jnp.float32) + resid_two_grad
    )
    gain_one = jnp.sum(hidden_grad * normed_one, axis=0)
    shift_one = jnp.sum(hidden_grad, axis=0)
    resid_one_grad = norm_back(hidden_grad, normed_one, spread_one, norm_gain[0])
    attention_grad = resid_one_grad.astype(jnp.bfloat16)
    bias_one = jnp.sum(attention_grad.astype(jnp.float32), axis=0)
    out_term = jnp.einsum("sd,se->de", attention_grad, mixed, preferred_element_type=jnp.float32)
    mixed_grad = (
        jnp.dot(attention_grad, out_whole, preferred_element_type=jnp.float32)
        .astype(jnp.bfloat16)
        .reshape(row_count, head_count, HEAD_DIM)
    )
    query_grad, key_grad, value_grad = micro_backward(
        query_rows, key_rows, value_rows, bucket_rows, length_rows, logsum, mixed_grad
    )
    stacked = jnp.stack([query_grad, key_grad, value_grad]).reshape(3, row_count, -1)
    qkv_term = jnp.einsum("sd,cse->cde", inputs, stacked, preferred_element_type=jnp.float32)
    query_bias_term = jnp.stack(
        [
            jnp.sum(stacked[0].astype(jnp.float32), axis=0),
            jnp.sum(stacked[2].astype(jnp.float32), axis=0),
        ]
    )
    input_part = jnp.einsum("cse,cde->sd", stacked, qkv_whole, preferred_element_type=jnp.float32)
    input_grad = (
        lax.psum(input_part.astype(jnp.bfloat16), "tensor").astype(jnp.float32) + resid_one_grad
    )
    matrix_terms = (qkv_term, out_term, in_term, down_term)
    small_terms = (
        query_bias_term,
        ffn_bias_term,
        jnp.stack([bias_one, bias_two]),
        jnp.stack([gain_one, gain_two]),
        jnp.stack([shift_one, shift_two]),
    )
    return (input_grad, matrix_terms, small_terms)


def on_device(
    tokens,
    cotangent,
    buckets,
    lengths,
    qkv_weight,
    qv_bias,
    out_weight,
    ffn_in_weight,
    ffn_in_bias,
    ffn_out_weight,
    out_bias,
    norm_gain,
    norm_bias,
):
    micro_count = buckets.shape[0] // SLABS_MB
    model_width = tokens.shape[1]
    micro_rows = tokens.shape[0] // micro_count
    layer_count = qkv_weight.shape[0]
    smalls_all = (qv_bias, ffn_in_bias, out_bias, norm_gain, norm_bias)
    zero_small = tuple((jnp.zeros(member.shape, jnp.float32) for member in smalls_all))
    zero_matrix = [
        tuple(
            (
                jnp.zeros(member.shape[1:], jnp.float32)
                for member in (qkv_weight, out_weight, ffn_in_weight, ffn_out_weight)
            )
        )
        for layer_index in range(layer_count)
    ]

    def micro_step(carry, sliced):
        matrix_sums, small_sums = carry
        inputs, cotangent_rows, bucket_rows, length_rows = sliced
        current = inputs
        kept_layers = []
        whole_layers = []
        results = []
        for layer_index in range(layer_count):
            whole = gather_forward(
                qkv_weight, out_weight, ffn_in_weight, ffn_out_weight, layer_index
            )
            smalls = tuple((member[layer_index] for member in smalls_all))
            current, kept = layer_forward(current, whole, smalls, bucket_rows, length_rows)
            kept_layers.append(kept)
            whole_layers.append(whole)
            results.append(current)
        gradient = cotangent_rows.astype(jnp.float32)
        matrix_sums = list(matrix_sums)
        for layer_index in reversed(range(layer_count)):
            whole = gather_backward(
                qkv_weight, out_weight, ffn_in_weight, ffn_out_weight, layer_index
            )
            smalls = tuple((member[layer_index] for member in smalls_all))
            gradient, matrix_terms, small_terms = layer_backward(
                gradient, kept_layers[layer_index], whole, smalls, bucket_rows, length_rows
            )
            qkv_term, out_term, in_term, down_term = matrix_terms
            matrix_terms = (
                lax.psum_scatter(qkv_term, "dp", scatter_dimension=1, tiled=True),
                lax.psum_scatter(out_term, "dp", scatter_dimension=0, tiled=True),
                lax.psum_scatter(in_term, "dp", scatter_dimension=0, tiled=True),
                lax.psum_scatter(down_term, "dp", scatter_dimension=0, tiled=True),
            )
            matrix_sums[layer_index] = tuple(
                (total + term for total, term in zip(matrix_sums[layer_index], matrix_terms))
            )
            small_sums = tuple(
                (total.at[layer_index].add(term) for total, term in zip(small_sums, small_terms))
            )
        return ((matrix_sums, small_sums), (results[0], results[layer_count - 1], gradient))

    sliced_inputs = (
        tokens.reshape(micro_count, micro_rows, model_width),
        cotangent.reshape(micro_count, micro_rows, model_width),
        buckets.reshape(micro_count, SLABS_MB),
        lengths.reshape(micro_count, SLABS_MB, 4),
    )
    (matrix_sums, small_sums), (first_out, second_out, input_grads) = lax.scan(
        micro_step, (zero_matrix, zero_small), sliced_inputs
    )
    query_small, ffn_small, branch_small, gain_small, shift_small = small_sums
    query_total, ffn_total, branch_total, gain_total, shift_total = lax.psum(
        (query_small, ffn_small, branch_small, gain_small, shift_small), "dp"
    )
    return (
        first_out.reshape(-1, model_width),
        second_out.reshape(-1, model_width),
        input_grads.reshape(-1, model_width),
        jnp.stack([member[0] for member in matrix_sums]),
        query_total,
        jnp.stack([member[1] for member in matrix_sums]),
        jnp.stack([member[2] for member in matrix_sums]),
        ffn_total,
        jnp.stack([member[3] for member in matrix_sums]),
        branch_total,
        gain_total,
        shift_total,
    )


def solution(mesh):
    placed = (
        P("dp", None),
        P("dp", None),
        P("dp"),
        P("dp", None),
        P(None, None, "dp", "tensor"),
        P(None, None, "tensor"),
        P(None, "dp", "tensor"),
        P(None, "dp", "tensor"),
        P(None, "tensor"),
        P(None, "dp", "tensor"),
        P(),
        P(),
        P(),
    )
    return jax.shard_map(
        on_device,
        mesh=mesh,
        in_specs=placed,
        out_specs=(
            P("dp", None),
            P("dp", None),
            P("dp", None),
            P(None, None, "dp", "tensor"),
            P(None, None, "tensor"),
            P(None, "dp", "tensor"),
            P(None, "dp", "tensor"),
            P(None, "tensor"),
            P(None, "dp", "tensor"),
            P(),
            P(),
            P(),
        ),
        check_vma=False,
    )
```

profile of v0, /device:TPU:0, one launch (start us, length us, event | category | flops | bytes accessed | tf_op | source)
XLA Modules:
  0.0 3256.8 jit_solution(3476526353462464551)
XLA Ops:
  11.5 3173.4 %while.54 = (s32[]{:T(128)}, f32[3,48,384]{2,0,1:T(4,128)}, f32[48,384]{1,0:T(8,128)}, f32[48,1536]{1,0:T(8,128)}, f32[48,1536]{1,0:T(8,128)}, /*index=5*/f32[3,...) while((s32[]{:T(128)}, f32[3,48,384]{2,0,1:T(4,128)}, ...), condition=%wide.region_65.66_spmd.clone, body=%wide.region_0.65_spmd.clone.sunk | while | flops 48897032192 | bytes 1402500352 | solution.py:407
  19.7 25.2 all-gather.24
  44.9 14.9 all-gather.39.cloned.1.call-done
  79.4 81.2 %all-reduce.16.cloned.1.call-done = f32[1024,768]{1,0:T(8,128)} async-done(((f32[1024,768]{1,0:T(8,128)}), f32[1024,768]{1,0:T(8,128)}) %all-reduce.16.cloned.1.call-update) | async-done | bytes 3145744 | tf_op jit(solution)/shard_map/while/body/eval_jaxpr/psum | solution.py:227
  164.0 42.1 %all-gather.43.cloned.1.call-done = bf16[1,768,1536]{2,1,0:T(8,128)(2,1)} async-done(((bf16[1,48,1536]{2,1,0:T(8,128)(2,1)}), bf16[1,768,1536]{2,1,0:T(8,128)(2,1)}) %all-gather.43.cloned.1.call-update) | async-done | bytes 2359312 | tf_op jit(solution)/shard_map/while/body/eval_jaxpr/all_gather | solution.py:197
  213.5 36.1 %all-gather.45.cloned.1.call-done = bf16[1,768,1536]{2,1,0:T(8,128)(2,1)} async-done(((bf16[1,48,1536]{2,1,0:T(8,128)(2,1)}), bf16[1,768,1536]{2,1,0:T(8,128)(2,1)}) %all-gather.45.cloned.1.call-update) | async-done | bytes 2359312 | tf_op jit(solution)/shard_map/while/body/eval_jaxpr/all_gather | solution.py:198
  256.7 22.2 all-gather.26
  278.9 27.6 all-reduce.18.cloned.1.call-done
  315.0 34.3 %all-gather.41.cloned.1.call-done = bf16[1,3,768,384]{3,2,1,0:T(8,128)(2,1)} async-done(((bf16[1,3,48,384]{3,2,1,0:T(8,128)(2,1)}), bf16[1,3,768,384]{3,2,1,0:T(8,128)(2,1)}) %all-gather.41.cloned.1.call-update) | async-done | bytes 1769488 | tf_op jit(solution)/shard_map/while/body/eval_jaxpr/all_gather | solution.py:195
  368.5 83.1 %all-reduce.20.cloned.1.call-done = f32[1024,768]{1,0:T(8,128)} async-done(((f32[1024,768]{1,0:T(8,128)}), f32[1024,768]{1,0:T(8,128)}) %all-reduce.20.cloned.1.call-update) | async-done | bytes 3145744 | tf_op jit(solution)/shard_map/while/body/eval_jaxpr/psum | solution.py:227
  456.7 40.4 %all-gather.47.cloned.1.call-done = bf16[1,768,1536]{2,1,0:T(8,128)(2,1)} async-done(((bf16[1,48,1536]{2,1,0:T(8,128)(2,1)}), bf16[1,768,1536]{2,1,0:T(8,128)(2,1)}) %all-gather.47.cloned.1.call-update) | async-done | bytes 2359312 | tf_op jit(solution)/shard_map/while/body/eval_jaxpr/all_gather | solution.py:197
  504.7 36.7 %all-gather.49.cloned.1.call-done = bf16[1,768,1536]{2,1,0:T(8,128)(2,1)} async-done(((bf16[1,48,1536]{2,1,0:T(8,128)(2,1)}), bf16[1,768,1536]{2,1,0:T(8,128)(2,1)}) %all-gather.49.cloned.1.call-update) | async-done | bytes 2359312 | tf_op jit(solution)/shard_map/while/body/eval_jaxpr/all_gather | solution.py:198
  547.8 50.4 %all-reduce.22.cloned.1.call-done = bf16[1024,768]{1,0:T(8,128)(2,1)} async-done(((bf16[1024,768]{1,0:T(8,128)(2,1)}), bf16[1024,768]{1,0:T(8,128)(2,1)}) %all-reduce.22.cloned.1.call-update) | async-done | bytes 1572880 | tf_op jit(solution)/shard_map/while/body/eval_jaxpr/psum | solution.py:236
  619.6 51.6 %all-reduce.24.cloned.1.call-done = bf16[1024,768]{1,0:T(8,128)(2,1)} async-done(((bf16[1024,768]{1,0:T(8,128)(2,1)}), bf16[1024,768]{1,0:T(8,128)(2,1)}) %all-reduce.24.cloned.1.call-update) | async-done | bytes 1572880 | tf_op jit(solution)/shard_map/while/body/eval_jaxpr/psum | solution.py:290
  739.0 13.5 fusion.606
  769.9 51.6 %all-reduce.26.cloned.1.call-done = bf16[1024,768]{1,0:T(8,128)(2,1)} async-done(((bf16[1024,768]{1,0:T(8,128)(2,1)}), bf16[1024,768]{1,0:T(8,128)(2,1)}) %all-reduce.26.cloned.1.call-update) | async-done | bytes 1572880 | tf_op jit(solution)/shard_map/while/body/eval_jaxpr/psum | solution.py:316
  844.9 47.4 %all-reduce.28.cloned.1.call-done = bf16[1024,768]{1,0:T(8,128)(2,1)} async-done(((bf16[1024,768]{1,0:T(8,128)(2,1)}), bf16[1024,768]{1,0:T(8,128)(2,1)}) %all-reduce.28.cloned.1.call-update) | async-done | bytes 1572880 | tf_op jit(solution)/shard_map/while/body/eval_jaxpr/psum | solution.py:290
  938.9 13.8 fusion.616
  1078.1 15.5 reduce-scatter.7.cloned.1.call-done
  1094.5 77.9 %reduce-scatter.17.cloned.1.call-done = f32[48,1536]{1,0:T(8,128)} async-done(((f32[768,1536]{1,0:T(8,128)}), f32[48,1536]{1,0:T(8,128)}) %reduce-scatter.17.cloned.1.call-update) | async-done | bytes 294928 | tf_op jit(solution)/shard_map/while/body/eval_jaxpr/reduce_scatter | solution.py:391
  1173.5 77.3 %reduce-scatter.15.cloned.1.call-done = f32[48,1536]{1,0:T(8,128)} async-done(((f32[768,1536]{1,0:T(8,128)}), f32[48,1536]{1,0:T(8,128)}) %reduce-scatter.15.cloned.1.call-update) | async-done | bytes 294928 | tf_op jit(solution)/shard_map/while/body/eval_jaxpr/reduce_scatter | solution.py:390
  1252.5 186.7 %all-reduce.30.cloned.1.call-done = (f32[3,768,384]{2,0,1:T(4,128)}, f32[3,768,384]{2,0,1:T(4,128)}) async-done(((f32[3,768,384]{2,0,1:T(4,128)}, f32[3,768,384]{2,0,1:T(4,128)}), (f32[3,768,384]{2,0,1:T(4,128)}, f32[3,768,384]{2,0,1:T(4,128)})) %all-reduce.30.cloned.1.call-update) | async-done | bytes 7077904 | tf_op jit(solution)/shard_map/while
  1441.2 77.8 %reduce-scatter.11.cloned.1.call-done = f32[48,1536]{1,0:T(8,128)} async-done(((f32[768,1536]{1,0:T(8,128)}), f32[48,1536]{1,0:T(8,128)}) %reduce-scatter.11.cloned.1.call-update) | async-done | bytes 294928 | tf_op jit(solution)/shard_map/while/body/eval_jaxpr/reduce_scatter | solution.py:391
  1520.1 77.4 %reduce-scatter.9.cloned.1.call-done = f32[48,1536]{1,0:T(8,128)} async-done(((f32[768,1536]{1,0:T(8,128)}), f32[48,1536]{1,0:T(8,128)}) %reduce-scatter.9.cloned.1.call-update) | async-done | bytes 294928 | tf_op jit(solution)/shard_map/while/body/eval_jaxpr/reduce_scatter | solution.py:390
  1607.6 22.4 all-gather.24
  1630.0 13.9 all-gather.39.cloned.1.call-done
  1663.1 81.6 %all-reduce.16.cloned.1.call-done = f32[1024,768]{1,0:T(8,128)} async-done(((f32[1024,768]{1,0:T(8,128)}), f32[1024,768]{1,0:T(8,128)}) %all-reduce.16.cloned.1.call-update) | async-done | bytes 3145744 | tf_op jit(solution)/shard_map/while/body/eval_jaxpr/psum | solution.py:227
  1748.1 42.0 %all-gather.43.cloned.1.call-done = bf16[1,768,1536]{2,1,0:T(8,128)(2,1)} async-done(((bf16[1,48,1536]{2,1,0:T(8,128)(2,1)}), bf16[1,768,1536]{2,1,0:T(8,128)(2,1)}) %all-gather.43.cloned.1.call-update) | async-done | bytes 2359312 | tf_op jit(solution)/shard_map/while/body/eval_jaxpr/all_gather | solution.py:197
  1797.5 36.3 %all-gather.45.cloned.1.call-done = bf16[1,768,1536]{2,1,0:T(8,128)(2,1)} async-done(((bf16[1,48,1536]{2,1,0:T(8,128)(2,1)}), bf16[1,768,1536]{2,1,0:T(8,128)(2,1)}) %all-gather.45.cloned.1.call-update) | async-done | bytes 2359312 | tf_op jit(solution)/shard_map/while/body/eval_jaxpr/all_gather | solution.py:198
  1840.8 22.2 all-gather.26
  1863.0 27.6 all-reduce.18.cloned.1.call-done
  1899.1 34.3 %all-gather.41.cloned.1.call-done = bf16[1,3,768,384]{3,2,1,0:T(8,128)(2,1)} async-done(((bf16[1,3,48,384]{3,2,1,0:T(8,128)(2,1)}), bf16[1,3,768,384]{3,2,1,0:T(8,128)(2,1)}) %all-gather.41.cloned.1.call-update) | async-done | bytes 1769488 | tf_op jit(solution)/shard_map/while/body/eval_jaxpr/all_gather | solution.py:195
  1952.6 83.1 %all-reduce.20.cloned.1.call-done = f32[1024,768]{1,0:T(8,128)} async-done(((f32[1024,768]{1,0:T(8,128)}), f32[1024,768]{1,0:T(8,128)}) %all-reduce.20.cloned.1.call-update) | async-done | bytes 3145744 | tf_op jit(solution)/shard_map/while/body/eval_jaxpr/psum | solution.py:227
  2040.7 40.4 %all-gather.47.cloned.1.call-done = bf16[1,768,1536]{2,1,0:T(8,128)(2,1)} async-done(((bf16[1,48,1536]{2,1,0:T(8,128)(2,1)}), bf16[1,768,1536]{2,1,0:T(8,128)(2,1)}) %all-gather.47.cloned.1.call-update) | async-done | bytes 2359312 | tf_op jit(solution)/shard_map/while/body/eval_jaxpr/all_gather | solution.py:197
  2088.7 36.5 %all-gather.49.cloned.1.call-done = bf16[1,768,1536]{2,1,0:T(8,128)(2,1)} async-done(((bf16[1,48,1536]{2,1,0:T(8,128)(2,1)}), bf16[1,768,1536]{2,1,0:T(8,128)(2,1)}) %all-gather.49.cloned.1.call-update) | async-done | bytes 2359312 | tf_op jit(solution)/shard_map/while/body/eval_jaxpr/all_gather | solution.py:198
  2131.8 50.4 %all-reduce.22.cloned.1.call-done = bf16[1024,768]{1,0:T(8,128)(2,1)} async-done(((bf16[1024,768]{1,0:T(8,128)(2,1)}), bf16[1024,768]{1,0:T(8,128)(2,1)}) %all-reduce.22.cloned.1.call-update) | async-done | bytes 1572880 | tf_op jit(solution)/shard_map/while/body/eval_jaxpr/psum | solution.py:236
  2203.5 51.6 %all-reduce.24.cloned.1.call-done = bf16[1024,768]{1,0:T(8,128)(2,1)} async-done(((bf16[1024,768]{1,0:T(8,128)(2,1)}), bf16[1024,768]{1,0:T(8,128)(2,1)}) %all-reduce.24.cloned.1.call-update) | async-done | bytes 1572880 | tf_op jit(solution)/shard_map/while/body/eval_jaxpr/psum | solution.py:290
  2322.6 13.5 fusion.606
  2353.8 51.6 %all-reduce.26.cloned.1.call-done = bf16[1024,768]{1,0:T(8,128)(2,1)} async-done(((bf16[1024,768]{1,0:T(8,128)(2,1)}), bf16[1024,768]{1,0:T(8,128)(2,1)}) %all-reduce.26.cloned.1.call-update) | async-done | bytes 1572880 | tf_op jit(solution)/shard_map/while/body/eval_jaxpr/psum | solution.py:316
  2428.8 47.4 %all-reduce.28.cloned.1.call-done = bf16[1024,768]{1,0:T(8,128)(2,1)} async-done(((bf16[1024,768]{1,0:T(8,128)(2,1)}), bf16[1024,768]{1,0:T(8,128)(2,1)}) %all-reduce.28.cloned.1.call-update) | async-done | bytes 1572880 | tf_op jit(solution)/shard_map/while/body/eval_jaxpr/psum | solution.py:290
  2522.8 13.6 fusion.616
  2662.0 15.3 reduce-scatter.7.cloned.1.call-done
  2678.2 78.0 %reduce-scatter.17.cloned.1.call-done = f32[48,1536]{1,0:T(8,128)} async-done(((f32[768,1536]{1,0:T(8,128)}), f32[48,1536]{1,0:T(8,128)}) %reduce-scatter.17.cloned.1.call-update) | async-done | bytes 294928 | tf_op jit(solution)/shard_map/while/body/eval_jaxpr/reduce_scatter | solution.py:391
  2757.3 77.3 %reduce-scatter.15.cloned.1.call-done = f32[48,1536]{1,0:T(8,128)} async-done(((f32[768,1536]{1,0:T(8,128)}), f32[48,1536]{1,0:T(8,128)}) %reduce-scatter.15.cloned.1.call-update) | async-done | bytes 294928 | tf_op jit(solution)/shard_map/while/body/eval_jaxpr/reduce_scatter | solution.py:390
  2836.3 186.6 %all-reduce.30.cloned.1.call-done = (f32[3,768,384]{2,0,1:T(4,128)}, f32[3,768,384]{2,0,1:T(4,128)}) async-done(((f32[3,768,384]{2,0,1:T(4,128)}, f32[3,768,384]{2,0,1:T(4,128)}), (f32[3,768,384]{2,0,1:T(4,128)}, f32[3,768,384]{2,0,1:T(4,128)})) %all-reduce.30.cloned.1.call-update) | async-done | bytes 7077904 | tf_op jit(solution)/shard_map/while
  3025.2 77.8 %reduce-scatter.11.cloned.1.call-done = f32[48,1536]{1,0:T(8,128)} async-done(((f32[768,1536]{1,0:T(8,128)}), f32[48,1536]{1,0:T(8,128)}) %reduce-scatter.11.cloned.1.call-update) | async-done | bytes 294928 | tf_op jit(solution)/shard_map/while/body/eval_jaxpr/reduce_scatter | solution.py:391
  3104.0 77.5 %reduce-scatter.9.cloned.1.call-done = f32[48,1536]{1,0:T(8,128)} async-done(((f32[768,1536]{1,0:T(8,128)}), f32[48,1536]{1,0:T(8,128)}) %reduce-scatter.9.cloned.1.call-update) | async-done | bytes 294928 | tf_op jit(solution)/shard_map/while/body/eval_jaxpr/reduce_scatter | solution.py:390
  3184.9 59.3 %all-reduce.3 = (f32[2,2,384]{2,1,0:T(2,128)}, f32[2,1536]{1,0:T(2,128)}, f32[2,2,768]{2,1,0:T(2,128)}, f32[2,2,768]{2,1,0:T(2,128)}, f32[2,2,768]{2,1,0:T(2,128)}) all-reduce(f32[2,2,384]{2,1,0:T(2,128)} %get-tuple-element.604, f32[2,1536]{1,0:T(2,128)} %get-tuple-element.609, ...), channel_id=1, replica_groups=mesh['dp'=16,'tensor'=2] {'dp'}, use_global_device_ids=true, to_apply=%region_66.67 | all-reduce | flops 13824 | bytes 110592 | tf_op jit(solution)/shard_map/psum | solution.py:411
  (919 shorter events, 808.0 us)
Async XLA Ops:
  11.8 48.0 %all-gather.39.cloned.1.call-start = ((), (), s32[]{:S(2)}) async-start(), calls=%async_computation.6 | async-start | bytes 1880064 | tf_op jit(solution)/shard_map/while/body/eval_jaxpr/all_gather | solution.py:195
  13.6 147.1 %all-reduce.16.cloned.1.call-start = ((), (), s32[]{:S(2)}) async-start(), calls=%async_computation.7 | async-start | bytes 6291456 | tf_op jit(solution)/shard_map/while/body/eval_jaxpr/psum | solution.py:227
  75.8 130.3 %all-gather.43.cloned.1.call-start = ((), (), s32[]{:S(2)}) async-start(), calls=%async_computation.9 | async-start | bytes 2506752 | tf_op jit(solution)/shard_map/while/body/eval_jaxpr/all_gather | solution.py:197
  76.6 173.0 %all-gather.45.cloned.1.call-start = ((), (), s32[]{:S(2)}) async-start(), calls=%async_computation.10 | async-start | bytes 2506752 | tf_op jit(solution)/shard_map/while/body/eval_jaxpr/all_gather | solution.py:198
  77.4 229.1 %all-reduce.18.cloned.1.call-start = ((), (), s32[]{:S(2)}) async-start(), calls=%async_computation.11 | async-start | bytes 3145728 | tf_op jit(solution)/shard_map/while/body/eval_jaxpr/psum | solution.py:236
  78.7 748.9 %copy-start.74 = (f32[768]{0:T(1024)}, f32[768]{0:T(1024)S(1)}, u32[]{:S(2)}) copy-start(f32[768]{0:T(1024)S(1)} %get-tuple-element.1223) | copy-start | bytes 9220 | tf_op jit(solution)/shard_map/while
  78.7 598.4 %copy-start.68 = (f32[768]{0:T(1024)}, f32[768]{0:T(1024)S(1)}, u32[]{:S(2)}) copy-start(f32[768]{0:T(1024)S(1)} %get-tuple-element.1251) | copy-start | bytes 9220 | tf_op jit(solution)/shard_map/while
  256.1 93.3 %all-gather.41.cloned.1.call-start = ((), (), s32[]{:S(2)}) async-start(), calls=%async_computation.8 | async-start | bytes 1880064 | tf_op jit(solution)/shard_map/while/body/eval_jaxpr/all_gather | solution.py:195
  256.6 195.0 %all-reduce.20.cloned.1.call-start = ((), (), s32[]{:S(2)}) async-start(), calls=%async_computation.12 | async-start | bytes 6291456 | tf_op jit(solution)/shard_map/while/body/eval_jaxpr/psum | solution.py:227
  366.8 130.3 %all-gather.47.cloned.1.call-start = ((), (), s32[]{:S(2)}) async-start(), calls=%async_computation.13 | async-start | bytes 2506752 | tf_op jit(solution)/shard_map/while/body/eval_jaxpr/all_gather | solution.py:197
  367.5 173.8 %all-gather.49.cloned.1.call-start = ((), (), s32[]{:S(2)}) async-start(), calls=%async_computation.14 | async-start | bytes 2506752 | tf_op jit(solution)/shard_map/while/body/eval_jaxpr/all_gather | solution.py:198
  368.2 230.0 %all-reduce.22.cloned.1.call-start = ((), (), s32[]{:S(2)}) async-start(), calls=%async_computation.15 | async-start | bytes 3145728 | tf_op jit(solution)/shard_map/while/body/eval_jaxpr/psum | solution.py:236
  547.8 123.4 %all-reduce.24.cloned.1.call-start = ((), (), s32[]{:S(2)}) async-start(), calls=%async_computation.16 | async-start | bytes 3145728 | tf_op jit(solution)/shard_map/while/body/eval_jaxpr/psum | solution.py:290
  619.6 201.9 %all-reduce.26.cloned.1.call-start = ((), (), s32[]{:S(2)}) async-start(), calls=%async_computation.17 | async-start | bytes 3145728 | tf_op jit(solution)/shard_map/while/body/eval_jaxpr/psum | solution.py:316
  769.8 122.5 %all-reduce.28.cloned.1.call-start = ((), (), s32[]{:S(2)}) async-start(), calls=%async_computation.18 | async-start | bytes 3145728 | tf_op jit(solution)/shard_map/while/body/eval_jaxpr/psum | solution.py:290
  840.6 221.9 %reduce-scatter.13.cloned.1.call-start = ((), (), s32[]{:S(2)}) async-start(), calls=%async_computation.23 | async-start | bytes 1253376 | tf_op jit(solution)/shard_map/while/body/eval_jaxpr/reduce_scatter | solution.py:389
  844.8 229.8 %all-reduce.32.cloned.1.call-start = ((), (), s32[]{:S(2)}) async-start(), calls=%async_computation.26 | async-start | bytes 3145728 | tf_op jit(solution)/shard_map/while/body/eval_jaxpr/psum | solution.py:316
  980.3 113.4 %reduce-scatter.7.cloned.1.call-start = ((), (), s32[]{:S(2)}) async-start(), calls=%async_computation.20 | async-start | bytes 1253376 | tf_op jit(solution)/shard_map/while/body/eval_jaxpr/reduce_scatter | solution.py:389
  984.5 187.9 %reduce-scatter.17.cloned.1.call-start = ((), (), s32[]{:S(2)}) async-start(), calls=%async_computation.25 | async-start | bytes 5013504 | tf_op jit(solution)/shard_map/while/body/eval_jaxpr/reduce_scatter | solution.py:391
  992.8 257.9 %reduce-scatter.15.cloned.1.call-start = ((), (), s32[]{:S(2)}) async-start(), calls=%async_computation.24 | async-start | bytes 5013504 | tf_op jit(solution)/shard_map/while/body/eval_jaxpr/reduce_scatter | solution.py:390
  1001.4 437.7 %all-reduce.30.cloned.1.call-start = ((), (), s32[]{:S(2)}) async-start(), calls=%async_computation.19 | async-start | bytes 18874368 | tf_op jit(solution)/shard_map/while
  1026.7 492.3 %reduce-scatter.11.cloned.1.call-start = ((), (), s32[]{:S(2)}) async-start(), calls=%async_computation.22 | async-start | bytes 5013504 | tf_op jit(solution)/shard_map/while/body/eval_jaxpr/reduce_scatter | solution.py:391
  1034.7 562.8 %reduce-scatter.9.cloned.1.call-start = ((), (), s32[]{:S(2)}) async-start(), calls=%async_computation.21 | async-start | bytes 5013504 | tf_op jit(solution)/shard_map/while/body/eval_jaxpr/reduce_scatter | solution.py:390
  1599.8 44.1 %all-gather.39.cloned.1.call-start = ((), (), s32[]{:S(2)}) async-start(), calls=%async_computation.6 | async-start | bytes 1880064 | tf_op jit(solution)/shard_map/while/body/eval_jaxpr/all_gather | solution.py:195
  1601.5 143.2 %all-reduce.16.cloned.1.call-start = ((), (), s32[]{:S(2)}) async-start(), calls=%async_computation.7 | async-start | bytes 6291456 | tf_op jit(solution)/shard_map/while/body/eval_jaxpr/psum | solution.py:227
  1659.9 130.2 %all-gather.43.cloned.1.call-start = ((), (), s32[]{:S(2)}) async-start(), calls=%async_computation.9 | async-start | bytes 2506752 | tf_op jit(solution)/shard_map/while/body/eval_jaxpr/all_gather | solution.py:197
  1660.7 173.0 %all-gather.45.cloned.1.call-start = ((), (), s32[]{:S(2)}) async-start(), calls=%async_computation.10 | async-start | bytes 2506752 | tf_op jit(solution)/shard_map/while/body/eval_jaxpr/all_gather | solution.py:198
  1661.5 229.0 %all-reduce.18.cloned.1.call-start = ((), (), s32[]{:S(2)}) async-start(), calls=%async_computation.11 | async-start | bytes 3145728 | tf_op jit(solution)/shard_map/while/body/eval_jaxpr/psum | solution.py:236
  1662.4 528.5 %copy-start.76 = (f32[768]{0:T(1024)}, f32[768]{0:T(1024)S(1)}, u32[]{:S(2)}) copy-start(f32[768]{0:T(1024)S(1)} %get-tuple-element.1250) | copy-start | bytes 9220 | tf_op jit(solution)/shard_map/while
  1662.4 749.1 %copy-start.74 = (f32[768]{0:T(1024)}, f32[768]{0:T(1024)S(1)}, u32[]{:S(2)}) copy-start(f32[768]{0:T(1024)S(1)} %get-tuple-element.1223) | copy-start | bytes 9220 | tf_op jit(solution)/shard_map/while
  1662.4 528.4 %copy-start.83 = (f32[768]{0:T(1024)}, f32[768]{0:T(1024)S(1)}, u32[]{:S(2)}) copy-start(f32[768]{0:T(1024)S(1)} %get-tuple-element.1255) | copy-start | bytes 9220 | tf_op jit(solution)/shard_map/while
  1662.4 598.6 %copy-start.68 = (f32[768]{0:T(1024)}, f32[768]{0:T(1024)S(1)}, u32[]{:S(2)}) copy-start(f32[768]{0:T(1024)S(1)} %get-tuple-element.1251) | copy-start | bytes 9220 | tf_op jit(solution)/shard_map/while
  1840.1 93.3 %all-gather.41.cloned.1.call-start = ((), (), s32[]{:S(2)}) async-start(), calls=%async_computation.8 | async-start | bytes 1880064 | tf_op jit(solution)/shard_map/while/body/eval_jaxpr/all_gather | solution.py:195
  1840.7 194.9 %all-reduce.20.cloned.1.call-start = ((), (), s32[]{:S(2)}) async-start(), calls=%async_computation.12 | async-start | bytes 6291456 | tf_op jit(solution)/shard_map/while/body/eval_jaxpr/psum | solution.py:227
  1950.8 130.3 %all-gather.47.cloned.1.call-start = ((), (), s32[]{:S(2)}) async-start(), calls=%async_computation.13 | async-start | bytes 2506752 | tf_op jit(solution)/shard_map/while/body/eval_jaxpr/all_gather | solution.py:197
  1951.6 173.7 %all-gather.49.cloned.1.call-start = ((), (), s32[]{:S(2)}) async-start(), calls=%async_computation.14 | async-start | bytes 2506752 | tf_op jit(solution)/shard_map/while/body/eval_jaxpr/all_gather | solution.py:198
  1952.2 230.0 %all-reduce.22.cloned.1.call-start = ((), (), s32[]{:S(2)}) async-start(), calls=%async_computation.15 | async-start | bytes 3145728 | tf_op jit(solution)/shard_map/while/body/eval_jaxpr/psum | solution.py:236
  2131.7 123.4 %all-reduce.24.cloned.1.call-start = ((), (), s32[]{:S(2)}) async-start(), calls=%async_computation.16 | async-start | bytes 3145728 | tf_op jit(solution)/shard_map/while/body/eval_jaxpr/psum | solution.py:290
  2203.5 201.9 %all-reduce.26.cloned.1.call-start = ((), (), s32[]{:S(2)}) async-start(), calls=%async_computation.17 | async-start | bytes 3145728 | tf_op jit(solution)/shard_map/while/body/eval_jaxpr/psum | solution.py:316
  2353.7 122.5 %all-reduce.28.cloned.1.call-start = ((), (), s32[]{:S(2)}) async-start(), calls=%async_computation.18 | async-start | bytes 3145728 | tf_op jit(solution)/shard_map/while/body/eval_jaxpr/psum | solution.py:290
  2424.5 221.9 %reduce-scatter.13.cloned.1.call-start = ((), (), s32[]{:S(2)}) async-start(), calls=%async_computation.23 | async-start | bytes 1253376 | tf_op jit(solution)/shard_map/while/body/eval_jaxpr/reduce_scatter | solution.py:389
  2428.7 229.8 %all-reduce.32.cloned.1.call-start = ((), (), s32[]{:S(2)}) async-start(), calls=%async_computation.26 | async-start | bytes 3145728 | tf_op jit(solution)/shard_map/while/body/eval_jaxpr/psum | solution.py:316
  2564.0 113.3 %reduce-scatter.7.cloned.1.call-start = ((), (), s32[]{:S(2)}) async-start(), calls=%async_computation.20 | async-start | bytes 1253376 | tf_op jit(solution)/shard_map/while/body/eval_jaxpr/reduce_scatter | solution.py:389
  2568.5 187.7 %reduce-scatter.17.cloned.1.call-start = ((), (), s32[]{:S(2)}) async-start(), calls=%async_computation.25 | async-start | bytes 5013504 | tf_op jit(solution)/shard_map/while/body/eval_jaxpr/reduce_scatter | solution.py:391
  2576.8 257.8 %reduce-scatter.15.cloned.1.call-start = ((), (), s32[]{:S(2)}) async-start(), calls=%async_computation.24 | async-start | bytes 5013504 | tf_op jit(solution)/shard_map/while/body/eval_jaxpr/reduce_scatter | solution.py:390
  2585.3 437.6 %all-reduce.30.cloned.1.call-start = ((), (), s32[]{:S(2)}) async-start(), calls=%async_computation.19 | async-start | bytes 18874368 | tf_op jit(solution)/shard_map/while
  2610.6 492.3 %reduce-scatter.11.cloned.1.call-start = ((), (), s32[]{:S(2)}) async-start(), calls=%async_computation.22 | async-start | bytes 5013504 | tf_op jit(solution)/shard_map/while/body/eval_jaxpr/reduce_scatter | solution.py:391
  2618.6 562.9 %reduce-scatter.9.cloned.1.call-start = ((), (), s32[]{:S(2)}) async-start(), calls=%async_computation.21 | async-start | bytes 5013504 | tf_op jit(solution)/shard_map/while/body/eval_jaxpr/reduce_scatter | solution.py:390
  (228 other events, 7778.1 us)
Sparse Core Ops, SparseCore 0:
  15.6 44.1 all-gather.38
  75.9 84.6 all-reduce.15
  163.7 42.3 all-gather.42
  208.5 41.0 all-gather.44
  256.2 50.2 all-reduce.17
  308.9 40.3 all-gather.40
  366.9 84.6 all-reduce.19
  454.7 42.3 all-gather.46
  500.2 41.0 all-gather.48
  547.9 50.2 all-reduce.21
  619.7 51.4 all-reduce.23
  769.9 51.4 all-reduce.25
  840.8 51.4 all-reduce.27
  895.7 58.0 reduce-scatter.12
  980.4 51.5 all-reduce.31
  1035.4 58.1 reduce-scatter.6
  1097.8 74.5 reduce-scatter.16
  1176.1 74.5 reduce-scatter.14
  1254.9 184.1 all-reduce.29
  1443.4 75.6 reduce-scatter.10
  1522.9 74.5 reduce-scatter.8
  1603.5 40.3 all-gather.38
  1660.0 84.6 all-reduce.15
  1747.7 42.3 all-gather.42
  1792.6 41.0 all-gather.44
  1840.3 50.2 all-reduce.17
  1893.0 40.3 all-gather.40
  1951.0 84.6 all-reduce.19
  2038.8 42.3 all-gather.46
  2084.1 41.0 all-gather.48
  2131.8 50.2 all-reduce.21
  2203.6 51.4 all-reduce.23
  2353.8 51.4 all-reduce.25
  2424.7 51.4 all-reduce.27
  2479.8 58.0 reduce-scatter.12
  2564.1 51.5 all-reduce.31
  2619.1 58.0 reduce-scatter.6
  2681.6 74.5 reduce-scatter.16
  2759.9 74.5 reduce-scatter.14
  2838.7 184.1 all-reduce.29
  3027.3 75.5 reduce-scatter.10
  3106.8 74.6 reduce-scatter.8
where the time goes:
time: 3260 us
  waiting for transfers between devices  2220 us (68%)
  matrix products  546 us (17%)
  other arithmetic  185 us (6%)
  blocking collectives  151 us (5%)
  local copies, waits for them, and re-layouts  123 us (4%)
    while x44, waiting for transfers between devices  378 us
    psum x4, waiting for transfers between devices, layer_forward(): attention_out = lax.psum(attention_part, 'tensor') + branch_bias[0]  329 us
    reduce_scatter x4, waiting for transfers between devices, micro_step(): lax.psum_scatter(down_term, 'dp', scatter_dimension=0, tiled=True)  311 us
    reduce_scatter x4, waiting for transfers between devices, micro_step(): lax.psum_scatter(in_term, 'dp', scatter_dimension=0, tiled=True)  309 us
    psum x4, waiting for transfers between devices, layer_backward(): lax.psum(hidden_part.astype(jnp.bfloat16), 'tensor').astype(jnp.float32)  198 us
    all_gather x4, waiting for transfers between devices, gather_forward(): lax.all_gather(ffn_in_weight[layer_index], 'dp', axis=0, tiled=True)  165 us
    psum x4, waiting for transfers between devices, layer_forward(): lax.psum(down_part.astype(jnp.bfloat16), 'tensor').astype(jnp.float32)  156 us
    all_gather x4, waiting for transfers between devices, gather_forward(): lax.all_gather(ffn_out_weight[layer_index], 'dp', axis=0, tiled=True)  146 us
  transfers between devices with their start and end apart: 42, of which 38 were waited for; matrix products, arithmetic and copies ran while one was open for 14% of the time, Pallas kernels for 0%

commit v1 on v0

--- a/solution.py
+++ b/solution.py
@@ -4,7 +4,6 @@
 from jax.sharding import PartitionSpec as P
 
 HEAD_DIM = 64
-SLABS_MB = 2
 
 
 norm_eps = 1e-06
@@ -190,22 +189,36 @@
     )
 
 
-def gather_forward(qkv_weight, out_weight, ffn_in_weight, ffn_out_weight, layer_index):
-    return (
-        lax.all_gather(qkv_weight[layer_index], "dp", axis=1, tiled=True),
-        lax.all_gather(out_weight[layer_index], "dp", axis=0, tiled=True),
-        lax.all_gather(ffn_in_weight[layer_index], "dp", axis=0, tiled=True),
-        lax.all_gather(ffn_out_weight[layer_index], "dp", axis=0, tiled=True),
-    )
-
-
-def gather_backward(qkv_weight, out_weight, ffn_in_weight, ffn_out_weight, layer_index):
-    return (
-        lax.all_gather(qkv_weight[layer_index], "dp", axis=1, tiled=True),
-        lax.all_gather(out_weight[layer_index], "dp", axis=0, tiled=True),
-        lax.all_gather(ffn_in_weight[layer_index], "dp", axis=0, tiled=True),
-        lax.all_gather(ffn_out_weight[layer_index], "dp", axis=0, tiled=True),
-    )
+AXES = ("tensor", "dp")
+
+
+def pack_shard(qkv_weight, out_weight, ffn_in_weight, ffn_out_weight):
+    rows = out_weight.shape[0]
+    qkv_flat = jnp.transpose(qkv_weight, (1, 0, 2)).reshape(rows, -1)
+    return jnp.concatenate([qkv_flat, out_weight], axis=1), jnp.concatenate(
+        [ffn_in_weight, ffn_out_weight], axis=1
+    )
+
+
+def whole_weights(shards, split):
+    attention_shard, ffn_shard = shards
+    attention_all = lax.all_gather(attention_shard, AXES, tiled=True)
+    ffn_all = lax.all_gather(ffn_shard, AXES, tiled=True)
+    model_width = attention_all.shape[0] // split
+    attention_all = attention_all.reshape(split, model_width, 4, -1)
+    ffn_all = ffn_all.reshape(split, model_width, 2, -1)
+    attention_all = jnp.transpose(attention_all, (2, 1, 0, 3)).reshape(4, model_width, -1)
+    ffn_all = jnp.transpose(ffn_all, (2, 1, 0, 3)).reshape(2, model_width, -1)
+    return attention_all[:3], attention_all[3], ffn_all[0], ffn_all[1]
+
+
+def scatter_gradient(terms, split):
+    count, model_width, columns = terms.shape
+    packed = jnp.transpose(
+        terms.astype(jnp.bfloat16).reshape(count, model_width, split, -1), (2, 1, 0, 3)
+    ).reshape(split * model_width, -1)
+    mine = lax.psum_scatter(packed, AXES, scatter_dimension=0, tiled=True)
+    return jnp.transpose(mine.astype(jnp.float32).reshape(-1, count, columns // split), (1, 0, 2))
 
 
 def layer_forward(inputs, whole, smalls, bucket_rows, length_rows):
@@ -223,17 +236,19 @@
     )
     mixed, logsum = micro_forward(query_rows, key_rows, value_rows, bucket_rows, length_rows)
     mixed = mixed.reshape(row_count, -1)
-    attention_part = jnp.einsum("se,de->sd", mixed, out_whole, preferred_element_type=jnp.float32)
-    attention_out = lax.psum(attention_part, "tensor") + branch_bias[0]
+    attention_out = (
+        jnp.einsum("se,de->sd", mixed, out_whole, preferred_element_type=jnp.float32)
+        + branch_bias[0]
+    )
     hidden, normed_one, spread_one = layer_norm(
         inputs.astype(jnp.float32) + attention_out, norm_gain[0], norm_shift[0]
     )
     hidden_low = hidden.astype(jnp.bfloat16)
     pre_gelu = jnp.dot(hidden_low, in_whole, preferred_element_type=jnp.float32) + ffn_bias
     activated = gelu_value(pre_gelu).astype(jnp.bfloat16)
-    down_part = jnp.einsum("sf,df->sd", activated, down_whole, preferred_element_type=jnp.float32)
     ffn_out = (
-        lax.psum(down_part.astype(jnp.bfloat16), "tensor").astype(jnp.float32) + branch_bias[1]
+        jnp.einsum("sf,df->sd", activated, down_whole, preferred_element_type=jnp.float32)
+        + branch_bias[1]
     )
     result, normed_two, spread_two = layer_norm(
         hidden_low.astype(jnp.float32) + ffn_out, norm_gain[1], norm_shift[1]
@@ -286,9 +301,7 @@
     ffn_bias_term = jnp.sum(pre_grad.astype(jnp.float32), axis=0)
     in_term = jnp.einsum("sd,sf->df", hidden_low, pre_grad, preferred_element_type=jnp.float32)
     hidden_part = jnp.einsum("sf,df->sd", pre_grad, in_whole, preferred_element_type=jnp.float32)
-    hidden_grad = (
-        lax.psum(hidden_part.astype(jnp.bfloat16), "tensor").astype(jnp.float32) + resid_two_grad
-    )
+    hidden_grad = hidden_part + resid_two_grad
     gain_one = jnp.sum(hidden_grad * normed_one, axis=0)
     shift_one = jnp.sum(hidden_grad, axis=0)
     resid_one_grad = norm_back(hidden_grad, normed_one, spread_one, norm_gain[0])
@@ -312,9 +325,7 @@
         ]
     )
     input_part = jnp.einsum("cse,cde->sd", stacked, qkv_whole, preferred_element_type=jnp.float32)
-    input_grad = (
-        lax.psum(input_part.astype(jnp.bfloat16), "tensor").astype(jnp.float32) + resid_one_grad
-    )
+    input_grad = input_part + resid_one_grad
     matrix_terms = (qkv_term, out_term, in_term, down_term)
     small_terms = (
         query_bias_term,
@@ -341,85 +352,61 @@
     norm_gain,
     norm_bias,
 ):
-    micro_count = buckets.shape[0] // SLABS_MB
-    model_width = tokens.shape[1]
-    micro_rows = tokens.shape[0] // micro_count
+    split = lax.axis_size("tensor")
+    place = lax.axis_index("tensor")
+    rows = tokens.shape[0] // split
+    slabs = buckets.shape[0] // split
     layer_count = qkv_weight.shape[0]
-    smalls_all = (qv_bias, ffn_in_bias, out_bias, norm_gain, norm_bias)
-    zero_small = tuple((jnp.zeros(member.shape, jnp.float32) for member in smalls_all))
-    zero_matrix = [
-        tuple(
-            (
-                jnp.zeros(member.shape[1:], jnp.float32)
-                for member in (qkv_weight, out_weight, ffn_in_weight, ffn_out_weight)
-            )
-        )
-        for layer_index in range(layer_count)
+    current = lax.dynamic_slice_in_dim(tokens, place * rows, rows)
+    gradient = lax.dynamic_slice_in_dim(cotangent, place * rows, rows).astype(jnp.float32)
+    bucket_rows = lax.dynamic_slice_in_dim(buckets, place * slabs, slabs)
+    length_rows = lax.dynamic_slice_in_dim(lengths, place * slabs, slabs)
+    qv_whole = lax.all_gather(qv_bias, "tensor", axis=2, tiled=True)
+    ffn_bias_whole = lax.all_gather(ffn_in_bias, "tensor", axis=1, tiled=True)
+    smalls_all = (qv_whole, ffn_bias_whole, out_bias, norm_gain, norm_bias)
+    whole_layers = [
+        whole_weights(
+            pack_shard(qkv_weight[index], out_weight[index], ffn_in_weight[index], ffn_out_weight[index]),
+            split,
+        )
+        for index in range(layer_count)
     ]
-
-    def micro_step(carry, sliced):
-        matrix_sums, small_sums = carry
-        inputs, cotangent_rows, bucket_rows, length_rows = sliced
-        current = inputs
-        kept_layers = []
-        whole_layers = []
-        results = []
-        for layer_index in range(layer_count):
-            whole = gather_forward(
-                qkv_weight, out_weight, ffn_in_weight, ffn_out_weight, layer_index
-            )
-            smalls = tuple((member[layer_index] for member in smalls_all))
-            current, kept = layer_forward(current, whole, smalls, bucket_rows, length_rows)
-            kept_layers.append(kept)
-            whole_layers.append(whole)
-            results.append(current)
-        gradient = cotangent_rows.astype(jnp.float32)
-        matrix_sums = list(matrix_sums)
-        for layer_index in reversed(range(layer_count)):
-            whole = gather_backward(
-                qkv_weight, out_weight, ffn_in_weight, ffn_out_weight, layer_index
-            )
-            smalls = tuple((member[layer_index] for member in smalls_all))
-            gradient, matrix_terms, small_terms = layer_backward(
-                gradient, kept_layers[layer_index], whole, smalls, bucket_rows, length_rows
-            )
-            qkv_term, out_term, in_term, down_term = matrix_terms
-            matrix_terms = (
-                lax.psum_scatter(qkv_term, "dp", scatter_dimension=1, tiled=True),
-                lax.psum_scatter(out_term, "dp", scatter_dimension=0, tiled=True),
-                lax.psum_scatter(in_term, "dp", scatter_dimension=0, tiled=True),
-                lax.psum_scatter(down_term, "dp", scatter_dimension=0, tiled=True),
-            )
-            matrix_sums[layer_index] = tuple(
-                (total + term for total, term in zip(matrix_sums[layer_index], matrix_terms))
-            )
-            small_sums = tuple(
-                (total.at[layer_index].add(term) for total, term in zip(small_sums, small_terms))
-            )
-        return ((matrix_sums, small_sums), (results[0], results[layer_count - 1], gradient))
-
-    sliced_inputs = (
-        tokens.reshape(micro_count, micro_rows, model_width),
-        cotangent.reshape(micro_count, micro_rows, model_width),
-        buckets.reshape(micro_count, SLABS_MB),
-        lengths.reshape(micro_count, SLABS_MB, 4),
-    )
-    (matrix_sums, small_sums), (first_out, second_out, input_grads) = lax.scan(
-        micro_step, (zero_matrix, zero_small), sliced_inputs
-    )
-    query_small, ffn_small, branch_small, gain_small, shift_small = small_sums
+    kept_layers = []
+    results = []
+    for layer_index in range(layer_count):
+        smalls = tuple((member[layer_index] for member in smalls_all))
+        current, kept = layer_forward(
+            current, whole_layers[layer_index], smalls, bucket_rows, length_rows
+        )
+        kept_layers.append(kept)
+        results.append(lax.all_gather(current, "tensor", axis=0, tiled=True))
+    matrix_sums = [None] * layer_count
+    small_sums = [None] * layer_count
+    for layer_index in reversed(range(layer_count)):
+        smalls = tuple((member[layer_index] for member in smalls_all))
+        gradient, (qkv_term, out_term, in_term, down_term), small_sums[layer_index] = layer_backward(
+            gradient, kept_layers[layer_index], whole_layers[layer_index], smalls, bucket_rows, length_rows
+        )
+        ffn_mine = scatter_gradient(jnp.stack([in_term, down_term]), split)
+        attention_mine = scatter_gradient(
+            jnp.concatenate([qkv_term, out_term[None]], axis=0), split
+        )
+        matrix_sums[layer_index] = (attention_mine[:3], attention_mine[3], ffn_mine[0], ffn_mine[1])
+    input_grads = lax.all_gather(gradient.astype(jnp.bfloat16), "tensor", axis=0, tiled=True)
     query_total, ffn_total, branch_total, gain_total, shift_total = lax.psum(
-        (query_small, ffn_small, branch_small, gain_small, shift_small), "dp"
-    )
+        tuple((jnp.stack(group) for group in zip(*small_sums))), AXES
+    )
+    qv_columns = qv_bias.shape[2]
+    ffn_columns = ffn_in_bias.shape[1]
     return (
-        first_out.reshape(-1, model_width),
-        second_out.reshape(-1, model_width),
-        input_grads.reshape(-1, model_width),
+        results[0],
+        results[layer_count - 1],
+        input_grads.astype(jnp.float32),
         jnp.stack([member[0] for member in matrix_sums]),
-        query_total,
+        lax.dynamic_slice_in_dim(query_total, place * qv_columns, qv_columns, axis=2),
         jnp.stack([member[1] for member in matrix_sums]),
         jnp.stack([member[2] for member in matrix_sums]),
-        ffn_total,
+        lax.dynamic_slice_in_dim(ffn_total, place * ffn_columns, ffn_columns, axis=1),
         jnp.stack([member[3] for member in matrix_sums]),
         branch_total,
         gain_total,

time: 3260 us -> 1550 us (0.48)
  waiting for transfers between devices: 2220 us -> 480 us
  local copies, waits for them, and re-layouts: 123 us -> 487 us
  blocking collectives: 151 us -> 9.66 us
  matrix products: 546 us -> 430 us
  other arithmetic: 185 us -> 113 us
    psum x16 -> x1, waiting for transfers between devices: 786 us -> 0.02 us  [on_device(): lax.psum(tuple((jnp.stack(group) for group in zip(*small_sums))), AXES)]
    while x44 -> x0, waiting for transfers between devices: 378 us -> none
    all_gather x12 -> x7, waiting for transfers between devices: 408 us -> 106 us  [the longest x2 96.7 us: whole_weights(): attention_all = lax.all_gather(attention_shard, AXES, tiled=True)]
    reduce_scatter x12 -> x4, waiting for transfers between devices: 652 us -> 372 us  [scatter_gradient(): mine = lax.psum_scatter(packed, AXES, scatter_dimension=0, tiled=True)]
    slice x22, local copies, waits for them, and re-layouts: 10.7 us -> 174 us  [the longest x12 164 us: whole_weights(): return (attention_all[:3], attention_all[3], ffn_all[0], ffn_all[1])]
    another operation x3 -> x8, local copies, waits for them, and re-layouts: 1.81 us -> 136 us  [on_device(): ffn_mine = scatter_gradient(jnp.stack([in_term, down_term]), split)]
    all_gather x4 -> x2, blocking collectives: 92 us -> 9.66 us  [the longest x1 5.27 us: on_device(): qv_whole = lax.all_gather(qv_bias, 'tensor', axis=2, tiled=True)]
    reshape x1 -> x6, local copies, waits for them, and re-layouts: 1.31 us -> 61.3 us  [the longest x2 43.2 us: whole_weights(): ffn_all = ffn_all.reshape(split, model_width, 2, -1)]
  transfers between devices with their start and end apart: 42 -> 12, of which waited for: 38 -> 6; matrix products, arithmetic and copies ran while one was open for 14% -> 37% of each run, Pallas kernels for 0% -> 0%
where the time goes in v1:
time: 1550 us; the launch traced here: 1540 us
  local copies, waits for them, and re-layouts  487 us (31%)
  waiting for transfers between devices  480 us (31%)
  matrix products  430 us (28%)
  other arithmetic  113 us (7%)
  between operations  17.7 us (1%)
    reduce_scatter x4, waiting for transfers between devices, scatter_gradient(): mine = lax.psum_scatter(packed, AXES, scatter_dimension=0, tiled=True)  372 us
    slice x12, local copies, waits for them, and re-layouts, whole_weights(): return (attention_all[:3], attention_all[3], ffn_all[0], ffn_all[1])  164 us
    another operation x8, local copies, waits for them, and re-layouts, on_device(): ffn_mine = scatter_gradient(jnp.stack([in_term, down_term]), split)  136 us
    all_gather x2, waiting for transfers between devices, whole_weights(): attention_all = lax.all_gather(attention_shard, AXES, tiled=True)  96.7 us
    dot_general x4, matrix products, attend_back(): jnp.einsum('ghqk,gqhe->gkhe', raw_grad, query_rows, preferred_element_typ...  81.7 us
    dot_general x4, matrix products, attend_back(): jnp.einsum('ghqk,gkhe->gqhe', raw_grad, key_rows, preferred_element_type=...  81 us
    unnamed x276, local copies, waits for them, and re-layouts  49.3 us
    another operation x2, other arithmetic, on_device(): ffn_mine = scatter_gradient(jnp.stack([in_term, down_term]), split)  46.3 us
  transfers between devices with their start and end apart: 12, of which 6 were waited for; matrix products, arithmetic and copies ran while one was open for 37% of the time, Pallas kernels for 0%

profile of v1, /device:TPU:0, one launch (start us, length us, event | category | flops | bytes accessed | tf_op | source)
XLA Modules:
  0.0 1538.5 jit_solution(16441952514936404522)
XLA Ops:
  28.1 49.7 %all-gather.8.cloned.1.call-done = bf16[1536,1536]{1,0:T(8,128)(2,1)} async-done(((bf16[48,1536]{1,0:T(8,128)(2,1)}), bf16[1536,1536]{1,0:T(8,128)(2,1)}) %all-gather.8.cloned.1.call-update) | async-done | bytes 4718608 | tf_op jit(solution)/shard_map/all_gather | solution.py:205
  77.9 9.0 reshape.949
  96.8 47.0 %all-gather.14.cloned.1.call-done = bf16[1536,1536]{1,0:T(8,128)(2,1)} async-done(((bf16[48,1536]{1,0:T(8,128)(2,1)}), bf16[1536,1536]{1,0:T(8,128)(2,1)}) %all-gather.14.cloned.1.call-update) | async-done | bytes 4718608 | tf_op jit(solution)/shard_map/all_gather | solution.py:205
  143.8 9.1 reshape.958
  218.4 9.6 all-gather.10.cloned.1.call-done
  228.0 21.6 %reshape.956 = bf16[2,768,2,1536]{3,2,1,0:T(2,128)(2,1)} reshape(bf16[1536,3072]{1,0:T(8,128)(2,1)} %all-gather.10.cloned.1.call-done) | data formatting | bytes 18874368 | tf_op jit(solution)/shard_map/reshape | solution.py:209
  249.6 19.1 %fusion.252 = (bf16[1,768,2,1536]{3,0,1,2:T(2,128)(2,1)}, bf16[1,768,2,1536]{3,0,1,2:T(2,128)(2,1)}) fusion(bf16[2,768,2,1536]{3,0,1,2:T(2,128)(2,1)} %bitcast.296), kind=kLoop, calls=%fused_computation.343 | loop fusion | bytes 18874368 | tf_op jit(solution)/shard_map/slice | solution.py:212
  268.7 22.5 %copy.172 = bf16[1,768,2,1536]{1,3,2,0:T(8,128)(2,1)} copy(bf16[1,768,2,1536]{3,0,1,2:T(2,128)(2,1)} %get-tuple-element.97) | data formatting | bytes 9437184 | tf_op jit(solution)/shard_map/slice | solution.py:212
  291.2 22.4 %copy.171 = bf16[1,768,2,1536]{1,3,2,0:T(8,128)(2,1)} copy(bf16[1,768,2,1536]{3,0,1,2:T(2,128)(2,1)} %get-tuple-element.98) | data formatting | bytes 9437184 | tf_op jit(solution)/shard_map/slice | solution.py:212
  313.7 21.6 %reshape.965 = bf16[2,768,2,1536]{3,2,1,0:T(2,128)(2,1)} reshape(bf16[1536,3072]{1,0:T(8,128)(2,1)} %all-gather.16.cloned.1.call-done) | data formatting | bytes 18874368 | tf_op jit(solution)/shard_map/reshape | solution.py:209
  335.2 19.2 %fusion.251 = (bf16[1,768,2,1536]{3,0,1,2:T(2,128)(2,1)}, bf16[1,768,2,1536]{3,0,1,2:T(2,128)(2,1)}) fusion(bf16[2,768,2,1536]{3,0,1,2:T(2,128)(2,1)} %bitcast.297), kind=kLoop, calls=%fused_computation.342 | loop fusion | bytes 18874368 | tf_op jit(solution)/shard_map/slice | solution.py:212
  354.4 22.4 %copy.180 = bf16[1,768,2,1536]{1,3,2,0:T(8,128)(2,1)} copy(bf16[1,768,2,1536]{3,0,1,2:T(2,128)(2,1)} %get-tuple-element.93) | data formatting | bytes 9437184 | tf_op jit(solution)/shard_map/slice | solution.py:212
  376.8 22.1 %copy.179 = bf16[1,768,2,1536]{1,3,2,0:T(8,128)(2,1)} copy(bf16[1,768,2,1536]{3,0,1,2:T(2,128)(2,1)} %get-tuple-element.94) | data formatting | bytes 9437184 | tf_op jit(solution)/shard_map/slice | solution.py:212
  398.9 11.6 multiply_convert_fusion.5
  410.6 10.0 fusion.267
  438.1 9.0 fusion.20
  465.0 15.3 multiply_convert_fusion.4
  493.8 14.8 convert_reduce_fusion
  533.6 20.2 %fusion.148 = bf16[12,64,512]{2,1,0:T(8,128)(2,1)} fusion(bf16[512,12,64]{0,2,1:T(8,128)(2,1)S(1)} %bitcast.353, f32[12,512,512]{1,2,0:T(8,128)} %fusion.271, f32[12,512,512]{1,2,0:T(8,128)} %get-tuple-element.153, f32[12,512]{1,0:T(8,128)S(1)} %log_add_fusion.1, pred[512,512]{0,1:T(8,128)(4,1)S(1)} %copy-done.14), kind=kOutput, calls=%fused_computation.183 | convolution fusion | flops 437656064 | bytes 27025408 | tf_op jit(solution)/shard_map/ghqk,gkhe->gqhe/dot_general | solution.py:76
  553.8 20.4 %fusion.151 = bf16[12,64,512]{2,1,0:T(8,128)(2,1)} fusion(bf16[512,12,64]{0,2,1:T(8,128)(2,1)S(1)} %bitcast.355, f32[12,512,512]{1,2,0:T(8,128)} %fusion.271, f32[12,512,512]{1,2,0:T(8,128)} %get-tuple-element.153, f32[12,512]{1,0:T(8,128)S(1)} %log_add_fusion.1, pred[512,512]{0,1:T(8,128)(4,1)S(1)} %copy-done.14), kind=kOutput, calls=%fused_computation.184 | convolution fusion | flops 437656064 | bytes 27025408 | tf_op jit(solution)/shard_map/ghqk,gqhe->gkhe/dot_general | solution.py:79
  587.9 20.4 %fusion.142 = bf16[12,64,512]{2,1,0:T(8,128)(2,1)} fusion(bf16[512,12,64]{0,2,1:T(8,128)(2,1)S(1)} %bitcast.349, f32[12,512,512]{1,2,0:T(8,128)} %fusion.272, f32[12,512,512]{1,2,0:T(8,128)} %copy-done.4, f32[12,512]{1,0:T(8,128)S(1)} %log_add_fusion, pred[512,512]{0,1:T(8,128)(4,1)S(1)} %compare_and_fusion), kind=kOutput, calls=%fused_computation.181 | convolution fusion | flops 437656064 | bytes 27025408 | tf_op jit(solution)/shard_map/ghqk,gkhe->gqhe/dot_general | solution.py:76
  608.3 20.9 %fusion.145 = bf16[12,64,512]{2,1,0:T(8,128)(2,1)} fusion(bf16[512,12,64]{0,2,1:T(8,128)(2,1)S(1)} %bitcast.351, f32[12,512,512]{1,2,0:T(8,128)} %fusion.272, f32[12,512,512]{1,2,0:T(8,128)} %copy-done.4, f32[12,512]{1,0:T(8,128)S(1)} %log_add_fusion, pred[512,512]{0,1:T(8,128)(4,1)S(1)} %compare_and_fusion), kind=kOutput, calls=%fused_computation.182 | convolution fusion | flops 437656064 | bytes 27025408 | tf_op jit(solution)/shard_map/ghqk,gqhe->gkhe/dot_general | solution.py:79
  643.3 9.9 multiply_reduce_fusion.5
  654.5 13.6 convert_reduce_fusion.1
  704.3 20.3 %fusion.160 = bf16[12,64,512]{2,1,0:T(8,128)(2,1)} fusion(bf16[512,12,64]{0,2,1:T(8,128)(2,1)S(1)} %bitcast.347, f32[12,512,512]{1,2,0:T(8,128)} %fusion.273, f32[12,512,512]{1,2,0:T(8,128)} %get-tuple-element.141, f32[12,512]{1,0:T(8,128)S(1)} %copy-done.71, pred[512,512]{0,1:T(8,128)(4,1)S(1)} %copy-done.15), kind=kOutput, calls=%fused_computation.187 | convolution fusion | flops 437656064 | bytes 27025408 | tf_op jit(solution)/shard_map/ghqk,gkhe->gqhe/dot_general | solution.py:76
  724.6 20.2 %fusion.154 = bf16[12,64,512]{2,1,0:T(8,128)(2,1)} fusion(bf16[512,12,64]{0,2,1:T(8,128)(2,1)S(1)} %bitcast.345, f32[12,512,512]{1,2,0:T(8,128)} %fusion.274, f32[12,512,512]{1,2,0:T(8,128)} %copy-done.2, f32[12,512]{1,0:T(8,128)S(1)} %copy-done.69, pred[512,512]{0,1:T(8,128)(4,1)S(1)} %compare_and_fusion), kind=kOutput, calls=%fused_computation.185 | convolution fusion | flops 437656064 | bytes 27025408 | tf_op jit(solution)/shard_map/ghqk,gkhe->gqhe/dot_general | solution.py:76
  753.6 20.8 %fusion.163 = bf16[12,64,512]{2,1,0:T(8,128)(2,1)} fusion(bf16[512,12,64]{0,2,1:T(8,128)(2,1)S(1)} %bitcast.343, f32[12,512,512]{1,2,0:T(8,128)} %fusion.273, f32[12,512,512]{1,2,0:T(8,128)} %get-tuple-element.141, f32[12,512]{1,0:T(8,128)S(1)} %copy-done.71, pred[512,512]{0,1:T(8,128)(4,1)S(1)} %copy-done.15), kind=kOutput, calls=%fused_computation.188 | convolution fusion | flops 437656064 | bytes 27025408 | tf_op jit(solution)/shard_map/ghqk,gqhe->gkhe/dot_general | solution.py:79
  777.9 19.6 %fusion.157 = bf16[12,64,512]{2,1,0:T(8,128)(2,1)S(1)} fusion(bf16[512,12,64]{0,2,1:T(8,128)(2,1)S(1)} %bitcast.341, f32[12,512,512]{1,2,0:T(8,128)} %fusion.274, f32[12,512,512]{1,2,0:T(8,128)} %copy-done.2, f32[12,512]{1,0:T(8,128)S(1)} %copy-done.69, pred[512,512]{0,1:T(8,128)(4,1)S(1)} %compare_and_fusion), kind=kOutput, calls=%fused_computation.186 | convolution fusion | flops 437656064 | bytes 27025408 | tf_op jit(solution)/shard_map/ghqk,gqhe->gkhe/dot_general | solution.py:79
  799.9 9.9 fusion.137
  886.3 9.6 convolution_convert_fusion
  895.9 11.8 stack.184
  907.7 9.9 convolution_convert_fusion.1
  917.6 11.8 stack.183
  929.4 8.9 copy.215
  938.3 35.4 %copy.216 = bf16[1,768,2,1536]{3,0,1,2:T(2,128)(2,1)S(1)} copy(bf16[1,768,2,1536]{3,2,1,0:T(2,128)(2,1)S(1)} %bitcast.313) | data formatting | bytes 9437184 | tf_op jit(solution)/shard_map/stack | solution.py:390
  973.7 23.2 %pad_maximum_fusion.1 = bf16[2,768,2,1536]{3,0,1,2:T(2,128)(2,1)} fusion(bf16[1,768,2,1536]{3,0,1,2:T(2,128)(2,1)S(1)} %copy.216, bf16[1,768,2,1536]{3,0,1,2:T(2,128)(2,1)S(1)} %copy.215), kind=kLoop, calls=%fused_computation.51 | loop fusion | flops 18874368 | bytes 18874368 | tf_op jit(solution)/shard_map/stack | solution.py:390
  996.9 9.8 copy.248
  1008.7 9.6 convolution_convert_fusion.2
  1018.2 11.8 stack.181
  1030.1 10.0 convolution_convert_fusion.3
  1040.1 11.7 stack.180
  1051.9 8.8 copy.213
  1060.8 35.4 %copy.214 = bf16[1,768,2,1536]{3,0,1,2:T(2,128)(2,1)S(1)} copy(bf16[1,768,2,1536]{3,2,1,0:T(2,128)(2,1)S(1)} %bitcast.315) | data formatting | bytes 9437184 | tf_op jit(solution)/shard_map/stack | solution.py:390
  1096.2 23.0 %pad_maximum_fusion = bf16[2,768,2,1536]{3,0,1,2:T(2,128)(2,1)} fusion(bf16[1,768,2,1536]{3,0,1,2:T(2,128)(2,1)S(1)} %copy.214, bf16[1,768,2,1536]{3,0,1,2:T(2,128)(2,1)S(1)} %copy.213), kind=kLoop, calls=%fused_computation.50 | loop fusion | flops 18874368 | bytes 18874368 | tf_op jit(solution)/shard_map/stack | solution.py:390
  1119.3 9.9 copy.247
  1138.0 98.3 %reduce-scatter.5.cloned.1.call-done = bf16[48,1536]{1,0:T(8,128)(2,1)} async-done(((bf16[1536,1536]{1,0:T(8,128)(2,1)}), bf16[48,1536]{1,0:T(8,128)(2,1)}) %reduce-scatter.5.cloned.1.call-update) | async-done | bytes 147472 | tf_op jit(solution)/shard_map/reduce_scatter | solution.py:220
  1239.2 137.8 %reduce-scatter.11.cloned.1.call-done = bf16[48,3072]{1,0:T(8,128)(2,1)} async-done(((bf16[1536,3072]{1,0:T(8,128)(2,1)}), bf16[48,3072]{1,0:T(8,128)(2,1)}) %reduce-scatter.11.cloned.1.call-update) | async-done | bytes 294928 | tf_op jit(solution)/shard_map/reduce_scatter | solution.py:220
  1382.0 136.2 %reduce-scatter.9.cloned.1.call-done = bf16[48,3072]{1,0:T(8,128)(2,1)} async-done(((bf16[1536,3072]{1,0:T(8,128)(2,1)}), bf16[48,3072]{1,0:T(8,128)(2,1)}) %reduce-scatter.9.cloned.1.call-update) | async-done | bytes 294928 | tf_op jit(solution)/shard_map/reduce_scatter | solution.py:220
  (482 shorter events, 355.6 us)
Async XLA Ops:
  7.2 17.9 %copy-start = (s32[4,4]{1,0:T(4,128)S(1)}, s32[4,4]{1,0:T(4,128)}, u32[]{:S(2)}) copy-start(s32[4,4]{1,0:T(4,128)} %param.16) | copy-start | bytes 196
  7.2 18.0 %copy-start.86 = (f32[2,2,768]{2,1,0:T(2,128)S(1)}, f32[2,2,768]{2,1,0:T(2,128)}, u32[]{:S(2)}) copy-start(f32[2,2,768]{2,1,0:T(2,128)} %param.23) | copy-start | bytes 36868
  7.2 18.8 %copy-start.87 = (f32[2,2,768]{2,1,0:T(2,128)S(1)}, f32[2,2,768]{2,1,0:T(2,128)}, u32[]{:S(2)}) copy-start(f32[2,2,768]{2,1,0:T(2,128)} %param.25) | copy-start | bytes 36868
  7.2 18.8 %copy-start.88 = (f32[2,2,768]{2,1,0:T(2,128)S(1)}, f32[2,2,768]{2,1,0:T(2,128)}, u32[]{:S(2)}) copy-start(f32[2,2,768]{2,1,0:T(2,128)} %param.24) | copy-start | bytes 36868
  7.3 70.6 %all-gather.8.cloned.1.call-start = ((), (), s32[]{:S(2)}) async-start(), calls=%async_computation.4 | async-start | bytes 4866048 | tf_op jit(solution)/shard_map/all_gather | solution.py:205
  9.8 134.0 %all-gather.14.cloned.1.call-start = ((), (), s32[]{:S(2)}) async-start(), calls=%async_computation.7 | async-start | bytes 4866048 | tf_op jit(solution)/shard_map/all_gather | solution.py:205
  10.6 217.5 %all-gather.10.cloned.1.call-start = ((), (), s32[]{:S(2)}) async-start(), calls=%async_computation.5 | async-start | bytes 9732096 | tf_op jit(solution)/shard_map/all_gather | solution.py:206
  12.5 301.1 %all-gather.16.cloned.1.call-start = ((), (), s32[]{:S(2)}) async-start(), calls=%async_computation.8 | async-start | bytes 9732096 | tf_op jit(solution)/shard_map/all_gather | solution.py:206
  13.4 1115.8 %all-reduce.3.cloned.1.call-start = ((), (), s32[]{:S(2)}) async-start(), calls=%async_computation.15 | async-start | bytes 147456 | tf_op jit(solution)/shard_map/psum | solution.py:396
  26.7 383.8 %copy-start.74 = (f32[768]{0:T(1024)}, f32[768]{0:T(1024)S(1)}, u32[]{:S(2)}) copy-start(f32[768]{0:T(1024)S(1)} %get-tuple-element.172) | copy-start | bytes 9220
  26.7 383.8 %copy-start.98 = (f32[768]{0:T(1024)}, f32[768]{0:T(1024)S(1)}, u32[]{:S(2)}) copy-start(f32[768]{0:T(1024)S(1)} %get-tuple-element.70) | copy-start | bytes 9220
  26.7 394.4 %copy-start.59 = (f32[768]{0:T(1024)}, f32[768]{0:T(1024)S(1)}, u32[]{:S(2)}) copy-start(f32[768]{0:T(1024)S(1)} %get-tuple-element.173) | copy-start | bytes 9220
  27.2 184.6 %copy-start.13 = (pred[512,512]{0,1:T(8,128)(4,1)}, pred[512,512]{0,1:T(8,128)(4,1)S(1)}, u32[]{:S(2)}) copy-start(pred[512,512]{0,1:T(8,128)(4,1)S(1)} %compare_and_fusion.1) | copy-start | bytes 786436
  28.1 370.8 %copy-start.93 = (f32[1,3072]{1,0:T(1,128)}, f32[1,3072]{1,0:T(1,128)S(1)}, u32[]{:S(2)}) copy-start(f32[1,3072]{1,0:T(1,128)S(1)} %get-tuple-element.131) | copy-start | bytes 36868
  190.7 17.2 %copy-start.2 = (f32[12,512,512]{1,2,0:T(8,128)}, f32[12,512,512]{1,2,0:T(8,128)S(1)}, u32[]{:S(2)}) copy-start(f32[12,512,512]{1,2,0:T(8,128)S(1)} %get-tuple-element.139) | copy-start | bytes 37748740
  193.3 14.5 copy-start.68
  217.9 192.7 %copy-start.8 = (f32[1024,768]{1,0:T(8,128)}, f32[1024,768]{1,0:T(8,128)S(1)}, u32[]{:S(2)}) copy-start(f32[1024,768]{1,0:T(8,128)S(1)} %get-tuple-element.143) | copy-start | bytes 9437188
  217.9 192.7 %copy-start.61 = (f32[1024]{0:T(1024)}, f32[1024]{0:T(1024)S(1)}, u32[]{:S(2)}) copy-start(f32[1024]{0:T(1024)S(1)} %broadcast_multiply_fusion.11) | copy-start | bytes 12292
  218.4 192.1 %copy-start.79 = (f32[1024]{0:T(1024)}, f32[1024]{0:T(1024)S(1)}, u32[]{:S(2)}) copy-start(f32[1024]{0:T(1024)S(1)} %add_rsqrt_fusion.3) | copy-start | bytes 12292
  422.8 39.7 %copy-start.16 = (bf16[1024,768]{1,0:T(8,128)(2,1)}, bf16[1024,768]{1,0:T(8,128)(2,1)S(1)}, u32[]{:S(2)}) copy-start(bf16[1024,768]{1,0:T(8,128)(2,1)S(1)} %add_convert_fusion.2) | copy-start | bytes 4718596
  435.3 19.0 %copy-start.4 = (f32[12,512,512]{1,2,0:T(8,128)}, f32[12,512,512]{1,2,0:T(8,128)S(1)}, u32[]{:S(2)}) copy-start(f32[12,512,512]{1,2,0:T(8,128)S(1)} %get-tuple-element.151) | copy-start | bytes 37748740
  464.3 52.5 %copy-start.11 = (f32[1024,768]{1,0:T(8,128)}, f32[1024,768]{1,0:T(8,128)S(1)}, u32[]{:S(2)}) copy-start(f32[1024,768]{1,0:T(8,128)S(1)} %get-tuple-element.155) | copy-start | bytes 9437188
  464.3 52.5 %copy-start.64 = (f32[1024]{0:T(1024)}, f32[1024]{0:T(1024)S(1)}, u32[]{:S(2)}) copy-start(f32[1024]{0:T(1024)S(1)} %broadcast_multiply_fusion.9) | copy-start | bytes 12292
  464.3 16.0 %slice-start.17 = ((s8[4718592]{0:T(1024)(128)(4,1)}), s8[4194304]{0:T(1024)(128)(4,1)S(1)}, s32[]{:S(2)}) async-start(s8[4718592]{0:T(1024)(128)(4,1)} %bitcast.330), calls=%async_computation.33 | async-start | bytes 8388608
  464.9 52.0 %copy-start.82 = (f32[1024]{0:T(1024)}, f32[1024]{0:T(1024)S(1)}, u32[]{:S(2)}) copy-start(f32[1024]{0:T(1024)S(1)} %add_rsqrt_fusion.1) | copy-start | bytes 12292
  465.0 15.4 slice-start.18
  465.0 15.4 copy-start.102
  493.8 14.8 copy-start.29
  533.6 20.2 %copy-start.28 = (bf16[512,768]{0,1:T(8,128)(2,1)S(1)}, bf16[512,768]{0,1:T(8,128)(2,1)}, u32[]{:S(2)}) copy-start(bf16[512,768]{0,1:T(8,128)(2,1)} %get-tuple-element.110) | copy-start | bytes 2359300
  553.8 20.4 %copy-start.46 = (bf16[512,768]{0,1:T(8,128)(2,1)S(1)}, bf16[512,768]{0,1:T(8,128)(2,1)}, u32[]{:S(2)}) copy-start(bf16[512,768]{0,1:T(8,128)(2,1)} %get-tuple-element.109) | copy-start | bytes 2359300
  587.9 20.4 %copy-start.26 = (bf16[512,768]{0,1:T(8,128)(2,1)S(1)}, bf16[512,768]{0,1:T(8,128)(2,1)}, u32[]{:S(2)}) copy-start(bf16[512,768]{0,1:T(8,128)(2,1)} %copy-done.25) | copy-start | bytes 2359300
  629.2 14.1 copy-start.7
  653.3 14.9 slice-start.13
  704.3 20.3 %copy-start.22 = (bf16[1,512,768]{1,2,0:T(8,128)(2,1)S(1)}, bf16[1,512,768]{1,2,0:T(8,128)(2,1)}, u32[]{:S(2)}) copy-start(bf16[1,512,768]{1,2,0:T(8,128)(2,1)} %copy-done.21) | copy-start | bytes 2359300
  724.6 22.1 %copy-start.96 = (f32[3072]{0:T(1024)S(1)}, f32[3072]{0:T(1024)}, u32[]{:S(2)}) copy-start(f32[3072]{0:T(1024)} %get-tuple-element.163) | copy-start | bytes 36868
  749.8 381.9 %all-gather.12.cloned.1.call-start = ((), (), s32[]{:S(2)}) async-start(), calls=%async_computation.6 | async-start | bytes 4718592 | tf_op jit(solution)/shard_map/all_gather | solution.py:382
  750.4 381.4 %all-gather.18.cloned.1.call-start = ((), (), s32[]{:S(2)}) async-start(), calls=%async_computation.9 | async-start | bytes 4718592 | tf_op jit(solution)/shard_map/all_gather | solution.py:382
  751.2 380.6 %all-gather.20.cloned.1.call-start = ((), (), s32[]{:S(2)}) async-start(), calls=%async_computation.10 | async-start | bytes 4718592 | tf_op jit(solution)/shard_map/all_gather | solution.py:395
  753.5 23.1 %copy-start.45 = (bf16[12,64,512]{2,1,0:T(8,128)(2,1)S(1)}, bf16[12,64,512]{2,1,0:T(8,128)(2,1)}, u32[]{:S(2)}) copy-start(bf16[12,64,512]{2,1,0:T(8,128)(2,1)} %fusion.160) | copy-start | bytes 2359300
  753.5 24.4 %copy-start.18 = (bf16[512,768]{0,1:T(8,128)(2,1)S(1)}, bf16[512,768]{0,1:T(8,128)(2,1)}, u32[]{:S(2)}) copy-start(bf16[512,768]{0,1:T(8,128)(2,1)} %copy-done.17) | copy-start | bytes 2359300
  777.9 20.8 %copy-start.41 = (bf16[12,64,512]{2,1,0:T(8,128)(2,1)S(1)}, bf16[12,64,512]{2,1,0:T(8,128)(2,1)}, u32[]{:S(2)}) copy-start(bf16[12,64,512]{2,1,0:T(8,128)(2,1)} %fusion.154) | copy-start | bytes 2359300
  809.8 327.1 %reduce-scatter.7.cloned.1.call-start = ((), (), s32[]{:S(2)}) async-start(), calls=%async_computation.12 | async-start | bytes 4866048 | tf_op jit(solution)/shard_map/reduce_scatter | solution.py:220
  846.4 389.9 %reduce-scatter.5.cloned.1.call-start = ((), (), s32[]{:S(2)}) async-start(), calls=%async_computation.11 | async-start | bytes 4866048 | tf_op jit(solution)/shard_map/reduce_scatter | solution.py:220
  884.4 492.7 %reduce-scatter.11.cloned.1.call-start = ((), (), s32[]{:S(2)}) async-start(), calls=%async_computation.14 | async-start | bytes 9732096 | tf_op jit(solution)/shard_map/reduce_scatter | solution.py:220
  917.6 20.7 %slice-start.9 = ((s8[4718592]{0:T(1024)(128)(4,1)}), s8[524288]{0:T(1024)(128)(4,1)S(1)}, s32[]{:S(2)}) async-start(s8[4718592]{0:T(1024)(128)(4,1)} %bitcast.312), calls=%async_computation.25 | async-start | bytes 1048576
  1006.8 511.4 %reduce-scatter.9.cloned.1.call-start = ((), (), s32[]{:S(2)}) async-start(), calls=%async_computation.13 | async-start | bytes 9732096 | tf_op jit(solution)/shard_map/reduce_scatter | solution.py:220
  1040.1 20.6 %slice-start.11 = ((s8[4718592]{0:T(1024)(128)(4,1)}), s8[524288]{0:T(1024)(128)(4,1)S(1)}, s32[]{:S(2)}) async-start(s8[4718592]{0:T(1024)(128)(4,1)} %bitcast.314), calls=%async_computation.27 | async-start | bytes 1048576
  1238.4 287.9 %copy-start.36 = (bf16[2048,768]{1,0:T(8,128)(2,1)S(1)}, bf16[2048,768]{1,0:T(8,128)(2,1)}, u32[]{:S(2)}) copy-start(bf16[2048,768]{1,0:T(8,128)(2,1)} %all-gather.12.cloned.1.call-done) | copy-start | bytes 9437188
  (95 other events, 620.7 us)
Sparse Core Ops, SparseCore 0:
  11.5 66.2 all-gather.7
  81.3 62.3 all-gather.13
  147.2 80.7 all-gather.9
  231.3 80.6 all-gather.15
  750.0 119.1 all-reduce.2
  870.6 47.9 all-gather.11
  920.1 44.9 all-gather.17
  966.6 44.9 all-gather.19
  1017.1 106.9 reduce-scatter.6
  1130.3 105.9 reduce-scatter.4
  1242.2 134.7 reduce-scatter.10
  1383.8 134.2 reduce-scatter.8

commit v2 on v1

v2 whole, which is shorter than its diff:
```python
import functools

import jax
import jax.numpy as jnp
from jax import lax
from jax.experimental import pallas as pl
from jax.experimental.pallas import tpu as pltpu
from jax.sharding import PartitionSpec as P

HEAD_DIM = 64
PAIR = 2 * HEAD_DIM
AXES = ("tensor", "dp")
CORE = ("dp", 1)
FFN_PARTS = 3
ROW_TILE = 256
TILE_ROWS = 16
PLANNED_BLOCKS = 16
VMEM_LIMIT = 58 * 1024 * 1024

norm_eps = 1e-06
big_negative = -1e30
inv_root_tau = 0.3989422804014327
log2_e = 1.4426950408889634
score_scale = HEAD_DIM ** (-0.5)
exponent_scale = score_scale * log2_e
erf_slope = 0.3275911 * 0.7071067811865476
erf_terms = (1.061405429, -1.453152027, 1.421413741, -0.284496736, 0.254829592)


def dot_nn(left, right):
    return lax.dot_general(
        left, right, (((1,), (0,)), ((), ())), preferred_element_type=jnp.float32
    )


def dot_nt(left, right):
    return lax.dot_general(
        left, right, (((1,), (1,)), ((), ())), preferred_element_type=jnp.float32
    )


def flipped(member):
    return member.astype(jnp.float32).T


def hop_orders(block_count):
    bits = []
    bit = block_count // 2
    while bit > 1:
        bits.append(("dp", bit))
        bit //= 2
    return (bits + [("tensor", 1)], bits[:-1] + [("tensor", 1), bits[-1]])


def slot_table(order):
    table = []
    for slot in range(2 ** len(order)):
        dp_part, tensor_part = 0, 0
        for position, (axis, bit) in enumerate(order):
            if slot >> position & 1:
                if axis == "dp":
                    dp_part ^= bit
                else:
                    tensor_part ^= bit
        table.append((dp_part, tensor_part))
    return table


def hop(member, dim):
    axis, bit = dim
    pairs = [(place, place ^ bit) for place in range(lax.axis_size(axis))]
    return lax.ppermute(member, axis, pairs)


def gather_piece(shard, order):
    current = shard[None]
    for dim in order[:-1]:
        current = jnp.concatenate([current, hop(current, dim)], axis=0)
    later = hop(current, order[-1])
    return (current, later, hop(current, CORE), hop(later, CORE))


def scatter_piece(keep, send, order):
    parts = [keep, hop(send, CORE)]
    for dim in reversed(order):
        half = parts[0].shape[0] // 2
        upper = sum(part[half:].astype(jnp.float32) for part in parts).astype(jnp.bfloat16)
        parts = [part[:half] for part in parts] + [hop(upper, dim)]
    return sum(part[0].astype(jnp.float32) for part in parts)


def gather_whole(shard, order):
    whole = lax.all_gather(shard, AXES, tiled=True)
    columns = shard.shape[1]
    split = lax.axis_size("tensor")
    blocks = whole.reshape(split, PLANNED_BLOCKS, -1, columns)
    half = 2 ** (len(order) - 1)
    table = slot_table(order)
    return tuple(
        jnp.stack(
            [blocks[tensor_part, dp_part ^ core] for dp_part, tensor_part in table[part * half :][:half]]
        )
        for core in range(2)
        for part in range(2)
    )


def scatter_whole(keep, send, order):
    split = lax.axis_size("tensor")
    placed = {}
    for slot, (dp_part, tensor_part) in enumerate(slot_table(order)):
        placed[tensor_part, dp_part] = keep[slot]
        placed[tensor_part, dp_part ^ 1] = send[slot]
    whole = jnp.stack(
        [placed[half, block] for half in range(split) for block in range(PLANNED_BLOCKS)]
    )
    whole = whole.reshape(-1, keep.shape[2])
    return lax.psum_scatter(whole, AXES, scatter_dimension=0, tiled=True).astype(jnp.float32)


def load_blocks(meta, sources, order, target, columns, source_columns, sems):
    table = slot_table(order)
    half = len(table) // 2
    block_rows = sources[0].shape[1]
    for slot, (dp_part, tensor_part) in enumerate(table):
        for core in range(2):
            source = sources[2 * core + slot // half]
            place = meta[0] ^ (dp_part ^ core)
            half_at = meta[1] ^ tensor_part
            rows = pl.ds(pl.multiple_of(place * block_rows, TILE_ROWS), block_rows)
            pltpu.make_async_copy(
                source.at[slot % half, :, source_columns],
                target.at[half_at, rows, columns],
                sems.at[half_at],
            ).start()


def await_blocks(target, half_at, columns, sems):
    view = target.at[half_at, :, columns]
    pltpu.make_async_copy(view, view, sems.at[half_at]).wait()


def store_blocks(meta, source, targets, order, relative_half, columns, sem):
    block_rows = targets[0].shape[1]
    tensor_weight = 2 ** order.index(("tensor", 1))
    for slot, (dp_part, tensor_part) in enumerate(slot_table(order)):
        if tensor_part:
            continue
        for core in range(2):
            place = meta[0] ^ (dp_part ^ core)
            rows = pl.ds(pl.multiple_of(place * block_rows, TILE_ROWS), block_rows)
            pltpu.make_async_copy(
                source.at[rows, :],
                targets[core].at[slot + tensor_weight * relative_half, :, columns],
                sem,
            ).start()


def await_stored(source, sem):
    pltpu.make_async_copy(source, source, sem).wait()


def norm_stats(residual):
    centered = residual - jnp.mean(residual, axis=-1, keepdims=True)
    inv_spread = lax.rsqrt(jnp.mean(centered * centered, axis=-1, keepdims=True) + norm_eps)
    return centered * inv_spread, inv_spread


def norm_back(gradient, normed, inv_spread, gain):
    scaled = gradient * gain
    inner = jnp.mean(scaled * normed, axis=-1, keepdims=True)
    return inv_spread * (scaled - jnp.mean(scaled, axis=-1, keepdims=True) - normed * inner)


def row_tiles(row_count):
    tile = min(ROW_TILE, row_count)
    return [slice(start, start + tile) for start in range(0, row_count, tile)]


def column_sum(member):
    return jnp.sum(member, axis=0, keepdims=True)


def gelu_parts(inputs):
    bell = jnp.exp(-0.5 * inputs * inputs)
    ratio = 1.0 / (1.0 + erf_slope * jnp.abs(inputs))
    series = 0.5 * erf_terms[0]
    for term in erf_terms[1:]:
        series = series * ratio + 0.5 * term
    tail = series * ratio * bell
    below = jnp.where(inputs < 0, tail, 1.0 - tail)
    return inputs * below, below + inputs * (bell * inv_root_tau)


def qkv_forward_kernel(orders, meta, inputs, bias, *refs):
    qk_sources, vo_sources, out, weights, qk_sems, v_sems = (
        refs[0:4], refs[4:8], refs[8], refs[9], refs[10], refs[11],
    )
    step = pl.program_id(0)
    columns = out.shape[2]

    @pl.when(step == 0)
    def _():
        load_blocks(
            meta, qk_sources, orders[0], weights, slice(0, 2 * columns), slice(None), qk_sems
        )
        load_blocks(
            meta, vo_sources, orders[1], weights, slice(2 * columns, 3 * columns),
            slice(0, columns), v_sems,
        )

    half_at = meta[1] ^ (step // 3)

    @pl.when(step % 3 == 0)
    def _():
        await_blocks(weights, half_at, slice(0, 2 * columns), qk_sems)
        await_blocks(weights, half_at, slice(2 * columns, 3 * columns), v_sems)

    which = pl.ds(pl.multiple_of((step % 3) * columns, 128), columns)
    for rows in row_tiles(inputs.shape[0]):
        out[0, rows, :] = (dot_nn(inputs[rows, :], weights[half_at, :, which]) + bias[0]).astype(
            jnp.bfloat16
        )


def slab_features(meta, slab, slab_rows, k_side, q_side):
    segment_rows = slab_rows // 4
    row = lax.broadcasted_iota(jnp.int32, (slab_rows, PAIR), 0)
    lane = lax.broadcasted_iota(jnp.int32, (slab_rows, PAIR), 1) & (HEAD_DIM - 1)
    short = meta[2 + slab] == 0
    segment = jnp.where(short, row // segment_rows, 0)
    offset = row - segment * segment_rows
    base = 2 + meta_slabs(meta) + 4 * slab
    length = jnp.where(
        segment == 0,
        meta[base],
        jnp.where(segment == 1, meta[base + 1], jnp.where(segment == 2, meta[base + 2], meta[base + 3])),
    )
    same = segment == lane
    k_value = jnp.where(lane < 4, jnp.where(same, 1.0, 0.0), jnp.where(offset >= length, 1.0, 0.0))
    q_value = jnp.where(lane < 4, jnp.where(same, 0.0, big_negative), big_negative)
    k_side[slab] = jnp.where(lane < 5, k_value, 0.0).astype(jnp.bfloat16)
    q_side[slab] = jnp.where(lane < 5, q_value, 0.0).astype(jnp.bfloat16)


def meta_slabs(meta):
    return (meta.shape[0] - 2) // 5


def lane_low(row_count):
    return lax.broadcasted_iota(jnp.int32, (row_count, PAIR), 1) < HEAD_DIM


def attention_forward_kernel(meta, qkv, mixed, logsum, k_side, q_side):
    slab, pair = pl.program_id(1), pl.program_id(0)
    slab_rows = qkv.shape[1]

    @pl.when(pair == 0)
    def _():
        slab_features(meta, slab, slab_rows, k_side, q_side)

    low = lane_low(slab_rows)
    query, key = qkv[0].astype(jnp.float32), qkv[1].astype(jnp.float32)
    k_extra, q_extra = k_side[slab].astype(jnp.float32), q_side[slab].astype(jnp.float32)
    value_flip = flipped(qkv[2])
    sub = lax.broadcasted_iota(jnp.int32, (PAIR, slab_rows), 0)
    outcomes = []
    for head in range(2):
        mine = low if head == 0 else jnp.logical_not(low)
        q_head = jnp.where(mine, query, q_extra).astype(jnp.bfloat16)
        k_head = jnp.where(mine, key, k_extra).astype(jnp.bfloat16)
        scores = dot_nt(k_head, q_head)
        top = jnp.max(scores, axis=0, keepdims=True)
        weight = jnp.exp2((scores - top) * exponent_scale).astype(jnp.bfloat16)
        sum_row = HEAD_DIM if head == 0 else 0
        kept = sub < HEAD_DIM if head == 0 else sub >= HEAD_DIM
        v_head = jnp.where(kept, value_flip, jnp.where(sub == sum_row, 1.0, 0.0))
        blend = dot_nn(v_head.astype(jnp.bfloat16), weight)
        total = blend[sum_row : sum_row + 1, :]
        logsum[0, 0, head : head + 1, :] = top * exponent_scale + jnp.log(total) * log2_e
        outcomes.append(blend / total)
    mixed[...] = jnp.where(sub < HEAD_DIM, outcomes[0], outcomes[1]).T.astype(jnp.bfloat16)


def ffn_forward_kernel(orders, meta, mixed, inputs, vectors, ffn_bias, *refs):
    vo_sources, in_sources, down_sources = refs[0:4], refs[4:8], refs[8:12]
    hidden, normed_one, spread_one, activated, slope, result, normed_two, spread_two = refs[12:20]
    out_whole, in_whole, down_whole, total, out_sems, in_sems, down_sems = refs[20:]
    step = pl.program_id(0)
    steps = pl.num_programs(0)
    everything = slice(None)
    out_columns = out_whole.shape[2]
    tiles = row_tiles(inputs.shape[0])
    lanes = spread_one.shape[1]

    @pl.when(step == 0)
    def _():
        load_blocks(
            meta, vo_sources, orders[1], out_whole, everything,
            slice(out_columns, 2 * out_columns), out_sems,
        )
        load_blocks(meta, in_sources, orders[0], in_whole, everything, everything, in_sems)
        load_blocks(meta, down_sources, orders[1], down_whole, everything, everything, down_sems)
        for half_at in range(2):
            await_blocks(out_whole, half_at, everything, out_sems)
        for rows in tiles:
            attention_out = vectors[0:1, :]
            for half_at in range(2):
                columns = slice(half_at * out_columns, (half_at + 1) * out_columns)
                attention_out = attention_out + dot_nt(mixed[rows, columns], out_whole[half_at])
            normed, spread = norm_stats(inputs[rows, :].astype(jnp.float32) + attention_out)
            low = (normed * vectors[2:3, :] + vectors[4:5, :]).astype(jnp.bfloat16)
            hidden[rows, :] = low
            normed_one[rows, :] = normed.astype(jnp.bfloat16)
            spread_one[rows, :] = jnp.broadcast_to(spread, (spread.shape[0], lanes))
            total[rows, :] = low.astype(jnp.float32) + vectors[1:2, :]

    half_at = meta[1] ^ (step // FFN_PARTS)
    width = activated.shape[1]
    part = pl.ds(pl.multiple_of((step % FFN_PARTS) * width, 128), width)

    @pl.when(step % FFN_PARTS == 0)
    def _():
        await_blocks(in_whole, half_at, everything, in_sems)
        await_blocks(down_whole, half_at, everything, down_sems)

    for rows in tiles:
        pre_gelu = dot_nn(hidden[rows, :], in_whole[half_at, :, part]) + ffn_bias[0]
        value, steep = gelu_parts(pre_gelu)
        low = value.astype(jnp.bfloat16)
        activated[rows, :] = low
        slope[rows, :] = steep.astype(jnp.bfloat16)
        total[rows, :] += dot_nt(low, down_whole[half_at, :, part])

    @pl.when(step == steps - 1)
    def _():
        for rows in tiles:
            normed, spread = norm_stats(total[rows, :])
            result[rows, :] = (normed * vectors[3:4, :] + vectors[5:6, :]).astype(jnp.bfloat16)
            normed_two[rows, :] = normed.astype(jnp.bfloat16)
            spread_two[rows, :] = jnp.broadcast_to(spread, (spread.shape[0], lanes))


def ffn_backward_kernel(
    orders, meta, gradient, normed_two, spread_two, hidden, normed_one, spread_one, activated,
    slope, vectors, *refs
):
    in_sources, down_sources = refs[0:4], refs[4:8]
    attention_grad, resid_grad, sums, bias_sums = refs[8:12]
    in_targets, down_targets = refs[12:14], refs[14:16]
    (
        in_whole, down_whole, total, branch, branch_flip, hidden_flip, pre_part, grad_parts,
        in_sems, down_sems, out_sems,
    ) = refs[16:]
    step = pl.program_id(0)
    steps = pl.num_programs(0)
    everything = slice(None)
    tiles = row_tiles(hidden.shape[0])
    slot = step % 2

    @pl.when(step == 0)
    def _():
        load_blocks(meta, in_sources, orders[0], in_whole, everything, everything, in_sems)
        load_blocks(meta, down_sources, orders[1], down_whole, everything, everything, down_sems)
        gain_sum, shift_sum, branch_sum = 0.0, 0.0, 0.0
        for rows in tiles:
            grad = gradient[rows, :].astype(jnp.float32)
            normed = normed_two[rows, :].astype(jnp.float32)
            resid = norm_back(grad, normed, spread_two[rows, 0:1], vectors[3:4, :])
            low = resid.astype(jnp.bfloat16)
            total[rows, :] = resid
            branch[rows, :] = low
            branch_flip[:, rows] = flipped(low).astype(jnp.bfloat16)
            hidden_flip[:, rows] = flipped(hidden[rows, :]).astype(jnp.bfloat16)
            gain_sum += column_sum(grad * normed)
            shift_sum += column_sum(grad)
            branch_sum += column_sum(low.astype(jnp.float32))
        sums[...] = jnp.zeros(sums.shape, jnp.float32)
        sums[1:2, :] = branch_sum
        sums[3:4, :] = gain_sum
        sums[5:6, :] = shift_sum

    half_at = meta[1] ^ (step // FFN_PARTS)
    width = activated.shape[1]
    part = pl.ds(pl.multiple_of((step % FFN_PARTS) * width, 128), width)

    @pl.when(step % FFN_PARTS == 0)
    def _():
        await_blocks(in_whole, half_at, everything, in_sems)
        await_blocks(down_whole, half_at, everything, down_sems)

    @pl.when(step >= 2)
    def _():
        await_stored(grad_parts.at[slot, 0], out_sems.at[slot, 0])
        await_stored(grad_parts.at[slot, 1], out_sems.at[slot, 1])

    grad_parts[slot, 1] = dot_nn(branch_flip[...], activated[...]).astype(jnp.bfloat16)
    store_blocks(
        meta, grad_parts.at[slot, 1], down_targets, orders[1], step // FFN_PARTS, part,
        out_sems.at[slot, 1],
    )
    bias_sum = 0.0
    for rows in tiles:
        active_grad = dot_nn(branch[rows, :], down_whole[half_at, :, part])
        low = (active_grad * slope[rows, :].astype(jnp.float32)).astype(jnp.bfloat16)
        pre_part[rows, :] = low
        bias_sum += column_sum(low.astype(jnp.float32))
        total[rows, :] += dot_nt(low, in_whole[half_at, :, part])
    bias_sums[0] = bias_sum
    grad_parts[slot, 0] = dot_nn(hidden_flip[...], pre_part[...]).astype(jnp.bfloat16)
    store_blocks(
        meta, grad_parts.at[slot, 0], in_targets, orders[0], step // FFN_PARTS, part,
        out_sems.at[slot, 0],
    )

    @pl.when(step == steps - 1)
    def _():
        gain_sum, shift_sum, branch_sum = 0.0, 0.0, 0.0
        for rows in tiles:
            grad = total[rows, :]
            normed = normed_one[rows, :].astype(jnp.float32)
            resid = norm_back(grad, normed, spread_one[rows, 0:1], vectors[2:3, :])
            low = resid.astype(jnp.bfloat16)
            resid_grad[rows, :] = resid
            attention_grad[rows, :] = low
            gain_sum += column_sum(grad * normed)
            shift_sum += column_sum(grad)
            branch_sum += column_sum(low.astype(jnp.float32))
        sums[0:1, :] = branch_sum
        sums[2:3, :] = gain_sum
        sums[4:5, :] = shift_sum
        for late in range(2):
            await_stored(grad_parts.at[late, 0], out_sems.at[late, 0])
            await_stored(grad_parts.at[late, 1], out_sems.at[late, 1])


def out_backward_kernel(orders, meta, attention_grad, mixed, *refs):
    vo_sources, mixed_grad, out_targets = refs[0:4], refs[4], refs[5:7]
    out_whole, grad_flip, grad_parts, load_sems, out_sems = refs[7:]
    step = pl.program_id(0)
    columns = mixed.shape[1]
    everything = slice(None)
    tiles = row_tiles(mixed.shape[0])

    @pl.when(step == 0)
    def _():
        load_blocks(
            meta, vo_sources, orders[1], out_whole, everything, slice(columns, 2 * columns), load_sems
        )
        for rows in tiles:
            grad_flip[:, rows] = flipped(attention_grad[rows, :]).astype(jnp.bfloat16)

    half_at = meta[1] ^ step
    grad_parts[step] = dot_nn(grad_flip[...], mixed[...]).astype(jnp.bfloat16)
    store_blocks(
        meta, grad_parts.at[step], out_targets, orders[0], step, everything, out_sems.at[step]
    )
    await_blocks(out_whole, half_at, everything, load_sems)
    for rows in tiles:
        mixed_grad[rows, :] = dot_nn(attention_grad[rows, :], out_whole[half_at]).astype(
            jnp.bfloat16
        )

    @pl.when(step == 1)
    def _():
        for late in range(2):
            await_stored(grad_parts.at[late], out_sems.at[late])


def attention_backward_kernel(meta, qkv, mixed, mixed_grad, logsum, grads, sums, k_side, q_side):
    slab, pair = pl.program_id(1), pl.program_id(0)
    slab_rows = qkv.shape[1]

    @pl.when(pair == 0)
    def _():
        slab_features(meta, slab, slab_rows, k_side, q_side)

    low = lane_low(slab_rows)
    query, key, value = (qkv[place].astype(jnp.float32) for place in range(3))
    k_extra, q_extra = k_side[slab].astype(jnp.float32), q_side[slab].astype(jnp.float32)
    grad_low = mixed_grad[...]
    grad = grad_low.astype(jnp.float32)
    product = (grad * mixed[...].astype(jnp.float32)).T
    key_flip = key.T
    sub = lax.broadcasted_iota(jnp.int32, (PAIR, slab_rows), 0)
    query_flip, key_grad, value_grad = 0.0, 0.0, 0.0
    for head in range(2):
        mine = low if head == 0 else jnp.logical_not(low)
        kept = sub < HEAD_DIM if head == 0 else sub >= HEAD_DIM
        span = slice(head * HEAD_DIM, (head + 1) * HEAD_DIM)
        q_head = jnp.where(mine, query, q_extra).astype(jnp.bfloat16)
        k_head = jnp.where(mine, key, k_extra).astype(jnp.bfloat16)
        v_head = jnp.where(mine, value, 0.0).astype(jnp.bfloat16)
        probs = jnp.exp2(
            dot_nt(k_head, q_head) * exponent_scale - logsum[0, 0, head : head + 1, :]
        )
        delta = column_sum(product[span, :])
        raw_grad = (probs * (dot_nt(v_head, grad_low) - delta)).astype(jnp.bfloat16)
        g_head = jnp.where(mine, grad, 0.0).astype(jnp.bfloat16)
        value_grad += dot_nn(probs.astype(jnp.bfloat16), g_head)
        key_grad += dot_nn(raw_grad, jnp.where(mine, query, 0.0).astype(jnp.bfloat16))
        query_flip += dot_nn(jnp.where(kept, key_flip, 0.0).astype(jnp.bfloat16), raw_grad)
    query_low = (query_flip * score_scale).T.astype(jnp.bfloat16)
    value_low = value_grad.astype(jnp.bfloat16)
    grads[0] = query_low
    grads[1] = (key_grad * score_scale).astype(jnp.bfloat16)
    grads[2] = value_low

    @pl.when(slab == 0)
    def _():
        sums[...] = jnp.zeros(sums.shape, jnp.float32)

    sums[0:1, :] += column_sum(query_low.astype(jnp.float32))
    sums[1:2, :] += column_sum(value_low.astype(jnp.float32))


def qkv_backward_kernel(orders, meta, inputs, grads, resid_grad, *refs):
    qk_sources, vo_sources, input_grad = refs[0:4], refs[4:8], refs[8]
    q_targets, kv_targets = refs[9:11], refs[11:13]
    weights, inputs_flip, grad_parts, qk_sems, v_sems, out_sems = refs[13:]
    step = pl.program_id(0)
    steps = pl.num_programs(0)
    columns = grads.shape[2]
    tiles = row_tiles(inputs.shape[0])
    slot = step % 2
    which = step % 3

    @pl.when(step == 0)
    def _():
        load_blocks(
            meta, qk_sources, orders[0], weights, slice(0, 2 * columns), slice(None), qk_sems
        )
        load_blocks(
            meta, vo_sources, orders[1], weights, slice(2 * columns, 3 * columns),
            slice(0, columns), v_sems,
        )
        for rows in tiles:
            inputs_flip[:, rows] = flipped(inputs[rows, :]).astype(jnp.bfloat16)
            input_grad[rows, :] = resid_grad[rows, :]

    @pl.when(step >= 2)
    def _():
        await_stored(grad_parts.at[slot], out_sems.at[slot])

    grad_parts[slot] = dot_nn(inputs_flip[...], grads[0]).astype(jnp.bfloat16)

    @pl.when(which == 0)
    def _():
        store_blocks(
            meta, grad_parts.at[slot], q_targets, orders[0], step // 3, slice(None), out_sems.at[slot]
        )

    @pl.when(which > 0)
    def _():
        store_blocks(
            meta, grad_parts.at[slot], kv_targets, orders[1], step // 3,
            pl.ds(pl.multiple_of((which - 1) * columns, 128), columns), out_sems.at[slot],
        )

    half_at = meta[1] ^ (step // 3)

    @pl.when(which == 0)
    def _():
        await_blocks(weights, half_at, slice(0, 2 * columns), qk_sems)
        await_blocks(weights, half_at, slice(2 * columns, 3 * columns), v_sems)

    span = pl.ds(pl.multiple_of(which * columns, 128), columns)
    for rows in tiles:
        input_grad[rows, :] += dot_nt(grads[0, rows, :], weights[half_at, :, span])

    @pl.when(step == steps - 1)
    def _():
        for late in range(2):
            await_stored(grad_parts.at[late], out_sems.at[late])


def fixed(shape):
    return pl.BlockSpec(
        shape, lambda *_: (0,) * len(shape), pipeline_mode=pl.Buffered(1)
    )


def fixed_out(shape):
    return pl.BlockSpec(shape, lambda *_: (0,) * len(shape))


ANYWHERE = pl.BlockSpec(memory_space=pl.ANY)


def run_kernel(kernel, meta, grid, ins, outs, scratch, flops, moved, name):
    in_specs, operands = zip(*ins)
    out_specs, out_shapes = zip(*outs)
    return pl.pallas_call(
        kernel,
        grid_spec=pltpu.PrefetchScalarGridSpec(
            num_scalar_prefetch=1,
            grid=grid,
            in_specs=list(in_specs),
            out_specs=list(out_specs),
            scratch_shapes=scratch,
        ),
        out_shape=list(out_shapes),
        compiler_params=pltpu.CompilerParams(vmem_limit_bytes=VMEM_LIMIT),
        cost_estimate=pl.CostEstimate(flops=flops, bytes_accessed=moved, transcendentals=0),
        name=name,
    )(meta, *operands)


def low_shape(*shape):
    return jax.ShapeDtypeStruct(shape, jnp.bfloat16)


def full_shape(*shape):
    return jax.ShapeDtypeStruct(shape, jnp.float32)


def pair_sems():
    return pltpu.SemaphoreType.DMA((2,))


def half_of(step, meta, count):
    return meta[1] ^ (step // count)


def qkv_forward(orders, meta, inputs, bias, qk_blocks, vo_blocks):
    rows, width = inputs.shape
    columns = width // 2
    (qkv,) = run_kernel(
        functools.partial(qkv_forward_kernel, orders),
        meta,
        (6,),
        [
            (fixed((rows, width)), inputs),
            (
                pl.BlockSpec((1, 1, columns), lambda i, m: ((i % 3) * 2 + half_of(i, m, 3), 0, 0)),
                bias,
            ),
        ]
        + [(ANYWHERE, member) for member in qk_blocks + vo_blocks],
        [
            (
                pl.BlockSpec((1, rows, columns), lambda i, m: (i % 3, 0, half_of(i, m, 3))),
                low_shape(3, rows, width),
            )
        ],
        [pltpu.VMEM((2, width, 3 * columns), jnp.bfloat16), pair_sems(), pair_sems()],
        6 * rows * width * width,
        8 * rows * width + 6 * width * width,
        "qkv_forward",
    )
    return qkv


def attention_forward(meta, qkv, slab_count):
    _, rows, width = qkv.shape
    slab_rows = rows // slab_count
    pairs = width // PAIR
    return run_kernel(
        attention_forward_kernel,
        meta,
        (pairs, slab_count),
        [(pl.BlockSpec((3, slab_rows, PAIR), lambda p, s, m: (0, s, p)), qkv)],
        [
            (pl.BlockSpec((slab_rows, PAIR), lambda p, s, m: (s, p)), low_shape(rows, width)),
            (
                pl.BlockSpec((1, 1, 8, slab_rows), lambda p, s, m: (s, p, 0, 0)),
                full_shape(slab_count, pairs, 8, slab_rows),
            ),
        ],
        [pltpu.VMEM((slab_count, slab_rows, PAIR), jnp.bfloat16)] * 2,
        16 * rows * slab_rows * width,
        8 * rows * width,
        "attention_forward",
    )


def ffn_forward(orders, meta, mixed, inputs, vectors, ffn_bias, vo_blocks, in_blocks, down_blocks):
    rows, width = inputs.shape
    half_width = in_blocks[0].shape[2]
    part = half_width // FFN_PARTS

    def part_at(i, m):
        return half_of(i, m, FFN_PARTS) * FFN_PARTS + i % FFN_PARTS

    whole_rows = (fixed_out((rows, width)), low_shape(rows, width))
    spread = (fixed_out((rows, 128)), full_shape(rows, 128))
    inner = (
        pl.BlockSpec((rows, part), lambda i, m: (0, part_at(i, m))),
        low_shape(rows, 2 * half_width),
    )
    return run_kernel(
        functools.partial(ffn_forward_kernel, orders),
        meta,
        (2 * FFN_PARTS,),
        [
            (fixed((rows, width)), mixed),
            (fixed((rows, width)), inputs),
            (fixed((8, width)), vectors),
            (pl.BlockSpec((1, 1, part), lambda i, m: (part_at(i, m), 0, 0)), ffn_bias),
        ]
        + [(ANYWHERE, member) for member in vo_blocks + in_blocks + down_blocks],
        [whole_rows, whole_rows, spread, inner, inner, whole_rows, whole_rows, spread],
        [
            pltpu.VMEM((2, width, width // 2), jnp.bfloat16),
            pltpu.VMEM((2, width, half_width), jnp.bfloat16),
            pltpu.VMEM((2, width, half_width), jnp.bfloat16),
            pltpu.VMEM((rows, width), jnp.float32),
            pair_sems(),
            pair_sems(),
            pair_sems(),
        ],
        8 * rows * width * half_width,
        24 * rows * width + 8 * width * half_width,
        "ffn_forward",
    )


def ffn_backward(orders, meta, gradient, kept, vectors, in_blocks, down_blocks):
    hidden, normed_one, spread_one, activated, slope, normed_two, spread_two = kept
    rows, width = hidden.shape
    half_width = in_blocks[0].shape[2]
    part = half_width // FFN_PARTS
    slots, block_rows = 2 * in_blocks[0].shape[0], in_blocks[0].shape[1]

    def part_at(i, m):
        return half_of(i, m, FFN_PARTS) * FFN_PARTS + i % FFN_PARTS

    low_rows = fixed((rows, width))
    spread = fixed((rows, 128))
    inner = pl.BlockSpec((rows, part), lambda i, m: (0, part_at(i, m)))
    target = (ANYWHERE, low_shape(slots, block_rows, half_width))
    return run_kernel(
        functools.partial(ffn_backward_kernel, orders),
        meta,
        (2 * FFN_PARTS,),
        [
            (low_rows, gradient),
            (low_rows, normed_two),
            (spread, spread_two),
            (low_rows, hidden),
            (low_rows, normed_one),
            (spread, spread_one),
            (inner, activated),
            (inner, slope),
            (fixed((8, width)), vectors),
        ]
        + [(ANYWHERE, member) for member in in_blocks + down_blocks],
        [
            (fixed_out((rows, width)), low_shape(rows, width)),
            (fixed_out((rows, width)), full_shape(rows, width)),
            (fixed_out((8, width)), full_shape(8, width)),
            (
                pl.BlockSpec((1, 1, part), lambda i, m: (part_at(i, m), 0, 0)),
                full_shape(2 * FFN_PARTS, 1, part),
            ),
            target,
            target,
            target,
            target,
        ],
        [
            pltpu.VMEM((2, width, half_width), jnp.bfloat16),
            pltpu.VMEM((2, width, half_width), jnp.bfloat16),
            pltpu.VMEM((rows, width), jnp.float32),
            pltpu.VMEM((rows, width), jnp.bfloat16),
            pltpu.VMEM((width, rows), jnp.bfloat16),
            pltpu.VMEM((width, rows), jnp.bfloat16),
            pltpu.VMEM((rows, part), jnp.bfloat16),
            pltpu.VMEM((2, 2, width, part), jnp.bfloat16),
            pair_sems(),
            pair_sems(),
            pltpu.SemaphoreType.DMA((2, 2)),
        ],
        16 * rows * width * half_width,
        40 * rows * width + 16 * width * half_width,
        "ffn_backward",
    )


def out_backward(orders, meta, attention_grad, mixed, vo_blocks):
    rows, width = mixed.shape
    columns = width // 2
    slots, block_rows = 2 * vo_blocks[0].shape[0], vo_blocks[0].shape[1]
    half = pl.BlockSpec((rows, columns), lambda i, m: (0, half_of(i, m, 1)))
    target = (ANYWHERE, low_shape(slots, block_rows, columns))
    return run_kernel(
        functools.partial(out_backward_kernel, orders),
        meta,
        (2,),
        [(fixed((rows, width)), attention_grad), (half, mixed)]
        + [(ANYWHERE, member) for member in vo_blocks],
        [(half, low_shape(rows, width)), target, target],
        [
            pltpu.VMEM((2, width, columns), jnp.bfloat16),
            pltpu.VMEM((width, rows), jnp.bfloat16),
            pltpu.VMEM((2, width, columns), jnp.bfloat16),
            pair_sems(),
            pair_sems(),
        ],
        4 * rows * width * width,
        6 * rows * width + 4 * width * width,
        "out_backward",
    )


def attention_backward(meta, qkv, mixed, mixed_grad, logsum, slab_count):
    _, rows, width = qkv.shape
    slab_rows = rows // slab_count
    pairs = width // PAIR
    three = pl.BlockSpec((3, slab_rows, PAIR), lambda p, s, m: (0, s, p))
    one = pl.BlockSpec((slab_rows, PAIR), lambda p, s, m: (s, p))
    return run_kernel(
        attention_backward_kernel,
        meta,
        (pairs, slab_count),
        [
            (three, qkv),
            (one, mixed),
            (one, mixed_grad),
            (pl.BlockSpec((1, 1, 8, slab_rows), lambda p, s, m: (s, p, 0, 0)), logsum),
        ],
        [
            (three, low_shape(3, rows, width)),
            (pl.BlockSpec((8, PAIR), lambda p, s, m: (0, p)), full_shape(8, width)),
        ],
        [pltpu.VMEM((slab_count, slab_rows, PAIR), jnp.bfloat16)] * 2,
        40 * rows * slab_rows * width,
        16 * rows * width,
        "attention_backward",
    )


def qkv_backward(orders, meta, inputs, grads, resid_grad, qk_blocks, vo_blocks):
    rows, width = inputs.shape
    columns = width // 2
    slots, block_rows = 2 * qk_blocks[0].shape[0], qk_blocks[0].shape[1]
    q_target = (ANYWHERE, low_shape(slots, block_rows, columns))
    kv_target = (ANYWHERE, low_shape(slots, block_rows, 2 * columns))
    return run_kernel(
        functools.partial(qkv_backward_kernel, orders),
        meta,
        (6,),
        [
            (fixed((rows, width)), inputs),
            (pl.BlockSpec((1, rows, columns), lambda i, m: (i % 3, 0, half_of(i, m, 3))), grads),
            (fixed((rows, width)), resid_grad),
        ]
        + [(ANYWHERE, member) for member in qk_blocks + vo_blocks],
        [
            (fixed_out((rows, width)), full_shape(rows, width)),
            q_target,
            q_target,
            kv_target,
            kv_target,
        ],
        [
            pltpu.VMEM((2, width, 3 * columns), jnp.bfloat16),
            pltpu.VMEM((width, rows), jnp.bfloat16),
            pltpu.VMEM((2, width, columns), jnp.bfloat16),
            pair_sems(),
            pair_sems(),
            pair_sems(),
        ],
        12 * rows * width * width,
        14 * rows * width + 12 * width * width,
        "qkv_backward",
    )


def both_halves(mine, theirs, place):
    first = jnp.concatenate([mine, theirs], axis=0)
    second = jnp.concatenate([theirs, mine], axis=0)
    return jnp.where(place == 0, first, second)


def on_device(
    tokens,
    cotangent,
    buckets,
    lengths,
    qkv_weight,
    qv_bias,
    out_weight,
    ffn_in_weight,
    ffn_in_bias,
    ffn_out_weight,
    out_bias,
    norm_gain,
    norm_bias,
):
    split = lax.axis_size("tensor")
    dp_size = lax.axis_size("dp")
    place = lax.axis_index("tensor")
    width = tokens.shape[1]
    rows = tokens.shape[0] // split
    slabs = buckets.shape[0] // split
    layer_count = qkv_weight.shape[0]
    block_rows = width // dp_size
    routed = block_rows % TILE_ROWS == 0 and dp_size & (dp_size - 1) == 0
    orders = hop_orders(dp_size if routed else PLANNED_BLOCKS)
    gather = gather_piece if routed else gather_whole
    scatter = scatter_piece if routed else scatter_whole

    own_tokens = lax.dynamic_slice_in_dim(tokens, place * rows, rows)
    own_cotangent = lax.dynamic_slice_in_dim(cotangent, place * rows, rows)
    own_buckets = lax.dynamic_slice_in_dim(buckets, place * slabs, slabs)
    own_lengths = lax.dynamic_slice_in_dim(lengths, place * slabs, slabs)
    if routed:
        position = jnp.stack([lax.axis_index("dp"), place]).astype(jnp.int32)
    else:
        position = jnp.zeros((2,), jnp.int32)
    meta = jnp.concatenate([position, own_buckets, own_lengths.reshape(-1)])

    pieces = []
    for index in range(layer_count):
        qk_shard = jnp.concatenate([qkv_weight[index, 0], qkv_weight[index, 1]], axis=1)
        vo_shard = jnp.concatenate([qkv_weight[index, 2], out_weight[index]], axis=1)
        pieces.append(
            (
                gather(qk_shard, orders[0]),
                gather(vo_shard, orders[1]),
                gather(ffn_in_weight[index], orders[0]),
                gather(ffn_out_weight[index], orders[1]),
            )
        )
    qv_whole = lax.all_gather(qv_bias, "tensor", axis=2, tiled=True)
    ffn_bias_whole = lax.all_gather(ffn_in_bias, "tensor", axis=1, tiled=True)

    current = own_tokens
    kept_layers = []
    results = []
    for index in range(layer_count):
        qk_blocks, vo_blocks, in_blocks, down_blocks = pieces[index]
        zero = jnp.zeros((width,), jnp.float32)
        bias = jnp.stack([qv_whole[index, 0], zero, qv_whole[index, 1]]).reshape(6, 1, -1)
        vectors = jnp.concatenate(
            [out_bias[index], norm_gain[index], norm_bias[index], jnp.zeros((2, width), jnp.float32)]
        )
        qkv = qkv_forward(orders, meta, current, bias, qk_blocks, vo_blocks)
        mixed, logsum = attention_forward(meta, qkv, slabs)
        hidden, normed_one, spread_one, activated, slope, result, normed_two, spread_two = ffn_forward(
            orders, meta, mixed, current, vectors,
            ffn_bias_whole[index].reshape(2 * FFN_PARTS, 1, -1), vo_blocks, in_blocks, down_blocks,
        )
        kept_layers.append(
            (
                current, qkv, mixed, logsum, vectors,
                (hidden, normed_one, spread_one, activated, slope, normed_two, spread_two),
            )
        )
        current = result
        results.append(both_halves(result, hop(result, ("tensor", 1)), place))

    gradient = own_cotangent
    matrix_grads = [None] * layer_count
    small_grads = [None] * layer_count
    for index in reversed(range(layer_count)):
        qk_blocks, vo_blocks, in_blocks, down_blocks = pieces[index]
        inputs, qkv, mixed, logsum, vectors, kept = kept_layers[index]
        attention_grad, resid_grad, sums, ffn_sums, in_keep, in_send, down_keep, down_send = (
            ffn_backward(orders, meta, gradient, kept, vectors, in_blocks, down_blocks)
        )
        in_grad = scatter(in_keep, in_send, orders[0])
        down_grad = scatter(down_keep, down_send, orders[1])
        mixed_grad, out_keep, out_send = out_backward(orders, meta, attention_grad, mixed, vo_blocks)
        out_grad = scatter(out_keep, out_send, orders[0])
        grads, qkv_sums = attention_backward(meta, qkv, mixed, mixed_grad, logsum, slabs)
        gradient, q_keep, q_send, kv_keep, kv_send = qkv_backward(
            orders, meta, inputs, grads, resid_grad, qk_blocks, vo_blocks
        )
        q_grad = scatter(q_keep, q_send, orders[0])
        kv_grad = scatter(kv_keep, kv_send, orders[1])
        columns = q_grad.shape[1]
        matrix_grads[index] = (
            jnp.stack([q_grad, kv_grad[:, :columns], kv_grad[:, columns:]]),
            out_grad,
            in_grad,
            down_grad,
        )
        small_grads[index] = lax.psum(
            jnp.concatenate([sums[:6].reshape(-1), qkv_sums[:2].reshape(-1), ffn_sums.reshape(-1)]),
            AXES,
        )
    low_gradient = gradient.astype(jnp.bfloat16)
    token_grad = both_halves(
        gradient, hop(low_gradient, ("tensor", 1)).astype(jnp.float32), place
    )

    smalls = jnp.stack(small_grads)
    eight = smalls[:, : 8 * width].reshape(layer_count, 4, 2, width)
    ffn_total = smalls[:, 8 * width :]
    qv_columns = qv_bias.shape[2]
    ffn_columns = ffn_in_bias.shape[1]
    return (
        results[0],
        results[layer_count - 1],
        token_grad,
        jnp.stack([member[0] for member in matrix_grads]),
        lax.dynamic_slice_in_dim(eight[:, 3], place * qv_columns, qv_columns, axis=2),
        jnp.stack([member[1] for member in matrix_grads]),
        jnp.stack([member[2] for member in matrix_grads]),
        lax.dynamic_slice_in_dim(ffn_total, place * ffn_columns, ffn_columns, axis=1),
        jnp.stack([member[3] for member in matrix_grads]),
        eight[:, 0],
        eight[:, 1],
        eight[:, 2],
    )


def solution(mesh):
    placed = (
        P("dp", None),
        P("dp", None),
        P("dp"),
        P("dp", None),
        P(None, None, "dp", "tensor"),
        P(None, None, "tensor"),
        P(None, "dp", "tensor"),
        P(None, "dp", "tensor"),
        P(None, "tensor"),
        P(None, "dp", "tensor"),
        P(),
        P(),
        P(),
    )
    return jax.shard_map(
        on_device,
        mesh=mesh,
        in_specs=placed,
        out_specs=(
            P("dp", None),
            P("dp", None),
            P("dp", None),
            P(None, None, "dp", "tensor"),
            P(None, None, "tensor"),
            P(None, "dp", "tensor"),
            P(None, "dp", "tensor"),
            P(None, "tensor"),
            P(None, "dp", "tensor"),
            P(),
            P(),
            P(),
        ),
        check_vma=False,
    )
```

time: 1550 us -> 917 us (0.59)
  local copies, waits for them, and re-layouts: 487 us -> 20 us
  matrix products: 430 us -> 0 us
  Pallas kernels: 0 us -> 296 us
  starting transfers between devices: 1.28 us -> 82.1 us
  waiting for transfers between devices: 480 us -> 419 us
  other arithmetic: 113 us -> 65.3 us
    dot_general x48 -> x0, matrix products: 430 us -> none  [the longest x4 81.7 us: attend_back(): jnp.einsum('ghqk,gqhe->gkhe', raw_grad, query_rows, preferred_element_typ...]
    reduce_scatter x4 -> x0, waiting for transfers between devices: 372 us -> none  [scatter_gradient(): mine = lax.psum_scatter(packed, AXES, scatter_dimension=0, tiled=True)]
    ppermute x0 -> x101, waiting for transfers between devices: none -> 321 us  [hop(): return lax.ppermute(member, axis, pairs)]
    pallas_call x0 -> x14, Pallas kernels: none -> 296 us  [run_kernel(): pl.pallas_call(kernel, grid_spec=pltpu.PrefetchScalarGridSpec(num_scalar_...]
    slice x28 -> x5, local copies, waits for them, and re-layouts: 178 us -> 4.45 us  [the longest x1 1.66 us: on_device(): ffn_in_weight[index]]
    another operation x26 -> x5, local copies, waits for them, and re-layouts: 136 us -> 0.7 us  [the longest x2 0.67 us: on_device(): jnp.stack([qv_whole[index, 0], zero, qv_whole[index, 1]]).reshape(6, 1, -1)]
    all_gather x7 -> x0, waiting for transfers between devices: 106 us -> none  [the longest x2 96.7 us: whole_weights(): attention_all = lax.all_gather(attention_shard, AXES, tiled=True)]
    psum x1, waiting for transfers between devices: 0.02 us -> 98.3 us  [on_device(): lax.psum(jnp.concatenate([sums[:6].reshape(-1), qkv_sums[:2].reshape(-1),...]
  transfers between devices with their start and end apart: 12 -> 102, of which waited for: 6 -> 54; matrix products, arithmetic and copies ran while one was open for 37% -> 8% of each run, Pallas kernels for 0% -> 12%
where the time goes in v2:
time: 917 us; the launch traced here: 910 us
  waiting for transfers between devices  419 us (46%)
  Pallas kernels  296 us (32%)
  starting transfers between devices  82.1 us (9%)
  other arithmetic  65.3 us (7%)
  local copies, waits for them, and re-layouts  20 us (2%)
  between operations  15.3 us (2%)
  blocking collectives  11.6 us (1%)
    ppermute x101, waiting for transfers between devices, hop(): return lax.ppermute(member, axis, pairs)  321 us
    pallas_call x14, Pallas kernels, run_kernel(): pl.pallas_call(kernel, grid_spec=pltpu.PrefetchScalarGridSpec(num_scalar_...  296 us
    psum x1, waiting for transfers between devices, on_device(): lax.psum(jnp.concatenate([sums[:6].reshape(-1), qkv_sums[:2].reshape(-1),...  98.3 us
    ppermute x101, starting transfers between devices, hop(): return lax.ppermute(member, axis, pairs)  82 us
    concatenate x24, other arithmetic, gather_piece(): current = jnp.concatenate([current, hop(current, dim)], axis=0)  23 us
    convert_element_type x40, other arithmetic, scatter_piece(): sum((part[half:].astype(jnp.float32) for part in parts))  19.4 us
  transfers between devices with their start and end apart: 102, of which 54 were waited for; matrix products, arithmetic and copies ran while one was open for 8% of the time, Pallas kernels for 12%

profile of v2, /device:TPU:0, one launch (start us, length us, event | category | flops | bytes accessed | tf_op | source)
XLA Modules:
  0.0 909.6 jit_solution(13604255207242850167)
XLA Ops:
  8.9 4.0 collective-permute-start
  23.3 4.5 all_gather.6
  35.5 6.7 collective-permute-done.25
  65.9 4.8 collective-permute-done.13
  79.6 3.8 collective-permute-done.38
  104.7 6.4 collective-permute-done.20
  112.5 11.1 %collective-permute-done.45 = bf16[4,48,1536]{2,1,0:T(8,128)(2,1)S(1)} collective-permute-done((bf16[4,48,1536]{2,1,0:T(8,128)(2,1)S(1)}, bf16[4,48,1536]{2,1,0:T(8,128)(2,1)S(1)}, u32[]{:S(2)}, u32[]{:S(2)}) %collective-permute-start.45) | collective-permute-done | bytes 589856 | tf_op jit(solution)/shard_map/ppermute | solution.py:72
  125.2 11.1 %collective-permute-done.3.refs_1_ = bf16[8,48,768]{2,1,0:T(8,128)(2,1)S(1)} collective-permute-done((bf16[8,48,768]{2,1,0:T(8,128)(2,1)S(1)}, bf16[8,48,768]{2,1,0:T(8,128)(2,1)S(1)}, u32[]{:S(2)}, u32[]{:S(2)}) %collective-permute-start.3) | collective-permute-done | bytes 589856 | tf_op jit(solution)/shard_map/ppermute | solution.py:72
  140.1 7.0 all_gather.7
  161.8 18.4 %collective-permute-done.15.refs_5_.refs_1_ = bf16[8,48,1536]{2,1,0:T(8,128)(2,1)} collective-permute-done((bf16[8,48,1536]{2,1,0:T(8,128)(2,1)S(1)}, bf16[8,48,1536]{2,1,0:T(8,128)(2,1)}, u32[]{:S(2)}, u32[]{:S(2)}) %collective-permute-start.15) | collective-permute-done | bytes 1179680 | tf_op jit(solution)/shard_map/ppermute | solution.py:72
  184.8 11.5 %qkv_forward.2.qkv = bf16[3,1024,768]{2,1,0:T(8,128)(2,1)} custom-call(s32[12]{0:T(128)} %pad_add_fusion.meta, bf16[1024,768]{1,0:T(8,128)(2,1)} %constant_dynamic-slice_fusion.1.inputs, f32[6,1,384]{2,1,0:T(1,128)} %reshape.78.bias, bf16[8,48,768]{2,1,0:T(8,128)(2,1)} %copy-done.17, bf16[8,48,768]{2,1,0:T(8,128)(2,1)} %copy-done.45, ...), custom_call_target="tpu_custom_call" | custom-call | flops 3623878656 | bytes 9830400 | tf_op jit(solution)/shard_map/qkv_forward/pallas_call | solution.py:593
  196.3 17.5 %attention_forward.2 = (bf16[1024,768]{1,0:T(8,128)(2,1)}, f32[2,6,8,512]{3,2,1,0:T(8,128)}) custom-call(s32[12]{0:T(128)} %pad_add_fusion.meta, bf16[3,1024,768]{2,1,0:T(8,128)(2,1)} %qkv_forward.2.qkv), custom_call_target="tpu_custom_call" | custom-call | flops 6442450944 | bytes 6291456 | tf_op jit(solution)/shard_map/attention_forward/pallas_call | solution.py:593
  215.9 34.4 %ffn_forward.2 = (bf16[1024,768]{1,0:T(8,128)(2,1)}, bf16[1024,768]{1,0:T(8,128)(2,1)}, f32[1024,128]{1,0:T(8,128)}, bf16[1024,3072]{1,0:T(8,128)(2,1)}, bf16[10...) custom-call(s32[12]{0:T(128)} %pad_add_fusion.meta, ...), custom_call_target="tpu_custom_call" | custom-call | flops 9663676416 | bytes 28311552 | tf_op jit(solution)/shard_map/ffn_forward/pallas_call | solution.py:593
  251.2 11.2 %qkv_forward.3.qkv = bf16[3,1024,768]{2,1,0:T(8,128)(2,1)} custom-call(s32[12]{0:T(128)} %pad_add_fusion.meta, bf16[1024,768]{1,0:T(8,128)(2,1)} %get-tuple-element.69.inputs, f32[6,1,384]{2,1,0:T(1,128)} %reshape.79.bias, bf16[8,48,768]{2,1,0:T(8,128)(2,1)} %pad_maximum_fusion.8.refs_0_, bf16[8,48,768]{2,1,0:T(8,128)(2,1)} %collective-permute-done.28.refs_1_, ...), custom_call_target="tpu_custom_call" | custom-call | flops 3623878656 | bytes 9830400 | tf_op jit(solution)/shard_map/qkv_forward/pallas_call | solution.py:593
  262.4 18.0 %attention_forward.3 = (bf16[1024,768]{1,0:T(8,128)(2,1)}, f32[2,6,8,512]{3,2,1,0:T(8,128)}) custom-call(s32[12]{0:T(128)} %pad_add_fusion.meta, bf16[3,1024,768]{2,1,0:T(8,128)(2,1)} %qkv_forward.3.qkv), custom_call_target="tpu_custom_call" | custom-call | flops 6442450944 | bytes 6291456 | tf_op jit(solution)/shard_map/attention_forward/pallas_call | solution.py:593
  281.8 34.5 %ffn_forward.3 = (bf16[1024,768]{1,0:T(8,128)(2,1)}, bf16[1024,768]{1,0:T(8,128)(2,1)}, f32[1024,128]{1,0:T(8,128)}, bf16[1024,3072]{1,0:T(8,128)(2,1)}, bf16[10...) custom-call(s32[12]{0:T(128)} %pad_add_fusion.meta, ...), custom_call_target="tpu_custom_call" | custom-call | flops 9663676416 | bytes 28311552 | tf_op jit(solution)/shard_map/ffn_forward/pallas_call | solution.py:593
  316.4 35.1 %ffn_backward.2 = (bf16[1024,768]{1,0:T(8,128)(2,1)}, f32[1024,768]{1,0:T(8,128)}, f32[8,768]{1,0:T(8,128)}, f32[6,1,512]{2,1,0:T(1,128)}, bf16[16,48,1536]{2,1,...) custom-call(s32[12]{0:T(128)} %pad_add_fusion.meta, ...), custom_call_target="tpu_custom_call" | custom-call | flops 19327352832 | bytes 50331648 | tf_op jit(solution)/shard_map/ffn_backward/pallas_call | solution.py:593
  351.4 7.8 out_backward.2
  359.2 22.5 %attention_backward.2 = (bf16[3,1024,768]{2,1,0:T(8,128)(2,1)}, f32[8,768]{1,0:T(8,128)}) custom-call(s32[12]{0:T(128)} %pad_add_fusion.meta, bf16[3,1024,768]{2,1,0:T(8,128)(2,1)} %qkv_forward.3.qkv, bf16[1024,768]{1,0:T(8,128)(2,1)} %get-tuple-element.70.mixed, bf16[1024,768]{1,0:T(8,128)(2,1)} %get-tuple-element.80.mixed_grad, ...), custom_call_target="tpu_custom_call" | custom-call | flops 16106127360 | bytes 12582912 | tf_op jit(solution)/shard_map/attention_backward/pallas_call | solution.py:593
  382.5 18.8 %qkv_backward.2 = (f32[1024,768]{1,0:T(8,128)}, bf16[16,48,384]{2,1,0:T(8,128)(2,1)}, bf16[16,48,384]{2,1,0:T(8,128)(2,1)}, bf16[16,48,768]{2,1,0:T(8,128)(2,1)}, bf16[16,48,768]{2,1,0:T(8,128)(2,1)}) custom-call(s32[12]{0:T(128)} %pad_add_fusion.meta, bf16[1024,768]{1,0:T(8,128)(2,1)} %get-tuple-element.69.inputs, ...), custom_call_target="tpu_custom_call" | custom-call | flops 7247757312 | bytes 18087936 | tf_op jit(solution)/shard_map/qkv_backward/pallas_call | solution.py:593
  401.3 35.4 %ffn_backward.3 = (bf16[1024,768]{1,0:T(8,128)(2,1)}, f32[1024,768]{1,0:T(8,128)}, f32[8,768]{1,0:T(8,128)}, f32[6,1,512]{2,1,0:T(1,128)}, bf16[16,48,1536]{2,1,...) custom-call(s32[12]{0:T(128)} %pad_add_fusion.meta, ...), custom_call_target="tpu_custom_call" | custom-call | flops 19327352832 | bytes 50331648 | tf_op jit(solution)/shard_map/ffn_backward/pallas_call | solution.py:593
  436.7 8.2 out_backward.3
  444.9 22.5 %attention_backward.3 = (bf16[3,1024,768]{2,1,0:T(8,128)(2,1)}, f32[8,768]{1,0:T(8,128)}) custom-call(s32[12]{0:T(128)} %pad_add_fusion.meta, bf16[3,1024,768]{2,1,0:T(8,128)(2,1)} %qkv_forward.2.qkv, bf16[1024,768]{1,0:T(8,128)(2,1)} %get-tuple-element.68.mixed, bf16[1024,768]{1,0:T(8,128)(2,1)} %get-tuple-element.93.mixed_grad, ...), custom_call_target="tpu_custom_call" | custom-call | flops 16106127360 | bytes 12582912 | tf_op jit(solution)/shard_map/attention_backward/pallas_call | solution.py:593
  470.0 18.7 %qkv_backward.3 = (f32[1024,768]{1,0:T(8,128)}, bf16[16,48,384]{2,1,0:T(8,128)(2,1)}, bf16[16,48,384]{2,1,0:T(8,128)(2,1)}, bf16[16,48,768]{2,1,0:T(8,128)(2,1)}, bf16[16,48,768]{2,1,0:T(8,128)(2,1)}) custom-call(s32[12]{0:T(128)} %pad_add_fusion.meta, bf16[1024,768]{1,0:T(8,128)(2,1)} %constant_dynamic-slice_fusion.1.inputs, ...), custom_call_target="tpu_custom_call" | custom-call | flops 7247757312 | bytes 18087936 | tf_op jit(solution)/shard_map/qkv_backward/pallas_call | solution.py:593
  491.5 98.3 %all-reduce.3.cloned.1.call-done = (f32[1,9216]{1,0:T(1,128)}, f32[1,9216]{1,0:T(1,128)}) async-done(((f32[1,9216]{1,0:T(1,128)}, f32[1,9216]{1,0:T(1,128)}), (f32[1,9216]{1,0:T(1,128)}, f32[1,9216]{1,0:T(1,128)})) %all-reduce.3.cloned.1.call-update) | async-done | bytes 73744 | tf_op jit(solution)/shard_map/psum | solution.py:980
  602.6 36.7 %collective-permute-done.72 = bf16[8,48,384]{2,1,0:T(8,128)(2,1)S(1)} collective-permute-done((bf16[8,48,384]{2,1,0:T(8,128)(2,1)S(1)}, bf16[8,48,384]{2,1,0:T(8,128)(2,1)S(1)}, u32[]{:S(2)}, u32[]{:S(2)}) %collective-permute-start.72) | collective-permute-done | bytes 294944 | tf_op jit(solution)/shard_map/ppermute | solution.py:72
  641.7 3.9 collective-permute-done.77
  654.4 3.9 collective-permute-done.62
  671.9 4.1 collective-permute-done.53
  700.1 4.0 collective-permute-done.75
  704.9 4.0 collective-permute-done.80
  709.8 4.1 collective-permute-done.55
  729.2 8.3 collective-permute-done.57
  737.6 12.1 %collective-permute-done.67 = bf16[8,48,768]{2,1,0:T(8,128)(2,1)S(1)} collective-permute-done((bf16[8,48,768]{2,1,0:T(8,128)(2,1)S(1)}, bf16[8,48,768]{2,1,0:T(8,128)(2,1)S(1)}, u32[]{:S(2)}, u32[]{:S(2)}) %collective-permute-start.67) | collective-permute-done | bytes 589856 | tf_op jit(solution)/shard_map/ppermute | solution.py:72
  754.2 5.4 collective-permute-done.58
  759.7 4.9 collective-permute-done.68
  765.6 4.1 collective-permute-done.59
  770.8 4.1 collective-permute-done.69
  775.0 7.3 collective-permute-done.60
  782.4 5.1 collective-permute-done.70
  794.6 23.1 %collective-permute-done.92 = bf16[8,48,1536]{2,1,0:T(8,128)(2,1)S(1)} collective-permute-done((bf16[8,48,1536]{2,1,0:T(8,128)(2,1)S(1)}, bf16[8,48,1536]{2,1,0:T(8,128)(2,1)S(1)}, u32[]{:S(2)}, u32[]{:S(2)}) %collective-permute-start.92) | collective-permute-done | bytes 1179680 | tf_op jit(solution)/shard_map/ppermute | solution.py:72
  818.6 20.8 %collective-permute-done.97 = bf16[8,48,1536]{2,1,0:T(8,128)(2,1)S(1)} collective-permute-done((bf16[8,48,1536]{2,1,0:T(8,128)(2,1)S(1)}, bf16[8,48,1536]{2,1,0:T(8,128)(2,1)S(1)}, u32[]{:S(2)}, u32[]{:S(2)}) %collective-permute-start.97) | collective-permute-done | bytes 1179680 | tf_op jit(solution)/shard_map/ppermute | solution.py:72
  842.3 4.1 collective-permute-done.87
  847.4 11.6 %collective-permute-done.93 = bf16[4,48,1536]{2,1,0:T(8,128)(2,1)S(1)} collective-permute-done((bf16[4,48,1536]{2,1,0:T(8,128)(2,1)S(1)}, bf16[4,48,1536]{2,1,0:T(8,128)(2,1)S(1)}, u32[]{:S(2)}, u32[]{:S(2)}) %collective-permute-start.93) | collective-permute-done | bytes 589856 | tf_op jit(solution)/shard_map/ppermute | solution.py:72
  859.2 6.2 collective-permute-done.98
  870.8 9.3 %collective-permute-done.99 = bf16[2,48,1536]{2,1,0:T(8,128)(2,1)S(1)} collective-permute-done((bf16[2,48,1536]{2,1,0:T(8,128)(2,1)S(1)}, bf16[2,48,1536]{2,1,0:T(8,128)(2,1)S(1)}, u32[]{:S(2)}, u32[]{:S(2)}) %collective-permute-start.99) | collective-permute-done | bytes 294944 | tf_op jit(solution)/shard_map/ppermute | solution.py:72
  880.3 8.1 collective-permute-done.84
  891.8 5.7 collective-permute-done.100
  (402 shorter events, 221.0 us)
Async XLA Ops:
  7.2 582.6 %all-reduce.3.cloned.1.call-start = ((), (), s32[]{:S(2)}) async-start(), calls=%async_computation | async-start | bytes 147456 | tf_op jit(solution)/shard_map/psum | solution.py:980
  16.1 30.2 %collective-permute-start.12 = (bf16[1,48,1536]{2,1,0:T(8,128)(2,1)}, bf16[1,48,1536]{2,1,0:T(8,128)(2,1)}, u32[]{:S(2)}, u32[]{:S(2)}) collective-permute-start(bf16[1,48,1536]{2,1,0:T(8,128)(2,1)} %get-tuple-element.129), channel_id=1, source_target_pairs={{0,16},{2,18},{4,20},{6,22},{8,24},{10,26},{12,28},{14,30},{16,0},... | collective-permute-start | bytes 442376 | tf_op jit(solution)/shard_map/ppermute | solution.py:72
  19.7 27.7 %collective-permute-start.18 = (bf16[1,48,1536]{2,1,0:T(8,128)(2,1)}, bf16[1,48,1536]{2,1,0:T(8,128)(2,1)}, u32[]{:S(2)}, u32[]{:S(2)}) collective-permute-start(bf16[1,48,1536]{2,1,0:T(8,128)(2,1)} %get-tuple-element.127), channel_id=1, source_target_pairs={{0,16},{2,18},{4,20},{6,22},{8,24},{10,26},{12,28},{14,30},{16,0},... | collective-permute-start | bytes 442376 | tf_op jit(solution)/shard_map/ppermute | solution.py:72
  58.1 25.3 %collective-permute-start.38 = (bf16[2,48,1536]{2,1,0:T(8,128)(2,1)S(1)}, bf16[2,48,1536]{2,1,0:T(8,128)(2,1)S(1)}, u32[]{:S(2)}, u32[]{:S(2)}) collective-permute-start(bf16[2,48,1536]{2,1,0:T(8,128)(2,1)S(1)} %pad_maximum_fusion.21), channel_id=1, source_target_pairs={{0,8},{2,10},{4,12},{6,14},{8,0},{10,2},{12,4},{14,6},{16,24},{18,... | collective-permute-start | bytes 884744 | tf_op jit(solution)/shard_map/ppermute | solution.py:72
  61.2 27.2 %collective-permute-start.44 = (bf16[2,48,1536]{2,1,0:T(8,128)(2,1)S(1)}, bf16[2,48,1536]{2,1,0:T(8,128)(2,1)S(1)}, u32[]{:S(2)}, u32[]{:S(2)}) collective-permute-start(bf16[2,48,1536]{2,1,0:T(8,128)(2,1)S(1)} %pad_maximum_fusion.22), channel_id=1, source_target_pairs={{0,8},{2,10},{4,12},{6,14},{8,0},{10,2},{12,4},{14,6},{16,24},{18,... | collective-permute-start | bytes 884744 | tf_op jit(solution)/shard_map/ppermute | solution.py:72
  64.4 25.6 %collective-permute-start.2 = (bf16[4,48,768]{2,1,0:T(8,128)(2,1)S(1)}, bf16[4,48,768]{2,1,0:T(8,128)(2,1)S(1)}, u32[]{:S(2)}, u32[]{:S(2)}) collective-permute-start(bf16[4,48,768]{2,1,0:T(8,128)(2,1)S(1)} %pad_maximum_fusion.15), channel_id=1, source_target_pairs={{0,4},{2,6},{4,0},{6,2},{8,12},{10,14},{12,8},{14,10},{16,20},{18,... | collective-permute-start | bytes 884744 | tf_op jit(solution)/shard_map/ppermute | solution.py:72
  93.2 30.5 %collective-permute-start.45 = (bf16[4,48,1536]{2,1,0:T(8,128)(2,1)S(1)}, bf16[4,48,1536]{2,1,0:T(8,128)(2,1)S(1)}, u32[]{:S(2)}, u32[]{:S(2)}) collective-permute-start(bf16[4,48,1536]{2,1,0:T(8,128)(2,1)S(1)} %pad_maximum_fusion.11), channel_id=1, source_target_pairs={{0,1},{1,0},{2,3},{3,2},{4,5},{5,4},{6,7},{7,6},{8,9},{9,8},{10,11... | collective-permute-start | bytes 1769480 | tf_op jit(solution)/shard_map/ppermute | solution.py:72
  98.4 37.9 %collective-permute-start.3 = (bf16[8,48,768]{2,1,0:T(8,128)(2,1)S(1)}, bf16[8,48,768]{2,1,0:T(8,128)(2,1)S(1)}, u32[]{:S(2)}, u32[]{:S(2)}) collective-permute-start(bf16[8,48,768]{2,1,0:T(8,128)(2,1)S(1)} %pad_maximum_fusion.4.refs_0_), channel_id=1, source_target_pairs={{0,1},{1,0},{2,3},{3,2},{4,5},{5,4},{6,7},{7,6},{8,9},{9,8},{10,11... | collective-permute-start | bytes 1769480 | tf_op jit(solution)/shard_map/ppermute | solution.py:72
  99.9 36.4 %collective-permute-start.4 = (bf16[8,48,768]{2,1,0:T(8,128)(2,1)S(1)}, bf16[8,48,768]{2,1,0:T(8,128)(2,1)S(1)}, u32[]{:S(2)}, u32[]{:S(2)}) collective-permute-start(bf16[8,48,768]{2,1,0:T(8,128)(2,1)S(1)} %pad_maximum_fusion.4.refs_0_), channel_id=1, source_target_pairs={{0,2},{2,0},{4,6},{6,4},{8,10},{10,8},{12,14},{14,12},{16,18},{18,... | collective-permute-start | bytes 1769480 | tf_op jit(solution)/shard_map/ppermute | solution.py:72
  111.0 40.2 %collective-permute-start.9 = (bf16[8,48,768]{2,1,0:T(8,128)(2,1)}, bf16[8,48,768]{2,1,0:T(8,128)(2,1)}, u32[]{:S(2)}, u32[]{:S(2)}) collective-permute-start(bf16[8,48,768]{2,1,0:T(8,128)(2,1)} %pad_maximum_fusion.5.refs_4_.refs_0_), channel_id=1, source_target_pairs={{0,4},{2,6},{4,0},{6,2},{8,12},{10,14},{12,8},{14,10},{16,20},{18,... | collective-permute-start | bytes 1769480 | tf_op jit(solution)/shard_map/ppermute | solution.py:72
  112.5 38.7 %collective-permute-start.10 = (bf16[8,48,768]{2,1,0:T(8,128)(2,1)}, bf16[8,48,768]{2,1,0:T(8,128)(2,1)}, u32[]{:S(2)}, u32[]{:S(2)}) collective-permute-start(bf16[8,48,768]{2,1,0:T(8,128)(2,1)} %pad_maximum_fusion.5.refs_4_.refs_0_), channel_id=1, source_target_pairs={{0,2},{2,0},{4,6},{6,4},{8,10},{10,8},{12,14},{14,12},{16,18},{18,... | collective-permute-start | bytes 1769480 | tf_op jit(solution)/shard_map/ppermute | solution.py:72
  123.7 29.1 %collective-permute-start.28 = (bf16[8,48,768]{2,1,0:T(8,128)(2,1)}, bf16[8,48,768]{2,1,0:T(8,128)(2,1)}, u32[]{:S(2)}, u32[]{:S(2)}) collective-permute-start(bf16[8,48,768]{2,1,0:T(8,128)(2,1)} %pad_maximum_fusion.8.refs_0_), channel_id=1, source_target_pairs={{0,1},{1,0},{2,3},{3,2},{4,5},{5,4},{6,7},{7,6},{8,9},{9,8},{10,11... | collective-permute-start | bytes 1769480 | tf_op jit(solution)/shard_map/ppermute | solution.py:72
  151.2 28.9 %collective-permute-start.15 = (bf16[8,48,1536]{2,1,0:T(8,128)(2,1)S(1)}, bf16[8,48,1536]{2,1,0:T(8,128)(2,1)}, u32[]{:S(2)}, u32[]{:S(2)}) collective-permute-start(bf16[8,48,1536]{2,1,0:T(8,128)(2,1)S(1)} %pad_maximum_fusion.refs_4_.refs_0_), channel_id=1, source_target_pairs={{0,1},{1,0},{2,3},{3,2},{4,5},{5,4},{6,7},{7,6},{8,9},{9,8},{10,11... | collective-permute-start | bytes 3538952 | tf_op jit(solution)/shard_map/ppermute | solution.py:72
  152.8 28.9 %collective-permute-start.16 = (bf16[8,48,1536]{2,1,0:T(8,128)(2,1)S(1)}, bf16[8,48,1536]{2,1,0:T(8,128)(2,1)}, u32[]{:S(2)}, u32[]{:S(2)}) collective-permute-start(bf16[8,48,1536]{2,1,0:T(8,128)(2,1)S(1)} %pad_maximum_fusion.refs_4_.refs_0_), channel_id=1, source_target_pairs={{0,2},{2,0},{4,6},{6,4},{8,10},{10,8},{12,14},{14,12},{16,18},{18,... | collective-permute-start | bytes 3538952 | tf_op jit(solution)/shard_map/ppermute | solution.py:72
  153.0 28.7 %collective-permute-start.21 = (bf16[8,48,1536]{2,1,0:T(8,128)(2,1)}, bf16[8,48,1536]{2,1,0:T(8,128)(2,1)}, u32[]{:S(2)}, u32[]{:S(2)}) collective-permute-start(bf16[8,48,1536]{2,1,0:T(8,128)(2,1)} %pad_maximum_fusion.1.refs_8_.refs_4_), channel_id=1, source_target_pairs={{0,4},{2,6},{4,0},{6,2},{8,12},{10,14},{12,8},{14,10},{16,20},{18,... | collective-permute-start | bytes 3538952 | tf_op jit(solution)/shard_map/ppermute | solution.py:72
  160.9 52.9 %collective-permute-start.22 = (bf16[8,48,1536]{2,1,0:T(8,128)(2,1)}, bf16[8,48,1536]{2,1,0:T(8,128)(2,1)S(1)}, u32[]{:S(2)}, u32[]{:S(2)}) collective-permute-start(bf16[8,48,1536]{2,1,0:T(8,128)(2,1)} %pad_maximum_fusion.1.refs_8_.refs_4_), channel_id=1, source_target_pairs={{0,2},{2,0},{4,6},{6,4},{8,10},{10,8},{12,14},{14,12},{16,18},{18,... | collective-permute-start | bytes 3538952 | tf_op jit(solution)/shard_map/ppermute | solution.py:72
  161.0 52.9 %collective-permute-start.40 = (bf16[8,48,1536]{2,1,0:T(8,128)(2,1)}, bf16[8,48,1536]{2,1,0:T(8,128)(2,1)}, u32[]{:S(2)}, u32[]{:S(2)}) collective-permute-start(bf16[8,48,1536]{2,1,0:T(8,128)(2,1)} %pad_maximum_fusion.2.refs_4_.refs_0_), channel_id=1, source_target_pairs={{0,1},{1,0},{2,3},{3,2},{4,5},{5,4},{6,7},{7,6},{8,9},{9,8},{10,11... | collective-permute-start | bytes 3538952 | tf_op jit(solution)/shard_map/ppermute | solution.py:72
  180.1 34.2 %collective-permute-start.46 = (bf16[8,48,1536]{2,1,0:T(8,128)(2,1)}, bf16[8,48,1536]{2,1,0:T(8,128)(2,1)}, u32[]{:S(2)}, u32[]{:S(2)}) collective-permute-start(bf16[8,48,1536]{2,1,0:T(8,128)(2,1)} %pad_maximum_fusion.3.refs_8_.refs_4_), channel_id=1, source_target_pairs={{0,4},{2,6},{4,0},{6,2},{8,12},{10,14},{12,8},{14,10},{16,20},{18,... | collective-permute-start | bytes 3538952 | tf_op jit(solution)/shard_map/ppermute | solution.py:72
  181.6 32.8 %collective-permute-start.17 = (bf16[8,48,1536]{2,1,0:T(8,128)(2,1)}, bf16[8,48,1536]{2,1,0:T(8,128)(2,1)}, u32[]{:S(2)}, u32[]{:S(2)}) collective-permute-start(bf16[8,48,1536]{2,1,0:T(8,128)(2,1)} %collective-permute-done.15.refs_5_.refs_1_), channel_id=1, source_target_pairs={{0,2},{2,0},{4,6},{6,4},{8,10},{10,8},{12,14},{14,12},{16,18},{18,... | collective-permute-start | bytes 3538952 | tf_op jit(solution)/shard_map/ppermute | solution.py:72
  181.7 33.2 %collective-permute-start.23 = (bf16[8,48,1536]{2,1,0:T(8,128)(2,1)}, bf16[8,48,1536]{2,1,0:T(8,128)(2,1)S(1)}, u32[]{:S(2)}, u32[]{:S(2)}) collective-permute-start(bf16[8,48,1536]{2,1,0:T(8,128)(2,1)} %collective-permute-done.21.refs_9_.refs_5_), channel_id=1, source_target_pairs={{0,2},{2,0},{4,6},{6,4},{8,10},{10,8},{12,14},{14,12},{16,18},{18,... | collective-permute-start | bytes 3538952 | tf_op jit(solution)/shard_map/ppermute | solution.py:72
  213.8 66.6 %collective-permute-start.41 = (bf16[8,48,1536]{2,1,0:T(8,128)(2,1)}, bf16[8,48,1536]{2,1,0:T(8,128)(2,1)S(1)}, u32[]{:S(2)}, u32[]{:S(2)}) collective-permute-start(bf16[8,48,1536]{2,1,0:T(8,128)(2,1)} %pad_maximum_fusion.2.refs_4_.refs_0_), channel_id=1, source_target_pairs={{0,2},{2,0},{4,6},{6,4},{8,10},{10,8},{12,14},{14,12},{16,18},{18,... | collective-permute-start | bytes 3538952 | tf_op jit(solution)/shard_map/ppermute | solution.py:72
  213.9 66.5 %collective-permute-start.47 = (bf16[8,48,1536]{2,1,0:T(8,128)(2,1)}, bf16[8,48,1536]{2,1,0:T(8,128)(2,1)S(1)}, u32[]{:S(2)}, u32[]{:S(2)}) collective-permute-start(bf16[8,48,1536]{2,1,0:T(8,128)(2,1)} %pad_maximum_fusion.3.refs_8_.refs_4_), channel_id=1, source_target_pairs={{0,2},{2,0},{4,6},{6,4},{8,10},{10,8},{12,14},{14,12},{16,18},{18,... | collective-permute-start | bytes 3538952 | tf_op jit(solution)/shard_map/ppermute | solution.py:72
  214.4 36.0 %collective-permute-start.36 = (bf16[8,48,768]{2,1,0:T(8,128)(2,1)}, bf16[8,48,768]{2,1,0:T(8,128)(2,1)S(1)}, u32[]{:S(2)}, u32[]{:S(2)}) collective-permute-start(bf16[8,48,768]{2,1,0:T(8,128)(2,1)} %collective-permute-done.34.refs_5_.refs_1_), channel_id=1, source_target_pairs={{0,2},{2,0},{4,6},{6,4},{8,10},{10,8},{12,14},{14,12},{16,18},{18,... | collective-permute-start | bytes 1769480 | tf_op jit(solution)/shard_map/ppermute | solution.py:72
  214.4 66.0 %collective-permute-start.42 = (bf16[8,48,1536]{2,1,0:T(8,128)(2,1)}, bf16[8,48,1536]{2,1,0:T(8,128)(2,1)}, u32[]{:S(2)}, u32[]{:S(2)}) collective-permute-start(bf16[8,48,1536]{2,1,0:T(8,128)(2,1)} %collective-permute-done.40.refs_5_.refs_1_), channel_id=1, source_target_pairs={{0,2},{2,0},{4,6},{6,4},{8,10},{10,8},{12,14},{14,12},{16,18},{18,... | collective-permute-start | bytes 3538952 | tf_op jit(solution)/shard_map/ppermute | solution.py:72
  214.9 65.6 %collective-permute-start.48 = (bf16[8,48,1536]{2,1,0:T(8,128)(2,1)}, bf16[8,48,1536]{2,1,0:T(8,128)(2,1)}, u32[]{:S(2)}, u32[]{:S(2)}) collective-permute-start(bf16[8,48,1536]{2,1,0:T(8,128)(2,1)} %collective-permute-done.46.refs_9_.refs_5_), channel_id=1, source_target_pairs={{0,2},{2,0},{4,6},{6,4},{8,10},{10,8},{12,14},{14,12},{16,18},{18,... | collective-permute-start | bytes 3538952 | tf_op jit(solution)/shard_map/ppermute | solution.py:72
  468.2 125.1 %collective-permute-start.71 = (bf16[16,48,384]{2,1,0:T(8,128)(2,1)}, bf16[16,48,384]{2,1,0:T(8,128)(2,1)}, u32[]{:S(2)}, u32[]{:S(2)}) collective-permute-start(bf16[16,48,384]{2,1,0:T(8,128)(2,1)} %get-tuple-element.113), channel_id=1, source_target_pairs={{0,2},{2,0},{4,6},{6,4},{8,10},{10,8},{12,14},{14,12},{16,18},{18,... | collective-permute-start | bytes 1769480 | tf_op jit(solution)/shard_map/ppermute | solution.py:72
  468.3 127.3 %collective-permute-start.76 = (bf16[16,48,384]{2,1,0:T(8,128)(2,1)}, bf16[16,48,384]{2,1,0:T(8,128)(2,1)}, u32[]{:S(2)}, u32[]{:S(2)}) collective-permute-start(bf16[16,48,384]{2,1,0:T(8,128)(2,1)} %get-tuple-element.115), channel_id=1, source_target_pairs={{0,2},{2,0},{4,6},{6,4},{8,10},{10,8},{12,14},{14,12},{16,18},{18,... | collective-permute-start | bytes 1769480 | tf_op jit(solution)/shard_map/ppermute | solution.py:72
  488.7 109.7 %collective-permute-start.51 = (bf16[16,48,384]{2,1,0:T(8,128)(2,1)}, bf16[16,48,384]{2,1,0:T(8,128)(2,1)}, u32[]{:S(2)}, u32[]{:S(2)}) collective-permute-start(bf16[16,48,384]{2,1,0:T(8,128)(2,1)} %get-tuple-element.99), channel_id=1, source_target_pairs={{0,2},{2,0},{4,6},{6,4},{8,10},{10,8},{12,14},{14,12},{16,18},{18,... | collective-permute-start | bytes 1769480 | tf_op jit(solution)/shard_map/ppermute | solution.py:72
  488.9 232.1 %collective-permute-start.56 = (bf16[16,48,768]{2,1,0:T(8,128)(2,1)}, bf16[16,48,768]{2,1,0:T(8,128)(2,1)S(1)}, u32[]{:S(2)}, u32[]{:S(2)}) collective-permute-start(bf16[16,48,768]{2,1,0:T(8,128)(2,1)} %get-tuple-element.101), channel_id=1, source_target_pairs={{0,2},{2,0},{4,6},{6,4},{8,10},{10,8},{12,14},{14,12},{16,18},{18,... | collective-permute-start | bytes 3538952 | tf_op jit(solution)/shard_map/ppermute | solution.py:72
  489.3 110.8 %collective-permute-start.61 = (bf16[16,48,384]{2,1,0:T(8,128)(2,1)}, bf16[16,48,384]{2,1,0:T(8,128)(2,1)}, u32[]{:S(2)}, u32[]{:S(2)}) collective-permute-start(bf16[16,48,384]{2,1,0:T(8,128)(2,1)} %get-tuple-element.103), channel_id=1, source_target_pairs={{0,2},{2,0},{4,6},{6,4},{8,10},{10,8},{12,14},{14,12},{16,18},{18,... | collective-permute-start | bytes 1769480 | tf_op jit(solution)/shard_map/ppermute | solution.py:72
  593.3 128.0 %collective-permute-start.66 = (bf16[16,48,768]{2,1,0:T(8,128)(2,1)}, bf16[16,48,768]{2,1,0:T(8,128)(2,1)S(1)}, u32[]{:S(2)}, u32[]{:S(2)}) collective-permute-start(bf16[16,48,768]{2,1,0:T(8,128)(2,1)} %get-tuple-element.105), channel_id=1, source_target_pairs={{0,2},{2,0},{4,6},{6,4},{8,10},{10,8},{12,14},{14,12},{16,18},{18,... | collective-permute-start | bytes 3538952 | tf_op jit(solution)/shard_map/ppermute | solution.py:72
  595.7 126.1 %collective-permute-start.50 = (bf16[1024,768]{1,0:T(8,128)(2,1)S(1)}, bf16[1024,768]{1,0:T(8,128)(2,1)S(1)}, u32[]{:S(2)}, u32[]{:S(2)}) collective-permute-start(bf16[1024,768]{1,0:T(8,128)(2,1)S(1)} %convert_element_type.794), channel_id=1, source_target_pairs={{0,1},{1,0},{2,3},{3,2},{4,5},{5,4},{6,7},{7,6},{8,9},{9,8},{10,11... | collective-permute-start | bytes 4718600 | tf_op jit(solution)/shard_map/ppermute | solution.py:72
  598.4 40.9 %collective-permute-start.72 = (bf16[8,48,384]{2,1,0:T(8,128)(2,1)S(1)}, bf16[8,48,384]{2,1,0:T(8,128)(2,1)S(1)}, u32[]{:S(2)}, u32[]{:S(2)}) collective-permute-start(bf16[8,48,384]{2,1,0:T(8,128)(2,1)S(1)} %add_convert_fusion.15), channel_id=1, source_target_pairs={{0,1},{1,0},{2,3},{3,2},{4,5},{5,4},{6,7},{7,6},{8,9},{9,8},{10,11... | collective-permute-start | bytes 884744 | tf_op jit(solution)/shard_map/ppermute | solution.py:72
  600.1 45.5 %collective-permute-start.77 = (bf16[8,48,384]{2,1,0:T(8,128)(2,1)S(1)}, bf16[8,48,384]{2,1,0:T(8,128)(2,1)S(1)}, u32[]{:S(2)}, u32[]{:S(2)}) collective-permute-start(bf16[8,48,384]{2,1,0:T(8,128)(2,1)S(1)} %add_convert_fusion.14), channel_id=1, source_target_pairs={{0,1},{1,0},{2,3},{3,2},{4,5},{5,4},{6,7},{7,6},{8,9},{9,8},{10,11... | collective-permute-start | bytes 884744 | tf_op jit(solution)/shard_map/ppermute | solution.py:72
  652.0 75.0 %collective-permute-start.49 = (bf16[1024,768]{1,0:T(8,128)(2,1)S(1)}, bf16[1024,768]{1,0:T(8,128)(2,1)S(1)}, u32[]{:S(2)}, u32[]{:S(2)}) collective-permute-start(bf16[1024,768]{1,0:T(8,128)(2,1)S(1)} %copy-done.8), channel_id=1, source_target_pairs={{0,1},{1,0},{2,3},{3,2},{4,5},{5,4},{6,7},{7,6},{8,9},{9,8},{10,11... | collective-permute-start | bytes 4718600 | tf_op jit(solution)/shard_map/ppermute | solution.py:72
  718.7 31.6 %collective-permute-start.24 = (bf16[1024,768]{1,0:T(8,128)(2,1)S(1)}, bf16[1024,768]{1,0:T(8,128)(2,1)S(1)}, u32[]{:S(2)}, u32[]{:S(2)}) collective-permute-start(bf16[1024,768]{1,0:T(8,128)(2,1)S(1)} %copy-done.7), channel_id=1, source_target_pairs={{0,1},{1,0},{2,3},{3,2},{4,5},{5,4},{6,7},{7,6},{8,9},{9,8},{10,11... | collective-permute-start | bytes 4718600 | tf_op jit(solution)/shard_map/ppermute | solution.py:72
  721.0 67.4 %collective-permute-start.91 = (bf16[16,48,1536]{2,1,0:T(8,128)(2,1)S(1)}, bf16[16,48,1536]{2,1,0:T(8,128)(2,1)S(1)}, u32[]{:S(2)}, u32[]{:S(2)}) collective-permute-start(bf16[16,48,1536]{2,1,0:T(8,128)(2,1)S(1)} %copy-done.40), channel_id=1, source_target_pairs={{0,2},{2,0},{4,6},{6,4},{8,10},{10,8},{12,14},{14,12},{16,18},{18,... | collective-permute-start | bytes 7077896 | tf_op jit(solution)/shard_map/ppermute | solution.py:72
  721.8 27.9 %collective-permute-start.67 = (bf16[8,48,768]{2,1,0:T(8,128)(2,1)S(1)}, bf16[8,48,768]{2,1,0:T(8,128)(2,1)S(1)}, u32[]{:S(2)}, u32[]{:S(2)}) collective-permute-start(bf16[8,48,768]{2,1,0:T(8,128)(2,1)S(1)} %add_convert_fusion.8), channel_id=1, source_target_pairs={{0,4},{2,6},{4,0},{6,2},{8,12},{10,14},{12,8},{14,10},{16,20},{18,... | collective-permute-start | bytes 1769480 | tf_op jit(solution)/shard_map/ppermute | solution.py:72
  727.0 62.6 %collective-permute-start.96 = (bf16[16,48,1536]{2,1,0:T(8,128)(2,1)S(1)}, bf16[16,48,1536]{2,1,0:T(8,128)(2,1)S(1)}, u32[]{:S(2)}, u32[]{:S(2)}) collective-permute-start(bf16[16,48,1536]{2,1,0:T(8,128)(2,1)S(1)} %copy-done.38), channel_id=1, source_target_pairs={{0,2},{2,0},{4,6},{6,4},{8,10},{10,8},{12,14},{14,12},{16,18},{18,... | collective-permute-start | bytes 7077896 | tf_op jit(solution)/shard_map/ppermute | solution.py:72
  737.4 53.8 %collective-permute-start.81 = (bf16[16,48,1536]{2,1,0:T(8,128)(2,1)S(1)}, bf16[16,48,1536]{2,1,0:T(8,128)(2,1)S(1)}, u32[]{:S(2)}, u32[]{:S(2)}) collective-permute-start(bf16[16,48,1536]{2,1,0:T(8,128)(2,1)S(1)} %copy-done.39), channel_id=1, source_target_pairs={{0,2},{2,0},{4,6},{6,4},{8,10},{10,8},{12,14},{14,12},{16,18},{18,... | collective-permute-start | bytes 7077896 | tf_op jit(solution)/shard_map/ppermute | solution.py:72
  759.6 33.4 %collective-permute-start.86 = (bf16[16,48,1536]{2,1,0:T(8,128)(2,1)S(1)}, bf16[16,48,1536]{2,1,0:T(8,128)(2,1)S(1)}, u32[]{:S(2)}, u32[]{:S(2)}) collective-permute-start(bf16[16,48,1536]{2,1,0:T(8,128)(2,1)S(1)} %copy-done.37), channel_id=1, source_target_pairs={{0,2},{2,0},{4,6},{6,4},{8,10},{10,8},{12,14},{14,12},{16,18},{18,... | collective-permute-start | bytes 7077896 | tf_op jit(solution)/shard_map/ppermute | solution.py:72
  788.8 29.0 %collective-permute-start.92 = (bf16[8,48,1536]{2,1,0:T(8,128)(2,1)S(1)}, bf16[8,48,1536]{2,1,0:T(8,128)(2,1)S(1)}, u32[]{:S(2)}, u32[]{:S(2)}) collective-permute-start(bf16[8,48,1536]{2,1,0:T(8,128)(2,1)S(1)} %add_convert_fusion.1), channel_id=1, source_target_pairs={{0,4},{2,6},{4,0},{6,2},{8,12},{10,14},{12,8},{14,10},{16,20},{18,... | collective-permute-start | bytes 3538952 | tf_op jit(solution)/shard_map/ppermute | solution.py:72
  790.5 48.9 %collective-permute-start.97 = (bf16[8,48,1536]{2,1,0:T(8,128)(2,1)S(1)}, bf16[8,48,1536]{2,1,0:T(8,128)(2,1)S(1)}, u32[]{:S(2)}, u32[]{:S(2)}) collective-permute-start(bf16[8,48,1536]{2,1,0:T(8,128)(2,1)S(1)} %add_convert_fusion), channel_id=1, source_target_pairs={{0,4},{2,6},{4,0},{6,2},{8,12},{10,14},{12,8},{14,10},{16,20},{18,... | collective-permute-start | bytes 3538952 | tf_op jit(solution)/shard_map/ppermute | solution.py:72
  792.1 47.6 %collective-permute-start.82 = (bf16[8,48,1536]{2,1,0:T(8,128)(2,1)S(1)}, bf16[8,48,1536]{2,1,0:T(8,128)(2,1)S(1)}, u32[]{:S(2)}, u32[]{:S(2)}) collective-permute-start(bf16[8,48,1536]{2,1,0:T(8,128)(2,1)S(1)} %add_convert_fusion.3), channel_id=1, source_target_pairs={{0,1},{1,0},{2,3},{3,2},{4,5},{5,4},{6,7},{7,6},{8,9},{9,8},{10,11... | collective-permute-start | bytes 3538952 | tf_op jit(solution)/shard_map/ppermute | solution.py:72
  793.8 52.6 %collective-permute-start.87 = (bf16[8,48,1536]{2,1,0:T(8,128)(2,1)S(1)}, bf16[8,48,1536]{2,1,0:T(8,128)(2,1)S(1)}, u32[]{:S(2)}, u32[]{:S(2)}) collective-permute-start(bf16[8,48,1536]{2,1,0:T(8,128)(2,1)S(1)} %add_convert_fusion.2), channel_id=1, source_target_pairs={{0,1},{1,0},{2,3},{3,2},{4,5},{5,4},{6,7},{7,6},{8,9},{9,8},{10,11... | collective-permute-start | bytes 3538952 | tf_op jit(solution)/shard_map/ppermute | solution.py:72
  818.0 41.0 %collective-permute-start.93 = (bf16[4,48,1536]{2,1,0:T(8,128)(2,1)S(1)}, bf16[4,48,1536]{2,1,0:T(8,128)(2,1)S(1)}, u32[]{:S(2)}, u32[]{:S(2)}) collective-permute-start(bf16[4,48,1536]{2,1,0:T(8,128)(2,1)S(1)} %add_convert_fusion.5), channel_id=1, source_target_pairs={{0,1},{1,0},{2,3},{3,2},{4,5},{5,4},{6,7},{7,6},{8,9},{9,8},{10,11... | collective-permute-start | bytes 1769480 | tf_op jit(solution)/shard_map/ppermute | solution.py:72
  839.6 25.9 %collective-permute-start.98 = (bf16[4,48,1536]{2,1,0:T(8,128)(2,1)S(1)}, bf16[4,48,1536]{2,1,0:T(8,128)(2,1)S(1)}, u32[]{:S(2)}, u32[]{:S(2)}) collective-permute-start(bf16[4,48,1536]{2,1,0:T(8,128)(2,1)S(1)} %add_convert_fusion.4), channel_id=1, source_target_pairs={{0,1},{1,0},{2,3},{3,2},{4,5},{5,4},{6,7},{7,6},{8,9},{9,8},{10,11... | collective-permute-start | bytes 1769480 | tf_op jit(solution)/shard_map/ppermute | solution.py:72
  839.9 25.8 %collective-permute-start.83 = (bf16[4,48,1536]{2,1,0:T(8,128)(2,1)S(1)}, bf16[4,48,1536]{2,1,0:T(8,128)(2,1)S(1)}, u32[]{:S(2)}, u32[]{:S(2)}) collective-permute-start(bf16[4,48,1536]{2,1,0:T(8,128)(2,1)S(1)} %add_convert_fusion.7), channel_id=1, source_target_pairs={{0,4},{2,6},{4,0},{6,2},{8,12},{10,14},{12,8},{14,10},{16,20},{18,... | collective-permute-start | bytes 1769480 | tf_op jit(solution)/shard_map/ppermute | solution.py:72
  (106 other events, 1554.9 us)
Sparse Core Ops, SparseCore 0:
  470.2 119.5 all-reduce.2

commit v3 on v2

--- a/solution.py
+++ b/solution.py
@@ -15,6 +15,11 @@
 ROW_TILE = 256
 TILE_ROWS = 16
 PLANNED_BLOCKS = 16
+HOPS = ((True, False), (True, False))
+HOPS_BACK = ((True, True), (True, False))
+COST_WEIGHT = 8
+LATE_WEIGHTS = True
+HOLD_TOKENS = False
 VMEM_LIMIT = 58 * 1024 * 1024
 
 norm_eps = 1e-06
@@ -44,12 +49,13 @@
 
 
 def hop_orders(block_count):
-    bits = []
-    bit = block_count // 2
-    while bit > 1:
-        bits.append(("dp", bit))
-        bit //= 2
-    return (bits + [("tensor", 1)], bits[:-1] + [("tensor", 1), bits[-1]])
+    far = []
+    bit = 4
+    while bit < block_count:
+        far.append(("dp", bit))
+        bit *= 2
+    across, along = ("dp", 2), ("tensor", 1)
+    return (far + [across, along], far + [along, across])
 
 
 def slot_table(order):
@@ -72,54 +78,169 @@
     return lax.ppermute(member, axis, pairs)
 
 
-def gather_piece(shard, order):
-    current = shard[None]
-    for dim in order[:-1]:
-        current = jnp.concatenate([current, hop(current, dim)], axis=0)
-    later = hop(current, order[-1])
-    return (current, later, hop(current, CORE), hop(later, CORE))
-
-
-def scatter_piece(keep, send, order):
-    parts = [keep, hop(send, CORE)]
-    for dim in reversed(order):
-        half = parts[0].shape[0] // 2
-        upper = sum(part[half:].astype(jnp.float32) for part in parts).astype(jnp.bfloat16)
-        parts = [part[:half] for part in parts] + [hop(upper, dim)]
-    return sum(part[0].astype(jnp.float32) for part in parts)
-
-
-def gather_whole(shard, order):
-    whole = lax.all_gather(shard, AXES, tiled=True)
-    columns = shard.shape[1]
-    split = lax.axis_size("tensor")
-    blocks = whole.reshape(split, PLANNED_BLOCKS, -1, columns)
-    half = 2 ** (len(order) - 1)
-    table = slot_table(order)
-    return tuple(
-        jnp.stack(
-            [blocks[tensor_part, dp_part ^ core] for dp_part, tensor_part in table[part * half :][:half]]
-        )
-        for core in range(2)
-        for part in range(2)
-    )
-
-
-def scatter_whole(keep, send, order):
-    split = lax.axis_size("tensor")
-    placed = {}
-    for slot, (dp_part, tensor_part) in enumerate(slot_table(order)):
-        placed[tensor_part, dp_part] = keep[slot]
-        placed[tensor_part, dp_part ^ 1] = send[slot]
-    whole = jnp.stack(
-        [placed[half, block] for half in range(split) for block in range(PLANNED_BLOCKS)]
-    )
-    whole = whole.reshape(-1, keep.shape[2])
-    return lax.psum_scatter(whole, AXES, scatter_dimension=0, tiled=True).astype(jnp.float32)
-
-
-def load_blocks(meta, sources, order, target, columns, source_columns, sems):
-    table = slot_table(order)
+def tied(member, others):
+    return lax.optimization_barrier((member, *others))[0] if others else member
+
+
+class Piece:
+    def __init__(self, arrays, order, first, count):
+        self.arrays, self.order, self.columns = tuple(arrays), order, slice(first, first + count)
+        self.count = count
+
+    def narrow(self, first, count):
+        return Piece(self.arrays, self.order, self.columns.start + first, count)
+
+
+class Gathering:
+    def __init__(self, shard, orders):
+        self.shard, self.orders, self.width = shard[None], orders, shard.shape[1] // 2
+
+    def halves(self, member):
+        return [member[..., : self.width], member[..., self.width :]]
+
+    def far(self, *others):
+        shard = tied(self.shard, others)
+        count = 2 ** (len(self.orders[0]) - 2)
+        parts = [shard] + [hop(shard, ("dp", 4 * step)) for step in range(1, count)]
+        self.current = [
+            jnp.concatenate(sides, axis=0) for sides in zip(*[self.halves(part) for part in parts])
+        ]
+        return self.current
+
+    def middle(self, *others):
+        current = [tied(member, others) for member in self.current]
+        self.current = [
+            jnp.concatenate([member, hop(member, order[-2])], axis=0)
+            for member, order in zip(current, self.orders)
+        ]
+        return self.current
+
+    def last(self, *others):
+        current = [tied(member, others) for member in self.current]
+        self.later = [hop(member, order[-1]) for member, order in zip(current, self.orders)]
+        self.core_current = [hop(member, CORE) for member in current]
+        return self.later
+
+    def core(self, *others):
+        self.core_later = [hop(tied(member, others), CORE) for member in self.later]
+        return self.core_later
+
+    def pieces(self):
+        sides = zip(self.current, self.later, self.core_current, self.core_later)
+        return [Piece(side, order, 0, self.width) for side, order in zip(sides, self.orders)]
+
+
+class WholeGathering:
+    def __init__(self, shard, orders, *others):
+        self.width, self.orders = shard.shape[1] // 2, orders
+        whole = lax.all_gather(tied(shard, others), AXES, tiled=True)
+        self.whole = whole.reshape(lax.axis_size("tensor"), -1, shard.shape[1])
+
+    def far(self, *others):
+        return [self.whole]
+
+    middle = last = core = far
+
+    def pieces(self):
+        return [
+            Piece([self.whole], order, side * self.width, self.width)
+            for side, order in enumerate(self.orders)
+        ]
+
+
+class Scattering:
+    def __init__(self, members, orders, sides):
+        self.members, self.orders, self.sides = members, orders, sides
+        self.begun = [members[-1][0]]
+
+    def core(self, *others):
+        arrived = [hop(tied(send, others), CORE) for keep, send in self.members]
+        both = [[keep, come] for (keep, send), come in zip(self.members, arrived)]
+        self.parts = [
+            [[part[..., first:end] for part in both[member]] for member, first, end in side]
+            for side in self.sides
+        ]
+        return arrived
+
+    def total(self, side, take):
+        sums = [
+            sum(take(part).astype(jnp.float32) for part in group) for group in self.parts[side]
+        ]
+        return jnp.concatenate(sums, axis=-1) if len(sums) > 1 else sums[0]
+
+    def halve(self, which, others):
+        arrived = []
+        for side, order in enumerate(self.orders):
+            half = self.parts[side][0][0].shape[0] // 2
+            upper = self.total(side, lambda part: part[half:]).astype(jnp.bfloat16)
+            come = hop(tied(upper, others), order[which])
+            arrived.append(come)
+            at = 0
+            for group in self.parts[side]:
+                width = group[0].shape[-1]
+                group[:] = [part[:half] for part in group] + [come[..., at : at + width]]
+                at += width
+        return arrived
+
+    def last(self, *others):
+        return self.halve(-1, others)
+
+    def middle(self, *others):
+        return self.halve(-2, others)
+
+    def far(self, *others):
+        count = self.parts[0][0][0].shape[0]
+        sides = range(len(self.orders))
+        mine = jnp.concatenate([self.total(side, lambda part: part[0]) for side in sides], axis=-1)
+        arrived = []
+        for step in range(1, count):
+            upper = jnp.concatenate(
+                [self.total(side, lambda part: part[step]) for side in sides], axis=-1
+            )
+            arrived.append(hop(tied(upper.astype(jnp.bfloat16), others), ("dp", 4 * step)))
+        self.result = sum([mine] + [part.astype(jnp.float32) for part in arrived])
+        return [self.result]
+
+
+class WholeScattering:
+    def __init__(self, members, orders, sides):
+        self.begun = [members[-1][0]]
+        mine = [
+            lax.psum_scatter(
+                whole.reshape(-1, whole.shape[2]), AXES, scatter_dimension=0, tiled=True
+            ).astype(jnp.float32)
+            for (whole,) in members
+        ]
+        taken = [mine[member][:, first:end] for side in sides for member, first, end in side]
+        self.result = jnp.concatenate(taken, axis=-1)
+
+    def core(self, *others):
+        return []
+
+    last = middle = far = core
+
+
+def sum_over_all(member, routed):
+    if not routed:
+        return lax.psum(member, AXES)
+    total = member
+    for dim in (CORE, ("dp", 2), ("tensor", 1)):
+        total = total + hop(total, dim)
+    parts = [total] + [hop(total, ("dp", bit)) for bit in range(4, lax.axis_size("dp"), 4)]
+    far_place = lax.axis_index("dp") // 4
+    stacked = jnp.stack(parts)
+    return sum(stacked[far_place ^ step] for step in range(len(parts)))
+
+
+def load_piece(meta, piece, sources, target, columns, sems):
+    if len(sources) == 1:
+        for half_at in range(2):
+            pltpu.make_async_copy(
+                sources[0].at[half_at, :, piece.columns], target.at[half_at, :, columns],
+                sems.at[half_at],
+            ).start()
+        return
+    table = slot_table(piece.order)
     half = len(table) // 2
     block_rows = sources[0].shape[1]
     for slot, (dp_part, tensor_part) in enumerate(table):
@@ -129,18 +250,23 @@
             half_at = meta[1] ^ tensor_part
             rows = pl.ds(pl.multiple_of(place * block_rows, TILE_ROWS), block_rows)
             pltpu.make_async_copy(
-                source.at[slot % half, :, source_columns],
+                source.at[slot % half, :, piece.columns],
                 target.at[half_at, rows, columns],
                 sems.at[half_at],
             ).start()
 
 
-def await_blocks(target, half_at, columns, sems):
+def await_piece(target, half_at, columns, sems):
     view = target.at[half_at, :, columns]
     pltpu.make_async_copy(view, view, sems.at[half_at]).wait()
 
 
-def store_blocks(meta, source, targets, order, relative_half, columns, sem):
+def store_piece(meta, source, targets, order, relative_half, columns, sem):
+    if len(targets) == 1:
+        pltpu.make_async_copy(
+            source, targets[0].at[meta[1] ^ relative_half, :, columns], sem
+        ).start()
+        return
     block_rows = targets[0].shape[1]
     tensor_weight = 2 ** order.index(("tensor", 1))
     for slot, (dp_part, tensor_part) in enumerate(slot_table(order)):
@@ -156,6 +282,14 @@
             ).start()
 
 
+def take(refs, *counts):
+    groups, at = [], 0
+    for count in counts:
+        groups.append(refs[at] if count is None else refs[at : at + count])
+        at += 1 if count is None else count
+    return groups
+
+
 def await_stored(source, sem):
     pltpu.make_async_copy(source, source, sem).wait()
 
@@ -192,29 +326,32 @@
     return inputs * below, below + inputs * (bell * inv_root_tau)
 
 
-def qkv_forward_kernel(orders, meta, inputs, bias, *refs):
-    qk_sources, vo_sources, out, weights, qk_sems, v_sems = (
-        refs[0:4], refs[4:8], refs[8], refs[9], refs[10], refs[11],
+def load_qkv(meta, pieces, sources, weights, columns, sems):
+    load_piece(meta, pieces[0], sources[0], weights, slice(0, 2 * columns), sems[0])
+    load_piece(meta, pieces[1], sources[1], weights, slice(2 * columns, 3 * columns), sems[1])
+
+
+def await_qkv(weights, half_at, columns, sems):
+    await_piece(weights, half_at, slice(0, 2 * columns), sems[0])
+    await_piece(weights, half_at, slice(2 * columns, 3 * columns), sems[1])
+
+
+def qkv_forward_kernel(pieces, meta, inputs, bias, *refs):
+    qk_sources, v_sources, out, weights, *sems = take(
+        refs, len(pieces[0].arrays), len(pieces[1].arrays), None, None, None, None
     )
     step = pl.program_id(0)
     columns = out.shape[2]
 
     @pl.when(step == 0)
     def _():
-        load_blocks(
-            meta, qk_sources, orders[0], weights, slice(0, 2 * columns), slice(None), qk_sems
-        )
-        load_blocks(
-            meta, vo_sources, orders[1], weights, slice(2 * columns, 3 * columns),
-            slice(0, columns), v_sems,
-        )
+        load_qkv(meta, pieces, (qk_sources, v_sources), weights, columns, sems)
 
     half_at = meta[1] ^ (step // 3)
 
     @pl.when(step % 3 == 0)
     def _():
-        await_blocks(weights, half_at, slice(0, 2 * columns), qk_sems)
-        await_blocks(weights, half_at, slice(2 * columns, 3 * columns), v_sems)
+        await_qkv(weights, half_at, columns, sems)
 
     which = pl.ds(pl.multiple_of((step % 3) * columns, 128), columns)
     for rows in row_tiles(inputs.shape[0]):
@@ -282,10 +419,12 @@
     mixed[...] = jnp.where(sub < HEAD_DIM, outcomes[0], outcomes[1]).T.astype(jnp.bfloat16)
 
 
-def ffn_forward_kernel(orders, meta, mixed, inputs, vectors, ffn_bias, *refs):
-    vo_sources, in_sources, down_sources = refs[0:4], refs[4:8], refs[8:12]
-    hidden, normed_one, spread_one, activated, slope, result, normed_two, spread_two = refs[12:20]
-    out_whole, in_whole, down_whole, total, out_sems, in_sems, down_sems = refs[20:]
+def ffn_forward_kernel(pieces, meta, mixed, inputs, vectors, ffn_bias, *refs):
+    out_sources, in_sources, down_sources, outputs, scratch = take(
+        refs, *[len(piece.arrays) for piece in pieces], 8, 7
+    )
+    hidden, normed_one, spread_one, activated, slope, result, normed_two, spread_two = outputs
+    out_whole, in_whole, down_whole, total, out_sems, in_sems, down_sems = scratch
     step = pl.program_id(0)
     steps = pl.num_programs(0)
     everything = slice(None)
@@ -295,14 +434,11 @@
 
     @pl.when(step == 0)
     def _():
-        load_blocks(
-            meta, vo_sources, orders[1], out_whole, everything,
-            slice(out_columns, 2 * out_columns), out_sems,
-        )
-        load_blocks(meta, in_sources, orders[0], in_whole, everything, everything, in_sems)
-        load_blocks(meta, down_sources, orders[1], down_whole, everything, everything, down_sems)
+        load_piece(meta, pieces[0], out_sources, out_whole, everything, out_sems)
+        load_piece(meta, pieces[1], in_sources, in_whole, everything, in_sems)
+        load_piece(meta, pieces[2], down_sources, down_whole, everything, down_sems)
         for half_at in range(2):
-            await_blocks(out_whole, half_at, everything, out_sems)
+            await_piece(out_whole, half_at, everything, out_sems)
         for rows in tiles:
             attention_out = vectors[0:1, :]
             for half_at in range(2):
@@ -321,8 +457,8 @@
 
     @pl.when(step % FFN_PARTS == 0)
     def _():
-        await_blocks(in_whole, half_at, everything, in_sems)
-        await_blocks(down_whole, half_at, everything, down_sems)
+        await_piece(in_whole, half_at, everything, in_sems)
+        await_piece(down_whole, half_at, everything, down_sems)
 
     for rows in tiles:
         pre_gelu = dot_nn(hidden[rows, :], in_whole[half_at, :, part]) + ffn_bias[0]
@@ -342,16 +478,17 @@
 
 
 def ffn_backward_kernel(
-    orders, meta, gradient, normed_two, spread_two, hidden, normed_one, spread_one, activated,
-    slope, vectors, *refs
+    pieces, target_count, meta, gradient, normed_two, spread_two, hidden, normed_one, spread_one,
+    activated, slope, vectors, *refs
 ):
-    in_sources, down_sources = refs[0:4], refs[4:8]
-    attention_grad, resid_grad, sums, bias_sums = refs[8:12]
-    in_targets, down_targets = refs[12:14], refs[14:16]
+    in_sources, down_sources, outputs, targets, scratch = take(
+        refs, *[len(piece.arrays) for piece in pieces], 4, target_count, 11
+    )
+    attention_grad, resid_grad, sums, bias_sums = outputs
     (
         in_whole, down_whole, total, branch, branch_flip, hidden_flip, pre_part, grad_parts,
         in_sems, down_sems, out_sems,
-    ) = refs[16:]
+    ) = scratch
     step = pl.program_id(0)
     steps = pl.num_programs(0)
     everything = slice(None)
@@ -360,8 +497,8 @@
 
     @pl.when(step == 0)
     def _():
-        load_blocks(meta, in_sources, orders[0], in_whole, everything, everything, in_sems)
-        load_blocks(meta, down_sources, orders[1], down_whole, everything, everything, down_sems)
+        load_piece(meta, pieces[0], in_sources, in_whole, everything, in_sems)
+        load_piece(meta, pieces[1], down_sources, down_whole, everything, down_sems)
         gain_sum, shift_sum, branch_sum = 0.0, 0.0, 0.0
         for rows in tiles:
             grad = gradient[rows, :].astype(jnp.float32)
@@ -386,8 +523,8 @@
 
     @pl.when(step % FFN_PARTS == 0)
     def _():
-        await_blocks(in_whole, half_at, everything, in_sems)
-        await_blocks(down_whole, half_at, everything, down_sems)
+        await_piece(in_whole, half_at, everything, in_sems)
+        await_piece(down_whole, half_at, everything, down_sems)
 
     @pl.when(step >= 2)
     def _():
@@ -395,8 +532,9 @@
         await_stored(grad_parts.at[slot, 1], out_sems.at[slot, 1])
 
     grad_parts[slot, 1] = dot_nn(branch_flip[...], activated[...]).astype(jnp.bfloat16)
-    store_blocks(
-        meta, grad_parts.at[slot, 1], down_targets, orders[1], step // FFN_PARTS, part,
+    down_part = pl.ds(pl.multiple_of(FFN_PARTS * width + (step % FFN_PARTS) * width, 128), width)
+    store_piece(
+        meta, grad_parts.at[slot, 1], targets, pieces[1].order, step // FFN_PARTS, down_part,
         out_sems.at[slot, 1],
     )
     bias_sum = 0.0
@@ -408,8 +546,8 @@
         total[rows, :] += dot_nt(low, in_whole[half_at, :, part])
     bias_sums[0] = bias_sum
     grad_parts[slot, 0] = dot_nn(hidden_flip[...], pre_part[...]).astype(jnp.bfloat16)
-    store_blocks(
-        meta, grad_parts.at[slot, 0], in_targets, orders[0], step // FFN_PARTS, part,
+    store_piece(
+        meta, grad_parts.at[slot, 0], targets, pieces[0].order, step // FFN_PARTS, part,
         out_sems.at[slot, 0],
     )
 
@@ -434,9 +572,11 @@
             await_stored(grad_parts.at[late, 1], out_sems.at[late, 1])
 
 
-def out_backward_kernel(orders, meta, attention_grad, mixed, *refs):
-    vo_sources, mixed_grad, out_targets = refs[0:4], refs[4], refs[5:7]
-    out_whole, grad_flip, grad_parts, load_sems, out_sems = refs[7:]
+def out_backward_kernel(pieces, order, target_count, meta, attention_grad, mixed, *refs):
+    sources, mixed_grad, targets, scratch = take(
+        refs, len(pieces[0].arrays), None, target_count, 5
+    )
+    out_whole, grad_flip, grad_parts, load_sems, out_sems = scratch
     step = pl.program_id(0)
     columns = mixed.shape[1]
     everything = slice(None)
@@ -444,18 +584,14 @@
 
     @pl.when(step == 0)
     def _():
-        load_blocks(
-            meta, vo_sources, orders[1], out_whole, everything, slice(columns, 2 * columns), load_sems
-        )
+        load_piece(meta, pieces[0], sources, out_whole, everything, load_sems)
         for rows in tiles:
             grad_flip[:, rows] = flipped(attention_grad[rows, :]).astype(jnp.bfloat16)
 
     half_at = meta[1] ^ step
     grad_parts[step] = dot_nn(grad_flip[...], mixed[...]).astype(jnp.bfloat16)
-    store_blocks(
-        meta, grad_parts.at[step], out_targets, orders[0], step, everything, out_sems.at[step]
-    )
-    await_blocks(out_whole, half_at, everything, load_sems)
+    store_piece(meta, grad_parts.at[step], targets, order, step, everything, out_sems.at[step])
+    await_piece(out_whole, half_at, everything, load_sems)
     for rows in tiles:
         mixed_grad[rows, :] = dot_nn(attention_grad[rows, :], out_whole[half_at]).astype(
             jnp.bfloat16
@@ -514,64 +650,67 @@
     sums[1:2, :] += column_sum(value_low.astype(jnp.float32))
 
 
-def qkv_backward_kernel(orders, meta, inputs, grads, resid_grad, *refs):
-    qk_sources, vo_sources, input_grad = refs[0:4], refs[4:8], refs[8]
-    q_targets, kv_targets = refs[9:11], refs[11:13]
-    weights, inputs_flip, grad_parts, qk_sems, v_sems, out_sems = refs[13:]
+def qkv_grad_kernel(orders, target_count, meta, inputs, grads, *refs):
+    targets, (inputs_flip, grad_parts, out_sems) = take(refs, target_count, 3)
     step = pl.program_id(0)
     steps = pl.num_programs(0)
     columns = grads.shape[2]
-    tiles = row_tiles(inputs.shape[0])
     slot = step % 2
     which = step % 3
 
     @pl.when(step == 0)
     def _():
-        load_blocks(
-            meta, qk_sources, orders[0], weights, slice(0, 2 * columns), slice(None), qk_sems
+        for rows in row_tiles(inputs.shape[0]):
+            inputs_flip[:, rows] = flipped(inputs[rows, :]).astype(jnp.bfloat16)
+
+    @pl.when(step >= 2)
+    def _():
+        await_stored(grad_parts.at[slot], out_sems.at[slot])
+
+    grad_parts[slot] = dot_nn(inputs_flip[...], grads[0]).astype(jnp.bfloat16)
+    span = pl.ds(pl.multiple_of(which * columns, 128), columns)
+
+    @pl.when(which == 0)
+    def _():
+        store_piece(
+            meta, grad_parts.at[slot], targets, orders[0], step // 3, span, out_sems.at[slot]
         )
-        load_blocks(
-            meta, vo_sources, orders[1], weights, slice(2 * columns, 3 * columns),
-            slice(0, columns), v_sems,
+
+    @pl.when(which > 0)
+    def _():
+        store_piece(
+            meta, grad_parts.at[slot], targets, orders[1], step // 3, span, out_sems.at[slot]
         )
+
+    @pl.when(step == steps - 1)
+    def _():
+        for late in range(2):
+            await_stored(grad_parts.at[late], out_sems.at[late])
+
+
+def input_grad_kernel(pieces, meta, grads, resid_grad, *refs):
+    qk_sources, v_sources, input_grad, weights, *sems = take(
+        refs, len(pieces[0].arrays), len(pieces[1].arrays), None, None, None, None
+    )
+    step = pl.program_id(0)
+    columns = grads.shape[2]
+    tiles = row_tiles(resid_grad.shape[0])
+
+    @pl.when(step == 0)
+    def _():
+        load_qkv(meta, pieces, (qk_sources, v_sources), weights, columns, sems)
         for rows in tiles:
-            inputs_flip[:, rows] = flipped(inputs[rows, :]).astype(jnp.bfloat16)
             input_grad[rows, :] = resid_grad[rows, :]
 
-    @pl.when(step >= 2)
-    def _():
-        await_stored(grad_parts.at[slot], out_sems.at[slot])
-
-    grad_parts[slot] = dot_nn(inputs_flip[...], grads[0]).astype(jnp.bfloat16)
-
-    @pl.when(which == 0)
-    def _():
-        store_blocks(
-            meta, grad_parts.at[slot], q_targets, orders[0], step // 3, slice(None), out_sems.at[slot]
-        )
-
-    @pl.when(which > 0)
-    def _():
-        store_blocks(
-            meta, grad_parts.at[slot], kv_targets, orders[1], step // 3,
-            pl.ds(pl.multiple_of((which - 1) * columns, 128), columns), out_sems.at[slot],
-        )
-
     half_at = meta[1] ^ (step // 3)
 
-    @pl.when(which == 0)
-    def _():
-        await_blocks(weights, half_at, slice(0, 2 * columns), qk_sems)
-        await_blocks(weights, half_at, slice(2 * columns, 3 * columns), v_sems)
-
-    span = pl.ds(pl.multiple_of(which * columns, 128), columns)
+    @pl.when(step % 3 == 0)
+    def _():
+        await_qkv(weights, half_at, columns, sems)
+
+    span = pl.ds(pl.multiple_of((step % 3) * columns, 128), columns)
     for rows in tiles:
         input_grad[rows, :] += dot_nt(grads[0, rows, :], weights[half_at, :, span])
-
-    @pl.when(step == steps - 1)
-    def _():
-        for late in range(2):
-            await_stored(grad_parts.at[late], out_sems.at[late])
 
 
 def fixed(shape):
@@ -587,11 +726,17 @@
 ANYWHERE = pl.BlockSpec(memory_space=pl.ANY)
 
 
-def run_kernel(kernel, meta, grid, ins, outs, scratch, flops, moved, name):
+def run_kernel(kernel, meta, grid, ins, outs, scratch, flops, moved, name, after=()):
+    used = len(ins)
+    ins = list(ins) + [(ANYWHERE, member) for member in after]
     in_specs, operands = zip(*ins)
     out_specs, out_shapes = zip(*outs)
+
+    def body(meta_ref, *refs):
+        kernel(meta_ref, *refs[:used], *refs[len(ins) :])
+
     return pl.pallas_call(
-        kernel,
+        body,
         grid_spec=pltpu.PrefetchScalarGridSpec(
             num_scalar_prefetch=1,
             grid=grid,
@@ -601,7 +746,7 @@
         ),
         out_shape=list(out_shapes),
         compiler_params=pltpu.CompilerParams(vmem_limit_bytes=VMEM_LIMIT),
-        cost_estimate=pl.CostEstimate(flops=flops, bytes_accessed=moved, transcendentals=0),
+        cost_estimate=pl.CostEstimate(flops=COST_WEIGHT * flops, bytes_accessed=moved, transcendentals=0),
         name=name,
     )(meta, *operands)
 
@@ -622,11 +767,22 @@
     return meta[1] ^ (step // count)
 
 
-def qkv_forward(orders, meta, inputs, bias, qk_blocks, vo_blocks):
+def sources_of(pieces):
+    return [(ANYWHERE, member) for piece in pieces for member in piece.arrays]
+
+
+def targets_of(routed, split, width, block_rows, columns):
+    if routed:
+        shape = low_shape(split * width // (2 * block_rows), block_rows, columns)
+        return [(ANYWHERE, shape), (ANYWHERE, shape)]
+    return [(ANYWHERE, low_shape(split, width, columns))]
+
+
+def qkv_forward(meta, inputs, bias, pieces, after=()):
     rows, width = inputs.shape
     columns = width // 2
     (qkv,) = run_kernel(
-        functools.partial(qkv_forward_kernel, orders),
+        functools.partial(qkv_forward_kernel, pieces),
         meta,
         (6,),
         [
@@ -636,7 +792,7 @@
                 bias,
             ),
         ]
-        + [(ANYWHERE, member) for member in qk_blocks + vo_blocks],
+        + sources_of(pieces),
         [
             (
                 pl.BlockSpec((1, rows, columns), lambda i, m: (i % 3, 0, half_of(i, m, 3))),
@@ -647,11 +803,12 @@
         6 * rows * width * width,
         8 * rows * width + 6 * width * width,
         "qkv_forward",
+        after,
     )
     return qkv
 
 
-def attention_forward(meta, qkv, slab_count):
+def attention_forward(meta, qkv, slab_count, after=()):
     _, rows, width = qkv.shape
     slab_rows = rows // slab_count
     pairs = width // PAIR
@@ -671,12 +828,13 @@
         16 * rows * slab_rows * width,
         8 * rows * width,
         "attention_forward",
-    )
-
-
-def ffn_forward(orders, meta, mixed, inputs, vectors, ffn_bias, vo_blocks, in_blocks, down_blocks):
+        after,
+    )
+
+
+def ffn_forward(meta, mixed, inputs, vectors, ffn_bias, pieces, after=()):
     rows, width = inputs.shape
-    half_width = in_blocks[0].shape[2]
+    half_width = pieces[1].count
     part = half_width // FFN_PARTS
 
     def part_at(i, m):
@@ -689,7 +847,7 @@
         low_shape(rows, 2 * half_width),
     )
     return run_kernel(
-        functools.partial(ffn_forward_kernel, orders),
+        functools.partial(ffn_forward_kernel, pieces),
         meta,
         (2 * FFN_PARTS,),
         [
@@ -698,7 +856,7 @@
             (fixed((8, width)), vectors),
             (pl.BlockSpec((1, 1, part), lambda i, m: (part_at(i, m), 0, 0)), ffn_bias),
         ]
-        + [(ANYWHERE, member) for member in vo_blocks + in_blocks + down_blocks],
+        + sources_of(pieces),
         [whole_rows, whole_rows, spread, inner, inner, whole_rows, whole_rows, spread],
         [
             pltpu.VMEM((2, width, width // 2), jnp.bfloat16),
@@ -712,15 +870,15 @@
         8 * rows * width * half_width,
         24 * rows * width + 8 * width * half_width,
         "ffn_forward",
-    )
-
-
-def ffn_backward(orders, meta, gradient, kept, vectors, in_blocks, down_blocks):
+        after,
+    )
+
+
+def ffn_backward(meta, gradient, kept, vectors, pieces, targets, after=()):
     hidden, normed_one, spread_one, activated, slope, normed_two, spread_two = kept
     rows, width = hidden.shape
-    half_width = in_blocks[0].shape[2]
+    half_width = pieces[0].count
     part = half_width // FFN_PARTS
-    slots, block_rows = 2 * in_blocks[0].shape[0], in_blocks[0].shape[1]
 
     def part_at(i, m):
         return half_of(i, m, FFN_PARTS) * FFN_PARTS + i % FFN_PARTS
@@ -728,9 +886,8 @@
     low_rows = fixed((rows, width))
     spread = fixed((rows, 128))
     inner = pl.BlockSpec((rows, part), lambda i, m: (0, part_at(i, m)))
-    target = (ANYWHERE, low_shape(slots, block_rows, half_width))
     return run_kernel(
-        functools.partial(ffn_backward_kernel, orders),
+        functools.partial(ffn_backward_kernel, pieces, len(targets)),
         meta,
         (2 * FFN_PARTS,),
         [
@@ -744,7 +901,7 @@
             (inner, slope),
             (fixed((8, width)), vectors),
         ]
-        + [(ANYWHERE, member) for member in in_blocks + down_blocks],
+        + sources_of(pieces),
         [
             (fixed_out((rows, width)), low_shape(rows, width)),
             (fixed_out((rows, width)), full_shape(rows, width)),
@@ -753,11 +910,8 @@
                 pl.BlockSpec((1, 1, part), lambda i, m: (part_at(i, m), 0, 0)),
                 full_shape(2 * FFN_PARTS, 1, part),
             ),
-            target,
-            target,
-            target,
-            target,
-        ],
+        ]
+        + targets,
         [
             pltpu.VMEM((2, width, half_width), jnp.bfloat16),
             pltpu.VMEM((2, width, half_width), jnp.bfloat16),
@@ -774,22 +928,20 @@
         16 * rows * width * half_width,
         40 * rows * width + 16 * width * half_width,
         "ffn_backward",
-    )
-
-
-def out_backward(orders, meta, attention_grad, mixed, vo_blocks):
+        after,
+    )
+
+
+def out_backward(meta, attention_grad, mixed, piece, order, targets, after=()):
     rows, width = mixed.shape
     columns = width // 2
-    slots, block_rows = 2 * vo_blocks[0].shape[0], vo_blocks[0].shape[1]
     half = pl.BlockSpec((rows, columns), lambda i, m: (0, half_of(i, m, 1)))
-    target = (ANYWHERE, low_shape(slots, block_rows, columns))
     return run_kernel(
-        functools.partial(out_backward_kernel, orders),
+        functools.partial(out_backward_kernel, [piece], order, len(targets)),
         meta,
         (2,),
-        [(fixed((rows, width)), attention_grad), (half, mixed)]
-        + [(ANYWHERE, member) for member in vo_blocks],
-        [(half, low_shape(rows, width)), target, target],
+        [(fixed((rows, width)), attention_grad), (half, mixed)] + sources_of([piece]),
+        [(half, low_shape(rows, width))] + targets,
         [
             pltpu.VMEM((2, width, columns), jnp.bfloat16),
             pltpu.VMEM((width, rows), jnp.bfloat16),
@@ -800,10 +952,11 @@
         4 * rows * width * width,
         6 * rows * width + 4 * width * width,
         "out_backward",
-    )
-
-
-def attention_backward(meta, qkv, mixed, mixed_grad, logsum, slab_count):
+        after,
+    )
+
+
+def attention_backward(meta, qkv, mixed, mixed_grad, logsum, slab_count, after=()):
     _, rows, width = qkv.shape
     slab_rows = rows // slab_count
     pairs = width // PAIR
@@ -827,44 +980,54 @@
         40 * rows * slab_rows * width,
         16 * rows * width,
         "attention_backward",
-    )
-
-
-def qkv_backward(orders, meta, inputs, grads, resid_grad, qk_blocks, vo_blocks):
+        after,
+    )
+
+
+def qkv_grad(meta, inputs, grads, orders, targets, after=()):
     rows, width = inputs.shape
     columns = width // 2
-    slots, block_rows = 2 * qk_blocks[0].shape[0], qk_blocks[0].shape[1]
-    q_target = (ANYWHERE, low_shape(slots, block_rows, columns))
-    kv_target = (ANYWHERE, low_shape(slots, block_rows, 2 * columns))
     return run_kernel(
-        functools.partial(qkv_backward_kernel, orders),
+        functools.partial(qkv_grad_kernel, orders, len(targets)),
         meta,
         (6,),
         [
             (fixed((rows, width)), inputs),
             (pl.BlockSpec((1, rows, columns), lambda i, m: (i % 3, 0, half_of(i, m, 3))), grads),
-            (fixed((rows, width)), resid_grad),
-        ]
-        + [(ANYWHERE, member) for member in qk_blocks + vo_blocks],
+        ],
+        targets,
         [
-            (fixed_out((rows, width)), full_shape(rows, width)),
-            q_target,
-            q_target,
-            kv_target,
-            kv_target,
-        ],
-        [
-            pltpu.VMEM((2, width, 3 * columns), jnp.bfloat16),
             pltpu.VMEM((width, rows), jnp.bfloat16),
             pltpu.VMEM((2, width, columns), jnp.bfloat16),
             pair_sems(),
-            pair_sems(),
-            pair_sems(),
         ],
-        12 * rows * width * width,
-        14 * rows * width + 12 * width * width,
-        "qkv_backward",
-    )
+        6 * rows * width * width,
+        8 * rows * width + 6 * width * width,
+        "qkv_grad",
+        after,
+    )
+
+
+def input_gradient(meta, grads, resid_grad, pieces, after=()):
+    rows, width = resid_grad.shape
+    columns = width // 2
+    (input_grad,) = run_kernel(
+        functools.partial(input_grad_kernel, pieces),
+        meta,
+        (6,),
+        [
+            (pl.BlockSpec((1, rows, columns), lambda i, m: (i % 3, 0, half_of(i, m, 3))), grads),
+            (fixed((rows, width)), resid_grad),
+        ]
+        + sources_of(pieces),
+        [(fixed_out((rows, width)), full_shape(rows, width))],
+        [pltpu.VMEM((2, width, 3 * columns), jnp.bfloat16), pair_sems(), pair_sems()],
+        6 * rows * width * width,
+        14 * rows * width + 6 * width * width,
+        "input_gradient",
+        after,
+    )
+    return input_grad
 
 
 def both_halves(mine, theirs, place):
@@ -898,8 +1061,6 @@
     block_rows = width // dp_size
     routed = block_rows % TILE_ROWS == 0 and dp_size & (dp_size - 1) == 0
     orders = hop_orders(dp_size if routed else PLANNED_BLOCKS)
-    gather = gather_piece if routed else gather_whole
-    scatter = scatter_piece if routed else scatter_whole
 
     own_tokens = lax.dynamic_slice_in_dim(tokens, place * rows, rows)
     own_cotangent = lax.dynamic_slice_in_dim(cotangent, place * rows, rows)
@@ -911,89 +1072,198 @@
         position = jnp.zeros((2,), jnp.int32)
     meta = jnp.concatenate([position, own_buckets, own_lengths.reshape(-1)])
 
-    pieces = []
-    for index in range(layer_count):
-        qk_shard = jnp.concatenate([qkv_weight[index, 0], qkv_weight[index, 1]], axis=1)
-        vo_shard = jnp.concatenate([qkv_weight[index, 2], out_weight[index]], axis=1)
-        pieces.append(
-            (
-                gather(qk_shard, orders[0]),
-                gather(vo_shard, orders[1]),
-                gather(ffn_in_weight[index], orders[0]),
-                gather(ffn_out_weight[index], orders[1]),
-            )
-        )
-    qv_whole = lax.all_gather(qv_bias, "tensor", axis=2, tiled=True)
-    ffn_bias_whole = lax.all_gather(ffn_in_bias, "tensor", axis=1, tiled=True)
-
-    current = own_tokens
-    kept_layers = []
-    results = []
-    for index in range(layer_count):
-        qk_blocks, vo_blocks, in_blocks, down_blocks = pieces[index]
-        zero = jnp.zeros((width,), jnp.float32)
-        bias = jnp.stack([qv_whole[index, 0], zero, qv_whole[index, 1]]).reshape(6, 1, -1)
+    bias_flat = jnp.concatenate([qv_bias.reshape(layer_count, -1), ffn_in_bias], axis=1)
+    bias_other = hop(bias_flat, ("tensor", 1))
+    bias_halves = jnp.where(
+        place == 0, jnp.stack([bias_flat, bias_other]), jnp.stack([bias_other, bias_flat])
+    )
+    qv_columns = qv_bias.shape[2]
+    ffn_columns = ffn_in_bias.shape[1]
+
+    def small_inputs(index):
+        halves = bias_halves[:, index]
+        value = halves[:, : 2 * qv_columns].reshape(2, 2, qv_columns)
+        zero = jnp.zeros((2, qv_columns), jnp.float32)
+        bias = jnp.stack([value[:, 0], zero, value[:, 1]]).reshape(6, 1, -1)
         vectors = jnp.concatenate(
             [out_bias[index], norm_gain[index], norm_bias[index], jnp.zeros((2, width), jnp.float32)]
         )
-        qkv = qkv_forward(orders, meta, current, bias, qk_blocks, vo_blocks)
-        mixed, logsum = attention_forward(meta, qkv, slabs)
-        hidden, normed_one, spread_one, activated, slope, result, normed_two, spread_two = ffn_forward(
-            orders, meta, mixed, current, vectors,
-            ffn_bias_whole[index].reshape(2 * FFN_PARTS, 1, -1), vo_blocks, in_blocks, down_blocks,
+        return bias, vectors, halves[:, 2 * qv_columns :].reshape(2 * FFN_PARTS, 1, -1)
+
+    def attention_weights(index, routed, *others):
+        shard = jnp.concatenate([*qkv_weight[index], out_weight[index]], axis=1)
+        return Gathering(shard, orders) if routed else WholeGathering(shard, orders, *others)
+
+    def ffn_weights(index, routed, *others):
+        shard = jnp.concatenate([ffn_in_weight[index], ffn_out_weight[index]], axis=1)
+        return Gathering(shard, orders) if routed else WholeGathering(shard, orders, *others)
+
+    def attention_split(pieces):
+        return [pieces[0], pieces[1].narrow(0, width // 2)], pieces[1].narrow(width // 2, width // 2)
+
+    hops = [[routed and flag for flag in flags] for flags in HOPS]
+    hops_back = [[routed and flag for flag in flags] for flags in HOPS_BACK]
+
+    def waits(flag, members):
+        return list(members) if flag else []
+
+    first, first_ffn = attention_weights(0, hops[0][0]), ffn_weights(0, hops[0][1])
+    first.far()
+    first.middle()
+    last = waits(hops[0][0], first.last())
+    first.core()
+    second, second_ffn = attention_weights(1, hops[1][0], *last), ffn_weights(1, hops[1][1], *last)
+    ffn_far = first_ffn.far()
+    ffn_middle = first_ffn.middle()
+    ffn_last = first_ffn.last()
+    bias, vectors, ffn_bias = small_inputs(0)
+    qkv_pieces, out_piece = attention_split(first.pieces())
+    qkv = qkv_forward(meta, own_tokens, bias, qkv_pieces, waits(hops[0][1], ffn_middle))
+    first_ffn.core(qkv)
+    second_far = second.far(*last)
+    second_middle = second.middle(qkv)
+    mixed, logsum = attention_forward(
+        meta, qkv, slabs, waits(hops[0][1], ffn_last) + waits(hops[1][0], second_far)
+    )
+    first_pieces = (qkv_pieces, out_piece, first_ffn.pieces())
+    second_ffn_far = second_ffn.far(mixed)
+    second_last = second.last(mixed)
+    out = ffn_forward(
+        meta, mixed, own_tokens, vectors, ffn_bias, [out_piece] + first_pieces[2],
+        waits(hops[1][0], second_middle),
+    )
+    kept_layers = [(own_tokens, qkv, mixed, logsum, vectors, out)]
+    layer_one = out[5]
+    second.core(layer_one)
+    second_ffn_middle = second_ffn.middle(layer_one)
+    bias, vectors, ffn_bias = small_inputs(1)
+    qkv_pieces, out_piece = attention_split(second.pieces())
+    qkv = qkv_forward(
+        meta, layer_one, bias, qkv_pieces,
+        waits(hops[1][1], second_ffn_far) + waits(hops[1][0], second_last),
+    )
+    second_ffn.last(qkv)
+    mixed, logsum = attention_forward(meta, qkv, slabs, waits(hops[1][1], second_ffn_middle))
+    one_other = hop(tied(layer_one, [mixed]), ("tensor", 1))
+    second_ffn.core(mixed)
+    second_pieces = (qkv_pieces, out_piece, second_ffn.pieces())
+    out = ffn_forward(
+        meta, mixed, layer_one, vectors, ffn_bias, [out_piece] + second_pieces[2]
+    )
+    kept_layers.append((layer_one, qkv, mixed, logsum, vectors, out))
+    layer_two = out[5]
+    two_other = hop(layer_two, ("tensor", 1))
+
+    def targets(flag, columns):
+        return targets_of(flag, split, width, block_rows, columns)
+
+    def scattering(flag, members, sides):
+        kind = Scattering if flag else WholeScattering
+        return kind(members, orders, sides)
+
+    half_ffn = first_ffn.width
+
+    def ffn_back(index, gradient, pieces, after=()):
+        inputs, qkv, mixed, logsum, vectors, out = kept_layers[index]
+        hidden, normed_one, spread_one, activated, slope, _, normed_two, spread_two = out
+        kept = (hidden, normed_one, spread_one, activated, slope, normed_two, spread_two)
+        attention_grad, resid_grad, sums, ffn_sums, *members = ffn_backward(
+            meta, gradient, kept, vectors, pieces[2], targets(hops_back[index][1], 2 * half_ffn), after
         )
-        kept_layers.append(
-            (
-                current, qkv, mixed, logsum, vectors,
-                (hidden, normed_one, spread_one, activated, slope, normed_two, spread_two),
-            )
+        scatter = scattering(
+            hops_back[index][1], [members], [[(0, 0, half_ffn)], [(0, half_ffn, 2 * half_ffn)]]
         )
-        current = result
-        results.append(both_halves(result, hop(result, ("tensor", 1)), place))
-
-    gradient = own_cotangent
-    matrix_grads = [None] * layer_count
-    small_grads = [None] * layer_count
-    for index in reversed(range(layer_count)):
-        qk_blocks, vo_blocks, in_blocks, down_blocks = pieces[index]
-        inputs, qkv, mixed, logsum, vectors, kept = kept_layers[index]
-        attention_grad, resid_grad, sums, ffn_sums, in_keep, in_send, down_keep, down_send = (
-            ffn_backward(orders, meta, gradient, kept, vectors, in_blocks, down_blocks)
+        return attention_grad, resid_grad, (sums, ffn_sums), scatter
+
+    def out_back(index, attention_grad, pieces, after=()):
+        mixed = kept_layers[index][2]
+        return out_backward(
+            meta, attention_grad, mixed, pieces[1], orders[0], targets(hops_back[index][0], width // 2), after
         )
-        in_grad = scatter(in_keep, in_send, orders[0])
-        down_grad = scatter(down_keep, down_send, orders[1])
-        mixed_grad, out_keep, out_send = out_backward(orders, meta, attention_grad, mixed, vo_blocks)
-        out_grad = scatter(out_keep, out_send, orders[0])
-        grads, qkv_sums = attention_backward(meta, qkv, mixed, mixed_grad, logsum, slabs)
-        gradient, q_keep, q_send, kv_keep, kv_send = qkv_backward(
-            orders, meta, inputs, grads, resid_grad, qk_blocks, vo_blocks
+
+    def attention_back(index, mixed_grad, after=()):
+        _, qkv, mixed, logsum, _, _ = kept_layers[index]
+        return attention_backward(meta, qkv, mixed, mixed_grad, logsum, slabs, after)
+
+    def qkv_grads(index, grads, out_members, after=()):
+        members = qkv_grad(
+            meta, kept_layers[index][0], grads, orders,
+            targets(hops_back[index][0], 3 * width // 2), after,
         )
-        q_grad = scatter(q_keep, q_send, orders[0])
-        kv_grad = scatter(kv_keep, kv_send, orders[1])
-        columns = q_grad.shape[1]
-        matrix_grads[index] = (
-            jnp.stack([q_grad, kv_grad[:, :columns], kv_grad[:, columns:]]),
-            out_grad,
-            in_grad,
-            down_grad,
+        columns = width // 2
+        return scattering(
+            hops_back[index][0],
+            [out_members, members],
+            [[(0, 0, columns), (1, 0, columns)], [(1, columns, 3 * columns)]],
         )
-        small_grads[index] = lax.psum(
-            jnp.concatenate([sums[:6].reshape(-1), qkv_sums[:2].reshape(-1), ffn_sums.reshape(-1)]),
-            AXES,
+
+    def flat_smalls(sums, ffn_sums, qkv_sums):
+        return jnp.concatenate(
+            [sums[:6].reshape(-1), qkv_sums[:2].reshape(-1), ffn_sums.reshape(-1)]
         )
+
+    attention_grad, resid_grad, sums, ffn_one = ffn_back(1, own_cotangent, second_pieces, [one_other])
+    layer_one_whole = both_halves(layer_one, one_other, place)
+    ffn_core = ffn_one.core()
+    mixed_grad, *out_members = out_back(1, attention_grad, second_pieces, [two_other])
+    layer_two_whole = both_halves(layer_two, two_other, place)
+    grads, qkv_sums = attention_back(1, mixed_grad, ffn_core)
+    smalls_one = flat_smalls(*sums, qkv_sums)
+    ffn_last = ffn_one.last(mixed_grad)
+    attention_one = qkv_grads(1, grads, out_members, waits(hops_back[1][1], ffn_last))
+    attention_core = attention_one.core()
+    gradient = input_gradient(meta, grads, resid_grad, second_pieces[0], attention_one.begun)
+    ffn_middle = ffn_one.middle(gradient)
+    attention_last = attention_one.last(gradient)
+    attention_grad, resid_grad, sums, ffn_zero = ffn_back(
+        0, gradient, first_pieces, waits(hops_back[1][1], ffn_middle) + attention_core
+    )
+    ffn_far = ffn_one.far(attention_grad)
+    ffn_core = ffn_zero.core()
+    attention_middle = attention_one.middle(attention_grad)
+    mixed_grad, *out_members = out_back(
+        0, attention_grad, first_pieces, waits(hops_back[1][0], attention_last)
+    )
+    ffn_last = ffn_zero.last(mixed_grad)
+    attention_far = attention_one.far(mixed_grad)
+    grads, qkv_sums = attention_back(
+        0, mixed_grad, ffn_core + waits(hops_back[1][0], attention_middle)
+    )
+    smalls_zero = flat_smalls(*sums, qkv_sums)
+    ffn_middle = ffn_zero.middle(grads)
+    before = ffn_last + waits(hops_back[1][0], attention_far) + waits(hops_back[1][1], ffn_far)
+    if LATE_WEIGHTS:
+        gradient = input_gradient(meta, grads, resid_grad, first_pieces[0], before)
+        attention_zero = qkv_grads(0, grads, out_members, [gradient, *ffn_middle])
+        attention_zero.core()
+    else:
+        attention_zero = qkv_grads(0, grads, out_members, before)
+        attention_zero.core()
+        gradient = input_gradient(
+            meta, grads, resid_grad, first_pieces[0], attention_zero.begun + ffn_middle
+        )
+    ffn_zero.far()
+    attention_last = attention_zero.last(gradient)
+    attention_zero.middle()
+    attention_zero.far()
+
     low_gradient = gradient.astype(jnp.bfloat16)
+    if HOLD_TOKENS:
+        low_gradient = tied(low_gradient, waits(hops_back[0][0], attention_last))
     token_grad = both_halves(
         gradient, hop(low_gradient, ("tensor", 1)).astype(jnp.float32), place
     )
-
-    smalls = jnp.stack(small_grads)
+    matrix_grads = []
+    for attention, ffn in ((attention_zero, ffn_zero), (attention_one, ffn_one)):
+        out_part, *qkv_parts = jnp.split(attention.result, 4, axis=1)
+        matrix_grads.append((jnp.stack(qkv_parts), out_part, *jnp.split(ffn.result, 2, axis=1)))
+    smalls = tied(jnp.stack([smalls_zero, smalls_one]), [gradient])
+    smalls = sum_over_all(smalls, routed)
     eight = smalls[:, : 8 * width].reshape(layer_count, 4, 2, width)
     ffn_total = smalls[:, 8 * width :]
-    qv_columns = qv_bias.shape[2]
-    ffn_columns = ffn_in_bias.shape[1]
     return (
-        results[0],
-        results[layer_count - 1],
+        layer_one_whole,
+        layer_two_whole,
         token_grad,
         jnp.stack([member[0] for member in matrix_grads]),
         lax.dynamic_slice_in_dim(eight[:, 3], place * qv_columns, qv_columns, axis=2),

time: 917 us -> 601 us (0.66)
  waiting for transfers between devices: 419 us -> 116 us
  other arithmetic: 65.3 us -> 51.7 us
  local copies, waits for them, and re-layouts: 20 us -> 33.4 us
  blocking collectives: 11.6 us -> 0 us
    ppermute x101 -> x58, waiting for transfers between devices: 321 us -> 116 us  [hop(): return lax.ppermute(member, axis, pairs)]
    psum x1 -> x0, waiting for transfers between devices: 98.3 us -> none  [on_device(): lax.psum(jnp.concatenate([sums[:6].reshape(-1), qkv_sums[:2].reshape(-1),...]
    concatenate x27 -> x21, other arithmetic: 24.9 us -> 4.25 us  [the longest x2 1.46 us: ffn_weights(): jnp.concatenate([ffn_in_weight[index], ffn_out_weight[index]], axis=1)]
    all_gather x2 -> x0, blocking collectives: 11.6 us -> none  [the longest x1 7.04 us: on_device(): ffn_bias_whole = lax.all_gather(ffn_in_bias, 'tensor', axis=1, tiled=True)]
    convert_element_type x40 -> x7, other arithmetic: 19.4 us -> 12.2 us  [the longest x6 11.1 us: halve(): upper = self.total(side, lambda part: part[half:]).astype(jnp.bfloat16)]
    pallas_call x14 -> x16, Pallas kernels: 296 us -> 301 us  [run_kernel(): pl.pallas_call(body, grid_spec=pltpu.PrefetchScalarGridSpec(num_scalar_pr...]
    ppermute x101 -> x58, starting transfers between devices: 82 us -> 78.1 us  [hop(): return lax.ppermute(member, axis, pairs)]
  transfers between devices with their start and end apart: 102 -> 61, of which waited for: 54 -> 25; matrix products, arithmetic and copies ran while one was open for 8% -> 12% of each run, Pallas kernels for 12% -> 51%
where the time goes in v3:
time: 601 us; the launch traced here: 596 us
  Pallas kernels  301 us (50%)
  waiting for transfers between devices  116 us (19%)
  starting transfers between devices  78.4 us (13%)
  other arithmetic  51.7 us (9%)
  local copies, waits for them, and re-layouts  33.4 us (6%)
  between operations  15 us (2%)
    pallas_call x16, Pallas kernels, run_kernel(): pl.pallas_call(body, grid_spec=pltpu.PrefetchScalarGridSpec(num_scalar_pr...  301 us
    ppermute x58, waiting for transfers between devices, hop(): return lax.ppermute(member, axis, pairs)  116 us
    ppermute x58, starting transfers between devices, hop(): return lax.ppermute(member, axis, pairs)  78.1 us
  transfers between devices with their start and end apart: 61, of which 25 were waited for; matrix products, arithmetic and copies ran while one was open for 12% of the time, Pallas kernels for 51%

profile of v3, /device:TPU:0, one launch (start us, length us, event | category | flops | bytes accessed | tf_op | source)
XLA Modules:
  0.0 596.0 jit_solution(9969394243384916197)
XLA Ops:
  11.6 3.0 collective-permute-start.1
  14.6 2.6 collective-permute-start.2
  37.0 3.8 collective-permute-done.8
  46.7 16.3 %collective-permute-done.9.refs_7_.refs_5_.refs_3_ = bf16[8,48,768]{2,1,0:T(8,128)(2,1)S(1)} collective-permute-done((bf16[8,48,768]{2,1,0:T(8,128)(2,1)S(1)}, bf16[8,48,768]{2,1,0:T(8,128)(2,1)S(1)}, u32[]{:S(2)}, u32[]{:S(2)}) %collective-permute-start.9) | collective-permute-done | bytes 589856 | tf_op jit(solution)/shard_map/ppermute | solution.py:78
  63.8 4.0 collective-permute-start.12
  70.0 5.3 collective-permute-done.12
  76.1 2.4 collective-permute-start.14
  78.5 8.7 %collective-permute-done.14 = bf16[1,48,1536]{2,1,0:T(8,128)(2,1)S(1)} collective-permute-done((bf16[1,48,1536]{2,1,0:T(8,128)(2,1)S(1)}, bf16[1,48,1536]{2,1,0:T(8,128)(2,1)S(1)}, u32[]{:S(2)}, u32[]{:S(2)}) %collective-permute-start.14) | collective-permute-done | bytes 147488 | tf_op jit(solution)/shard_map/ppermute | solution.py:78
  89.7 11.2 %qkv_forward.2.refs_0_ = bf16[3,1024,768]{2,1,0:T(8,128)(2,1)} custom-call(s32[12]{0:T(128)} %pad_add_fusion.meta_ref, bf16[1024,768]{1,0:T(8,128)(2,1)} %constant_dynamic-slice_fusion.2.refs_0_.refs_1_, f32[6,1,384]{2,1,0:T(1,128)} %reshape.345.refs_1_, bf16[8,48,768]{2,1,0:T(8,128)(2,1)} %copy-done.45, bf16[8,48,768]{2,1,0:T(8,128)(2,1)} %copy-done.49, ...), custom_call_target="tpu_custom_call" | custom-call | flops 28991029248 | bytes 9830400 | tf_op jit(solution)/shard_map/qkv_forward/pallas_call | solution.py:738
  101.6 17.6 %attention_forward.2 = (bf16[1024,768]{1,0:T(8,128)(2,1)}, f32[2,6,8,512]{3,2,1,0:T(8,128)}) custom-call(s32[12]{0:T(128)} %pad_add_fusion.meta_ref, bf16[3,1024,768]{2,1,0:T(8,128)(2,1)} %qkv_forward.2.refs_0_, bf16[4,48,768]{2,1,0:T(8,128)(2,1)} %get-tuple-element.82.refs_1_, bf16[4,48,768]{2,1,0:T(8,128)(2,1)} %get-tuple-element.83.refs_2_), custom_call_target="tpu_custom_call" | custom-call | flops 51539607552 | bytes 6291456 | tf_op jit(solution)/shard_map/attention_forward/pallas_call | solution.py:738
  124.5 6.8 %collective-permute-done.15 = bf16[4,48,768]{2,1,0:T(8,128)(2,1)S(1)} collective-permute-done((bf16[4,48,768]{2,1,0:T(8,128)(2,1)S(1)}, bf16[4,48,768]{2,1,0:T(8,128)(2,1)S(1)}, u32[]{:S(2)}, u32[]{:S(2)}) %collective-permute-start.15) | collective-permute-done | bytes 294944 | tf_op jit(solution)/shard_map/ppermute | solution.py:78
  133.5 32.6 %ffn_forward.2 = (bf16[1024,768]{1,0:T(8,128)(2,1)}, bf16[1024,768]{1,0:T(8,128)(2,1)}, f32[1024,128]{1,0:T(8,128)}, bf16[1024,3072]{1,0:T(8,128)(2,1)}, bf16[10...) custom-call(s32[12]{0:T(128)} %pad_add_fusion.meta_ref, ...), custom_call_target="tpu_custom_call" | custom-call | flops 77309411328 | bytes 28311552 | tf_op jit(solution)/shard_map/ffn_forward/pallas_call | solution.py:738
  169.6 11.2 %qkv_forward.3.refs_0_ = bf16[3,1024,768]{2,1,0:T(8,128)(2,1)} custom-call(s32[12]{0:T(128)} %pad_add_fusion.meta_ref, bf16[1024,768]{1,0:T(8,128)(2,1)} %get-tuple-element.90.refs_0_.refs_1_, f32[6,1,384]{2,1,0:T(1,128)} %reshape.349.refs_1_, bf16[8,48,768]{2,1,0:T(8,128)(2,1)} %constant_dynamic-update-slice_fusion.12.refs_10_.refs_2_, ...), custom_call_target="tpu_custom_call" | custom-call | flops 28991029248 | bytes 9830400 | tf_op jit(solution)/shard_map/qkv_forward/pallas_call | solution.py:738
  180.8 17.8 %attention_forward.3 = (bf16[1024,768]{1,0:T(8,128)(2,1)}, f32[2,6,8,512]{3,2,1,0:T(8,128)}) custom-call(s32[12]{0:T(128)} %pad_add_fusion.meta_ref, bf16[3,1024,768]{2,1,0:T(8,128)(2,1)} %qkv_forward.3.refs_0_), custom_call_target="tpu_custom_call" | custom-call | flops 51539607552 | bytes 6291456 | tf_op jit(solution)/shard_map/attention_forward/pallas_call | solution.py:738
  199.8 31.9 %ffn_forward.3 = (bf16[1024,768]{1,0:T(8,128)(2,1)}, bf16[1024,768]{1,0:T(8,128)(2,1)}, f32[1024,128]{1,0:T(8,128)}, bf16[1024,3072]{1,0:T(8,128)(2,1)}, bf16[10...) custom-call(s32[12]{0:T(128)} %pad_add_fusion.meta_ref, ...), custom_call_target="tpu_custom_call" | custom-call | flops 77309411328 | bytes 28311552 | tf_op jit(solution)/shard_map/ffn_forward/pallas_call | solution.py:738
  233.2 2.6 collective-permute-done.23.refs_11_
  237.0 34.8 %ffn_backward.2 = (bf16[1024,768]{1,0:T(8,128)(2,1)}, f32[1024,768]{1,0:T(8,128)}, f32[8,768]{1,0:T(8,128)}, f32[6,1,512]{2,1,0:T(1,128)}, bf16[2,768,3072]{2,1,0:T(8,128)(2,1)}) custom-call(s32[12]{0:T(128)} %pad_add_fusion.meta_ref, bf16[1024,768]{1,0:T(8,128)(2,1)} %constant_dynamic-slice_fusion.1.refs_0_, bf16[1024,768]{1,0:T(8,128)(2,1)} %get-tuple-element.93.refs_1_, ...), custom_call_target="tpu_custom_call" | custom-call | flops 154618822656 | bytes 50331648 | tf_op jit(solution)/shard_map/ffn_backward/pallas_call | solution.py:738
  273.7 2.0 maximum_select_fusion.1
  275.8 7.8 %out_backward.2 = (bf16[1024,768]{1,0:T(8,128)(2,1)}, bf16[16,48,384]{2,1,0:T(8,128)(2,1)}, bf16[16,48,384]{2,1,0:T(8,128)(2,1)}) custom-call(s32[12]{0:T(128)} %pad_add_fusion.meta_ref, bf16[1024,768]{1,0:T(8,128)(2,1)} %get-tuple-element.100.refs_0_, bf16[1024,768]{1,0:T(8,128)(2,1)} %get-tuple-element.89.refs_0_.refs_1_, ...), custom_call_target="tpu_custom_call" | custom-call | flops 19327352832 | bytes 7077888 | tf_op jit(solution)/shard_map/out_backward/pallas_call | solution.py:738
  283.5 22.4 %attention_backward.2 = (bf16[3,1024,768]{2,1,0:T(8,128)(2,1)}, f32[8,768]{1,0:T(8,128)}) custom-call(s32[12]{0:T(128)} %pad_add_fusion.meta_ref, bf16[3,1024,768]{2,1,0:T(8,128)(2,1)} %qkv_forward.3.refs_0_, bf16[1024,768]{1,0:T(8,128)(2,1)} %get-tuple-element.89.refs_0_.refs_1_, bf16[1024,768]{1,0:T(8,128)(2,1)} %get-tuple-element.101.refs_2_, ...), custom_call_target="tpu_custom_call" | custom-call | flops 128849018880 | bytes 12582912 | tf_op jit(solution)/shard_map/attention_backward/pallas_call | solution.py:738
  306.0 11.1 %qkv_grad.2 = (bf16[16,48,1152]{2,1,0:T(8,128)(2,1)}, bf16[16,48,1152]{2,1,0:T(8,128)(2,1)}) custom-call(s32[12]{0:T(128)} %pad_add_fusion.meta_ref, bf16[1024,768]{1,0:T(8,128)(2,1)} %get-tuple-element.90.refs_0_.refs_1_, bf16[3,1024,768]{2,1,0:T(8,128)(2,1)} %get-tuple-element.103.refs_1_.refs_0_), custom_call_target="tpu_custom_call" | custom-call | flops 28991029248 | bytes 9830400 | tf_op jit(solution)/shard_map/qkv_grad/pallas_call | solution.py:738
  317.6 13.2 %input_gradient.2.refs_0_ = f32[1024,768]{1,0:T(8,128)} custom-call(s32[12]{0:T(128)} %pad_add_fusion.meta_ref, bf16[3,1024,768]{2,1,0:T(8,128)(2,1)} %get-tuple-element.103.refs_1_.refs_0_, f32[1024,768]{1,0:T(8,128)} %get-tuple-element.104.refs_1_, bf16[8,48,768]{2,1,0:T(8,128)(2,1)} %constant_dynamic-update-slice_fusion.12.refs_10_.refs_2_, ...), custom_call_target="tpu_custom_call" | custom-call | flops 28991029248 | bytes 14548992 | tf_op jit(solution)/shard_map/input_gradient/pallas_call | solution.py:738
  333.3 2.1 add_convert_fusion.5
  338.1 2.0 collective-permute-start.27
  340.1 35.2 %ffn_backward.3 = (bf16[1024,768]{1,0:T(8,128)(2,1)}, f32[1024,768]{1,0:T(8,128)}, f32[8,768]{1,0:T(8,128)}, f32[6,1,512]{2,1,0:T(1,128)}, bf16[16,48,3072]{2,1,0:T(8,128)(2,1)}, /*index=5*/bf16[16,48,3072]{2,1,0:T(8,128)(2,1)}) custom-call(s32[12]{0:T(128)} %pad_add_fusion.meta_ref, f32[1024,768]{1,0:T(8,128)} %input_gradient.2.refs_0_, ...), custom_call_target="tpu_custom_call" | custom-call | flops 154618822656 | bytes 50331648 | tf_op jit(solution)/shard_map/ffn_backward/pallas_call | solution.py:738
  375.4 3.7 maximum_select_fusion.2
  384.2 8.1 %out_backward.3 = (bf16[1024,768]{1,0:T(8,128)(2,1)}, bf16[16,48,384]{2,1,0:T(8,128)(2,1)}, bf16[16,48,384]{2,1,0:T(8,128)(2,1)}) custom-call(s32[12]{0:T(128)} %pad_add_fusion.meta_ref, bf16[1024,768]{1,0:T(8,128)(2,1)} %get-tuple-element.115.refs_0_, bf16[1024,768]{1,0:T(8,128)(2,1)} %get-tuple-element.81.refs_0_.refs_1_, bf16[8,48,768]{2,1,0:T(8,128)(2,1)} %copy-done.46, ...), custom_call_target="tpu_custom_call" | custom-call | flops 19327352832 | bytes 7077888 | tf_op jit(solution)/shard_map/out_backward/pallas_call | solution.py:738
  395.9 3.6 collective-permute-start.34
  402.9 3.2 collective-permute-done.34
  406.1 8.7 %collective-permute-done.35 = bf16[48,1536]{1,0:T(8,128)(2,1)S(1)} collective-permute-done((bf16[48,1536]{1,0:T(8,128)(2,1)S(1)}, bf16[48,1536]{1,0:T(8,128)(2,1)S(1)}, u32[]{:S(2)}, u32[]{:S(2)}) %collective-permute-start.35) | collective-permute-done | bytes 147488 | tf_op jit(solution)/shard_map/ppermute | solution.py:78
  415.5 4.5 add_convert_fusion
  421.9 22.5 %attention_backward.3 = (bf16[3,1024,768]{2,1,0:T(8,128)(2,1)}, f32[8,768]{1,0:T(8,128)}) custom-call(s32[12]{0:T(128)} %pad_add_fusion.meta_ref, bf16[3,1024,768]{2,1,0:T(8,128)(2,1)} %qkv_forward.2.refs_0_, bf16[1024,768]{1,0:T(8,128)(2,1)} %get-tuple-element.81.refs_0_.refs_1_, bf16[1024,768]{1,0:T(8,128)(2,1)} %get-tuple-element.119.refs_2_, ...), custom_call_target="tpu_custom_call" | custom-call | flops 128849018880 | bytes 12582912 | tf_op jit(solution)/shard_map/attention_backward/pallas_call | solution.py:738
  446.6 13.1 %input_gradient.3.refs_2_ = f32[1024,768]{1,0:T(8,128)} custom-call(s32[12]{0:T(128)} %pad_add_fusion.meta_ref, bf16[3,1024,768]{2,1,0:T(8,128)(2,1)} %get-tuple-element.124.refs_0_.refs_1_, f32[1024,768]{1,0:T(8,128)} %get-tuple-element.125.refs_1_, bf16[8,48,768]{2,1,0:T(8,128)(2,1)} %copy-done.45, bf16[8,48,768]{2,1,0:T(8,128)(2,1)} %copy-done.49, ...), custom_call_target="tpu_custom_call" | custom-call | flops 28991029248 | bytes 14548992 | tf_op jit(solution)/shard_map/input_gradient/pallas_call | solution.py:738
  462.7 2.8 collective-permute-done.50
  470.1 6.7 %collective-permute-start.52 = (f32[2,9216]{1,0:T(2,128)S(1)}, f32[2,9216]{1,0:T(2,128)S(1)}, u32[]{:S(2)}, u32[]{:S(2)}) collective-permute-start(f32[2,9216]{1,0:T(2,128)S(1)} %add.729), channel_id=1, source_target_pairs={{0,8},{2,10},{4,12},{6,14},{8,0},{10,2},{12,4},{14,6},{16,24},{18,... | collective-permute-start | bytes 221192 | tf_op jit(solution)/shard_map/ppermute | solution.py:78
  476.8 2.7 collective-permute-start.53
  480.9 3.1 add_convert_fusion.3
  490.4 7.6 %collective-permute-done.39.refs_3_ = bf16[4,48,1536]{2,1,0:T(8,128)(2,1)S(1)} collective-permute-done((bf16[4,48,1536]{2,1,0:T(8,128)(2,1)}, bf16[4,48,1536]{2,1,0:T(8,128)(2,1)S(1)}, u32[]{:S(2)}, u32[]{:S(2)}) %collective-permute-start.39) | collective-permute-done | bytes 589856 | tf_op jit(solution)/shard_map/ppermute | solution.py:78
  498.0 4.7 collective-permute-done.40.refs_4_
  503.5 10.8 %qkv_grad.3 = (bf16[16,48,1152]{2,1,0:T(8,128)(2,1)}, bf16[16,48,1152]{2,1,0:T(8,128)(2,1)}) custom-call(s32[12]{0:T(128)} %pad_add_fusion.meta_ref, bf16[1024,768]{1,0:T(8,128)(2,1)} %constant_dynamic-slice_fusion.2.refs_0_.refs_1_, bf16[3,1024,768]{2,1,0:T(8,128)(2,1)} %get-tuple-element.124.refs_0_.refs_1_, f32[1024,768]{1,0:T(8,128)} %input_gradient.3.refs_2_, ...), custom_call_target="tpu_custom_call" | custom-call | flops 28991029248 | bytes 9830400 | tf_op jit(solution)/shard_map/qkv_grad/pallas_call | solution.py:738
  518.8 2.5 collective-permute-start.56
  523.4 10.1 %collective-permute-done.55 = bf16[48,3072]{1,0:T(8,128)(2,1)S(1)} collective-permute-done((bf16[48,3072]{1,0:T(8,128)(2,1)S(1)}, bf16[48,3072]{1,0:T(8,128)(2,1)S(1)}, u32[]{:S(2)}, u32[]{:S(2)}) %collective-permute-start.55) | collective-permute-done | bytes 294944 | tf_op jit(solution)/shard_map/ppermute | solution.py:78
  533.5 8.8 %collective-permute-done.56 = bf16[48,3072]{1,0:T(8,128)(2,1)S(1)} collective-permute-done((bf16[48,3072]{1,0:T(8,128)(2,1)S(1)}, bf16[48,3072]{1,0:T(8,128)(2,1)S(1)}, u32[]{:S(2)}, u32[]{:S(2)}) %collective-permute-start.56) | collective-permute-done | bytes 294944 | tf_op jit(solution)/shard_map/ppermute | solution.py:78
  549.7 9.3 %collective-permute-done.44 = bf16[8,48,768]{2,1,0:T(8,128)(2,1)S(1)} collective-permute-done((bf16[8,48,768]{2,1,0:T(8,128)(2,1)S(1)}, bf16[8,48,768]{2,1,0:T(8,128)(2,1)S(1)}, u32[]{:S(2)}, u32[]{:S(2)}) %collective-permute-start.44) | collective-permute-done | bytes 589856 | tf_op jit(solution)/shard_map/ppermute | solution.py:78
  559.5 3.6 collective-permute-done.43
  566.1 6.1 %collective-permute-start.46 = (bf16[48,1536]{1,0:T(8,128)(2,1)S(1)}, bf16[48,1536]{1,0:T(8,128)(2,1)S(1)}, u32[]{:S(2)}, u32[]{:S(2)}) collective-permute-start(bf16[48,1536]{1,0:T(8,128)(2,1)S(1)} %pad_maximum_fusion.20), channel_id=1, source_target_pairs={{0,8},{2,10},{4,12},{6,14},{8,0},{10,2},{12,4},{14,6},{16,24},{18,... | collective-permute-start | bytes 442376 | tf_op jit(solution)/shard_map/ppermute | solution.py:78
  575.3 3.1 maximum_select_fusion
  578.4 5.3 collective-permute-done.47
  (324 shorter events, 117.7 us)
Async XLA Ops:
  7.2 126.3 %all-gather.3.cloned.1.call-start = ((), (), s32[]{:S(2)}) async-start(), calls=%async_computation.1 | async-start | bytes 9732096 | tf_op jit(solution)/shard_map/all_gather | solution.py:136
  9.3 190.5 %all-gather.5.cloned.1.call-start = ((), (), s32[]{:S(2)}) async-start(), calls=%async_computation.2 | async-start | bytes 9732096 | tf_op jit(solution)/shard_map/all_gather | solution.py:136
  11.6 18.5 %collective-permute-start.1 = (bf16[1,48,1536]{2,1,0:T(8,128)(2,1)}, bf16[1,48,1536]{2,1,0:T(8,128)(2,1)}, u32[]{:S(2)}, u32[]{:S(2)}) collective-permute-start(bf16[1,48,1536]{2,1,0:T(8,128)(2,1)} %maximum_bitcast_fusion.2), channel_id=1, source_target_pairs={{0,8},{2,10},{4,12},{6,14},{8,0},{10,2},{12,4},{14,6},{16,24},{18,... | collective-permute-start | bytes 442376 | tf_op jit(solution)/shard_map/ppermute | solution.py:78
  14.6 16.9 %collective-permute-start.2 = (bf16[1,48,1536]{2,1,0:T(8,128)(2,1)}, bf16[1,48,1536]{2,1,0:T(8,128)(2,1)}, u32[]{:S(2)}, u32[]{:S(2)}) collective-permute-start(bf16[1,48,1536]{2,1,0:T(8,128)(2,1)} %maximum_bitcast_fusion.2), channel_id=1, source_target_pairs={{0,16},{2,18},{4,20},{6,22},{8,24},{10,26},{12,28},{14,30},{16,0},... | collective-permute-start | bytes 442376 | tf_op jit(solution)/shard_map/ppermute | solution.py:78
  17.2 15.3 %collective-permute-start.3 = (bf16[1,48,1536]{2,1,0:T(8,128)(2,1)}, bf16[1,48,1536]{2,1,0:T(8,128)(2,1)}, u32[]{:S(2)}, u32[]{:S(2)}) collective-permute-start(bf16[1,48,1536]{2,1,0:T(8,128)(2,1)} %maximum_bitcast_fusion.2), channel_id=1, source_target_pairs={{0,24},{2,26},{4,28},{6,30},{8,16},{10,18},{12,20},{14,22},{16,8},... | collective-permute-start | bytes 442376 | tf_op jit(solution)/shard_map/ppermute | solution.py:78
  40.8 22.2 %collective-permute-start.9 = (bf16[8,48,768]{2,1,0:T(8,128)(2,1)S(1)}, bf16[8,48,768]{2,1,0:T(8,128)(2,1)S(1)}, u32[]{:S(2)}, u32[]{:S(2)}) collective-permute-start(bf16[8,48,768]{2,1,0:T(8,128)(2,1)S(1)} %constant_dynamic-update-slice_fusion.7.refs_6_.refs_4_.refs_2_), channel_id=1, source_target_pairs={{0,4},{2,6},{4,0},{6,2},{8,12},{10,14},{12,8},{14,10},{16,20},{18,... | collective-permute-start | bytes 1769480 | tf_op jit(solution)/shard_map/ppermute | solution.py:78
  42.9 20.9 %collective-permute-start.5 = (bf16[8,48,768]{2,1,0:T(8,128)(2,1)S(1)}, bf16[8,48,768]{2,1,0:T(8,128)(2,1)S(1)}, u32[]{:S(2)}, u32[]{:S(2)}) collective-permute-start(bf16[8,48,768]{2,1,0:T(8,128)(2,1)S(1)} %constant_dynamic-update-slice_fusion.2.refs_2_), channel_id=1, source_target_pairs={{0,1},{1,0},{2,3},{3,2},{4,5},{5,4},{6,7},{7,6},{8,9},{9,8},{10,11... | collective-permute-start | bytes 1769480 | tf_op jit(solution)/shard_map/ppermute | solution.py:78
  46.2 41.9 %collective-permute-start.10 = (bf16[8,48,768]{2,1,0:T(8,128)(2,1)S(1)}, bf16[8,48,768]{2,1,0:T(8,128)(2,1)}, u32[]{:S(2)}, u32[]{:S(2)}) collective-permute-start(bf16[8,48,768]{2,1,0:T(8,128)(2,1)S(1)} %constant_dynamic-update-slice_fusion.7.refs_6_.refs_4_.refs_2_), channel_id=1, source_target_pairs={{0,2},{2,0},{4,6},{6,4},{8,10},{10,8},{12,14},{14,12},{16,18},{18,... | collective-permute-start | bytes 1769480 | tf_op jit(solution)/shard_map/ppermute | solution.py:78
  46.2 41.9 %collective-permute-start.6 = (bf16[8,48,768]{2,1,0:T(8,128)(2,1)S(1)}, bf16[8,48,768]{2,1,0:T(8,128)(2,1)}, u32[]{:S(2)}, u32[]{:S(2)}) collective-permute-start(bf16[8,48,768]{2,1,0:T(8,128)(2,1)S(1)} %constant_dynamic-update-slice_fusion.2.refs_2_), channel_id=1, source_target_pairs={{0,2},{2,0},{4,6},{6,4},{8,10},{10,8},{12,14},{14,12},{16,18},{18,... | collective-permute-start | bytes 1769480 | tf_op jit(solution)/shard_map/ppermute | solution.py:78
  63.8 11.5 %collective-permute-start.12 = (bf16[1,48,1536]{2,1,0:T(8,128)(2,1)S(1)}, bf16[1,48,1536]{2,1,0:T(8,128)(2,1)S(1)}, u32[]{:S(2)}, u32[]{:S(2)}) collective-permute-start(bf16[1,48,1536]{2,1,0:T(8,128)(2,1)S(1)} %maximum_bitcast_fusion.3), channel_id=1, source_target_pairs={{0,8},{2,10},{4,12},{6,14},{8,0},{10,2},{12,4},{14,6},{16,24},{18,... | collective-permute-start | bytes 442376 | tf_op jit(solution)/shard_map/ppermute | solution.py:78
  69.7 515.6 %reduce-scatter.2.cloned.1.call-start = ((), (), s32[]{:S(2)}) async-start(), calls=%async_computation.3 | async-start | bytes 9732096 | tf_op jit(solution)/shard_map/reduce_scatter | solution.py:209
  69.9 18.2 %collective-permute-start.11 = (bf16[8,48,768]{2,1,0:T(8,128)(2,1)}, bf16[8,48,768]{2,1,0:T(8,128)(2,1)S(1)}, u32[]{:S(2)}, u32[]{:S(2)}) collective-permute-start(bf16[8,48,768]{2,1,0:T(8,128)(2,1)} %copy-done.48), channel_id=1, source_target_pairs={{0,2},{2,0},{4,6},{6,4},{8,10},{10,8},{12,14},{14,12},{16,18},{18,... | collective-permute-start | bytes 1769480 | tf_op jit(solution)/shard_map/ppermute | solution.py:78
  75.3 12.8 %collective-permute-start.7 = (bf16[8,48,768]{2,1,0:T(8,128)(2,1)S(1)}, bf16[8,48,768]{2,1,0:T(8,128)(2,1)S(1)}, u32[]{:S(2)}, u32[]{:S(2)}) collective-permute-start(bf16[8,48,768]{2,1,0:T(8,128)(2,1)S(1)} %collective-permute-done.5.refs_3_), channel_id=1, source_target_pairs={{0,2},{2,0},{4,6},{6,4},{8,10},{10,8},{12,14},{14,12},{16,18},{18,... | collective-permute-start | bytes 1769480 | tf_op jit(solution)/shard_map/ppermute | solution.py:78
  76.1 11.1 %collective-permute-start.14 = (bf16[1,48,1536]{2,1,0:T(8,128)(2,1)S(1)}, bf16[1,48,1536]{2,1,0:T(8,128)(2,1)S(1)}, u32[]{:S(2)}, u32[]{:S(2)}) collective-permute-start(bf16[1,48,1536]{2,1,0:T(8,128)(2,1)S(1)} %maximum_bitcast_fusion.3), channel_id=1, source_target_pairs={{0,24},{2,26},{4,28},{6,30},{8,16},{10,18},{12,20},{14,22},{16,8},... | collective-permute-start | bytes 442376 | tf_op jit(solution)/shard_map/ppermute | solution.py:78
  101.0 20.7 %collective-permute-start.16 = (bf16[4,48,768]{2,1,0:T(8,128)(2,1)}, bf16[4,48,768]{2,1,0:T(8,128)(2,1)S(1)}, u32[]{:S(2)}, u32[]{:S(2)}) collective-permute-start(bf16[4,48,768]{2,1,0:T(8,128)(2,1)} %get-tuple-element.83.refs_2_), channel_id=1, source_target_pairs={{0,1},{1,0},{2,3},{3,2},{4,5},{5,4},{6,7},{7,6},{8,9},{9,8},{10,11... | collective-permute-start | bytes 884744 | tf_op jit(solution)/shard_map/ppermute | solution.py:78
  119.2 12.0 %collective-permute-start.15 = (bf16[4,48,768]{2,1,0:T(8,128)(2,1)S(1)}, bf16[4,48,768]{2,1,0:T(8,128)(2,1)S(1)}, u32[]{:S(2)}, u32[]{:S(2)}) collective-permute-start(bf16[4,48,768]{2,1,0:T(8,128)(2,1)S(1)} %copy-done.19), channel_id=1, source_target_pairs={{0,4},{2,6},{4,0},{6,2},{8,12},{10,14},{12,8},{14,10},{16,20},{18,... | collective-permute-start | bytes 884744 | tf_op jit(solution)/shard_map/ppermute | solution.py:78
  122.5 43.7 %collective-permute-start.20 = (bf16[8,48,768]{2,1,0:T(8,128)(2,1)}, bf16[8,48,768]{2,1,0:T(8,128)(2,1)}, u32[]{:S(2)}, u32[]{:S(2)}) collective-permute-start(bf16[8,48,768]{2,1,0:T(8,128)(2,1)} %constant_dynamic-update-slice_fusion.14.refs_11_.refs_6_.refs_4_.refs_2_), channel_id=1, source_target_pairs={{0,4},{2,6},{4,0},{6,2},{8,12},{10,14},{12,8},{14,10},{16,20},{18,... | collective-permute-start | bytes 1769480 | tf_op jit(solution)/shard_map/ppermute | solution.py:78
  124.5 44.9 %collective-permute-start.21 = (bf16[8,48,768]{2,1,0:T(8,128)(2,1)}, bf16[8,48,768]{2,1,0:T(8,128)(2,1)}, u32[]{:S(2)}, u32[]{:S(2)}) collective-permute-start(bf16[8,48,768]{2,1,0:T(8,128)(2,1)} %constant_dynamic-update-slice_fusion.14.refs_11_.refs_6_.refs_4_.refs_2_), channel_id=1, source_target_pairs={{0,2},{2,0},{4,6},{6,4},{8,10},{10,8},{12,14},{14,12},{16,18},{18,... | collective-permute-start | bytes 1769480 | tf_op jit(solution)/shard_map/ppermute | solution.py:78
  132.0 34.8 %collective-permute-start.17 = (bf16[8,48,768]{2,1,0:T(8,128)(2,1)}, bf16[8,48,768]{2,1,0:T(8,128)(2,1)}, u32[]{:S(2)}, u32[]{:S(2)}) collective-permute-start(bf16[8,48,768]{2,1,0:T(8,128)(2,1)} %constant_dynamic-update-slice_fusion.12.refs_10_.refs_2_), channel_id=1, source_target_pairs={{0,1},{1,0},{2,3},{3,2},{4,5},{5,4},{6,7},{7,6},{8,9},{9,8},{10,11... | collective-permute-start | bytes 1769480 | tf_op jit(solution)/shard_map/ppermute | solution.py:78
  133.5 35.9 %collective-permute-start.18 = (bf16[8,48,768]{2,1,0:T(8,128)(2,1)}, bf16[8,48,768]{2,1,0:T(8,128)(2,1)}, u32[]{:S(2)}, u32[]{:S(2)}) collective-permute-start(bf16[8,48,768]{2,1,0:T(8,128)(2,1)} %constant_dynamic-update-slice_fusion.12.refs_10_.refs_2_), channel_id=1, source_target_pairs={{0,2},{2,0},{4,6},{6,4},{8,10},{10,8},{12,14},{14,12},{16,18},{18,... | collective-permute-start | bytes 1769480 | tf_op jit(solution)/shard_map/ppermute | solution.py:78
  198.6 37.2 %collective-permute-start.23 = (bf16[1024,768]{1,0:T(8,128)(2,1)S(1)}, bf16[1024,768]{1,0:T(8,128)(2,1)S(1)}, u32[]{:S(2)}, u32[]{:S(2)}) collective-permute-start(bf16[1024,768]{1,0:T(8,128)(2,1)S(1)} %copy-done.7), channel_id=1, source_target_pairs={{0,1},{1,0},{2,3},{3,2},{4,5},{5,4},{6,7},{7,6},{8,9},{9,8},{10,11... | collective-permute-start | bytes 4718600 | tf_op jit(solution)/shard_map/ppermute | solution.py:78
  231.8 44.0 %collective-permute-start.24 = (bf16[1024,768]{1,0:T(8,128)(2,1)}, bf16[1024,768]{1,0:T(8,128)(2,1)}, u32[]{:S(2)}, u32[]{:S(2)}) collective-permute-start(bf16[1024,768]{1,0:T(8,128)(2,1)} %get-tuple-element.92), channel_id=1, source_target_pairs={{0,1},{1,0},{2,3},{3,2},{4,5},{5,4},{6,7},{7,6},{8,9},{9,8},{10,11... | collective-permute-start | bytes 4718600 | tf_op jit(solution)/shard_map/ppermute | solution.py:78
  317.1 16.2 %collective-permute-start.26 = (bf16[16,48,1152]{2,1,0:T(8,128)(2,1)}, bf16[16,48,1152]{2,1,0:T(8,128)(2,1)}, u32[]{:S(2)}, u32[]{:S(2)}) collective-permute-start(bf16[16,48,1152]{2,1,0:T(8,128)(2,1)} %get-tuple-element.114), channel_id=1, source_target_pairs={{0,2},{2,0},{4,6},{6,4},{8,10},{10,8},{12,14},{14,12},{16,18},{18,... | collective-permute-start | bytes 5308424 | tf_op jit(solution)/shard_map/ppermute | solution.py:78
  317.1 15.1 %collective-permute-start.25 = (bf16[16,48,384]{2,1,0:T(8,128)(2,1)S(1)}, bf16[16,48,384]{2,1,0:T(8,128)(2,1)}, u32[]{:S(2)}, u32[]{:S(2)}) collective-permute-start(bf16[16,48,384]{2,1,0:T(8,128)(2,1)S(1)} %copy-done.52), channel_id=1, source_target_pairs={{0,2},{2,0},{4,6},{6,4},{8,10},{10,8},{12,14},{14,12},{16,18},{18,... | collective-permute-start | bytes 1769480 | tf_op jit(solution)/shard_map/ppermute | solution.py:78
  335.4 43.7 %collective-permute-start.28 = (bf16[8,48,768]{2,1,0:T(8,128)(2,1)}, bf16[8,48,768]{2,1,0:T(8,128)(2,1)}, u32[]{:S(2)}, u32[]{:S(2)}) collective-permute-start(bf16[8,48,768]{2,1,0:T(8,128)(2,1)} %add_convert_fusion.5), channel_id=1, source_target_pairs={{0,4},{2,6},{4,0},{6,2},{8,12},{10,14},{12,8},{14,10},{16,20},{18,... | collective-permute-start | bytes 1769480 | tf_op jit(solution)/shard_map/ppermute | solution.py:78
  338.1 43.5 %collective-permute-start.27 = (bf16[8,48,768]{2,1,0:T(8,128)(2,1)}, bf16[8,48,768]{2,1,0:T(8,128)(2,1)}, u32[]{:S(2)}, u32[]{:S(2)}) collective-permute-start(bf16[8,48,768]{2,1,0:T(8,128)(2,1)} %pad_maximum_fusion), channel_id=1, source_target_pairs={{0,1},{1,0},{2,3},{3,2},{4,5},{5,4},{6,7},{7,6},{8,9},{9,8},{10,11... | collective-permute-start | bytes 1769480 | tf_op jit(solution)/shard_map/ppermute | solution.py:78
  375.4 40.2 %collective-permute-start.29 = (bf16[16,48,3072]{2,1,0:T(8,128)(2,1)}, bf16[16,48,3072]{2,1,0:T(8,128)(2,1)}, u32[]{:S(2)}, u32[]{:S(2)}) collective-permute-start(bf16[16,48,3072]{2,1,0:T(8,128)(2,1)} %get-tuple-element.121), channel_id=1, source_target_pairs={{0,2},{2,0},{4,6},{6,4},{8,10},{10,8},{12,14},{14,12},{16,18},{18,... | collective-permute-start | bytes 14155784 | tf_op jit(solution)/shard_map/ppermute | solution.py:78
  380.3 14.1 %collective-permute-start.31 = (bf16[4,48,768]{2,1,0:T(8,128)(2,1)S(1)}, bf16[4,48,768]{2,1,0:T(8,128)(2,1)S(1)}, u32[]{:S(2)}, u32[]{:S(2)}) collective-permute-start(bf16[4,48,768]{2,1,0:T(8,128)(2,1)S(1)} %add_convert_fusion.9), channel_id=1, source_target_pairs={{0,1},{1,0},{2,3},{3,2},{4,5},{5,4},{6,7},{7,6},{8,9},{9,8},{10,11... | collective-permute-start | bytes 884744 | tf_op jit(solution)/shard_map/ppermute | solution.py:78
  395.9 10.2 %collective-permute-start.34 = (bf16[48,1536]{1,0:T(8,128)(2,1)S(1)}, bf16[48,1536]{1,0:T(8,128)(2,1)S(1)}, u32[]{:S(2)}, u32[]{:S(2)}) collective-permute-start(bf16[48,1536]{1,0:T(8,128)(2,1)S(1)} %pad_maximum_fusion.17), channel_id=1, source_target_pairs={{0,8},{2,10},{4,12},{6,14},{8,0},{10,2},{12,4},{14,6},{16,24},{18,... | collective-permute-start | bytes 442376 | tf_op jit(solution)/shard_map/ppermute | solution.py:78
  399.5 15.2 %collective-permute-start.35 = (bf16[48,1536]{1,0:T(8,128)(2,1)S(1)}, bf16[48,1536]{1,0:T(8,128)(2,1)S(1)}, u32[]{:S(2)}, u32[]{:S(2)}) collective-permute-start(bf16[48,1536]{1,0:T(8,128)(2,1)S(1)} %pad_maximum_fusion.18), channel_id=1, source_target_pairs={{0,16},{2,18},{4,20},{6,22},{8,24},{10,26},{12,28},{14,30},{16,0},... | collective-permute-start | bytes 442376 | tf_op jit(solution)/shard_map/ppermute | solution.py:78
  401.2 13.6 %collective-permute-start.36 = (bf16[48,1536]{1,0:T(8,128)(2,1)S(1)}, bf16[48,1536]{1,0:T(8,128)(2,1)S(1)}, u32[]{:S(2)}, u32[]{:S(2)}) collective-permute-start(bf16[48,1536]{1,0:T(8,128)(2,1)S(1)} %pad_maximum_fusion.19), channel_id=1, source_target_pairs={{0,24},{2,26},{4,28},{6,30},{8,16},{10,18},{12,20},{14,22},{16,8},... | collective-permute-start | bytes 442376 | tf_op jit(solution)/shard_map/ppermute | solution.py:78
  402.8 64.5 %collective-permute-start.38 = (bf16[16,48,384]{2,1,0:T(8,128)(2,1)}, bf16[16,48,384]{2,1,0:T(8,128)(2,1)}, u32[]{:S(2)}, u32[]{:S(2)}) collective-permute-start(bf16[16,48,384]{2,1,0:T(8,128)(2,1)} %get-tuple-element.133), channel_id=1, source_target_pairs={{0,2},{2,0},{4,6},{6,4},{8,10},{10,8},{12,14},{14,12},{16,18},{18,... | collective-permute-start | bytes 1769480 | tf_op jit(solution)/shard_map/ppermute | solution.py:78
  420.1 25.2 %collective-permute-start.33 = (bf16[8,48,1536]{2,1,0:T(8,128)(2,1)}, bf16[8,48,1536]{2,1,0:T(8,128)(2,1)S(1)}, u32[]{:S(2)}, u32[]{:S(2)}) collective-permute-start(bf16[8,48,1536]{2,1,0:T(8,128)(2,1)} %get-tuple-element.128), channel_id=1, source_target_pairs={{0,4},{2,6},{4,0},{6,2},{8,12},{10,14},{12,8},{14,10},{16,20},{18,... | collective-permute-start | bytes 3538952 | tf_op jit(solution)/shard_map/ppermute | solution.py:78
  421.5 24.1 %collective-permute-start.32 = (bf16[8,48,1536]{2,1,0:T(8,128)(2,1)}, bf16[8,48,1536]{2,1,0:T(8,128)(2,1)S(1)}, u32[]{:S(2)}, u32[]{:S(2)}) collective-permute-start(bf16[8,48,1536]{2,1,0:T(8,128)(2,1)} %get-tuple-element.127), channel_id=1, source_target_pairs={{0,1},{1,0},{2,3},{3,2},{4,5},{5,4},{6,7},{7,6},{8,9},{9,8},{10,11... | collective-permute-start | bytes 3538952 | tf_op jit(solution)/shard_map/ppermute | solution.py:78
  470.1 16.5 %collective-permute-start.52 = (f32[2,9216]{1,0:T(2,128)S(1)}, f32[2,9216]{1,0:T(2,128)S(1)}, u32[]{:S(2)}, u32[]{:S(2)}) collective-permute-start(f32[2,9216]{1,0:T(2,128)S(1)} %add.729), channel_id=1, source_target_pairs={{0,8},{2,10},{4,12},{6,14},{8,0},{10,2},{12,4},{14,6},{16,24},{18,... | collective-permute-start | bytes 221192 | tf_op jit(solution)/shard_map/ppermute | solution.py:78
  476.8 11.5 %collective-permute-start.53 = (f32[2,9216]{1,0:T(2,128)S(1)}, f32[2,9216]{1,0:T(2,128)S(1)}, u32[]{:S(2)}, u32[]{:S(2)}) collective-permute-start(f32[2,9216]{1,0:T(2,128)S(1)} %add.729), channel_id=1, source_target_pairs={{0,16},{2,18},{4,20},{6,22},{8,24},{10,26},{12,28},{14,30},{16,0},... | collective-permute-start | bytes 221192 | tf_op jit(solution)/shard_map/ppermute | solution.py:78
  485.3 12.7 %collective-permute-start.39 = (bf16[4,48,1536]{2,1,0:T(8,128)(2,1)}, bf16[4,48,1536]{2,1,0:T(8,128)(2,1)S(1)}, u32[]{:S(2)}, u32[]{:S(2)}) collective-permute-start(bf16[4,48,1536]{2,1,0:T(8,128)(2,1)} %get-tuple-element.134), channel_id=1, source_target_pairs={{0,4},{2,6},{4,0},{6,2},{8,12},{10,14},{12,8},{14,10},{16,20},{18,... | collective-permute-start | bytes 1769480 | tf_op jit(solution)/shard_map/ppermute | solution.py:78
  486.2 16.5 %collective-permute-start.40 = (bf16[4,48,1536]{2,1,0:T(8,128)(2,1)}, bf16[4,48,1536]{2,1,0:T(8,128)(2,1)S(1)}, u32[]{:S(2)}, u32[]{:S(2)}) collective-permute-start(bf16[4,48,1536]{2,1,0:T(8,128)(2,1)} %get-tuple-element.135), channel_id=1, source_target_pairs={{0,1},{1,0},{2,3},{3,2},{4,5},{5,4},{6,7},{7,6},{8,9},{9,8},{10,11... | collective-permute-start | bytes 1769480 | tf_op jit(solution)/shard_map/ppermute | solution.py:78
  486.6 61.4 %collective-permute-start.37 = (bf16[1024,768]{1,0:T(8,128)(2,1)}, bf16[1024,768]{1,0:T(8,128)(2,1)}, u32[]{:S(2)}, u32[]{:S(2)}) collective-permute-start(bf16[1024,768]{1,0:T(8,128)(2,1)} %convert_element_type.779), channel_id=1, source_target_pairs={{0,1},{1,0},{2,3},{3,2},{4,5},{5,4},{6,7},{7,6},{8,9},{9,8},{10,11... | collective-permute-start | bytes 4718600 | tf_op jit(solution)/shard_map/ppermute | solution.py:78
  518.1 15.4 %collective-permute-start.55 = (bf16[48,3072]{1,0:T(8,128)(2,1)S(1)}, bf16[48,3072]{1,0:T(8,128)(2,1)S(1)}, u32[]{:S(2)}, u32[]{:S(2)}) collective-permute-start(bf16[48,3072]{1,0:T(8,128)(2,1)S(1)} %pad_maximum_fusion.14), channel_id=1, source_target_pairs={{0,8},{2,10},{4,12},{6,14},{8,0},{10,2},{12,4},{14,6},{16,24},{18,... | collective-permute-start | bytes 884744 | tf_op jit(solution)/shard_map/ppermute | solution.py:78
  518.8 23.5 %collective-permute-start.56 = (bf16[48,3072]{1,0:T(8,128)(2,1)S(1)}, bf16[48,3072]{1,0:T(8,128)(2,1)S(1)}, u32[]{:S(2)}, u32[]{:S(2)}) collective-permute-start(bf16[48,3072]{1,0:T(8,128)(2,1)S(1)} %pad_maximum_fusion.15), channel_id=1, source_target_pairs={{0,16},{2,18},{4,20},{6,22},{8,24},{10,26},{12,28},{14,30},{16,0},... | collective-permute-start | bytes 884744 | tf_op jit(solution)/shard_map/ppermute | solution.py:78
  521.3 21.0 %collective-permute-start.57 = (bf16[48,3072]{1,0:T(8,128)(2,1)S(1)}, bf16[48,3072]{1,0:T(8,128)(2,1)S(1)}, u32[]{:S(2)}, u32[]{:S(2)}) collective-permute-start(bf16[48,3072]{1,0:T(8,128)(2,1)S(1)} %pad_maximum_fusion.16), channel_id=1, source_target_pairs={{0,24},{2,26},{4,28},{6,30},{8,16},{10,18},{12,20},{14,22},{16,8},... | collective-permute-start | bytes 884744 | tf_op jit(solution)/shard_map/ppermute | solution.py:78
  522.9 22.1 %collective-permute-start.42 = (bf16[8,48,768]{2,1,0:T(8,128)(2,1)S(1)}, bf16[8,48,768]{2,1,0:T(8,128)(2,1)S(1)}, u32[]{:S(2)}, u32[]{:S(2)}) collective-permute-start(bf16[8,48,768]{2,1,0:T(8,128)(2,1)S(1)} %pad_maximum_fusion.1), channel_id=1, source_target_pairs={{0,1},{1,0},{2,3},{3,2},{4,5},{5,4},{6,7},{7,6},{8,9},{9,8},{10,11... | collective-permute-start | bytes 1769480 | tf_op jit(solution)/shard_map/ppermute | solution.py:78
  542.6 16.3 %collective-permute-start.44 = (bf16[8,48,768]{2,1,0:T(8,128)(2,1)S(1)}, bf16[8,48,768]{2,1,0:T(8,128)(2,1)S(1)}, u32[]{:S(2)}, u32[]{:S(2)}) collective-permute-start(bf16[8,48,768]{2,1,0:T(8,128)(2,1)S(1)} %add_convert_fusion.2), channel_id=1, source_target_pairs={{0,4},{2,6},{4,0},{6,2},{8,12},{10,14},{12,8},{14,10},{16,20},{18,... | collective-permute-start | bytes 1769480 | tf_op jit(solution)/shard_map/ppermute | solution.py:78
  546.1 17.0 %collective-permute-start.43 = (bf16[4,48,768]{2,1,0:T(8,128)(2,1)S(1)}, bf16[4,48,768]{2,1,0:T(8,128)(2,1)S(1)}, u32[]{:S(2)}, u32[]{:S(2)}) collective-permute-start(bf16[4,48,768]{2,1,0:T(8,128)(2,1)S(1)} %pad_maximum_fusion.12), channel_id=1, source_target_pairs={{0,4},{2,6},{4,0},{6,2},{8,12},{10,14},{12,8},{14,10},{16,20},{18,... | collective-permute-start | bytes 884744 | tf_op jit(solution)/shard_map/ppermute | solution.py:78
  566.1 12.3 %collective-permute-start.46 = (bf16[48,1536]{1,0:T(8,128)(2,1)S(1)}, bf16[48,1536]{1,0:T(8,128)(2,1)S(1)}, u32[]{:S(2)}, u32[]{:S(2)}) collective-permute-start(bf16[48,1536]{1,0:T(8,128)(2,1)S(1)} %pad_maximum_fusion.20), channel_id=1, source_target_pairs={{0,8},{2,10},{4,12},{6,14},{8,0},{10,2},{12,4},{14,6},{16,24},{18,... | collective-permute-start | bytes 442376 | tf_op jit(solution)/shard_map/ppermute | solution.py:78
  572.2 11.5 %collective-permute-start.47 = (bf16[48,1536]{1,0:T(8,128)(2,1)S(1)}, bf16[48,1536]{1,0:T(8,128)(2,1)S(1)}, u32[]{:S(2)}, u32[]{:S(2)}) collective-permute-start(bf16[48,1536]{1,0:T(8,128)(2,1)S(1)} %pad_maximum_fusion.21), channel_id=1, source_target_pairs={{0,16},{2,18},{4,20},{6,22},{8,24},{10,26},{12,28},{14,30},{16,0},... | collective-permute-start | bytes 442376 | tf_op jit(solution)/shard_map/ppermute | solution.py:78
  573.7 9.9 %collective-permute-start.48 = (bf16[48,1536]{1,0:T(8,128)(2,1)S(1)}, bf16[48,1536]{1,0:T(8,128)(2,1)S(1)}, u32[]{:S(2)}, u32[]{:S(2)}) collective-permute-start(bf16[48,1536]{1,0:T(8,128)(2,1)S(1)} %pad_maximum_fusion.22), channel_id=1, source_target_pairs={{0,24},{2,26},{4,28},{6,30},{8,16},{10,18},{12,20},{14,22},{16,8},... | collective-permute-start | bytes 442376 | tf_op jit(solution)/shard_map/ppermute | solution.py:78
  (66 other events, 673.6 us)
Sparse Core Ops, SparseCore 0:
  11.5 99.6 all-gather.2
  114.1 82.6 all-gather.4
  272.0 152.2 reduce-scatter.1

commit v4 on v3

--- a/solution.py
+++ b/solution.py
@@ -11,15 +11,15 @@
 PAIR = 2 * HEAD_DIM
 AXES = ("tensor", "dp")
 CORE = ("dp", 1)
-FFN_PARTS = 3
-ROW_TILE = 256
+FFN_PARTS = 2
+ROW_TILE = 512
 TILE_ROWS = 16
 PLANNED_BLOCKS = 16
-HOPS = ((True, False), (True, False))
 HOPS_BACK = ((True, True), (True, False))
 COST_WEIGHT = 8
-LATE_WEIGHTS = True
-HOLD_TOKENS = False
+BACK_WEIGHT = 16
+SPLIT_DOWN = False
+HOLD_TOKENS = True
 VMEM_LIMIT = 58 * 1024 * 1024
 
 norm_eps = 1e-06
@@ -91,6 +91,12 @@
         return Piece(self.arrays, self.order, self.columns.start + first, count)
 
 
+class Joined:
+    def __init__(self, parts):
+        self.parts, self.count = tuple(parts), sum(part.count for part in parts)
+        self.arrays = tuple(member for part in parts for member in part.arrays)
+
+
 class Gathering:
     def __init__(self, shard, orders):
         self.shard, self.orders, self.width = shard[None], orders, shard.shape[1] // 2
@@ -98,30 +104,38 @@
     def halves(self, member):
         return [member[..., : self.width], member[..., self.width :]]
 
-    def far(self, *others):
+    def send_far(self, *others):
         shard = tied(self.shard, others)
         count = 2 ** (len(self.orders[0]) - 2)
-        parts = [shard] + [hop(shard, ("dp", 4 * step)) for step in range(1, count)]
+        self.coming = [hop(shard, ("dp", 4 * step)) for step in range(1, count)]
+
+    def land_far(self, *others):
+        parts = [self.shard] + [tied(member, others) for member in self.coming]
         self.current = [
             jnp.concatenate(sides, axis=0) for sides in zip(*[self.halves(part) for part in parts])
         ]
         return self.current
 
-    def middle(self, *others):
-        current = [tied(member, others) for member in self.current]
+    def send_middle(self, *others):
+        self.coming = [
+            hop(tied(member, others), order[-2])
+            for member, order in zip(self.current, self.orders)
+        ]
+
+    def land_middle(self, *others):
         self.current = [
-            jnp.concatenate([member, hop(member, order[-2])], axis=0)
-            for member, order in zip(current, self.orders)
+            jnp.concatenate([member, tied(come, others)], axis=0)
+            for member, come in zip(self.current, self.coming)
         ]
         return self.current
 
-    def last(self, *others):
+    def send_last(self, *others):
         current = [tied(member, others) for member in self.current]
         self.later = [hop(member, order[-1]) for member, order in zip(current, self.orders)]
         self.core_current = [hop(member, CORE) for member in current]
         return self.later
 
-    def core(self, *others):
+    def send_core(self, *others):
         self.core_later = [hop(tied(member, others), CORE) for member in self.later]
         return self.core_later
 
@@ -131,15 +145,15 @@
 
 
 class WholeGathering:
-    def __init__(self, shard, orders, *others):
+    def __init__(self, shard, orders):
         self.width, self.orders = shard.shape[1] // 2, orders
-        whole = lax.all_gather(tied(shard, others), AXES, tiled=True)
+        whole = lax.all_gather(shard, AXES, tiled=True)
         self.whole = whole.reshape(lax.axis_size("tensor"), -1, shard.shape[1])
 
-    def far(self, *others):
-        return [self.whole]
-
-    middle = last = core = far
+    def send_far(self, *others):
+        return []
+
+    land_far = send_middle = land_middle = send_last = send_core = send_far
 
     def pieces(self):
         return [
@@ -153,14 +167,18 @@
         self.members, self.orders, self.sides = members, orders, sides
         self.begun = [members[-1][0]]
 
-    def core(self, *others):
-        arrived = [hop(tied(send, others), CORE) for keep, send in self.members]
-        both = [[keep, come] for (keep, send), come in zip(self.members, arrived)]
+    def send_core(self, *others):
+        self.coming = [hop(tied(send, others), CORE) for keep, send in self.members]
+        return self.coming
+
+    def land_core(self, *others):
+        both = [
+            [keep, tied(come, others)] for (keep, send), come in zip(self.members, self.coming)
+        ]
         self.parts = [
             [[part[..., first:end] for part in both[member]] for member, first, end in side]
             for side in self.sides
         ]
-        return arrived
 
     def total(self, side, take):
         sums = [
@@ -169,36 +187,44 @@
         return jnp.concatenate(sums, axis=-1) if len(sums) > 1 else sums[0]
 
     def halve(self, which, others):
-        arrived = []
+        self.coming = []
         for side, order in enumerate(self.orders):
             half = self.parts[side][0][0].shape[0] // 2
             upper = self.total(side, lambda part: part[half:]).astype(jnp.bfloat16)
-            come = hop(tied(upper, others), order[which])
-            arrived.append(come)
-            at = 0
-            for group in self.parts[side]:
-                width = group[0].shape[-1]
+            self.coming.append(hop(tied(upper, others), order[which]))
+        return self.coming
+
+    def land(self, *others):
+        for groups, come in zip(self.parts, self.coming):
+            come, at = tied(come, others), 0
+            for group in groups:
+                width, half = group[0].shape[-1], group[0].shape[0] // 2
                 group[:] = [part[:half] for part in group] + [come[..., at : at + width]]
                 at += width
-        return arrived
-
-    def last(self, *others):
+
+    def send_last(self, *others):
         return self.halve(-1, others)
 
-    def middle(self, *others):
+    def send_middle(self, *others):
         return self.halve(-2, others)
 
-    def far(self, *others):
+    def send_far(self, *others):
         count = self.parts[0][0][0].shape[0]
         sides = range(len(self.orders))
-        mine = jnp.concatenate([self.total(side, lambda part: part[0]) for side in sides], axis=-1)
-        arrived = []
+        self.mine = jnp.concatenate(
+            [self.total(side, lambda part: part[0]) for side in sides], axis=-1
+        )
+        self.coming = []
         for step in range(1, count):
             upper = jnp.concatenate(
                 [self.total(side, lambda part: part[step]) for side in sides], axis=-1
             )
-            arrived.append(hop(tied(upper.astype(jnp.bfloat16), others), ("dp", 4 * step)))
-        self.result = sum([mine] + [part.astype(jnp.float32) for part in arrived])
+            self.coming.append(hop(tied(upper.astype(jnp.bfloat16), others), ("dp", 4 * step)))
+        return self.coming
+
+    def land_far(self, *others):
+        come = [tied(part, others).astype(jnp.float32) for part in self.coming]
+        self.result = sum([self.mine] + come)
         return [self.result]
 
 
@@ -214,25 +240,37 @@
         taken = [mine[member][:, first:end] for side in sides for member, first, end in side]
         self.result = jnp.concatenate(taken, axis=-1)
 
-    def core(self, *others):
+    def send_core(self, *others):
         return []
 
-    last = middle = far = core
-
-
-def sum_over_all(member, routed):
-    if not routed:
-        return lax.psum(member, AXES)
-    total = member
-    for dim in (CORE, ("dp", 2), ("tensor", 1)):
-        total = total + hop(total, dim)
-    parts = [total] + [hop(total, ("dp", bit)) for bit in range(4, lax.axis_size("dp"), 4)]
-    far_place = lax.axis_index("dp") // 4
-    stacked = jnp.stack(parts)
-    return sum(stacked[far_place ^ step] for step in range(len(parts)))
+    land_core = send_last = send_middle = land = send_far = land_far = send_core
+
+
+class Totals:
+    def __init__(self, member, routed):
+        self.routed, self.total = routed, member if routed else lax.psum(member, AXES)
+
+    def send(self, axis, first, count, *others):
+        if self.routed:
+            total = tied(self.total, others)
+            self.place = lax.axis_index(axis) // first % count
+            self.coming = [hop(total, (axis, first * step)) for step in range(1, count)]
+
+    def land(self, *others):
+        if self.routed:
+            stacked = jnp.stack([self.total] + [tied(come, others) for come in self.coming])
+            self.total = sum(stacked[self.place ^ step] for step in range(len(self.coming) + 1))
 
 
 def load_piece(meta, piece, sources, target, columns, sems):
+    if isinstance(piece, Joined):
+        at = 0
+        for part in piece.parts:
+            load_piece(
+                meta, part, sources[: len(part.arrays)], target, slice(at, at + part.count), sems
+            )
+            sources, at = sources[len(part.arrays) :], at + part.count
+        return
     if len(sources) == 1:
         for half_at in range(2):
             pltpu.make_async_copy(
@@ -256,9 +294,53 @@
             ).start()
 
 
+def load_flat(meta, piece, sources, target, sem):
+    count = piece.count
+    if len(sources) == 1:
+        for half_at in range(2):
+            pltpu.make_async_copy(
+                sources[0].at[half_at, :, piece.columns],
+                target.at[:, slice(half_at * count, (half_at + 1) * count)], sem,
+            ).start()
+        return
+    table = slot_table(piece.order)
+    half = len(table) // 2
+    block_rows = sources[0].shape[1]
+    for slot, (dp_part, tensor_part) in enumerate(table):
+        columns = pl.ds(pl.multiple_of((meta[1] ^ tensor_part) * count, 128), count)
+        for core in range(2):
+            place = meta[0] ^ (dp_part ^ core)
+            rows = pl.ds(pl.multiple_of(place * block_rows, TILE_ROWS), block_rows)
+            pltpu.make_async_copy(
+                sources[2 * core + slot // half].at[slot % half, :, piece.columns],
+                target.at[rows, columns],
+                sem,
+            ).start()
+
+
 def await_piece(target, half_at, columns, sems):
     view = target.at[half_at, :, columns]
     pltpu.make_async_copy(view, view, sems.at[half_at]).wait()
+
+
+def store_flat(meta, source, targets, order, columns, sem):
+    count = source.shape[1] // 2
+    if len(targets) == 1:
+        for half_at in range(2):
+            pltpu.make_async_copy(
+                source.at[:, slice(half_at * count, (half_at + 1) * count)],
+                targets[0].at[half_at, :, columns], sem,
+            ).start()
+        return
+    block_rows = targets[0].shape[1]
+    for slot, (dp_part, tensor_part) in enumerate(slot_table(order)):
+        mine = pl.ds(pl.multiple_of((meta[1] ^ tensor_part) * count, 128), count)
+        for core in range(2):
+            place = meta[0] ^ (dp_part ^ core)
+            rows = pl.ds(pl.multiple_of(place * block_rows, TILE_ROWS), block_rows)
+            pltpu.make_async_copy(
+                source.at[rows, mine], targets[core].at[slot, :, columns], sem
+            ).start()
 
 
 def store_piece(meta, source, targets, order, relative_half, columns, sem):
@@ -326,38 +408,18 @@
     return inputs * below, below + inputs * (bell * inv_root_tau)
 
 
-def load_qkv(meta, pieces, sources, weights, columns, sems):
-    load_piece(meta, pieces[0], sources[0], weights, slice(0, 2 * columns), sems[0])
-    load_piece(meta, pieces[1], sources[1], weights, slice(2 * columns, 3 * columns), sems[1])
-
-
-def await_qkv(weights, half_at, columns, sems):
-    await_piece(weights, half_at, slice(0, 2 * columns), sems[0])
-    await_piece(weights, half_at, slice(2 * columns, 3 * columns), sems[1])
-
-
 def qkv_forward_kernel(pieces, meta, inputs, bias, *refs):
-    qk_sources, v_sources, out, weights, *sems = take(
-        refs, len(pieces[0].arrays), len(pieces[1].arrays), None, None, None, None
-    )
+    *sources, (out, weights, sems) = take(refs, *[len(piece.arrays) for piece in pieces], 3)
     step = pl.program_id(0)
-    columns = out.shape[2]
 
     @pl.when(step == 0)
     def _():
-        load_qkv(meta, pieces, (qk_sources, v_sources), weights, columns, sems)
-
-    half_at = meta[1] ^ (step // 3)
-
-    @pl.when(step % 3 == 0)
-    def _():
-        await_qkv(weights, half_at, columns, sems)
-
-    which = pl.ds(pl.multiple_of((step % 3) * columns, 128), columns)
+        for which, piece in enumerate(pieces):
+            load_flat(meta, piece, sources[which], weights.at[which], sems.at[which])
+
+    await_stored(weights.at[step], sems.at[step])
     for rows in row_tiles(inputs.shape[0]):
-        out[0, rows, :] = (dot_nn(inputs[rows, :], weights[half_at, :, which]) + bias[0]).astype(
-            jnp.bfloat16
-        )
+        out[0, rows, :] = (dot_nn(inputs[rows, :], weights[step]) + bias[0]).astype(jnp.bfloat16)
 
 
 def slab_features(meta, slab, slab_rows, k_side, q_side):
@@ -478,7 +540,7 @@
 
 
 def ffn_backward_kernel(
-    pieces, target_count, meta, gradient, normed_two, spread_two, hidden, normed_one, spread_one,
+    pieces, orders, target_count, meta, gradient, normed_two, spread_two, hidden, normed_one, spread_one,
     activated, slope, vectors, *refs
 ):
     in_sources, down_sources, outputs, targets, scratch = take(
@@ -534,7 +596,7 @@
     grad_parts[slot, 1] = dot_nn(branch_flip[...], activated[...]).astype(jnp.bfloat16)
     down_part = pl.ds(pl.multiple_of(FFN_PARTS * width + (step % FFN_PARTS) * width, 128), width)
     store_piece(
-        meta, grad_parts.at[slot, 1], targets, pieces[1].order, step // FFN_PARTS, down_part,
+        meta, grad_parts.at[slot, 1], targets, orders[1], step // FFN_PARTS, down_part,
         out_sems.at[slot, 1],
     )
     bias_sum = 0.0
@@ -547,7 +609,7 @@
     bias_sums[0] = bias_sum
     grad_parts[slot, 0] = dot_nn(hidden_flip[...], pre_part[...]).astype(jnp.bfloat16)
     store_piece(
-        meta, grad_parts.at[slot, 0], targets, pieces[0].order, step // FFN_PARTS, part,
+        meta, grad_parts.at[slot, 0], targets, orders[0], step // FFN_PARTS, part,
         out_sems.at[slot, 0],
     )
 
@@ -576,31 +638,17 @@
     sources, mixed_grad, targets, scratch = take(
         refs, len(pieces[0].arrays), None, target_count, 5
     )
-    out_whole, grad_flip, grad_parts, load_sems, out_sems = scratch
-    step = pl.program_id(0)
-    columns = mixed.shape[1]
-    everything = slice(None)
+    out_whole, grad_flip, grad_part, load_sem, out_sem = scratch
     tiles = row_tiles(mixed.shape[0])
-
-    @pl.when(step == 0)
-    def _():
-        load_piece(meta, pieces[0], sources, out_whole, everything, load_sems)
-        for rows in tiles:
-            grad_flip[:, rows] = flipped(attention_grad[rows, :]).astype(jnp.bfloat16)
-
-    half_at = meta[1] ^ step
-    grad_parts[step] = dot_nn(grad_flip[...], mixed[...]).astype(jnp.bfloat16)
-    store_piece(meta, grad_parts.at[step], targets, order, step, everything, out_sems.at[step])
-    await_piece(out_whole, half_at, everything, load_sems)
+    load_flat(meta, pieces[0], sources, out_whole, load_sem)
     for rows in tiles:
-        mixed_grad[rows, :] = dot_nn(attention_grad[rows, :], out_whole[half_at]).astype(
-            jnp.bfloat16
-        )
-
-    @pl.when(step == 1)
-    def _():
-        for late in range(2):
-            await_stored(grad_parts.at[late], out_sems.at[late])
+        grad_flip[:, rows] = flipped(attention_grad[rows, :]).astype(jnp.bfloat16)
+    grad_part[...] = dot_nn(grad_flip[...], mixed[...]).astype(jnp.bfloat16)
+    store_flat(meta, grad_part, targets, order, slice(None), out_sem)
+    await_stored(out_whole, load_sem)
+    for rows in tiles:
+        mixed_grad[rows, :] = dot_nn(attention_grad[rows, :], out_whole[...]).astype(jnp.bfloat16)
+    await_stored(grad_part, out_sem)
 
 
 def attention_backward_kernel(meta, qkv, mixed, mixed_grad, logsum, grads, sums, k_side, q_side):
@@ -653,64 +701,53 @@
 def qkv_grad_kernel(orders, target_count, meta, inputs, grads, *refs):
     targets, (inputs_flip, grad_parts, out_sems) = take(refs, target_count, 3)
     step = pl.program_id(0)
-    steps = pl.num_programs(0)
-    columns = grads.shape[2]
-    slot = step % 2
-    which = step % 3
+    columns = grads.shape[2] // 2
 
     @pl.when(step == 0)
     def _():
         for rows in row_tiles(inputs.shape[0]):
             inputs_flip[:, rows] = flipped(inputs[rows, :]).astype(jnp.bfloat16)
 
-    @pl.when(step >= 2)
+    grad_parts[step] = dot_nn(inputs_flip[...], grads[0]).astype(jnp.bfloat16)
+    for which, order in enumerate((orders[0], orders[1], orders[1])):
+
+        @pl.when(step == which)
+        def _():
+            span = slice(which * columns, (which + 1) * columns)
+            store_flat(meta, grad_parts.at[which], targets, order, span, out_sems.at[which])
+
+    @pl.when(step == 2)
     def _():
-        await_stored(grad_parts.at[slot], out_sems.at[slot])
-
-    grad_parts[slot] = dot_nn(inputs_flip[...], grads[0]).astype(jnp.bfloat16)
-    span = pl.ds(pl.multiple_of(which * columns, 128), columns)
-
-    @pl.when(which == 0)
-    def _():
-        store_piece(
-            meta, grad_parts.at[slot], targets, orders[0], step // 3, span, out_sems.at[slot]
-        )
-
-    @pl.when(which > 0)
-    def _():
-        store_piece(
-            meta, grad_parts.at[slot], targets, orders[1], step // 3, span, out_sems.at[slot]
-        )
-
-    @pl.when(step == steps - 1)
-    def _():
-        for late in range(2):
-            await_stored(grad_parts.at[late], out_sems.at[late])
+        for which in range(3):
+            await_stored(grad_parts.at[which], out_sems.at[which])
 
 
 def input_grad_kernel(pieces, meta, grads, resid_grad, *refs):
-    qk_sources, v_sources, input_grad, weights, *sems = take(
-        refs, len(pieces[0].arrays), len(pieces[1].arrays), None, None, None, None
-    )
+    *sources, outputs, (weights, sems) = take(
+        refs, *[len(piece.arrays) for piece in pieces], len(refs) - 2 - sum(
+            len(piece.arrays) for piece in pieces
+        ), 2,
+    )
+    input_grad = outputs[0]
     step = pl.program_id(0)
-    columns = grads.shape[2]
     tiles = row_tiles(resid_grad.shape[0])
 
     @pl.when(step == 0)
     def _():
-        load_qkv(meta, pieces, (qk_sources, v_sources), weights, columns, sems)
+        for which, piece in enumerate(pieces):
+            load_flat(meta, piece, sources[which], weights.at[which], sems.at[which])
         for rows in tiles:
             input_grad[rows, :] = resid_grad[rows, :]
 
-    half_at = meta[1] ^ (step // 3)
-
-    @pl.when(step % 3 == 0)
-    def _():
-        await_qkv(weights, half_at, columns, sems)
-
-    span = pl.ds(pl.multiple_of((step % 3) * columns, 128), columns)
+    await_stored(weights.at[step], sems.at[step])
     for rows in tiles:
-        input_grad[rows, :] += dot_nt(grads[0, rows, :], weights[half_at, :, span])
+        input_grad[rows, :] += dot_nt(grads[0, rows, :], weights[step])
+
+    if len(outputs) > 1:
+
+        @pl.when(step == 2)
+        def _():
+            outputs[1][...] = input_grad[...].astype(jnp.bfloat16)
 
 
 def fixed(shape):
@@ -746,7 +783,7 @@
         ),
         out_shape=list(out_shapes),
         compiler_params=pltpu.CompilerParams(vmem_limit_bytes=VMEM_LIMIT),
-        cost_estimate=pl.CostEstimate(flops=COST_WEIGHT * flops, bytes_accessed=moved, transcendentals=0),
+        cost_estimate=pl.CostEstimate(flops=(BACK_WEIGHT if "forward" not in name else COST_WEIGHT) * flops, bytes_accessed=moved, transcendentals=0),
         name=name,
     )(meta, *operands)
 
@@ -778,28 +815,23 @@
     return [(ANYWHERE, low_shape(split, width, columns))]
 
 
+def three_sems():
+    return pltpu.SemaphoreType.DMA((3,))
+
+
 def qkv_forward(meta, inputs, bias, pieces, after=()):
     rows, width = inputs.shape
-    columns = width // 2
     (qkv,) = run_kernel(
         functools.partial(qkv_forward_kernel, pieces),
         meta,
-        (6,),
+        (3,),
         [
             (fixed((rows, width)), inputs),
-            (
-                pl.BlockSpec((1, 1, columns), lambda i, m: ((i % 3) * 2 + half_of(i, m, 3), 0, 0)),
-                bias,
-            ),
+            (pl.BlockSpec((1, 1, width), lambda i, m: (i, 0, 0)), bias),
         ]
         + sources_of(pieces),
-        [
-            (
-                pl.BlockSpec((1, rows, columns), lambda i, m: (i % 3, 0, half_of(i, m, 3))),
-                low_shape(3, rows, width),
-            )
-        ],
-        [pltpu.VMEM((2, width, 3 * columns), jnp.bfloat16), pair_sems(), pair_sems()],
+        [(pl.BlockSpec((1, rows, width), lambda i, m: (i, 0, 0)), low_shape(3, rows, width))],
+        [pltpu.VMEM((3, width, width), jnp.bfloat16), three_sems()],
         6 * rows * width * width,
         8 * rows * width + 6 * width * width,
         "qkv_forward",
@@ -874,7 +906,7 @@
     )
 
 
-def ffn_backward(meta, gradient, kept, vectors, pieces, targets, after=()):
+def ffn_backward(meta, gradient, kept, vectors, pieces, orders, targets, after=()):
     hidden, normed_one, spread_one, activated, slope, normed_two, spread_two = kept
     rows, width = hidden.shape
     half_width = pieces[0].count
@@ -887,7 +919,7 @@
     spread = fixed((rows, 128))
     inner = pl.BlockSpec((rows, part), lambda i, m: (0, part_at(i, m)))
     return run_kernel(
-        functools.partial(ffn_backward_kernel, pieces, len(targets)),
+        functools.partial(ffn_backward_kernel, pieces, orders, len(targets)),
         meta,
         (2 * FFN_PARTS,),
         [
@@ -934,20 +966,19 @@
 
 def out_backward(meta, attention_grad, mixed, piece, order, targets, after=()):
     rows, width = mixed.shape
-    columns = width // 2
-    half = pl.BlockSpec((rows, columns), lambda i, m: (0, half_of(i, m, 1)))
     return run_kernel(
         functools.partial(out_backward_kernel, [piece], order, len(targets)),
         meta,
-        (2,),
-        [(fixed((rows, width)), attention_grad), (half, mixed)] + sources_of([piece]),
-        [(half, low_shape(rows, width))] + targets,
+        (1,),
+        [(fixed((rows, width)), attention_grad), (fixed((rows, width)), mixed)]
+        + sources_of([piece]),
+        [(fixed_out((rows, width)), low_shape(rows, width))] + targets,
         [
-            pltpu.VMEM((2, width, columns), jnp.bfloat16),
+            pltpu.VMEM((width, width), jnp.bfloat16),
             pltpu.VMEM((width, rows), jnp.bfloat16),
-            pltpu.VMEM((2, width, columns), jnp.bfloat16),
-            pair_sems(),
-            pair_sems(),
+            pltpu.VMEM((width, width), jnp.bfloat16),
+            pltpu.SemaphoreType.DMA,
+            pltpu.SemaphoreType.DMA,
         ],
         4 * rows * width * width,
         6 * rows * width + 4 * width * width,
@@ -986,20 +1017,19 @@
 
 def qkv_grad(meta, inputs, grads, orders, targets, after=()):
     rows, width = inputs.shape
-    columns = width // 2
     return run_kernel(
         functools.partial(qkv_grad_kernel, orders, len(targets)),
         meta,
-        (6,),
+        (3,),
         [
             (fixed((rows, width)), inputs),
-            (pl.BlockSpec((1, rows, columns), lambda i, m: (i % 3, 0, half_of(i, m, 3))), grads),
+            (pl.BlockSpec((1, rows, width), lambda i, m: (i, 0, 0)), grads),
         ],
         targets,
         [
             pltpu.VMEM((width, rows), jnp.bfloat16),
-            pltpu.VMEM((2, width, columns), jnp.bfloat16),
-            pair_sems(),
+            pltpu.VMEM((3, width, width), jnp.bfloat16),
+            three_sems(),
         ],
         6 * rows * width * width,
         8 * rows * width + 6 * width * width,
@@ -1008,26 +1038,27 @@
     )
 
 
-def input_gradient(meta, grads, resid_grad, pieces, after=()):
+def input_gradient(meta, grads, resid_grad, pieces, after=(), low=False):
     rows, width = resid_grad.shape
-    columns = width // 2
-    (input_grad,) = run_kernel(
+    outs = [(fixed_out((rows, width)), full_shape(rows, width))]
+    if low:
+        outs.append((fixed_out((rows, width)), low_shape(rows, width)))
+    return run_kernel(
         functools.partial(input_grad_kernel, pieces),
         meta,
-        (6,),
+        (3,),
         [
-            (pl.BlockSpec((1, rows, columns), lambda i, m: (i % 3, 0, half_of(i, m, 3))), grads),
+            (pl.BlockSpec((1, rows, width), lambda i, m: (i, 0, 0)), grads),
             (fixed((rows, width)), resid_grad),
         ]
         + sources_of(pieces),
-        [(fixed_out((rows, width)), full_shape(rows, width))],
-        [pltpu.VMEM((2, width, 3 * columns), jnp.bfloat16), pair_sems(), pair_sems()],
+        outs,
+        [pltpu.VMEM((3, width, width), jnp.bfloat16), three_sems()],
         6 * rows * width * width,
         14 * rows * width + 6 * width * width,
         "input_gradient",
         after,
     )
-    return input_grad
 
 
 def both_halves(mine, theirs, place):
@@ -1084,75 +1115,84 @@
         halves = bias_halves[:, index]
         value = halves[:, : 2 * qv_columns].reshape(2, 2, qv_columns)
         zero = jnp.zeros((2, qv_columns), jnp.float32)
-        bias = jnp.stack([value[:, 0], zero, value[:, 1]]).reshape(6, 1, -1)
+        bias = jnp.stack([value[:, 0], zero, value[:, 1]]).reshape(3, 1, -1)
         vectors = jnp.concatenate(
             [out_bias[index], norm_gain[index], norm_bias[index], jnp.zeros((2, width), jnp.float32)]
         )
         return bias, vectors, halves[:, 2 * qv_columns :].reshape(2 * FFN_PARTS, 1, -1)
 
-    def attention_weights(index, routed, *others):
-        shard = jnp.concatenate([*qkv_weight[index], out_weight[index]], axis=1)
-        return Gathering(shard, orders) if routed else WholeGathering(shard, orders, *others)
-
-    def ffn_weights(index, routed, *others):
-        shard = jnp.concatenate([ffn_in_weight[index], ffn_out_weight[index]], axis=1)
-        return Gathering(shard, orders) if routed else WholeGathering(shard, orders, *others)
+    def gathering(flag, *members):
+        shard = jnp.concatenate(members, axis=1)
+        return (Gathering if flag else WholeGathering)(shard, orders)
 
     def attention_split(pieces):
-        return [pieces[0], pieces[1].narrow(0, width // 2)], pieces[1].narrow(width // 2, width // 2)
-
-    hops = [[routed and flag for flag in flags] for flags in HOPS]
+        half = width // 2
+        query_key, value_out = pieces
+        qkv = [query_key.narrow(0, half), query_key.narrow(half, half), value_out.narrow(0, half)]
+        return qkv, value_out.narrow(half, half)
+
     hops_back = [[routed and flag for flag in flags] for flags in HOPS_BACK]
 
     def waits(flag, members):
         return list(members) if flag else []
 
-    first, first_ffn = attention_weights(0, hops[0][0]), ffn_weights(0, hops[0][1])
-    first.far()
-    first.middle()
-    last = waits(hops[0][0], first.last())
-    first.core()
-    second, second_ffn = attention_weights(1, hops[1][0], *last), ffn_weights(1, hops[1][1], *last)
-    ffn_far = first_ffn.far()
-    ffn_middle = first_ffn.middle()
-    ffn_last = first_ffn.last()
+    first = gathering(routed, *qkv_weight[0], out_weight[0])
+    first_ffn = gathering(False, ffn_in_weight[0], ffn_out_weight[0])
+    second = gathering(routed, *qkv_weight[1], out_weight[1])
+    if SPLIT_DOWN:
+        second_in = gathering(False, ffn_in_weight[1])
+        second_down = gathering(routed, ffn_out_weight[1])
+    else:
+        second_in = gathering(False, ffn_in_weight[1], ffn_out_weight[1])
+        second_down = second_in
+    first.send_far()
+    first.land_far()
+    first.send_middle()
+    first.land_middle()
+    last = first.send_last()
+    first.send_core()
+    second.send_far(*waits(routed, last))
     bias, vectors, ffn_bias = small_inputs(0)
     qkv_pieces, out_piece = attention_split(first.pieces())
-    qkv = qkv_forward(meta, own_tokens, bias, qkv_pieces, waits(hops[0][1], ffn_middle))
-    first_ffn.core(qkv)
-    second_far = second.far(*last)
-    second_middle = second.middle(qkv)
-    mixed, logsum = attention_forward(
-        meta, qkv, slabs, waits(hops[0][1], ffn_last) + waits(hops[1][0], second_far)
-    )
+    qkv = qkv_forward(meta, own_tokens, bias, qkv_pieces)
+    second.land_far(qkv)
+    second.send_middle(qkv)
+    mixed, logsum = attention_forward(meta, qkv, slabs)
+    second.land_middle(mixed)
+    second_last = second.send_last(mixed)
+    if SPLIT_DOWN:
+        second_down.send_far(mixed)
     first_pieces = (qkv_pieces, out_piece, first_ffn.pieces())
-    second_ffn_far = second_ffn.far(mixed)
-    second_last = second.last(mixed)
     out = ffn_forward(
-        meta, mixed, own_tokens, vectors, ffn_bias, [out_piece] + first_pieces[2],
-        waits(hops[1][0], second_middle),
+        meta, mixed, own_tokens, vectors, ffn_bias, [out_piece] + first_pieces[2]
     )
     kept_layers = [(own_tokens, qkv, mixed, logsum, vectors, out)]
     layer_one = out[5]
-    second.core(layer_one)
-    second_ffn_middle = second_ffn.middle(layer_one)
+    second.send_core(layer_one)
+    if SPLIT_DOWN:
+        second_down.land_far(layer_one)
+        second_down.send_middle(layer_one)
     bias, vectors, ffn_bias = small_inputs(1)
     qkv_pieces, out_piece = attention_split(second.pieces())
-    qkv = qkv_forward(
-        meta, layer_one, bias, qkv_pieces,
-        waits(hops[1][1], second_ffn_far) + waits(hops[1][0], second_last),
-    )
-    second_ffn.last(qkv)
-    mixed, logsum = attention_forward(meta, qkv, slabs, waits(hops[1][1], second_ffn_middle))
+    qkv = qkv_forward(meta, layer_one, bias, qkv_pieces, waits(routed, second_last))
+    if SPLIT_DOWN:
+        second_down.land_middle(qkv)
+        second_down.send_last(qkv)
+    mixed, logsum = attention_forward(meta, qkv, slabs)
+    if SPLIT_DOWN:
+        second_down.send_core(mixed)
+        ffn_pieces = [Joined(second_in.pieces()), Joined(second_down.pieces())]
+    else:
+        ffn_pieces = second_in.pieces()
     one_other = hop(tied(layer_one, [mixed]), ("tensor", 1))
-    second_ffn.core(mixed)
-    second_pieces = (qkv_pieces, out_piece, second_ffn.pieces())
+    second_pieces = (qkv_pieces, out_piece, ffn_pieces)
     out = ffn_forward(
         meta, mixed, layer_one, vectors, ffn_bias, [out_piece] + second_pieces[2]
     )
     kept_layers.append((layer_one, qkv, mixed, logsum, vectors, out))
     layer_two = out[5]
     two_other = hop(layer_two, ("tensor", 1))
+    layer_one_whole = both_halves(layer_one, tied(one_other, [layer_two]), place)
 
     def targets(flag, columns):
         return targets_of(flag, split, width, block_rows, columns)
@@ -1161,14 +1201,14 @@
         kind = Scattering if flag else WholeScattering
         return kind(members, orders, sides)
 
-    half_ffn = first_ffn.width
+    half_ffn = ffn_in_weight.shape[2]
 
     def ffn_back(index, gradient, pieces, after=()):
         inputs, qkv, mixed, logsum, vectors, out = kept_layers[index]
         hidden, normed_one, spread_one, activated, slope, _, normed_two, spread_two = out
         kept = (hidden, normed_one, spread_one, activated, slope, normed_two, spread_two)
         attention_grad, resid_grad, sums, ffn_sums, *members = ffn_backward(
-            meta, gradient, kept, vectors, pieces[2], targets(hops_back[index][1], 2 * half_ffn), after
+            meta, gradient, kept, vectors, pieces[2], orders, targets(hops_back[index][1], 2 * half_ffn), after
         )
         scatter = scattering(
             hops_back[index][1], [members], [[(0, 0, half_ffn)], [(0, half_ffn, 2 * half_ffn)]]
@@ -1203,62 +1243,74 @@
         )
 
     attention_grad, resid_grad, sums, ffn_one = ffn_back(1, own_cotangent, second_pieces, [one_other])
-    layer_one_whole = both_halves(layer_one, one_other, place)
-    ffn_core = ffn_one.core()
+    layer_two_whole = both_halves(layer_two, tied(two_other, [attention_grad]), place)
+    ffn_one.send_core()
     mixed_grad, *out_members = out_back(1, attention_grad, second_pieces, [two_other])
-    layer_two_whole = both_halves(layer_two, two_other, place)
-    grads, qkv_sums = attention_back(1, mixed_grad, ffn_core)
+    ffn_one.land_core(mixed_grad)
+    ffn_one.send_last(mixed_grad)
+    grads, qkv_sums = attention_back(1, mixed_grad)
+    ffn_one.land(grads)
     smalls_one = flat_smalls(*sums, qkv_sums)
-    ffn_last = ffn_one.last(mixed_grad)
-    attention_one = qkv_grads(1, grads, out_members, waits(hops_back[1][1], ffn_last))
-    attention_core = attention_one.core()
-    gradient = input_gradient(meta, grads, resid_grad, second_pieces[0], attention_one.begun)
-    ffn_middle = ffn_one.middle(gradient)
-    attention_last = attention_one.last(gradient)
+    attention_one = qkv_grads(1, grads, out_members)
+    begun = attention_one.begun
+    one_core = attention_one.send_core()
+    ffn_one.send_middle(*begun)
+    (gradient,) = input_gradient(meta, grads, resid_grad, second_pieces[0], begun)
+    attention_one.land_core(gradient)
+    ffn_one.land(gradient)
+    one_last = attention_one.send_last(gradient)
+    ffn_one.send_far(gradient)
     attention_grad, resid_grad, sums, ffn_zero = ffn_back(
-        0, gradient, first_pieces, waits(hops_back[1][1], ffn_middle) + attention_core
-    )
-    ffn_far = ffn_one.far(attention_grad)
-    ffn_core = ffn_zero.core()
-    attention_middle = attention_one.middle(attention_grad)
+        0, gradient, first_pieces, waits(hops_back[1][0], one_core)
+    )
+    attention_one.land(attention_grad)
+    ffn_one.land_far(attention_grad)
+    one_middle = attention_one.send_middle(attention_grad)
+    zero_core = ffn_zero.send_core(attention_grad)
     mixed_grad, *out_members = out_back(
-        0, attention_grad, first_pieces, waits(hops_back[1][0], attention_last)
-    )
-    ffn_last = ffn_zero.last(mixed_grad)
-    attention_far = attention_one.far(mixed_grad)
-    grads, qkv_sums = attention_back(
-        0, mixed_grad, ffn_core + waits(hops_back[1][0], attention_middle)
-    )
+        0, attention_grad, first_pieces, waits(hops_back[1][0], one_last)
+    )
+    ffn_zero.land_core(mixed_grad)
+    attention_one.land(mixed_grad)
+    ffn_last = ffn_zero.send_last(mixed_grad)
+    one_far = attention_one.send_far(mixed_grad)
+    grads, qkv_sums = attention_back(0, mixed_grad, waits(routed, one_middle + zero_core))
+    ffn_zero.land(grads)
+    attention_one.land_far(grads)
     smalls_zero = flat_smalls(*sums, qkv_sums)
-    ffn_middle = ffn_zero.middle(grads)
-    before = ffn_last + waits(hops_back[1][0], attention_far) + waits(hops_back[1][1], ffn_far)
-    if LATE_WEIGHTS:
-        gradient = input_gradient(meta, grads, resid_grad, first_pieces[0], before)
-        attention_zero = qkv_grads(0, grads, out_members, [gradient, *ffn_middle])
-        attention_zero.core()
-    else:
-        attention_zero = qkv_grads(0, grads, out_members, before)
-        attention_zero.core()
-        gradient = input_gradient(
-            meta, grads, resid_grad, first_pieces[0], attention_zero.begun + ffn_middle
-        )
-    ffn_zero.far()
-    attention_last = attention_zero.last(gradient)
-    attention_zero.middle()
-    attention_zero.far()
-
-    low_gradient = gradient.astype(jnp.bfloat16)
+    totals = Totals(jnp.stack([smalls_zero, smalls_one]), routed)
+    totals.send("dp", 1, 4, grads)
+    zero_middle = ffn_zero.send_middle(grads)
+    attention_zero = qkv_grads(0, grads, out_members, waits(routed, ffn_last + one_far))
+    begun = attention_zero.begun
+    totals.land(*begun)
+    totals.send("dp", 4, dp_size // 4, *begun)
+    attention_zero.send_core(*begun)
+    gradient, token_low = input_gradient(
+        meta, grads, resid_grad, first_pieces[0], begun + waits(routed, zero_middle), True
+    )
+    totals.land(gradient)
+    attention_zero.land_core(gradient)
+    zero_last = attention_zero.send_last(gradient)
+    ffn_zero.land(gradient)
+    ffn_zero.send_far(gradient)
     if HOLD_TOKENS:
-        low_gradient = tied(low_gradient, waits(hops_back[0][0], attention_last))
-    token_grad = both_halves(
-        gradient, hop(low_gradient, ("tensor", 1)).astype(jnp.float32), place
-    )
+        token_low = tied(token_low, waits(routed, zero_last))
+    token_other = hop(token_low, ("tensor", 1))
+    totals.send("tensor", 1, 2, gradient, *waits(routed, zero_last))
+    attention_zero.land(gradient)
+    zero_middle = attention_zero.send_middle(gradient)
+    totals.land(gradient, *waits(routed, zero_middle))
+    smalls = totals.total
+    ffn_zero.land_far(gradient, *waits(routed, zero_middle))
+    attention_zero.land(gradient)
+    attention_zero.send_far(gradient)
+    attention_zero.land_far(gradient)
+    token_grad = both_halves(gradient, token_other.astype(jnp.float32), place)
     matrix_grads = []
     for attention, ffn in ((attention_zero, ffn_zero), (attention_one, ffn_one)):
         out_part, *qkv_parts = jnp.split(attention.result, 4, axis=1)
         matrix_grads.append((jnp.stack(qkv_parts), out_part, *jnp.split(ffn.result, 2, axis=1)))
-    smalls = tied(jnp.stack([smalls_zero, smalls_one]), [gradient])
-    smalls = sum_over_all(smalls, routed)
     eight = smalls[:, : 8 * width].reshape(layer_count, 4, 2, width)
     ffn_total = smalls[:, 8 * width :]
     return (

time: 601 us -> 574 us (0.955)
  Pallas kernels: 301 us -> 286 us
  waiting for transfers between devices: 116 us -> 105 us
  other arithmetic: 51.7 us -> 61.4 us
  starting transfers between devices: 78.4 us -> 70.7 us
    ppermute x58 -> x59, waiting for transfers between devices: 116 us -> 80.5 us  [hop(): return lax.ppermute(member, axis, pairs)]
    all_gather x2, waiting for transfers between devices: 0.01 us -> 24.1 us  [__init__(): whole = lax.all_gather(shard, AXES, tiled=True)]
    pallas_call x16, Pallas kernels: 301 us -> 286 us  [run_kernel(): pl.pallas_call(body, grid_spec=pltpu.PrefetchScalarGridSpec(num_scalar_pr...]
    unnamed x111 -> x99, local copies, waits for them, and re-layouts: 10.8 us -> 1.8 us
    ppermute x58 -> x59, starting transfers between devices: 78.1 us -> 70.6 us  [hop(): return lax.ppermute(member, axis, pairs)]
  transfers between devices with their start and end apart: 61 -> 62, of which waited for: 25 -> 15; matrix products, arithmetic and copies ran while one was open for 12% -> 15% of each run, Pallas kernels for 51% -> 43%
where the time goes in v4:
time: 574 us; the launch traced here: 569 us
  Pallas kernels  286 us (50%)
  waiting for transfers between devices  105 us (18%)
  starting transfers between devices  70.7 us (12%)
  other arithmetic  61.4 us (11%)
  local copies, waits for them, and re-layouts  30.7 us (5%)
  between operations  15.1 us (3%)
    pallas_call x16, Pallas kernels, run_kernel(): pl.pallas_call(body, grid_spec=pltpu.PrefetchScalarGridSpec(num_scalar_pr...  286 us
    ppermute x59, waiting for transfers between devices, hop(): return lax.ppermute(member, axis, pairs)  80.5 us
    ppermute x59, starting transfers between devices, hop(): return lax.ppermute(member, axis, pairs)  70.6 us
    all_gather x2, waiting for transfers between devices, __init__(): whole = lax.all_gather(shard, AXES, tiled=True)  24.1 us
  transfers between devices with their start and end apart: 62, of which 15 were waited for; matrix products, arithmetic and copies ran while one was open for 15% of the time, Pallas kernels for 43%

profile of v4, /device:TPU:0, one launch (start us, length us, event | category | flops | bytes accessed | tf_op | source)
XLA Modules:
  0.0 568.7 jit_solution(16634753907251765635)
XLA Ops:
  12.2 3.0 collective-permute-start.1
  15.2 2.6 collective-permute-start.2
  40.9 7.1 %collective-permute-done.8 = bf16[4,48,768]{2,1,0:T(8,128)(2,1)S(1)} collective-permute-done((bf16[4,48,768]{2,1,0:T(8,128)(2,1)S(1)}, bf16[4,48,768]{2,1,0:T(8,128)(2,1)S(1)}, u32[]{:S(2)}, u32[]{:S(2)}) %collective-permute-start.8) | collective-permute-done | bytes 294944 | tf_op jit(solution)/shard_map/ppermute | solution.py:78
  53.6 14.3 %collective-permute-done.9.refs_11_.refs_5_.refs_3_ = bf16[8,48,768]{2,1,0:T(8,128)(2,1)S(1)} collective-permute-done((bf16[8,48,768]{2,1,0:T(8,128)(2,1)}, bf16[8,48,768]{2,1,0:T(8,128)(2,1)S(1)}, u32[]{:S(2)}, u32[]{:S(2)}) %collective-permute-start.9) | collective-permute-done | bytes 589856 | tf_op jit(solution)/shard_map/ppermute | solution.py:78
  69.8 2.2 collective-permute-start.12
  71.9 1.9 collective-permute-start.13
  74.8 9.0 %qkv_forward.2.refs_0_ = bf16[3,1024,768]{2,1,0:T(8,128)(2,1)} custom-call(s32[12]{0:T(128)} %pad_add_fusion.meta_ref, bf16[1024,768]{1,0:T(8,128)(2,1)} %constant_dynamic-slice_fusion.2.refs_0_.refs_1_, f32[3,1,768]{2,1,0:T(1,128)} %get-tuple-element.375.refs_1_, bf16[8,48,768]{2,1,0:T(8,128)(2,1)} %copy-done.38, bf16[8,48,768]{2,1,0:T(8,128)(2,1)} %copy-done.41, ...), custom_call_target="tpu_custom_call" | custom-call | flops 28991029248 | bytes 9830400 | tf_op jit(solution)/shard_map/qkv_forward/pallas_call | solution.py:775
  83.8 8.8 %collective-permute-done.13 = bf16[1,48,1536]{2,1,0:T(8,128)(2,1)S(1)} collective-permute-done((bf16[1,48,1536]{2,1,0:T(8,128)(2,1)S(1)}, bf16[1,48,1536]{2,1,0:T(8,128)(2,1)S(1)}, u32[]{:S(2)}, u32[]{:S(2)}) %collective-permute-start.13) | collective-permute-done | bytes 147488 | tf_op jit(solution)/shard_map/ppermute | solution.py:78
  96.3 17.5 %attention_forward.2 = (bf16[1024,768]{1,0:T(8,128)(2,1)}, f32[2,6,8,512]{3,2,1,0:T(8,128)}) custom-call(s32[12]{0:T(128)} %pad_add_fusion.meta_ref, bf16[3,1024,768]{2,1,0:T(8,128)(2,1)} %qkv_forward.2.refs_0_), custom_call_target="tpu_custom_call" | custom-call | flops 51539607552 | bytes 6291456 | tf_op jit(solution)/shard_map/attention_forward/pallas_call | solution.py:775
  115.9 2.0 collective-permute-start.16
  118.1 30.8 %ffn_forward.2 = (bf16[1024,768]{1,0:T(8,128)(2,1)}, bf16[1024,768]{1,0:T(8,128)(2,1)}, f32[1024,128]{1,0:T(8,128)}, bf16[1024,3072]{1,0:T(8,128)(2,1)}, bf16[10...) custom-call(s32[12]{0:T(128)} %pad_add_fusion.meta_ref, ...), custom_call_target="tpu_custom_call" | custom-call | flops 77309411328 | bytes 28311552 | tf_op jit(solution)/shard_map/ffn_forward/pallas_call | solution.py:775
  152.3 9.1 %qkv_forward.3.refs_0_ = bf16[3,1024,768]{2,1,0:T(8,128)(2,1)} custom-call(s32[12]{0:T(128)} %pad_add_fusion.meta_ref, bf16[1024,768]{1,0:T(8,128)(2,1)} %get-tuple-element.150.refs_0_.refs_1_, f32[3,1,768]{2,1,0:T(1,128)} %get-tuple-element.374.refs_1_, bf16[8,48,768]{2,1,0:T(8,128)(2,1)} %constant_dynamic-update-slice_fusion.12.refs_2_.refs_6_, ...), custom_call_target="tpu_custom_call" | custom-call | flops 28991029248 | bytes 9830400 | tf_op jit(solution)/shard_map/qkv_forward/pallas_call | solution.py:775
  161.3 17.6 %attention_forward.3 = (bf16[1024,768]{1,0:T(8,128)(2,1)}, f32[2,6,8,512]{3,2,1,0:T(8,128)}) custom-call(s32[12]{0:T(128)} %pad_add_fusion.meta_ref, bf16[3,1024,768]{2,1,0:T(8,128)(2,1)} %qkv_forward.3.refs_0_), custom_call_target="tpu_custom_call" | custom-call | flops 51539607552 | bytes 6291456 | tf_op jit(solution)/shard_map/attention_forward/pallas_call | solution.py:775
  179.3 24.1 %all-gather.5.cloned.1.call-done = bf16[1536,3072]{1,0:T(8,128)(2,1)} async-done(((bf16[48,3072]{1,0:T(8,128)(2,1)}), bf16[1536,3072]{1,0:T(8,128)(2,1)}) %all-gather.5.cloned.1.call-update) | async-done | bytes 9437200 | tf_op jit(solution)/shard_map/all_gather | solution.py:150
  203.4 30.6 %ffn_forward.3 = (bf16[1024,768]{1,0:T(8,128)(2,1)}, bf16[1024,768]{1,0:T(8,128)(2,1)}, f32[1024,128]{1,0:T(8,128)}, bf16[1024,3072]{1,0:T(8,128)(2,1)}, bf16[10...) custom-call(s32[12]{0:T(128)} %pad_add_fusion.meta_ref, ...), custom_call_target="tpu_custom_call" | custom-call | flops 77309411328 | bytes 28311552 | tf_op jit(solution)/shard_map/ffn_forward/pallas_call | solution.py:775
  234.6 33.9 %ffn_backward.2 = (bf16[1024,768]{1,0:T(8,128)(2,1)}, f32[1024,768]{1,0:T(8,128)}, f32[8,768]{1,0:T(8,128)}, f32[4,1,768]{2,1,0:T(1,128)}, bf16[2,768,3072]{2,1,0:T(8,128)(2,1)}) custom-call(s32[12]{0:T(128)} %pad_add_fusion.meta_ref, bf16[1024,768]{1,0:T(8,128)(2,1)} %constant_dynamic-slice_fusion.1.refs_0_, bf16[1024,768]{1,0:T(8,128)(2,1)} %get-tuple-element.153.refs_1_, ...), custom_call_target="tpu_custom_call" | custom-call | flops 309237645312 | bytes 50331648 | tf_op jit(solution)/shard_map/ffn_backward/pallas_call | solution.py:775
  269.8 8.8 %out_backward.2 = (bf16[1024,768]{1,0:T(8,128)(2,1)}, bf16[16,48,384]{2,1,0:T(8,128)(2,1)}, bf16[16,48,384]{2,1,0:T(8,128)(2,1)}) custom-call(s32[12]{0:T(128)} %pad_add_fusion.meta_ref, bf16[1024,768]{1,0:T(8,128)(2,1)} %get-tuple-element.160.refs_0_, bf16[1024,768]{1,0:T(8,128)(2,1)} %get-tuple-element.149.refs_0_.refs_1_, ...), custom_call_target="tpu_custom_call" | custom-call | flops 38654705664 | bytes 7077888 | tf_op jit(solution)/shard_map/out_backward/pallas_call | solution.py:775
  278.6 22.5 %attention_backward.2 = (bf16[3,1024,768]{2,1,0:T(8,128)(2,1)}, f32[8,768]{1,0:T(8,128)}) custom-call(s32[12]{0:T(128)} %pad_add_fusion.meta_ref, bf16[3,1024,768]{2,1,0:T(8,128)(2,1)} %qkv_forward.3.refs_0_, bf16[1024,768]{1,0:T(8,128)(2,1)} %get-tuple-element.149.refs_0_.refs_1_, bf16[1024,768]{1,0:T(8,128)(2,1)} %get-tuple-element.162.refs_2_, ...), custom_call_target="tpu_custom_call" | custom-call | flops 257698037760 | bytes 12582912 | tf_op jit(solution)/shard_map/attention_backward/pallas_call | solution.py:775
  301.1 8.8 %qkv_grad.2 = (bf16[16,48,1152]{2,1,0:T(8,128)(2,1)}, bf16[16,48,1152]{2,1,0:T(8,128)(2,1)}) custom-call(s32[12]{0:T(128)} %pad_add_fusion.meta_ref, bf16[1024,768]{1,0:T(8,128)(2,1)} %get-tuple-element.150.refs_0_.refs_1_, bf16[3,1024,768]{2,1,0:T(8,128)(2,1)} %get-tuple-element.164.refs_1_.refs_0_), custom_call_target="tpu_custom_call" | custom-call | flops 57982058496 | bytes 9830400 | tf_op jit(solution)/shard_map/qkv_grad/pallas_call | solution.py:775
  310.6 10.4 %input_gradient.2.refs_0_ = f32[1024,768]{1,0:T(8,128)} custom-call(s32[12]{0:T(128)} %pad_add_fusion.meta_ref, bf16[3,1024,768]{2,1,0:T(8,128)(2,1)} %get-tuple-element.164.refs_1_.refs_0_, f32[1024,768]{1,0:T(8,128)} %get-tuple-element.165.refs_1_, bf16[8,48,768]{2,1,0:T(8,128)(2,1)} %constant_dynamic-update-slice_fusion.12.refs_2_.refs_6_, ...), custom_call_target="tpu_custom_call" | custom-call | flops 57982058496 | bytes 14548992 | tf_op jit(solution)/shard_map/input_gradient/pallas_call | solution.py:775
  321.1 3.7 maximum_select_fusion.2
  326.2 3.7 maximum_select_fusion.1
  335.9 35.2 %ffn_backward.3 = (bf16[1024,768]{1,0:T(8,128)(2,1)}, f32[1024,768]{1,0:T(8,128)}, f32[8,768]{1,0:T(8,128)}, f32[4,1,768]{2,1,0:T(1,128)}, bf16[16,48,3072]{2,1,0:T(8,128)(2,1)}, /*index=5*/bf16[16,48,3072]{2,1,0:T(8,128)(2,1)}) custom-call(s32[12]{0:T(128)} %pad_add_fusion.meta_ref, f32[1024,768]{1,0:T(8,128)} %input_gradient.2.refs_0_, ...), custom_call_target="tpu_custom_call" | custom-call | flops 309237645312 | bytes 50331648 | tf_op jit(solution)/shard_map/ffn_backward/pallas_call | solution.py:775
  372.5 2.0 add_convert_fusion.9
  374.5 2.1 collective-permute-start.30
  378.8 9.0 %out_backward.3 = (bf16[1024,768]{1,0:T(8,128)(2,1)}, bf16[16,48,384]{2,1,0:T(8,128)(2,1)}, bf16[16,48,384]{2,1,0:T(8,128)(2,1)}) custom-call(s32[12]{0:T(128)} %pad_add_fusion.meta_ref, bf16[1024,768]{1,0:T(8,128)(2,1)} %get-tuple-element.176.refs_0_, bf16[1024,768]{1,0:T(8,128)(2,1)} %get-tuple-element.135.refs_0_.refs_1_, ...), custom_call_target="tpu_custom_call" | custom-call | flops 38654705664 | bytes 7077888 | tf_op jit(solution)/shard_map/out_backward/pallas_call | solution.py:775
  391.4 2.1 add_bitcast_fusion.2
  394.2 2.1 collective-permute-start.36
  397.0 7.4 %collective-permute-start.35 = (bf16[48,1536]{1,0:T(8,128)(2,1)}, bf16[48,1536]{1,0:T(8,128)(2,1)}, u32[]{:S(2)}, u32[]{:S(2)}) collective-permute-start(bf16[48,1536]{1,0:T(8,128)(2,1)} %pad_maximum_fusion.19), channel_id=1, source_target_pairs={{0,16},{2,18},{4,20},{6,22},{8,24},{10,26},{12,28},{14,30},{16,0},... | collective-permute-start | bytes 442376 | tf_op jit(solution)/shard_map/ppermute | solution.py:78
  405.1 3.7 add_convert_fusion
  409.4 22.7 %attention_backward.3 = (bf16[3,1024,768]{2,1,0:T(8,128)(2,1)}, f32[8,768]{1,0:T(8,128)}) custom-call(s32[12]{0:T(128)} %pad_add_fusion.meta_ref, bf16[3,1024,768]{2,1,0:T(8,128)(2,1)} %qkv_forward.2.refs_0_, bf16[1024,768]{1,0:T(8,128)(2,1)} %get-tuple-element.135.refs_0_.refs_1_, bf16[1024,768]{1,0:T(8,128)(2,1)} %get-tuple-element.182.refs_2_, ...), custom_call_target="tpu_custom_call" | custom-call | flops 257698037760 | bytes 12582912 | tf_op jit(solution)/shard_map/attention_backward/pallas_call | solution.py:775
  436.2 6.8 %collective-permute-done.32.refs_2_ = bf16[8,48,1536]{2,1,0:T(8,128)(2,1)} collective-permute-done((bf16[8,48,1536]{2,1,0:T(8,128)(2,1)}, bf16[8,48,1536]{2,1,0:T(8,128)(2,1)}, u32[]{:S(2)}, u32[]{:S(2)}) %collective-permute-start.32) | collective-permute-done | bytes 1179680 | tf_op jit(solution)/shard_map/ppermute | solution.py:78
  443.0 8.9 %qkv_grad.3 = (bf16[16,48,1152]{2,1,0:T(8,128)(2,1)}, bf16[16,48,1152]{2,1,0:T(8,128)(2,1)}) custom-call(s32[12]{0:T(128)} %pad_add_fusion.meta_ref, bf16[1024,768]{1,0:T(8,128)(2,1)} %constant_dynamic-slice_fusion.2.refs_0_.refs_1_, bf16[3,1024,768]{2,1,0:T(8,128)(2,1)} %get-tuple-element.190.refs_1_.refs_0_, ...), custom_call_target="tpu_custom_call" | custom-call | flops 57982058496 | bytes 9830400 | tf_op jit(solution)/shard_map/qkv_grad/pallas_call | solution.py:775
  452.8 1.8 collective-permute-start.52
  455.3 1.9 collective-permute-start.54
  457.2 2.1 add_convert_fusion.3
  461.4 9.1 %collective-permute-done.38.refs_16_ = bf16[4,48,1536]{2,1,0:T(8,128)(2,1)S(1)} collective-permute-done((bf16[4,48,1536]{2,1,0:T(8,128)(2,1)S(1)}, bf16[4,48,1536]{2,1,0:T(8,128)(2,1)S(1)}, u32[]{:S(2)}, u32[]{:S(2)}) %collective-permute-start.38) | collective-permute-done | bytes 589856 | tf_op jit(solution)/shard_map/ppermute | solution.py:78
  471.4 11.2 %input_gradient.3 = (f32[1024,768]{1,0:T(8,128)}, bf16[1024,768]{1,0:T(8,128)(2,1)}) custom-call(s32[12]{0:T(128)} %pad_add_fusion.meta_ref, bf16[3,1024,768]{2,1,0:T(8,128)(2,1)} %get-tuple-element.190.refs_1_.refs_0_, f32[1024,768]{1,0:T(8,128)} %get-tuple-element.191.refs_1_, bf16[8,48,768]{2,1,0:T(8,128)(2,1)} %copy-done.38, ...), custom_call_target="tpu_custom_call" | custom-call | flops 57982058496 | bytes 14548992 | tf_op jit(solution)/shard_map/input_gradient/pallas_call | solution.py:775
  482.6 1.9 fusion.6
  493.5 2.6 collective-permute-start.57
  496.0 9.1 %collective-permute-done.41 = bf16[8,48,768]{2,1,0:T(8,128)(2,1)S(1)} collective-permute-done((bf16[8,48,768]{2,1,0:T(8,128)(2,1)S(1)}, bf16[8,48,768]{2,1,0:T(8,128)(2,1)S(1)}, u32[]{:S(2)}, u32[]{:S(2)}) %collective-permute-start.41) | collective-permute-done | bytes 589856 | tf_op jit(solution)/shard_map/ppermute | solution.py:78
  510.9 7.6 %collective-permute-done.55 = f32[2,9216]{1,0:T(2,128)S(1)} collective-permute-done((f32[2,9216]{1,0:T(2,128)S(1)}, f32[2,9216]{1,0:T(2,128)S(1)}, u32[]{:S(2)}, u32[]{:S(2)}) %collective-permute-start.55) | collective-permute-done | bytes 73760 | tf_op jit(solution)/shard_map/ppermute | solution.py:78
  518.5 2.6 collective-permute-start.58
  522.9 4.6 collective-permute-done.58
  530.4 5.8 %collective-permute-start.46 = (bf16[48,1536]{1,0:T(8,128)(2,1)}, bf16[48,1536]{1,0:T(8,128)(2,1)}, u32[]{:S(2)}, u32[]{:S(2)}) collective-permute-start(bf16[48,1536]{1,0:T(8,128)(2,1)} %pad_maximum_fusion.21), channel_id=1, source_target_pairs={{0,8},{2,10},{4,12},{6,14},{8,0},{10,2},{12,4},{14,6},{16,24},{18,... | collective-permute-start | bytes 442376 | tf_op jit(solution)/shard_map/ppermute | solution.py:78
  543.5 6.3 %collective-permute-done.47 = bf16[48,1536]{1,0:T(8,128)(2,1)} collective-permute-done((bf16[48,1536]{1,0:T(8,128)(2,1)S(1)}, bf16[48,1536]{1,0:T(8,128)(2,1)}, u32[]{:S(2)}, u32[]{:S(2)}) %collective-permute-start.47) | collective-permute-done | bytes 147488 | tf_op jit(solution)/shard_map/ppermute | solution.py:78
  552.5 3.1 collective-permute-done.43
  555.8 3.1 maximum_select_fusion
  (321 shorter events, 106.4 us)
Async XLA Ops:
  7.2 110.9 %all-gather.3.cloned.1.call-start = ((), (), s32[]{:S(2)}) async-start(), calls=%async_computation.1 | async-start | bytes 9732096 | tf_op jit(solution)/shard_map/all_gather | solution.py:150
  9.3 194.1 %all-gather.5.cloned.1.call-start = ((), (), s32[]{:S(2)}) async-start(), calls=%async_computation.2 | async-start | bytes 9732096 | tf_op jit(solution)/shard_map/all_gather | solution.py:150
  12.2 20.7 %collective-permute-start.1 = (bf16[1,48,1536]{2,1,0:T(8,128)(2,1)}, bf16[1,48,1536]{2,1,0:T(8,128)(2,1)}, u32[]{:S(2)}, u32[]{:S(2)}) collective-permute-start(bf16[1,48,1536]{2,1,0:T(8,128)(2,1)} %maximum_bitcast_fusion.2), channel_id=1, source_target_pairs={{0,8},{2,10},{4,12},{6,14},{8,0},{10,2},{12,4},{14,6},{16,24},{18,... | collective-permute-start | bytes 442376 | tf_op jit(solution)/shard_map/ppermute | solution.py:78
  15.2 19.3 %collective-permute-start.2 = (bf16[1,48,1536]{2,1,0:T(8,128)(2,1)}, bf16[1,48,1536]{2,1,0:T(8,128)(2,1)}, u32[]{:S(2)}, u32[]{:S(2)}) collective-permute-start(bf16[1,48,1536]{2,1,0:T(8,128)(2,1)} %maximum_bitcast_fusion.2), channel_id=1, source_target_pairs={{0,16},{2,18},{4,20},{6,22},{8,24},{10,26},{12,28},{14,30},{16,0},... | collective-permute-start | bytes 442376 | tf_op jit(solution)/shard_map/ppermute | solution.py:78
  17.8 18.3 %collective-permute-start.3 = (bf16[1,48,1536]{2,1,0:T(8,128)(2,1)}, bf16[1,48,1536]{2,1,0:T(8,128)(2,1)}, u32[]{:S(2)}, u32[]{:S(2)}) collective-permute-start(bf16[1,48,1536]{2,1,0:T(8,128)(2,1)} %maximum_bitcast_fusion.2), channel_id=1, source_target_pairs={{0,24},{2,26},{4,28},{6,30},{8,16},{10,18},{12,20},{14,22},{16,8},... | collective-permute-start | bytes 442376 | tf_op jit(solution)/shard_map/ppermute | solution.py:78
  22.9 536.0 %reduce-scatter.2.cloned.1.call-start = ((), (), s32[]{:S(2)}) async-start(), calls=%async_computation.3 | async-start | bytes 9732096 | tf_op jit(solution)/shard_map/reduce_scatter | solution.py:235
  48.8 19.1 %collective-permute-start.9 = (bf16[8,48,768]{2,1,0:T(8,128)(2,1)}, bf16[8,48,768]{2,1,0:T(8,128)(2,1)S(1)}, u32[]{:S(2)}, u32[]{:S(2)}) collective-permute-start(bf16[8,48,768]{2,1,0:T(8,128)(2,1)} %constant_dynamic-update-slice_fusion.7.refs_10_.refs_4_.refs_2_), channel_id=1, source_target_pairs={{0,4},{2,6},{4,0},{6,2},{8,12},{10,14},{12,8},{14,10},{16,20},{18,... | collective-permute-start | bytes 1769480 | tf_op jit(solution)/shard_map/ppermute | solution.py:78
  51.5 16.3 %collective-permute-start.5 = (bf16[8,48,768]{2,1,0:T(8,128)(2,1)S(1)}, bf16[8,48,768]{2,1,0:T(8,128)(2,1)S(1)}, u32[]{:S(2)}, u32[]{:S(2)}) collective-permute-start(bf16[8,48,768]{2,1,0:T(8,128)(2,1)S(1)} %constant_dynamic-update-slice_fusion.2.refs_2_.refs_6_), channel_id=1, source_target_pairs={{0,1},{1,0},{2,3},{3,2},{4,5},{5,4},{6,7},{7,6},{8,9},{9,8},{10,11... | collective-permute-start | bytes 1769480 | tf_op jit(solution)/shard_map/ppermute | solution.py:78
  53.0 18.9 %collective-permute-start.10 = (bf16[8,48,768]{2,1,0:T(8,128)(2,1)}, bf16[8,48,768]{2,1,0:T(8,128)(2,1)S(1)}, u32[]{:S(2)}, u32[]{:S(2)}) collective-permute-start(bf16[8,48,768]{2,1,0:T(8,128)(2,1)} %constant_dynamic-update-slice_fusion.7.refs_10_.refs_4_.refs_2_), channel_id=1, source_target_pairs={{0,2},{2,0},{4,6},{6,4},{8,10},{10,8},{12,14},{14,12},{16,18},{18,... | collective-permute-start | bytes 1769480 | tf_op jit(solution)/shard_map/ppermute | solution.py:78
  53.1 20.8 %collective-permute-start.6 = (bf16[8,48,768]{2,1,0:T(8,128)(2,1)S(1)}, bf16[8,48,768]{2,1,0:T(8,128)(2,1)S(1)}, u32[]{:S(2)}, u32[]{:S(2)}) collective-permute-start(bf16[8,48,768]{2,1,0:T(8,128)(2,1)S(1)} %constant_dynamic-update-slice_fusion.2.refs_2_.refs_6_), channel_id=1, source_target_pairs={{0,2},{2,0},{4,6},{6,4},{8,10},{10,8},{12,14},{14,12},{16,18},{18,... | collective-permute-start | bytes 1769480 | tf_op jit(solution)/shard_map/ppermute | solution.py:78
  69.8 14.0 %collective-permute-start.12 = (bf16[1,48,1536]{2,1,0:T(8,128)(2,1)S(1)}, bf16[1,48,1536]{2,1,0:T(8,128)(2,1)S(1)}, u32[]{:S(2)}, u32[]{:S(2)}) collective-permute-start(bf16[1,48,1536]{2,1,0:T(8,128)(2,1)S(1)} %maximum_bitcast_fusion.3), channel_id=1, source_target_pairs={{0,8},{2,10},{4,12},{6,14},{8,0},{10,2},{12,4},{14,6},{16,24},{18,... | collective-permute-start | bytes 442376 | tf_op jit(solution)/shard_map/ppermute | solution.py:78
  71.9 20.7 %collective-permute-start.13 = (bf16[1,48,1536]{2,1,0:T(8,128)(2,1)S(1)}, bf16[1,48,1536]{2,1,0:T(8,128)(2,1)S(1)}, u32[]{:S(2)}, u32[]{:S(2)}) collective-permute-start(bf16[1,48,1536]{2,1,0:T(8,128)(2,1)S(1)} %maximum_bitcast_fusion.3), channel_id=1, source_target_pairs={{0,16},{2,18},{4,20},{6,22},{8,24},{10,26},{12,28},{14,30},{16,0},... | collective-permute-start | bytes 442376 | tf_op jit(solution)/shard_map/ppermute | solution.py:78
  73.9 18.7 %collective-permute-start.14 = (bf16[1,48,1536]{2,1,0:T(8,128)(2,1)S(1)}, bf16[1,48,1536]{2,1,0:T(8,128)(2,1)S(1)}, u32[]{:S(2)}, u32[]{:S(2)}) collective-permute-start(bf16[1,48,1536]{2,1,0:T(8,128)(2,1)S(1)} %maximum_bitcast_fusion.3), channel_id=1, source_target_pairs={{0,24},{2,26},{4,28},{6,30},{8,16},{10,18},{12,20},{14,22},{16,8},... | collective-permute-start | bytes 442376 | tf_op jit(solution)/shard_map/ppermute | solution.py:78
  94.7 19.1 %collective-permute-start.19 = (bf16[4,48,768]{2,1,0:T(8,128)(2,1)S(1)}, bf16[4,48,768]{2,1,0:T(8,128)(2,1)S(1)}, u32[]{:S(2)}, u32[]{:S(2)}) collective-permute-start(bf16[4,48,768]{2,1,0:T(8,128)(2,1)S(1)} %pad_maximum_fusion.9), channel_id=1, source_target_pairs={{0,1},{1,0},{2,3},{3,2},{4,5},{5,4},{6,7},{7,6},{8,9},{9,8},{10,11... | collective-permute-start | bytes 884744 | tf_op jit(solution)/shard_map/ppermute | solution.py:78
  94.8 20.3 %collective-permute-start.15 = (bf16[4,48,768]{2,1,0:T(8,128)(2,1)S(1)}, bf16[4,48,768]{2,1,0:T(8,128)(2,1)S(1)}, u32[]{:S(2)}, u32[]{:S(2)}) collective-permute-start(bf16[4,48,768]{2,1,0:T(8,128)(2,1)S(1)} %pad_maximum_fusion.8), channel_id=1, source_target_pairs={{0,4},{2,6},{4,0},{6,2},{8,12},{10,14},{12,8},{14,10},{16,20},{18,... | collective-permute-start | bytes 884744 | tf_op jit(solution)/shard_map/ppermute | solution.py:78
  114.5 34.5 %collective-permute-start.20 = (bf16[8,48,768]{2,1,0:T(8,128)(2,1)}, bf16[8,48,768]{2,1,0:T(8,128)(2,1)}, u32[]{:S(2)}, u32[]{:S(2)}) collective-permute-start(bf16[8,48,768]{2,1,0:T(8,128)(2,1)} %constant_dynamic-update-slice_fusion.17.refs_10_.refs_4_.refs_2_), channel_id=1, source_target_pairs={{0,4},{2,6},{4,0},{6,2},{8,12},{10,14},{12,8},{14,10},{16,20},{18,... | collective-permute-start | bytes 1769480 | tf_op jit(solution)/shard_map/ppermute | solution.py:78
  115.2 36.3 %collective-permute-start.21 = (bf16[8,48,768]{2,1,0:T(8,128)(2,1)}, bf16[8,48,768]{2,1,0:T(8,128)(2,1)}, u32[]{:S(2)}, u32[]{:S(2)}) collective-permute-start(bf16[8,48,768]{2,1,0:T(8,128)(2,1)} %constant_dynamic-update-slice_fusion.17.refs_10_.refs_4_.refs_2_), channel_id=1, source_target_pairs={{0,2},{2,0},{4,6},{6,4},{8,10},{10,8},{12,14},{14,12},{16,18},{18,... | collective-permute-start | bytes 1769480 | tf_op jit(solution)/shard_map/ppermute | solution.py:78
  115.9 33.5 %collective-permute-start.16 = (bf16[8,48,768]{2,1,0:T(8,128)(2,1)}, bf16[8,48,768]{2,1,0:T(8,128)(2,1)}, u32[]{:S(2)}, u32[]{:S(2)}) collective-permute-start(bf16[8,48,768]{2,1,0:T(8,128)(2,1)} %constant_dynamic-update-slice_fusion.12.refs_2_.refs_6_), channel_id=1, source_target_pairs={{0,1},{1,0},{2,3},{3,2},{4,5},{5,4},{6,7},{7,6},{8,9},{9,8},{10,11... | collective-permute-start | bytes 1769480 | tf_op jit(solution)/shard_map/ppermute | solution.py:78
  117.9 33.6 %collective-permute-start.17 = (bf16[8,48,768]{2,1,0:T(8,128)(2,1)}, bf16[8,48,768]{2,1,0:T(8,128)(2,1)}, u32[]{:S(2)}, u32[]{:S(2)}) collective-permute-start(bf16[8,48,768]{2,1,0:T(8,128)(2,1)} %constant_dynamic-update-slice_fusion.12.refs_2_.refs_6_), channel_id=1, source_target_pairs={{0,2},{2,0},{4,6},{6,4},{8,10},{10,8},{12,14},{14,12},{16,18},{18,... | collective-permute-start | bytes 1769480 | tf_op jit(solution)/shard_map/ppermute | solution.py:78
  178.9 55.7 %collective-permute-start.23 = (bf16[1024,768]{1,0:T(8,128)(2,1)S(1)}, bf16[1024,768]{1,0:T(8,128)(2,1)}, u32[]{:S(2)}, u32[]{:S(2)}) collective-permute-start(bf16[1024,768]{1,0:T(8,128)(2,1)S(1)} %copy-done.6), channel_id=1, source_target_pairs={{0,1},{1,0},{2,3},{3,2},{4,5},{5,4},{6,7},{7,6},{8,9},{9,8},{10,11... | collective-permute-start | bytes 4718600 | tf_op jit(solution)/shard_map/ppermute | solution.py:78
  234.0 35.8 %collective-permute-start.24 = (bf16[1024,768]{1,0:T(8,128)(2,1)}, bf16[1024,768]{1,0:T(8,128)(2,1)}, u32[]{:S(2)}, u32[]{:S(2)}) collective-permute-start(bf16[1024,768]{1,0:T(8,128)(2,1)} %get-tuple-element.151), channel_id=1, source_target_pairs={{0,1},{1,0},{2,3},{3,2},{4,5},{5,4},{6,7},{7,6},{8,9},{9,8},{10,11... | collective-permute-start | bytes 4718600 | tf_op jit(solution)/shard_map/ppermute | solution.py:78
  310.0 21.0 %collective-permute-start.26 = (bf16[16,48,1152]{2,1,0:T(8,128)(2,1)}, bf16[16,48,1152]{2,1,0:T(8,128)(2,1)S(1)}, u32[]{:S(2)}, u32[]{:S(2)}) collective-permute-start(bf16[16,48,1152]{2,1,0:T(8,128)(2,1)} %get-tuple-element.175), channel_id=1, source_target_pairs={{0,2},{2,0},{4,6},{6,4},{8,10},{10,8},{12,14},{14,12},{16,18},{18,... | collective-permute-start | bytes 5308424 | tf_op jit(solution)/shard_map/ppermute | solution.py:78
  310.0 19.8 %collective-permute-start.25 = (bf16[16,48,384]{2,1,0:T(8,128)(2,1)}, bf16[16,48,384]{2,1,0:T(8,128)(2,1)}, u32[]{:S(2)}, u32[]{:S(2)}) collective-permute-start(bf16[16,48,384]{2,1,0:T(8,128)(2,1)} %get-tuple-element.174), channel_id=1, source_target_pairs={{0,2},{2,0},{4,6},{6,4},{8,10},{10,8},{12,14},{14,12},{16,18},{18,... | collective-permute-start | bytes 1769480 | tf_op jit(solution)/shard_map/ppermute | solution.py:78
  332.2 40.3 %collective-permute-start.28 = (bf16[8,48,768]{2,1,0:T(8,128)(2,1)}, bf16[8,48,768]{2,1,0:T(8,128)(2,1)}, u32[]{:S(2)}, u32[]{:S(2)}) collective-permute-start(bf16[8,48,768]{2,1,0:T(8,128)(2,1)} %add_convert_fusion.5), channel_id=1, source_target_pairs={{0,4},{2,6},{4,0},{6,2},{8,12},{10,14},{12,8},{14,10},{16,20},{18,... | collective-permute-start | bytes 1769480 | tf_op jit(solution)/shard_map/ppermute | solution.py:78
  334.4 42.1 %collective-permute-start.27 = (bf16[8,48,768]{2,1,0:T(8,128)(2,1)}, bf16[8,48,768]{2,1,0:T(8,128)(2,1)}, u32[]{:S(2)}, u32[]{:S(2)}) collective-permute-start(bf16[8,48,768]{2,1,0:T(8,128)(2,1)} %pad_maximum_fusion), channel_id=1, source_target_pairs={{0,1},{1,0},{2,3},{3,2},{4,5},{5,4},{6,7},{7,6},{8,9},{9,8},{10,11... | collective-permute-start | bytes 1769480 | tf_op jit(solution)/shard_map/ppermute | solution.py:78
  371.1 33.9 %collective-permute-start.31 = (bf16[16,48,3072]{2,1,0:T(8,128)(2,1)}, bf16[16,48,3072]{2,1,0:T(8,128)(2,1)}, u32[]{:S(2)}, u32[]{:S(2)}) collective-permute-start(bf16[16,48,3072]{2,1,0:T(8,128)(2,1)} %get-tuple-element.189), channel_id=1, source_target_pairs={{0,2},{2,0},{4,6},{6,4},{8,10},{10,8},{12,14},{14,12},{16,18},{18,... | collective-permute-start | bytes 14155784 | tf_op jit(solution)/shard_map/ppermute | solution.py:78
  374.5 13.4 %collective-permute-start.30 = (bf16[4,48,768]{2,1,0:T(8,128)(2,1)}, bf16[4,48,768]{2,1,0:T(8,128)(2,1)S(1)}, u32[]{:S(2)}, u32[]{:S(2)}) collective-permute-start(bf16[4,48,768]{2,1,0:T(8,128)(2,1)} %add_convert_fusion.9), channel_id=1, source_target_pairs={{0,1},{1,0},{2,3},{3,2},{4,5},{5,4},{6,7},{7,6},{8,9},{9,8},{10,11... | collective-permute-start | bytes 884744 | tf_op jit(solution)/shard_map/ppermute | solution.py:78
  394.2 40.4 %collective-permute-start.36 = (bf16[48,1536]{1,0:T(8,128)(2,1)}, bf16[48,1536]{1,0:T(8,128)(2,1)}, u32[]{:S(2)}, u32[]{:S(2)}) collective-permute-start(bf16[48,1536]{1,0:T(8,128)(2,1)} %pad_maximum_fusion.20), channel_id=1, source_target_pairs={{0,24},{2,26},{4,28},{6,30},{8,16},{10,18},{12,20},{14,22},{16,8},... | collective-permute-start | bytes 442376 | tf_op jit(solution)/shard_map/ppermute | solution.py:78
  397.0 36.2 %collective-permute-start.35 = (bf16[48,1536]{1,0:T(8,128)(2,1)}, bf16[48,1536]{1,0:T(8,128)(2,1)}, u32[]{:S(2)}, u32[]{:S(2)}) collective-permute-start(bf16[48,1536]{1,0:T(8,128)(2,1)} %pad_maximum_fusion.19), channel_id=1, source_target_pairs={{0,16},{2,18},{4,20},{6,22},{8,24},{10,26},{12,28},{14,30},{16,0},... | collective-permute-start | bytes 442376 | tf_op jit(solution)/shard_map/ppermute | solution.py:78
  405.1 28.0 %collective-permute-start.34 = (bf16[48,1536]{1,0:T(8,128)(2,1)}, bf16[48,1536]{1,0:T(8,128)(2,1)}, u32[]{:S(2)}, u32[]{:S(2)}) collective-permute-start(bf16[48,1536]{1,0:T(8,128)(2,1)} %pad_maximum_fusion.18), channel_id=1, source_target_pairs={{0,8},{2,10},{4,12},{6,14},{8,0},{10,2},{12,4},{14,6},{16,24},{18,... | collective-permute-start | bytes 442376 | tf_op jit(solution)/shard_map/ppermute | solution.py:78
  408.8 34.2 %collective-permute-start.32 = (bf16[8,48,1536]{2,1,0:T(8,128)(2,1)}, bf16[8,48,1536]{2,1,0:T(8,128)(2,1)}, u32[]{:S(2)}, u32[]{:S(2)}) collective-permute-start(bf16[8,48,1536]{2,1,0:T(8,128)(2,1)} %get-tuple-element.194), channel_id=1, source_target_pairs={{0,1},{1,0},{2,3},{3,2},{4,5},{5,4},{6,7},{7,6},{8,9},{9,8},{10,11... | collective-permute-start | bytes 3538952 | tf_op jit(solution)/shard_map/ppermute | solution.py:78
  408.8 34.2 %collective-permute-start.33 = (bf16[8,48,1536]{2,1,0:T(8,128)(2,1)}, bf16[8,48,1536]{2,1,0:T(8,128)(2,1)}, u32[]{:S(2)}, u32[]{:S(2)}) collective-permute-start(bf16[8,48,1536]{2,1,0:T(8,128)(2,1)} %get-tuple-element.195), channel_id=1, source_target_pairs={{0,4},{2,6},{4,0},{6,2},{8,12},{10,14},{12,8},{14,10},{16,20},{18,... | collective-permute-start | bytes 3538952 | tf_op jit(solution)/shard_map/ppermute | solution.py:78
  433.1 18.8 %collective-permute-start.49 = (f32[2,9216]{1,0:T(2,128)S(1)}, f32[2,9216]{1,0:T(2,128)S(1)}, u32[]{:S(2)}, u32[]{:S(2)}) collective-permute-start(f32[2,9216]{1,0:T(2,128)S(1)} %get-tuple-element.239), channel_id=1, source_target_pairs={{0,2},{2,0},{4,6},{6,4},{8,10},{10,8},{12,14},{14,12},{16,18},{18,... | collective-permute-start | bytes 221192 | tf_op jit(solution)/shard_map/ppermute | solution.py:78
  433.2 18.7 %collective-permute-start.50 = (f32[2,9216]{1,0:T(2,128)S(1)}, f32[2,9216]{1,0:T(2,128)S(1)}, u32[]{:S(2)}, u32[]{:S(2)}) collective-permute-start(f32[2,9216]{1,0:T(2,128)S(1)} %get-tuple-element.239), channel_id=1, source_target_pairs={{0,4},{2,6},{4,0},{6,2},{8,12},{10,14},{12,8},{14,10},{16,20},{18,... | collective-permute-start | bytes 221192 | tf_op jit(solution)/shard_map/ppermute | solution.py:78
  434.5 17.4 %collective-permute-start.51 = (f32[2,9216]{1,0:T(2,128)S(1)}, f32[2,9216]{1,0:T(2,128)S(1)}, u32[]{:S(2)}, u32[]{:S(2)}) collective-permute-start(f32[2,9216]{1,0:T(2,128)S(1)} %get-tuple-element.239), channel_id=1, source_target_pairs={{0,6},{2,4},{4,2},{6,0},{8,14},{10,12},{12,10},{14,8},{16,22},{18,... | collective-permute-start | bytes 221192 | tf_op jit(solution)/shard_map/ppermute | solution.py:78
  452.8 34.4 %collective-permute-start.52 = (f32[2,9216]{1,0:T(2,128)}, f32[2,9216]{1,0:T(2,128)}, u32[]{:S(2)}, u32[]{:S(2)}) collective-permute-start(f32[2,9216]{1,0:T(2,128)} %fusion.47), channel_id=1, source_target_pairs={{0,8},{2,10},{4,12},{6,14},{8,0},{10,2},{12,4},{14,6},{16,24},{18,... | collective-permute-start | bytes 221192 | tf_op jit(solution)/shard_map/ppermute | solution.py:78
  454.6 32.5 %collective-permute-start.53 = (f32[2,9216]{1,0:T(2,128)}, f32[2,9216]{1,0:T(2,128)}, u32[]{:S(2)}, u32[]{:S(2)}) collective-permute-start(f32[2,9216]{1,0:T(2,128)} %fusion.47), channel_id=1, source_target_pairs={{0,16},{2,18},{4,20},{6,22},{8,24},{10,26},{12,28},{14,30},{16,0},... | collective-permute-start | bytes 221192 | tf_op jit(solution)/shard_map/ppermute | solution.py:78
  455.3 31.8 %collective-permute-start.54 = (f32[2,9216]{1,0:T(2,128)}, f32[2,9216]{1,0:T(2,128)}, u32[]{:S(2)}, u32[]{:S(2)}) collective-permute-start(f32[2,9216]{1,0:T(2,128)} %fusion.47), channel_id=1, source_target_pairs={{0,24},{2,26},{4,28},{6,30},{8,16},{10,18},{12,20},{14,22},{16,8},... | collective-permute-start | bytes 221192 | tf_op jit(solution)/shard_map/ppermute | solution.py:78
  470.5 15.7 %collective-permute-start.39 = (bf16[16,48,384]{2,1,0:T(8,128)(2,1)}, bf16[16,48,384]{2,1,0:T(8,128)(2,1)S(1)}, u32[]{:S(2)}, u32[]{:S(2)}) collective-permute-start(bf16[16,48,384]{2,1,0:T(8,128)(2,1)} %get-tuple-element.210), channel_id=1, source_target_pairs={{0,2},{2,0},{4,6},{6,4},{8,10},{10,8},{12,14},{14,12},{16,18},{18,... | collective-permute-start | bytes 1769480 | tf_op jit(solution)/shard_map/ppermute | solution.py:78
  471.4 17.1 %collective-permute-start.40 = (bf16[16,48,1152]{2,1,0:T(8,128)(2,1)}, bf16[16,48,1152]{2,1,0:T(8,128)(2,1)}, u32[]{:S(2)}, u32[]{:S(2)}) collective-permute-start(bf16[16,48,1152]{2,1,0:T(8,128)(2,1)} %get-tuple-element.213), channel_id=1, source_target_pairs={{0,2},{2,0},{4,6},{6,4},{8,10},{10,8},{12,14},{14,12},{16,18},{18,... | collective-permute-start | bytes 5308424 | tf_op jit(solution)/shard_map/ppermute | solution.py:78
  486.3 36.6 %collective-permute-start.56 = (bf16[48,3072]{1,0:T(8,128)(2,1)S(1)}, bf16[48,3072]{1,0:T(8,128)(2,1)S(1)}, u32[]{:S(2)}, u32[]{:S(2)}) collective-permute-start(bf16[48,3072]{1,0:T(8,128)(2,1)S(1)} %pad_maximum_fusion.15), channel_id=1, source_target_pairs={{0,8},{2,10},{4,12},{6,14},{8,0},{10,2},{12,4},{14,6},{16,24},{18,... | collective-permute-start | bytes 884744 | tf_op jit(solution)/shard_map/ppermute | solution.py:78
  489.6 15.5 %collective-permute-start.41 = (bf16[8,48,768]{2,1,0:T(8,128)(2,1)S(1)}, bf16[8,48,768]{2,1,0:T(8,128)(2,1)S(1)}, u32[]{:S(2)}, u32[]{:S(2)}) collective-permute-start(bf16[8,48,768]{2,1,0:T(8,128)(2,1)S(1)} %pad_maximum_fusion.1), channel_id=1, source_target_pairs={{0,1},{1,0},{2,3},{3,2},{4,5},{5,4},{6,7},{7,6},{8,9},{9,8},{10,11... | collective-permute-start | bytes 1769480 | tf_op jit(solution)/shard_map/ppermute | solution.py:78
  491.9 15.8 %collective-permute-start.42 = (bf16[8,48,768]{2,1,0:T(8,128)(2,1)S(1)}, bf16[8,48,768]{2,1,0:T(8,128)(2,1)S(1)}, u32[]{:S(2)}, u32[]{:S(2)}) collective-permute-start(bf16[8,48,768]{2,1,0:T(8,128)(2,1)S(1)} %add_convert_fusion.2), channel_id=1, source_target_pairs={{0,4},{2,6},{4,0},{6,2},{8,12},{10,14},{12,8},{14,10},{16,20},{18,... | collective-permute-start | bytes 1769480 | tf_op jit(solution)/shard_map/ppermute | solution.py:78
  493.5 29.4 %collective-permute-start.57 = (bf16[48,3072]{1,0:T(8,128)(2,1)S(1)}, bf16[48,3072]{1,0:T(8,128)(2,1)S(1)}, u32[]{:S(2)}, u32[]{:S(2)}) collective-permute-start(bf16[48,3072]{1,0:T(8,128)(2,1)S(1)} %pad_maximum_fusion.16), channel_id=1, source_target_pairs={{0,16},{2,18},{4,20},{6,22},{8,24},{10,26},{12,28},{14,30},{16,0},... | collective-permute-start | bytes 884744 | tf_op jit(solution)/shard_map/ppermute | solution.py:78
  506.2 14.9 %collective-permute-start.44 = (bf16[4,48,768]{2,1,0:T(8,128)(2,1)S(1)}, bf16[4,48,768]{2,1,0:T(8,128)(2,1)S(1)}, u32[]{:S(2)}, u32[]{:S(2)}) collective-permute-start(bf16[4,48,768]{2,1,0:T(8,128)(2,1)S(1)} %pad_maximum_fusion.12), channel_id=1, source_target_pairs={{0,4},{2,6},{4,0},{6,2},{8,12},{10,14},{12,8},{14,10},{16,20},{18,... | collective-permute-start | bytes 884744 | tf_op jit(solution)/shard_map/ppermute | solution.py:78
  508.8 13.3 %collective-permute-start.45 = (bf16[4,48,768]{2,1,0:T(8,128)(2,1)S(1)}, bf16[4,48,768]{2,1,0:T(8,128)(2,1)S(1)}, u32[]{:S(2)}, u32[]{:S(2)}) collective-permute-start(bf16[4,48,768]{2,1,0:T(8,128)(2,1)S(1)} %add_convert_fusion.6), channel_id=1, source_target_pairs={{0,1},{1,0},{2,3},{3,2},{4,5},{5,4},{6,7},{7,6},{8,9},{9,8},{10,11... | collective-permute-start | bytes 884744 | tf_op jit(solution)/shard_map/ppermute | solution.py:78
  521.1 34.4 %collective-permute-start.43 = (bf16[1024,768]{1,0:T(8,128)(2,1)}, bf16[1024,768]{1,0:T(8,128)(2,1)S(1)}, u32[]{:S(2)}, u32[]{:S(2)}) collective-permute-start(bf16[1024,768]{1,0:T(8,128)(2,1)} %get-tuple-element.217), channel_id=1, source_target_pairs={{0,1},{1,0},{2,3},{3,2},{4,5},{5,4},{6,7},{7,6},{8,9},{9,8},{10,11... | collective-permute-start | bytes 4718600 | tf_op jit(solution)/shard_map/ppermute | solution.py:78
  536.3 13.5 %collective-permute-start.47 = (bf16[48,1536]{1,0:T(8,128)(2,1)S(1)}, bf16[48,1536]{1,0:T(8,128)(2,1)}, u32[]{:S(2)}, u32[]{:S(2)}) collective-permute-start(bf16[48,1536]{1,0:T(8,128)(2,1)S(1)} %pad_maximum_fusion.22), channel_id=1, source_target_pairs={{0,16},{2,18},{4,20},{6,22},{8,24},{10,26},{12,28},{14,30},{16,0},... | collective-permute-start | bytes 442376 | tf_op jit(solution)/shard_map/ppermute | solution.py:78
  (63 other events, 726.6 us)
Sparse Core Ops, SparseCore 0:
  11.5 103.8 all-gather.2
  118.9 84.4 all-gather.4
  310.7 148.9 reduce-scatter.1

commit v5 on v4

--- a/solution.py
+++ b/solution.py
@@ -1287,7 +1287,7 @@
     totals.send("dp", 4, dp_size // 4, *begun)
     attention_zero.send_core(*begun)
     gradient, token_low = input_gradient(
-        meta, grads, resid_grad, first_pieces[0], begun + waits(routed, zero_middle), True
+        meta, grads, resid_grad, first_pieces[0], begun, True
     )
     totals.land(gradient)
     attention_zero.land_core(gradient)

time: 574 us -> 560 us (0.976)
  waiting for transfers between devices: 105 us -> 97.3 us
    ppermute x59, waiting for transfers between devices: 80.5 us -> 73.1 us  [hop(): return lax.ppermute(member, axis, pairs)]
  transfers between devices with their start and end apart: 62 -> 62, of which waited for: 15 -> 15; matrix products, arithmetic and copies ran while one was open for 15% -> 15% of each run, Pallas kernels for 43% -> 44%
where the time goes in v5:
time: 560 us; the launch traced here: 555 us
  Pallas kernels  286 us (51%)
  waiting for transfers between devices  97.3 us (17%)
  starting transfers between devices  69.9 us (12%)
  other arithmetic  55.7 us (10%)
  local copies, waits for them, and re-layouts  31.2 us (6%)
  between operations  15.1 us (3%)
    pallas_call x16, Pallas kernels, run_kernel(): pl.pallas_call(body, grid_spec=pltpu.PrefetchScalarGridSpec(num_scalar_pr...  286 us
    ppermute x59, waiting for transfers between devices, hop(): return lax.ppermute(member, axis, pairs)  73.1 us
    ppermute x59, starting transfers between devices, hop(): return lax.ppermute(member, axis, pairs)  69.7 us
    all_gather x2, waiting for transfers between devices, __init__(): whole = lax.all_gather(shard, AXES, tiled=True)  24.2 us
  transfers between devices with their start and end apart: 62, of which 15 were waited for; matrix products, arithmetic and copies ran while one was open for 15% of the time, Pallas kernels for 44%

profile of v5, /device:TPU:0, one launch (start us, length us, event | category | flops | bytes accessed | tf_op | source)
XLA Modules:
  0.0 555.1 jit_solution(8818214432289243)
XLA Ops:
  12.2 3.0 collective-permute-start.1
  15.2 2.6 collective-permute-start.2
  41.0 7.2 %collective-permute-done.8 = bf16[4,48,768]{2,1,0:T(8,128)(2,1)S(1)} collective-permute-done((bf16[4,48,768]{2,1,0:T(8,128)(2,1)S(1)}, bf16[4,48,768]{2,1,0:T(8,128)(2,1)S(1)}, u32[]{:S(2)}, u32[]{:S(2)}) %collective-permute-start.8) | collective-permute-done | bytes 294944 | tf_op jit(solution)/shard_map/ppermute | solution.py:78
  53.8 14.1 %collective-permute-done.9.refs_11_.refs_5_.refs_3_ = bf16[8,48,768]{2,1,0:T(8,128)(2,1)S(1)} collective-permute-done((bf16[8,48,768]{2,1,0:T(8,128)(2,1)}, bf16[8,48,768]{2,1,0:T(8,128)(2,1)S(1)}, u32[]{:S(2)}, u32[]{:S(2)}) %collective-permute-start.9) | collective-permute-done | bytes 589856 | tf_op jit(solution)/shard_map/ppermute | solution.py:78
  69.8 2.1 collective-permute-start.12
  71.9 2.0 collective-permute-start.13
  74.8 9.0 %qkv_forward.2.refs_0_ = bf16[3,1024,768]{2,1,0:T(8,128)(2,1)} custom-call(s32[12]{0:T(128)} %pad_add_fusion.meta_ref, bf16[1024,768]{1,0:T(8,128)(2,1)} %constant_dynamic-slice_fusion.2.refs_0_.refs_1_, f32[3,1,768]{2,1,0:T(1,128)} %get-tuple-element.375.refs_1_, bf16[8,48,768]{2,1,0:T(8,128)(2,1)} %copy-done.36, bf16[8,48,768]{2,1,0:T(8,128)(2,1)} %copy-done.39, ...), custom_call_target="tpu_custom_call" | custom-call | flops 28991029248 | bytes 9830400 | tf_op jit(solution)/shard_map/qkv_forward/pallas_call | solution.py:775
  83.8 8.9 %collective-permute-done.13 = bf16[1,48,1536]{2,1,0:T(8,128)(2,1)S(1)} collective-permute-done((bf16[1,48,1536]{2,1,0:T(8,128)(2,1)S(1)}, bf16[1,48,1536]{2,1,0:T(8,128)(2,1)S(1)}, u32[]{:S(2)}, u32[]{:S(2)}) %collective-permute-start.13) | collective-permute-done | bytes 147488 | tf_op jit(solution)/shard_map/ppermute | solution.py:78
  96.4 17.5 %attention_forward.2 = (bf16[1024,768]{1,0:T(8,128)(2,1)}, f32[2,6,8,512]{3,2,1,0:T(8,128)}) custom-call(s32[12]{0:T(128)} %pad_add_fusion.meta_ref, bf16[3,1024,768]{2,1,0:T(8,128)(2,1)} %qkv_forward.2.refs_0_), custom_call_target="tpu_custom_call" | custom-call | flops 51539607552 | bytes 6291456 | tf_op jit(solution)/shard_map/attention_forward/pallas_call | solution.py:775
  115.9 2.0 collective-permute-start.16
  118.2 30.7 %ffn_forward.2 = (bf16[1024,768]{1,0:T(8,128)(2,1)}, bf16[1024,768]{1,0:T(8,128)(2,1)}, f32[1024,128]{1,0:T(8,128)}, bf16[1024,3072]{1,0:T(8,128)(2,1)}, bf16[10...) custom-call(s32[12]{0:T(128)} %pad_add_fusion.meta_ref, ...), custom_call_target="tpu_custom_call" | custom-call | flops 77309411328 | bytes 28311552 | tf_op jit(solution)/shard_map/ffn_forward/pallas_call | solution.py:775
  152.2 9.0 %qkv_forward.3.refs_0_ = bf16[3,1024,768]{2,1,0:T(8,128)(2,1)} custom-call(s32[12]{0:T(128)} %pad_add_fusion.meta_ref, bf16[1024,768]{1,0:T(8,128)(2,1)} %get-tuple-element.150.refs_0_.refs_1_, f32[3,1,768]{2,1,0:T(1,128)} %get-tuple-element.374.refs_1_, bf16[8,48,768]{2,1,0:T(8,128)(2,1)} %constant_dynamic-update-slice_fusion.12.refs_2_.refs_6_, ...), custom_call_target="tpu_custom_call" | custom-call | flops 28991029248 | bytes 9830400 | tf_op jit(solution)/shard_map/qkv_forward/pallas_call | solution.py:775
  161.2 17.6 %attention_forward.3 = (bf16[1024,768]{1,0:T(8,128)(2,1)}, f32[2,6,8,512]{3,2,1,0:T(8,128)}) custom-call(s32[12]{0:T(128)} %pad_add_fusion.meta_ref, bf16[3,1024,768]{2,1,0:T(8,128)(2,1)} %qkv_forward.3.refs_0_), custom_call_target="tpu_custom_call" | custom-call | flops 51539607552 | bytes 6291456 | tf_op jit(solution)/shard_map/attention_forward/pallas_call | solution.py:775
  179.4 24.2 %all-gather.5.cloned.1.call-done = bf16[1536,3072]{1,0:T(8,128)(2,1)} async-done(((bf16[48,3072]{1,0:T(8,128)(2,1)}), bf16[1536,3072]{1,0:T(8,128)(2,1)}) %all-gather.5.cloned.1.call-update) | async-done | bytes 9437200 | tf_op jit(solution)/shard_map/all_gather | solution.py:150
  203.6 30.7 %ffn_forward.3 = (bf16[1024,768]{1,0:T(8,128)(2,1)}, bf16[1024,768]{1,0:T(8,128)(2,1)}, f32[1024,128]{1,0:T(8,128)}, bf16[1024,3072]{1,0:T(8,128)(2,1)}, bf16[10...) custom-call(s32[12]{0:T(128)} %pad_add_fusion.meta_ref, ...), custom_call_target="tpu_custom_call" | custom-call | flops 77309411328 | bytes 28311552 | tf_op jit(solution)/shard_map/ffn_forward/pallas_call | solution.py:775
  234.8 33.8 %ffn_backward.2 = (bf16[1024,768]{1,0:T(8,128)(2,1)}, f32[1024,768]{1,0:T(8,128)}, f32[8,768]{1,0:T(8,128)}, f32[4,1,768]{2,1,0:T(1,128)}, bf16[2,768,3072]{2,1,0:T(8,128)(2,1)}) custom-call(s32[12]{0:T(128)} %pad_add_fusion.meta_ref, bf16[1024,768]{1,0:T(8,128)(2,1)} %constant_dynamic-slice_fusion.1.refs_0_, bf16[1024,768]{1,0:T(8,128)(2,1)} %get-tuple-element.153.refs_1_, ...), custom_call_target="tpu_custom_call" | custom-call | flops 309237645312 | bytes 50331648 | tf_op jit(solution)/shard_map/ffn_backward/pallas_call | solution.py:775
  270.0 8.8 %out_backward.2 = (bf16[1024,768]{1,0:T(8,128)(2,1)}, bf16[16,48,384]{2,1,0:T(8,128)(2,1)}, bf16[16,48,384]{2,1,0:T(8,128)(2,1)}) custom-call(s32[12]{0:T(128)} %pad_add_fusion.meta_ref, bf16[1024,768]{1,0:T(8,128)(2,1)} %get-tuple-element.160.refs_0_, bf16[1024,768]{1,0:T(8,128)(2,1)} %get-tuple-element.149.refs_0_.refs_1_, ...), custom_call_target="tpu_custom_call" | custom-call | flops 38654705664 | bytes 7077888 | tf_op jit(solution)/shard_map/out_backward/pallas_call | solution.py:775
  278.8 22.6 %attention_backward.2 = (bf16[3,1024,768]{2,1,0:T(8,128)(2,1)}, f32[8,768]{1,0:T(8,128)}) custom-call(s32[12]{0:T(128)} %pad_add_fusion.meta_ref, bf16[3,1024,768]{2,1,0:T(8,128)(2,1)} %qkv_forward.3.refs_0_, bf16[1024,768]{1,0:T(8,128)(2,1)} %get-tuple-element.149.refs_0_.refs_1_, bf16[1024,768]{1,0:T(8,128)(2,1)} %get-tuple-element.162.refs_2_, ...), custom_call_target="tpu_custom_call" | custom-call | flops 257698037760 | bytes 12582912 | tf_op jit(solution)/shard_map/attention_backward/pallas_call | solution.py:775
  301.5 8.8 %qkv_grad.2 = (bf16[16,48,1152]{2,1,0:T(8,128)(2,1)}, bf16[16,48,1152]{2,1,0:T(8,128)(2,1)}) custom-call(s32[12]{0:T(128)} %pad_add_fusion.meta_ref, bf16[1024,768]{1,0:T(8,128)(2,1)} %get-tuple-element.150.refs_0_.refs_1_, bf16[3,1024,768]{2,1,0:T(8,128)(2,1)} %get-tuple-element.164.refs_1_.refs_0_), custom_call_target="tpu_custom_call" | custom-call | flops 57982058496 | bytes 9830400 | tf_op jit(solution)/shard_map/qkv_grad/pallas_call | solution.py:775
  310.9 10.5 %input_gradient.2.refs_0_ = f32[1024,768]{1,0:T(8,128)} custom-call(s32[12]{0:T(128)} %pad_add_fusion.meta_ref, bf16[3,1024,768]{2,1,0:T(8,128)(2,1)} %get-tuple-element.164.refs_1_.refs_0_, f32[1024,768]{1,0:T(8,128)} %get-tuple-element.165.refs_1_, bf16[8,48,768]{2,1,0:T(8,128)(2,1)} %constant_dynamic-update-slice_fusion.12.refs_2_.refs_6_, ...), custom_call_target="tpu_custom_call" | custom-call | flops 57982058496 | bytes 14548992 | tf_op jit(solution)/shard_map/input_gradient/pallas_call | solution.py:775
  321.4 3.7 maximum_select_fusion.2
  326.5 3.7 maximum_select_fusion.1
  336.4 35.2 %ffn_backward.3 = (bf16[1024,768]{1,0:T(8,128)(2,1)}, f32[1024,768]{1,0:T(8,128)}, f32[8,768]{1,0:T(8,128)}, f32[4,1,768]{2,1,0:T(1,128)}, bf16[16,48,3072]{2,1,0:T(8,128)(2,1)}, /*index=5*/bf16[16,48,3072]{2,1,0:T(8,128)(2,1)}) custom-call(s32[12]{0:T(128)} %pad_add_fusion.meta_ref, f32[1024,768]{1,0:T(8,128)} %input_gradient.2.refs_0_, ...), custom_call_target="tpu_custom_call" | custom-call | flops 309237645312 | bytes 50331648 | tf_op jit(solution)/shard_map/ffn_backward/pallas_call | solution.py:775
  373.0 2.0 add_convert_fusion.9
  374.9 2.0 collective-permute-start.30
  379.2 9.0 %out_backward.3 = (bf16[1024,768]{1,0:T(8,128)(2,1)}, bf16[16,48,384]{2,1,0:T(8,128)(2,1)}, bf16[16,48,384]{2,1,0:T(8,128)(2,1)}) custom-call(s32[12]{0:T(128)} %pad_add_fusion.meta_ref, bf16[1024,768]{1,0:T(8,128)(2,1)} %get-tuple-element.176.refs_0_, bf16[1024,768]{1,0:T(8,128)(2,1)} %get-tuple-element.135.refs_0_.refs_1_, ...), custom_call_target="tpu_custom_call" | custom-call | flops 38654705664 | bytes 7077888 | tf_op jit(solution)/shard_map/out_backward/pallas_call | solution.py:775
  391.7 2.1 add_bitcast_fusion.2
  394.5 2.3 collective-permute-start.36
  397.5 7.4 %collective-permute-start.35 = (bf16[48,1536]{1,0:T(8,128)(2,1)}, bf16[48,1536]{1,0:T(8,128)(2,1)}, u32[]{:S(2)}, u32[]{:S(2)}) collective-permute-start(bf16[48,1536]{1,0:T(8,128)(2,1)} %pad_maximum_fusion.19), channel_id=1, source_target_pairs={{0,16},{2,18},{4,20},{6,22},{8,24},{10,26},{12,28},{14,30},{16,0},... | collective-permute-start | bytes 442376 | tf_op jit(solution)/shard_map/ppermute | solution.py:78
  405.6 3.7 add_convert_fusion
  409.9 22.7 %attention_backward.3 = (bf16[3,1024,768]{2,1,0:T(8,128)(2,1)}, f32[8,768]{1,0:T(8,128)}) custom-call(s32[12]{0:T(128)} %pad_add_fusion.meta_ref, bf16[3,1024,768]{2,1,0:T(8,128)(2,1)} %qkv_forward.2.refs_0_, bf16[1024,768]{1,0:T(8,128)(2,1)} %get-tuple-element.135.refs_0_.refs_1_, bf16[1024,768]{1,0:T(8,128)(2,1)} %get-tuple-element.182.refs_2_, ...), custom_call_target="tpu_custom_call" | custom-call | flops 257698037760 | bytes 12582912 | tf_op jit(solution)/shard_map/attention_backward/pallas_call | solution.py:775
  436.7 4.1 collective-permute-done.33.refs_3_
  440.8 3.6 collective-permute-done.32.refs_2_
  444.4 8.8 %qkv_grad.3 = (bf16[16,48,1152]{2,1,0:T(8,128)(2,1)}, bf16[16,48,1152]{2,1,0:T(8,128)(2,1)}) custom-call(s32[12]{0:T(128)} %pad_add_fusion.meta_ref, bf16[1024,768]{1,0:T(8,128)(2,1)} %constant_dynamic-slice_fusion.2.refs_0_.refs_1_, bf16[3,1024,768]{2,1,0:T(8,128)(2,1)} %get-tuple-element.190.refs_1_.refs_0_, ...), custom_call_target="tpu_custom_call" | custom-call | flops 57982058496 | bytes 9830400 | tf_op jit(solution)/shard_map/qkv_grad/pallas_call | solution.py:775
  454.1 1.8 collective-permute-start.50
  458.5 2.9 add_convert_fusion.3
  462.7 11.2 %input_gradient.3 = (f32[1024,768]{1,0:T(8,128)}, bf16[1024,768]{1,0:T(8,128)(2,1)}) custom-call(s32[12]{0:T(128)} %pad_add_fusion.meta_ref, bf16[3,1024,768]{2,1,0:T(8,128)(2,1)} %get-tuple-element.190.refs_1_.refs_0_, f32[1024,768]{1,0:T(8,128)} %get-tuple-element.191.refs_1_, bf16[8,48,768]{2,1,0:T(8,128)(2,1)} %copy-done.36, ...), custom_call_target="tpu_custom_call" | custom-call | flops 57982058496 | bytes 14548992 | tf_op jit(solution)/shard_map/input_gradient/pallas_call | solution.py:775
  474.9 1.8 fusion.6
  476.7 2.0 fusion.7
  483.0 1.9 collective-permute-start.57
  484.9 10.2 %collective-permute-done.39 = bf16[8,48,768]{2,1,0:T(8,128)(2,1)S(1)} collective-permute-done((bf16[8,48,768]{2,1,0:T(8,128)(2,1)S(1)}, bf16[8,48,768]{2,1,0:T(8,128)(2,1)S(1)}, u32[]{:S(2)}, u32[]{:S(2)}) %collective-permute-start.39) | collective-permute-done | bytes 589856 | tf_op jit(solution)/shard_map/ppermute | solution.py:78
  498.8 7.0 %collective-permute-done.53 = f32[2,9216]{1,0:T(2,128)S(1)} collective-permute-done((f32[2,9216]{1,0:T(2,128)S(1)}, f32[2,9216]{1,0:T(2,128)S(1)}, u32[]{:S(2)}, u32[]{:S(2)}) %collective-permute-start.53) | collective-permute-done | bytes 73760 | tf_op jit(solution)/shard_map/ppermute | solution.py:78
  505.9 2.1 collective-permute-start.58
  510.9 3.6 collective-permute-done.58
  515.5 5.5 collective-permute-start.44
  528.6 6.1 %collective-permute-done.45 = bf16[48,1536]{1,0:T(8,128)(2,1)} collective-permute-done((bf16[48,1536]{1,0:T(8,128)(2,1)}, bf16[48,1536]{1,0:T(8,128)(2,1)}, u32[]{:S(2)}, u32[]{:S(2)}) %collective-permute-start.45) | collective-permute-done | bytes 147488 | tf_op jit(solution)/shard_map/ppermute | solution.py:78
  537.3 4.6 collective-permute-done.41
  542.2 3.1 maximum_select_fusion
  (317 shorter events, 100.5 us)
Async XLA Ops:
  7.2 111.0 %all-gather.3.cloned.1.call-start = ((), (), s32[]{:S(2)}) async-start(), calls=%async_computation.1 | async-start | bytes 9732096 | tf_op jit(solution)/shard_map/all_gather | solution.py:150
  9.3 194.2 %all-gather.5.cloned.1.call-start = ((), (), s32[]{:S(2)}) async-start(), calls=%async_computation.2 | async-start | bytes 9732096 | tf_op jit(solution)/shard_map/all_gather | solution.py:150
  12.2 20.8 %collective-permute-start.1 = (bf16[1,48,1536]{2,1,0:T(8,128)(2,1)}, bf16[1,48,1536]{2,1,0:T(8,128)(2,1)}, u32[]{:S(2)}, u32[]{:S(2)}) collective-permute-start(bf16[1,48,1536]{2,1,0:T(8,128)(2,1)} %maximum_bitcast_fusion.2), channel_id=1, source_target_pairs={{0,8},{2,10},{4,12},{6,14},{8,0},{10,2},{12,4},{14,6},{16,24},{18,... | collective-permute-start | bytes 442376 | tf_op jit(solution)/shard_map/ppermute | solution.py:78
  15.2 19.4 %collective-permute-start.2 = (bf16[1,48,1536]{2,1,0:T(8,128)(2,1)}, bf16[1,48,1536]{2,1,0:T(8,128)(2,1)}, u32[]{:S(2)}, u32[]{:S(2)}) collective-permute-start(bf16[1,48,1536]{2,1,0:T(8,128)(2,1)} %maximum_bitcast_fusion.2), channel_id=1, source_target_pairs={{0,16},{2,18},{4,20},{6,22},{8,24},{10,26},{12,28},{14,30},{16,0},... | collective-permute-start | bytes 442376 | tf_op jit(solution)/shard_map/ppermute | solution.py:78
  17.8 18.4 %collective-permute-start.3 = (bf16[1,48,1536]{2,1,0:T(8,128)(2,1)}, bf16[1,48,1536]{2,1,0:T(8,128)(2,1)}, u32[]{:S(2)}, u32[]{:S(2)}) collective-permute-start(bf16[1,48,1536]{2,1,0:T(8,128)(2,1)} %maximum_bitcast_fusion.2), channel_id=1, source_target_pairs={{0,24},{2,26},{4,28},{6,30},{8,16},{10,18},{12,20},{14,22},{16,8},... | collective-permute-start | bytes 442376 | tf_op jit(solution)/shard_map/ppermute | solution.py:78
  22.9 522.4 %reduce-scatter.2.cloned.1.call-start = ((), (), s32[]{:S(2)}) async-start(), calls=%async_computation.3 | async-start | bytes 9732096 | tf_op jit(solution)/shard_map/reduce_scatter | solution.py:235
  48.9 19.0 %collective-permute-start.9 = (bf16[8,48,768]{2,1,0:T(8,128)(2,1)}, bf16[8,48,768]{2,1,0:T(8,128)(2,1)S(1)}, u32[]{:S(2)}, u32[]{:S(2)}) collective-permute-start(bf16[8,48,768]{2,1,0:T(8,128)(2,1)} %constant_dynamic-update-slice_fusion.7.refs_10_.refs_4_.refs_2_), channel_id=1, source_target_pairs={{0,4},{2,6},{4,0},{6,2},{8,12},{10,14},{12,8},{14,10},{16,20},{18,... | collective-permute-start | bytes 1769480 | tf_op jit(solution)/shard_map/ppermute | solution.py:78
  51.8 16.2 %collective-permute-start.5 = (bf16[8,48,768]{2,1,0:T(8,128)(2,1)S(1)}, bf16[8,48,768]{2,1,0:T(8,128)(2,1)S(1)}, u32[]{:S(2)}, u32[]{:S(2)}) collective-permute-start(bf16[8,48,768]{2,1,0:T(8,128)(2,1)S(1)} %constant_dynamic-update-slice_fusion.2.refs_2_.refs_6_), channel_id=1, source_target_pairs={{0,1},{1,0},{2,3},{3,2},{4,5},{5,4},{6,7},{7,6},{8,9},{9,8},{10,11... | collective-permute-start | bytes 1769480 | tf_op jit(solution)/shard_map/ppermute | solution.py:78
  53.2 18.7 %collective-permute-start.10 = (bf16[8,48,768]{2,1,0:T(8,128)(2,1)}, bf16[8,48,768]{2,1,0:T(8,128)(2,1)S(1)}, u32[]{:S(2)}, u32[]{:S(2)}) collective-permute-start(bf16[8,48,768]{2,1,0:T(8,128)(2,1)} %constant_dynamic-update-slice_fusion.7.refs_10_.refs_4_.refs_2_), channel_id=1, source_target_pairs={{0,2},{2,0},{4,6},{6,4},{8,10},{10,8},{12,14},{14,12},{16,18},{18,... | collective-permute-start | bytes 1769480 | tf_op jit(solution)/shard_map/ppermute | solution.py:78
  53.3 20.6 %collective-permute-start.6 = (bf16[8,48,768]{2,1,0:T(8,128)(2,1)S(1)}, bf16[8,48,768]{2,1,0:T(8,128)(2,1)S(1)}, u32[]{:S(2)}, u32[]{:S(2)}) collective-permute-start(bf16[8,48,768]{2,1,0:T(8,128)(2,1)S(1)} %constant_dynamic-update-slice_fusion.2.refs_2_.refs_6_), channel_id=1, source_target_pairs={{0,2},{2,0},{4,6},{6,4},{8,10},{10,8},{12,14},{14,12},{16,18},{18,... | collective-permute-start | bytes 1769480 | tf_op jit(solution)/shard_map/ppermute | solution.py:78
  69.8 13.9 %collective-permute-start.12 = (bf16[1,48,1536]{2,1,0:T(8,128)(2,1)S(1)}, bf16[1,48,1536]{2,1,0:T(8,128)(2,1)S(1)}, u32[]{:S(2)}, u32[]{:S(2)}) collective-permute-start(bf16[1,48,1536]{2,1,0:T(8,128)(2,1)S(1)} %maximum_bitcast_fusion.3), channel_id=1, source_target_pairs={{0,8},{2,10},{4,12},{6,14},{8,0},{10,2},{12,4},{14,6},{16,24},{18,... | collective-permute-start | bytes 442376 | tf_op jit(solution)/shard_map/ppermute | solution.py:78
  71.9 20.7 %collective-permute-start.13 = (bf16[1,48,1536]{2,1,0:T(8,128)(2,1)S(1)}, bf16[1,48,1536]{2,1,0:T(8,128)(2,1)S(1)}, u32[]{:S(2)}, u32[]{:S(2)}) collective-permute-start(bf16[1,48,1536]{2,1,0:T(8,128)(2,1)S(1)} %maximum_bitcast_fusion.3), channel_id=1, source_target_pairs={{0,16},{2,18},{4,20},{6,22},{8,24},{10,26},{12,28},{14,30},{16,0},... | collective-permute-start | bytes 442376 | tf_op jit(solution)/shard_map/ppermute | solution.py:78
  73.9 18.7 %collective-permute-start.14 = (bf16[1,48,1536]{2,1,0:T(8,128)(2,1)S(1)}, bf16[1,48,1536]{2,1,0:T(8,128)(2,1)S(1)}, u32[]{:S(2)}, u32[]{:S(2)}) collective-permute-start(bf16[1,48,1536]{2,1,0:T(8,128)(2,1)S(1)} %maximum_bitcast_fusion.3), channel_id=1, source_target_pairs={{0,24},{2,26},{4,28},{6,30},{8,16},{10,18},{12,20},{14,22},{16,8},... | collective-permute-start | bytes 442376 | tf_op jit(solution)/shard_map/ppermute | solution.py:78
  94.8 19.1 %collective-permute-start.19 = (bf16[4,48,768]{2,1,0:T(8,128)(2,1)S(1)}, bf16[4,48,768]{2,1,0:T(8,128)(2,1)S(1)}, u32[]{:S(2)}, u32[]{:S(2)}) collective-permute-start(bf16[4,48,768]{2,1,0:T(8,128)(2,1)S(1)} %pad_maximum_fusion.9), channel_id=1, source_target_pairs={{0,1},{1,0},{2,3},{3,2},{4,5},{5,4},{6,7},{7,6},{8,9},{9,8},{10,11... | collective-permute-start | bytes 884744 | tf_op jit(solution)/shard_map/ppermute | solution.py:78
  94.9 20.3 %collective-permute-start.15 = (bf16[4,48,768]{2,1,0:T(8,128)(2,1)S(1)}, bf16[4,48,768]{2,1,0:T(8,128)(2,1)S(1)}, u32[]{:S(2)}, u32[]{:S(2)}) collective-permute-start(bf16[4,48,768]{2,1,0:T(8,128)(2,1)S(1)} %pad_maximum_fusion.8), channel_id=1, source_target_pairs={{0,4},{2,6},{4,0},{6,2},{8,12},{10,14},{12,8},{14,10},{16,20},{18,... | collective-permute-start | bytes 884744 | tf_op jit(solution)/shard_map/ppermute | solution.py:78
  114.6 34.3 %collective-permute-start.20 = (bf16[8,48,768]{2,1,0:T(8,128)(2,1)}, bf16[8,48,768]{2,1,0:T(8,128)(2,1)}, u32[]{:S(2)}, u32[]{:S(2)}) collective-permute-start(bf16[8,48,768]{2,1,0:T(8,128)(2,1)} %constant_dynamic-update-slice_fusion.17.refs_10_.refs_4_.refs_2_), channel_id=1, source_target_pairs={{0,4},{2,6},{4,0},{6,2},{8,12},{10,14},{12,8},{14,10},{16,20},{18,... | collective-permute-start | bytes 1769480 | tf_op jit(solution)/shard_map/ppermute | solution.py:78
  115.2 36.2 %collective-permute-start.21 = (bf16[8,48,768]{2,1,0:T(8,128)(2,1)}, bf16[8,48,768]{2,1,0:T(8,128)(2,1)}, u32[]{:S(2)}, u32[]{:S(2)}) collective-permute-start(bf16[8,48,768]{2,1,0:T(8,128)(2,1)} %constant_dynamic-update-slice_fusion.17.refs_10_.refs_4_.refs_2_), channel_id=1, source_target_pairs={{0,2},{2,0},{4,6},{6,4},{8,10},{10,8},{12,14},{14,12},{16,18},{18,... | collective-permute-start | bytes 1769480 | tf_op jit(solution)/shard_map/ppermute | solution.py:78
  115.9 33.3 %collective-permute-start.16 = (bf16[8,48,768]{2,1,0:T(8,128)(2,1)}, bf16[8,48,768]{2,1,0:T(8,128)(2,1)}, u32[]{:S(2)}, u32[]{:S(2)}) collective-permute-start(bf16[8,48,768]{2,1,0:T(8,128)(2,1)} %constant_dynamic-update-slice_fusion.12.refs_2_.refs_6_), channel_id=1, source_target_pairs={{0,1},{1,0},{2,3},{3,2},{4,5},{5,4},{6,7},{7,6},{8,9},{9,8},{10,11... | collective-permute-start | bytes 1769480 | tf_op jit(solution)/shard_map/ppermute | solution.py:78
  118.0 33.4 %collective-permute-start.17 = (bf16[8,48,768]{2,1,0:T(8,128)(2,1)}, bf16[8,48,768]{2,1,0:T(8,128)(2,1)}, u32[]{:S(2)}, u32[]{:S(2)}) collective-permute-start(bf16[8,48,768]{2,1,0:T(8,128)(2,1)} %constant_dynamic-update-slice_fusion.12.refs_2_.refs_6_), channel_id=1, source_target_pairs={{0,2},{2,0},{4,6},{6,4},{8,10},{10,8},{12,14},{14,12},{16,18},{18,... | collective-permute-start | bytes 1769480 | tf_op jit(solution)/shard_map/ppermute | solution.py:78
  178.8 55.9 %collective-permute-start.23 = (bf16[1024,768]{1,0:T(8,128)(2,1)S(1)}, bf16[1024,768]{1,0:T(8,128)(2,1)}, u32[]{:S(2)}, u32[]{:S(2)}) collective-permute-start(bf16[1024,768]{1,0:T(8,128)(2,1)S(1)} %copy-done.6), channel_id=1, source_target_pairs={{0,1},{1,0},{2,3},{3,2},{4,5},{5,4},{6,7},{7,6},{8,9},{9,8},{10,11... | collective-permute-start | bytes 4718600 | tf_op jit(solution)/shard_map/ppermute | solution.py:78
  234.3 35.8 %collective-permute-start.24 = (bf16[1024,768]{1,0:T(8,128)(2,1)}, bf16[1024,768]{1,0:T(8,128)(2,1)}, u32[]{:S(2)}, u32[]{:S(2)}) collective-permute-start(bf16[1024,768]{1,0:T(8,128)(2,1)} %get-tuple-element.151), channel_id=1, source_target_pairs={{0,1},{1,0},{2,3},{3,2},{4,5},{5,4},{6,7},{7,6},{8,9},{9,8},{10,11... | collective-permute-start | bytes 4718600 | tf_op jit(solution)/shard_map/ppermute | solution.py:78
  310.3 21.0 %collective-permute-start.26 = (bf16[16,48,1152]{2,1,0:T(8,128)(2,1)}, bf16[16,48,1152]{2,1,0:T(8,128)(2,1)S(1)}, u32[]{:S(2)}, u32[]{:S(2)}) collective-permute-start(bf16[16,48,1152]{2,1,0:T(8,128)(2,1)} %get-tuple-element.175), channel_id=1, source_target_pairs={{0,2},{2,0},{4,6},{6,4},{8,10},{10,8},{12,14},{14,12},{16,18},{18,... | collective-permute-start | bytes 5308424 | tf_op jit(solution)/shard_map/ppermute | solution.py:78
  310.4 19.8 %collective-permute-start.25 = (bf16[16,48,384]{2,1,0:T(8,128)(2,1)}, bf16[16,48,384]{2,1,0:T(8,128)(2,1)}, u32[]{:S(2)}, u32[]{:S(2)}) collective-permute-start(bf16[16,48,384]{2,1,0:T(8,128)(2,1)} %get-tuple-element.174), channel_id=1, source_target_pairs={{0,2},{2,0},{4,6},{6,4},{8,10},{10,8},{12,14},{14,12},{16,18},{18,... | collective-permute-start | bytes 1769480 | tf_op jit(solution)/shard_map/ppermute | solution.py:78
  332.5 40.4 %collective-permute-start.28 = (bf16[8,48,768]{2,1,0:T(8,128)(2,1)}, bf16[8,48,768]{2,1,0:T(8,128)(2,1)}, u32[]{:S(2)}, u32[]{:S(2)}) collective-permute-start(bf16[8,48,768]{2,1,0:T(8,128)(2,1)} %add_convert_fusion.5), channel_id=1, source_target_pairs={{0,4},{2,6},{4,0},{6,2},{8,12},{10,14},{12,8},{14,10},{16,20},{18,... | collective-permute-start | bytes 1769480 | tf_op jit(solution)/shard_map/ppermute | solution.py:78
  334.8 42.2 %collective-permute-start.27 = (bf16[8,48,768]{2,1,0:T(8,128)(2,1)}, bf16[8,48,768]{2,1,0:T(8,128)(2,1)}, u32[]{:S(2)}, u32[]{:S(2)}) collective-permute-start(bf16[8,48,768]{2,1,0:T(8,128)(2,1)} %pad_maximum_fusion), channel_id=1, source_target_pairs={{0,1},{1,0},{2,3},{3,2},{4,5},{5,4},{6,7},{7,6},{8,9},{9,8},{10,11... | collective-permute-start | bytes 1769480 | tf_op jit(solution)/shard_map/ppermute | solution.py:78
  371.5 34.0 %collective-permute-start.31 = (bf16[16,48,3072]{2,1,0:T(8,128)(2,1)}, bf16[16,48,3072]{2,1,0:T(8,128)(2,1)}, u32[]{:S(2)}, u32[]{:S(2)}) collective-permute-start(bf16[16,48,3072]{2,1,0:T(8,128)(2,1)} %get-tuple-element.189), channel_id=1, source_target_pairs={{0,2},{2,0},{4,6},{6,4},{8,10},{10,8},{12,14},{14,12},{16,18},{18,... | collective-permute-start | bytes 14155784 | tf_op jit(solution)/shard_map/ppermute | solution.py:78
  374.9 13.3 %collective-permute-start.30 = (bf16[4,48,768]{2,1,0:T(8,128)(2,1)}, bf16[4,48,768]{2,1,0:T(8,128)(2,1)S(1)}, u32[]{:S(2)}, u32[]{:S(2)}) collective-permute-start(bf16[4,48,768]{2,1,0:T(8,128)(2,1)} %add_convert_fusion.9), channel_id=1, source_target_pairs={{0,1},{1,0},{2,3},{3,2},{4,5},{5,4},{6,7},{7,6},{8,9},{9,8},{10,11... | collective-permute-start | bytes 884744 | tf_op jit(solution)/shard_map/ppermute | solution.py:78
  394.5 40.5 %collective-permute-start.36 = (bf16[48,1536]{1,0:T(8,128)(2,1)}, bf16[48,1536]{1,0:T(8,128)(2,1)}, u32[]{:S(2)}, u32[]{:S(2)}) collective-permute-start(bf16[48,1536]{1,0:T(8,128)(2,1)} %pad_maximum_fusion.20), channel_id=1, source_target_pairs={{0,24},{2,26},{4,28},{6,30},{8,16},{10,18},{12,20},{14,22},{16,8},... | collective-permute-start | bytes 442376 | tf_op jit(solution)/shard_map/ppermute | solution.py:78
  397.5 36.2 %collective-permute-start.35 = (bf16[48,1536]{1,0:T(8,128)(2,1)}, bf16[48,1536]{1,0:T(8,128)(2,1)}, u32[]{:S(2)}, u32[]{:S(2)}) collective-permute-start(bf16[48,1536]{1,0:T(8,128)(2,1)} %pad_maximum_fusion.19), channel_id=1, source_target_pairs={{0,16},{2,18},{4,20},{6,22},{8,24},{10,26},{12,28},{14,30},{16,0},... | collective-permute-start | bytes 442376 | tf_op jit(solution)/shard_map/ppermute | solution.py:78
  405.5 28.0 %collective-permute-start.34 = (bf16[48,1536]{1,0:T(8,128)(2,1)}, bf16[48,1536]{1,0:T(8,128)(2,1)}, u32[]{:S(2)}, u32[]{:S(2)}) collective-permute-start(bf16[48,1536]{1,0:T(8,128)(2,1)} %pad_maximum_fusion.18), channel_id=1, source_target_pairs={{0,8},{2,10},{4,12},{6,14},{8,0},{10,2},{12,4},{14,6},{16,24},{18,... | collective-permute-start | bytes 442376 | tf_op jit(solution)/shard_map/ppermute | solution.py:78
  409.3 31.5 %collective-permute-start.33 = (bf16[8,48,1536]{2,1,0:T(8,128)(2,1)}, bf16[8,48,1536]{2,1,0:T(8,128)(2,1)}, u32[]{:S(2)}, u32[]{:S(2)}) collective-permute-start(bf16[8,48,1536]{2,1,0:T(8,128)(2,1)} %get-tuple-element.195), channel_id=1, source_target_pairs={{0,4},{2,6},{4,0},{6,2},{8,12},{10,14},{12,8},{14,10},{16,20},{18,... | collective-permute-start | bytes 3538952 | tf_op jit(solution)/shard_map/ppermute | solution.py:78
  409.9 34.5 %collective-permute-start.32 = (bf16[8,48,1536]{2,1,0:T(8,128)(2,1)}, bf16[8,48,1536]{2,1,0:T(8,128)(2,1)}, u32[]{:S(2)}, u32[]{:S(2)}) collective-permute-start(bf16[8,48,1536]{2,1,0:T(8,128)(2,1)} %get-tuple-element.194), channel_id=1, source_target_pairs={{0,1},{1,0},{2,3},{3,2},{4,5},{5,4},{6,7},{7,6},{8,9},{9,8},{10,11... | collective-permute-start | bytes 3538952 | tf_op jit(solution)/shard_map/ppermute | solution.py:78
  433.6 19.6 %collective-permute-start.47 = (f32[2,9216]{1,0:T(2,128)S(1)}, f32[2,9216]{1,0:T(2,128)S(1)}, u32[]{:S(2)}, u32[]{:S(2)}) collective-permute-start(f32[2,9216]{1,0:T(2,128)S(1)} %get-tuple-element.235), channel_id=1, source_target_pairs={{0,2},{2,0},{4,6},{6,4},{8,10},{10,8},{12,14},{14,12},{16,18},{18,... | collective-permute-start | bytes 221192 | tf_op jit(solution)/shard_map/ppermute | solution.py:78
  433.6 19.6 %collective-permute-start.48 = (f32[2,9216]{1,0:T(2,128)S(1)}, f32[2,9216]{1,0:T(2,128)S(1)}, u32[]{:S(2)}, u32[]{:S(2)}) collective-permute-start(f32[2,9216]{1,0:T(2,128)S(1)} %get-tuple-element.235), channel_id=1, source_target_pairs={{0,4},{2,6},{4,0},{6,2},{8,12},{10,14},{12,8},{14,10},{16,20},{18,... | collective-permute-start | bytes 221192 | tf_op jit(solution)/shard_map/ppermute | solution.py:78
  435.0 18.2 %collective-permute-start.49 = (f32[2,9216]{1,0:T(2,128)S(1)}, f32[2,9216]{1,0:T(2,128)S(1)}, u32[]{:S(2)}, u32[]{:S(2)}) collective-permute-start(f32[2,9216]{1,0:T(2,128)S(1)} %get-tuple-element.235), channel_id=1, source_target_pairs={{0,6},{2,4},{4,2},{6,0},{8,14},{10,12},{12,10},{14,8},{16,22},{18,... | collective-permute-start | bytes 221192 | tf_op jit(solution)/shard_map/ppermute | solution.py:78
  454.1 19.9 %collective-permute-start.50 = (f32[2,9216]{1,0:T(2,128)}, f32[2,9216]{1,0:T(2,128)S(1)}, u32[]{:S(2)}, u32[]{:S(2)}) collective-permute-start(f32[2,9216]{1,0:T(2,128)} %fusion.47), channel_id=1, source_target_pairs={{0,8},{2,10},{4,12},{6,14},{8,0},{10,2},{12,4},{14,6},{16,24},{18,... | collective-permute-start | bytes 221192 | tf_op jit(solution)/shard_map/ppermute | solution.py:78
  455.9 18.2 %collective-permute-start.51 = (f32[2,9216]{1,0:T(2,128)}, f32[2,9216]{1,0:T(2,128)S(1)}, u32[]{:S(2)}, u32[]{:S(2)}) collective-permute-start(f32[2,9216]{1,0:T(2,128)} %fusion.47), channel_id=1, source_target_pairs={{0,16},{2,18},{4,20},{6,22},{8,24},{10,26},{12,28},{14,30},{16,0},... | collective-permute-start | bytes 221192 | tf_op jit(solution)/shard_map/ppermute | solution.py:78
  456.8 17.7 %collective-permute-start.52 = (f32[2,9216]{1,0:T(2,128)}, f32[2,9216]{1,0:T(2,128)S(1)}, u32[]{:S(2)}, u32[]{:S(2)}) collective-permute-start(f32[2,9216]{1,0:T(2,128)} %fusion.47), channel_id=1, source_target_pairs={{0,24},{2,26},{4,28},{6,30},{8,16},{10,18},{12,20},{14,22},{16,8},... | collective-permute-start | bytes 221192 | tf_op jit(solution)/shard_map/ppermute | solution.py:78
  461.4 13.5 %collective-permute-start.54 = (bf16[4,48,1536]{2,1,0:T(8,128)(2,1)}, bf16[4,48,1536]{2,1,0:T(8,128)(2,1)}, u32[]{:S(2)}, u32[]{:S(2)}) collective-permute-start(bf16[4,48,1536]{2,1,0:T(8,128)(2,1)} %get-tuple-element.246), channel_id=1, source_target_pairs={{0,4},{2,6},{4,0},{6,2},{8,12},{10,14},{12,8},{14,10},{16,20},{18,... | collective-permute-start | bytes 1769480 | tf_op jit(solution)/shard_map/ppermute | solution.py:78
  478.7 31.4 %collective-permute-start.56 = (bf16[48,3072]{1,0:T(8,128)(2,1)S(1)}, bf16[48,3072]{1,0:T(8,128)(2,1)S(1)}, u32[]{:S(2)}, u32[]{:S(2)}) collective-permute-start(bf16[48,3072]{1,0:T(8,128)(2,1)S(1)} %pad_maximum_fusion.15), channel_id=1, source_target_pairs={{0,8},{2,10},{4,12},{6,14},{8,0},{10,2},{12,4},{14,6},{16,24},{18,... | collective-permute-start | bytes 884744 | tf_op jit(solution)/shard_map/ppermute | solution.py:78
  480.0 15.1 %collective-permute-start.39 = (bf16[8,48,768]{2,1,0:T(8,128)(2,1)S(1)}, bf16[8,48,768]{2,1,0:T(8,128)(2,1)S(1)}, u32[]{:S(2)}, u32[]{:S(2)}) collective-permute-start(bf16[8,48,768]{2,1,0:T(8,128)(2,1)S(1)} %pad_maximum_fusion.1), channel_id=1, source_target_pairs={{0,1},{1,0},{2,3},{3,2},{4,5},{5,4},{6,7},{7,6},{8,9},{9,8},{10,11... | collective-permute-start | bytes 1769480 | tf_op jit(solution)/shard_map/ppermute | solution.py:78
  481.8 14.8 %collective-permute-start.40 = (bf16[8,48,768]{2,1,0:T(8,128)(2,1)S(1)}, bf16[8,48,768]{2,1,0:T(8,128)(2,1)S(1)}, u32[]{:S(2)}, u32[]{:S(2)}) collective-permute-start(bf16[8,48,768]{2,1,0:T(8,128)(2,1)S(1)} %add_convert_fusion.4), channel_id=1, source_target_pairs={{0,4},{2,6},{4,0},{6,2},{8,12},{10,14},{12,8},{14,10},{16,20},{18,... | collective-permute-start | bytes 1769480 | tf_op jit(solution)/shard_map/ppermute | solution.py:78
  483.0 27.1 %collective-permute-start.57 = (bf16[48,3072]{1,0:T(8,128)(2,1)S(1)}, bf16[48,3072]{1,0:T(8,128)(2,1)S(1)}, u32[]{:S(2)}, u32[]{:S(2)}) collective-permute-start(bf16[48,3072]{1,0:T(8,128)(2,1)S(1)} %pad_maximum_fusion.16), channel_id=1, source_target_pairs={{0,16},{2,18},{4,20},{6,22},{8,24},{10,26},{12,28},{14,30},{16,0},... | collective-permute-start | bytes 884744 | tf_op jit(solution)/shard_map/ppermute | solution.py:78
  495.3 12.7 %collective-permute-start.42 = (bf16[4,48,768]{2,1,0:T(8,128)(2,1)S(1)}, bf16[4,48,768]{2,1,0:T(8,128)(2,1)S(1)}, u32[]{:S(2)}, u32[]{:S(2)}) collective-permute-start(bf16[4,48,768]{2,1,0:T(8,128)(2,1)S(1)} %pad_maximum_fusion.12), channel_id=1, source_target_pairs={{0,4},{2,6},{4,0},{6,2},{8,12},{10,14},{12,8},{14,10},{16,20},{18,... | collective-permute-start | bytes 884744 | tf_op jit(solution)/shard_map/ppermute | solution.py:78
  496.7 12.6 %collective-permute-start.43 = (bf16[4,48,768]{2,1,0:T(8,128)(2,1)S(1)}, bf16[4,48,768]{2,1,0:T(8,128)(2,1)S(1)}, u32[]{:S(2)}, u32[]{:S(2)}) collective-permute-start(bf16[4,48,768]{2,1,0:T(8,128)(2,1)S(1)} %add_convert_fusion.6), channel_id=1, source_target_pairs={{0,1},{1,0},{2,3},{3,2},{4,5},{5,4},{6,7},{7,6},{8,9},{9,8},{10,11... | collective-permute-start | bytes 884744 | tf_op jit(solution)/shard_map/ppermute | solution.py:78
  508.0 33.9 %collective-permute-start.41 = (bf16[1024,768]{1,0:T(8,128)(2,1)}, bf16[1024,768]{1,0:T(8,128)(2,1)S(1)}, u32[]{:S(2)}, u32[]{:S(2)}) collective-permute-start(bf16[1024,768]{1,0:T(8,128)(2,1)} %get-tuple-element.213), channel_id=1, source_target_pairs={{0,1},{1,0},{2,3},{3,2},{4,5},{5,4},{6,7},{7,6},{8,9},{9,8},{10,11... | collective-permute-start | bytes 4718600 | tf_op jit(solution)/shard_map/ppermute | solution.py:78
  515.5 13.1 %collective-permute-start.44 = (bf16[48,1536]{1,0:T(8,128)(2,1)}, bf16[48,1536]{1,0:T(8,128)(2,1)}, u32[]{:S(2)}, u32[]{:S(2)}) collective-permute-start(bf16[48,1536]{1,0:T(8,128)(2,1)} %pad_maximum_fusion.21), channel_id=1, source_target_pairs={{0,8},{2,10},{4,12},{6,14},{8,0},{10,2},{12,4},{14,6},{16,24},{18,... | collective-permute-start | bytes 442376 | tf_op jit(solution)/shard_map/ppermute | solution.py:78
  521.7 13.0 %collective-permute-start.45 = (bf16[48,1536]{1,0:T(8,128)(2,1)}, bf16[48,1536]{1,0:T(8,128)(2,1)}, u32[]{:S(2)}, u32[]{:S(2)}) collective-permute-start(bf16[48,1536]{1,0:T(8,128)(2,1)} %pad_maximum_fusion.22), channel_id=1, source_target_pairs={{0,16},{2,18},{4,20},{6,22},{8,24},{10,26},{12,28},{14,30},{16,0},... | collective-permute-start | bytes 442376 | tf_op jit(solution)/shard_map/ppermute | solution.py:78
  (61 other events, 695.2 us)
Sparse Core Ops, SparseCore 0:
  11.5 103.8 all-gather.2
  118.9 84.6 all-gather.4
  311.0 148.8 reduce-scatter.1

commit v6 on v5

--- a/solution.py
+++ b/solution.py
@@ -1281,7 +1281,7 @@
     totals = Totals(jnp.stack([smalls_zero, smalls_one]), routed)
     totals.send("dp", 1, 4, grads)
     zero_middle = ffn_zero.send_middle(grads)
-    attention_zero = qkv_grads(0, grads, out_members, waits(routed, ffn_last + one_far))
+    attention_zero = qkv_grads(0, grads, out_members, waits(routed, one_far))
     begun = attention_zero.begun
     totals.land(*begun)
     totals.send("dp", 4, dp_size // 4, *begun)

time: 560 us -> 571 us (1.020)
  waiting for transfers between devices: 97.3 us -> 112 us
    ppermute x59, waiting for transfers between devices: 73.1 us -> 87.8 us  [hop(): return lax.ppermute(member, axis, pairs)]
  transfers between devices with their start and end apart: 62 -> 62, of which waited for: 15 -> 17; matrix products, arithmetic and copies ran while one was open for 15% -> 14% of each run, Pallas kernels for 44% -> 44%
where the time goes in v6:
time: 571 us; the launch traced here: 566 us
  Pallas kernels  286 us (50%)
  waiting for transfers between devices  112 us (20%)
  starting transfers between devices  68.1 us (12%)
  other arithmetic  53.8 us (9%)
  local copies, waits for them, and re-layouts  30.4 us (5%)
  between operations  15.1 us (3%)
    pallas_call x16, Pallas kernels, run_kernel(): pl.pallas_call(body, grid_spec=pltpu.PrefetchScalarGridSpec(num_scalar_pr...  286 us
    ppermute x59, waiting for transfers between devices, hop(): return lax.ppermute(member, axis, pairs)  87.8 us
    ppermute x59, starting transfers between devices, hop(): return lax.ppermute(member, axis, pairs)  68 us
    all_gather x2, waiting for transfers between devices, __init__(): whole = lax.all_gather(shard, AXES, tiled=True)  24.2 us
  transfers between devices with their start and end apart: 62, of which 17 were waited for; matrix products, arithmetic and copies ran while one was open for 14% of the time, Pallas kernels for 44%

profile of v6, /device:TPU:0, one launch (start us, length us, event | category | flops | bytes accessed | tf_op | source)
XLA Modules:
  0.0 565.9 jit_solution(1487698387559045774)
XLA Ops:
  12.2 3.0 collective-permute-start.1
  15.2 2.6 collective-permute-start.2
  40.9 7.2 %collective-permute-done.8 = bf16[4,48,768]{2,1,0:T(8,128)(2,1)S(1)} collective-permute-done((bf16[4,48,768]{2,1,0:T(8,128)(2,1)S(1)}, bf16[4,48,768]{2,1,0:T(8,128)(2,1)S(1)}, u32[]{:S(2)}, u32[]{:S(2)}) %collective-permute-start.8) | collective-permute-done | bytes 294944 | tf_op jit(solution)/shard_map/ppermute | solution.py:78
  53.7 14.2 %collective-permute-done.9.refs_11_.refs_5_.refs_3_ = bf16[8,48,768]{2,1,0:T(8,128)(2,1)S(1)} collective-permute-done((bf16[8,48,768]{2,1,0:T(8,128)(2,1)}, bf16[8,48,768]{2,1,0:T(8,128)(2,1)S(1)}, u32[]{:S(2)}, u32[]{:S(2)}) %collective-permute-start.9) | collective-permute-done | bytes 589856 | tf_op jit(solution)/shard_map/ppermute | solution.py:78
  69.8 2.1 collective-permute-start.12
  71.9 2.0 collective-permute-start.13
  74.8 9.0 %qkv_forward.2.refs_0_ = bf16[3,1024,768]{2,1,0:T(8,128)(2,1)} custom-call(s32[12]{0:T(128)} %pad_add_fusion.meta_ref, bf16[1024,768]{1,0:T(8,128)(2,1)} %constant_dynamic-slice_fusion.2.refs_0_.refs_1_, f32[3,1,768]{2,1,0:T(1,128)} %get-tuple-element.375.refs_1_, bf16[8,48,768]{2,1,0:T(8,128)(2,1)} %copy-done.38, bf16[8,48,768]{2,1,0:T(8,128)(2,1)} %copy-done.42, ...), custom_call_target="tpu_custom_call" | custom-call | flops 28991029248 | bytes 9830400 | tf_op jit(solution)/shard_map/qkv_forward/pallas_call | solution.py:775
  83.7 8.9 %collective-permute-done.13 = bf16[1,48,1536]{2,1,0:T(8,128)(2,1)S(1)} collective-permute-done((bf16[1,48,1536]{2,1,0:T(8,128)(2,1)S(1)}, bf16[1,48,1536]{2,1,0:T(8,128)(2,1)S(1)}, u32[]{:S(2)}, u32[]{:S(2)}) %collective-permute-start.13) | collective-permute-done | bytes 147488 | tf_op jit(solution)/shard_map/ppermute | solution.py:78
  96.4 17.5 %attention_forward.2 = (bf16[1024,768]{1,0:T(8,128)(2,1)}, f32[2,6,8,512]{3,2,1,0:T(8,128)}) custom-call(s32[12]{0:T(128)} %pad_add_fusion.meta_ref, bf16[3,1024,768]{2,1,0:T(8,128)(2,1)} %qkv_forward.2.refs_0_), custom_call_target="tpu_custom_call" | custom-call | flops 51539607552 | bytes 6291456 | tf_op jit(solution)/shard_map/attention_forward/pallas_call | solution.py:775
  115.9 2.0 collective-permute-start.16
  118.1 30.8 %ffn_forward.2 = (bf16[1024,768]{1,0:T(8,128)(2,1)}, bf16[1024,768]{1,0:T(8,128)(2,1)}, f32[1024,128]{1,0:T(8,128)}, bf16[1024,3072]{1,0:T(8,128)(2,1)}, bf16[10...) custom-call(s32[12]{0:T(128)} %pad_add_fusion.meta_ref, ...), custom_call_target="tpu_custom_call" | custom-call | flops 77309411328 | bytes 28311552 | tf_op jit(solution)/shard_map/ffn_forward/pallas_call | solution.py:775
  152.2 9.0 %qkv_forward.3.refs_0_ = bf16[3,1024,768]{2,1,0:T(8,128)(2,1)} custom-call(s32[12]{0:T(128)} %pad_add_fusion.meta_ref, bf16[1024,768]{1,0:T(8,128)(2,1)} %get-tuple-element.150.refs_0_.refs_1_, f32[3,1,768]{2,1,0:T(1,128)} %get-tuple-element.374.refs_1_, bf16[8,48,768]{2,1,0:T(8,128)(2,1)} %constant_dynamic-update-slice_fusion.12.refs_2_.refs_6_, ...), custom_call_target="tpu_custom_call" | custom-call | flops 28991029248 | bytes 9830400 | tf_op jit(solution)/shard_map/qkv_forward/pallas_call | solution.py:775
  161.3 17.6 %attention_forward.3 = (bf16[1024,768]{1,0:T(8,128)(2,1)}, f32[2,6,8,512]{3,2,1,0:T(8,128)}) custom-call(s32[12]{0:T(128)} %pad_add_fusion.meta_ref, bf16[3,1024,768]{2,1,0:T(8,128)(2,1)} %qkv_forward.3.refs_0_), custom_call_target="tpu_custom_call" | custom-call | flops 51539607552 | bytes 6291456 | tf_op jit(solution)/shard_map/attention_forward/pallas_call | solution.py:775
  179.3 24.2 %all-gather.5.cloned.1.call-done = bf16[1536,3072]{1,0:T(8,128)(2,1)} async-done(((bf16[48,3072]{1,0:T(8,128)(2,1)}), bf16[1536,3072]{1,0:T(8,128)(2,1)}) %all-gather.5.cloned.1.call-update) | async-done | bytes 9437200 | tf_op jit(solution)/shard_map/all_gather | solution.py:150
  203.5 30.5 %ffn_forward.3 = (bf16[1024,768]{1,0:T(8,128)(2,1)}, bf16[1024,768]{1,0:T(8,128)(2,1)}, f32[1024,128]{1,0:T(8,128)}, bf16[1024,3072]{1,0:T(8,128)(2,1)}, bf16[10...) custom-call(s32[12]{0:T(128)} %pad_add_fusion.meta_ref, ...), custom_call_target="tpu_custom_call" | custom-call | flops 77309411328 | bytes 28311552 | tf_op jit(solution)/shard_map/ffn_forward/pallas_call | solution.py:775
  234.8 33.9 %ffn_backward.2 = (bf16[1024,768]{1,0:T(8,128)(2,1)}, f32[1024,768]{1,0:T(8,128)}, f32[8,768]{1,0:T(8,128)}, f32[4,1,768]{2,1,0:T(1,128)}, bf16[2,768,3072]{2,1,0:T(8,128)(2,1)}) custom-call(s32[12]{0:T(128)} %pad_add_fusion.meta_ref, bf16[1024,768]{1,0:T(8,128)(2,1)} %constant_dynamic-slice_fusion.1.refs_0_, bf16[1024,768]{1,0:T(8,128)(2,1)} %get-tuple-element.153.refs_1_, ...), custom_call_target="tpu_custom_call" | custom-call | flops 309237645312 | bytes 50331648 | tf_op jit(solution)/shard_map/ffn_backward/pallas_call | solution.py:775
  269.8 8.8 %out_backward.2 = (bf16[1024,768]{1,0:T(8,128)(2,1)}, bf16[16,48,384]{2,1,0:T(8,128)(2,1)}, bf16[16,48,384]{2,1,0:T(8,128)(2,1)}) custom-call(s32[12]{0:T(128)} %pad_add_fusion.meta_ref, bf16[1024,768]{1,0:T(8,128)(2,1)} %get-tuple-element.160.refs_0_, bf16[1024,768]{1,0:T(8,128)(2,1)} %get-tuple-element.149.refs_0_.refs_1_, ...), custom_call_target="tpu_custom_call" | custom-call | flops 38654705664 | bytes 7077888 | tf_op jit(solution)/shard_map/out_backward/pallas_call | solution.py:775
  278.7 22.5 %attention_backward.2 = (bf16[3,1024,768]{2,1,0:T(8,128)(2,1)}, f32[8,768]{1,0:T(8,128)}) custom-call(s32[12]{0:T(128)} %pad_add_fusion.meta_ref, bf16[3,1024,768]{2,1,0:T(8,128)(2,1)} %qkv_forward.3.refs_0_, bf16[1024,768]{1,0:T(8,128)(2,1)} %get-tuple-element.149.refs_0_.refs_1_, bf16[1024,768]{1,0:T(8,128)(2,1)} %get-tuple-element.162.refs_2_, ...), custom_call_target="tpu_custom_call" | custom-call | flops 257698037760 | bytes 12582912 | tf_op jit(solution)/shard_map/attention_backward/pallas_call | solution.py:775
  301.2 8.8 %qkv_grad.2 = (bf16[16,48,1152]{2,1,0:T(8,128)(2,1)}, bf16[16,48,1152]{2,1,0:T(8,128)(2,1)}) custom-call(s32[12]{0:T(128)} %pad_add_fusion.meta_ref, bf16[1024,768]{1,0:T(8,128)(2,1)} %get-tuple-element.150.refs_0_.refs_1_, bf16[3,1024,768]{2,1,0:T(8,128)(2,1)} %get-tuple-element.164.refs_1_.refs_0_), custom_call_target="tpu_custom_call" | custom-call | flops 57982058496 | bytes 9830400 | tf_op jit(solution)/shard_map/qkv_grad/pallas_call | solution.py:775
  310.6 10.5 %input_gradient.2.refs_0_ = f32[1024,768]{1,0:T(8,128)} custom-call(s32[12]{0:T(128)} %pad_add_fusion.meta_ref, bf16[3,1024,768]{2,1,0:T(8,128)(2,1)} %get-tuple-element.164.refs_1_.refs_0_, f32[1024,768]{1,0:T(8,128)} %get-tuple-element.165.refs_1_, bf16[8,48,768]{2,1,0:T(8,128)(2,1)} %constant_dynamic-update-slice_fusion.12.refs_2_.refs_6_, ...), custom_call_target="tpu_custom_call" | custom-call | flops 57982058496 | bytes 14548992 | tf_op jit(solution)/shard_map/input_gradient/pallas_call | solution.py:775
  321.1 3.7 maximum_select_fusion.2
  326.2 3.7 maximum_select_fusion.1
  335.9 35.4 %ffn_backward.3 = (bf16[1024,768]{1,0:T(8,128)(2,1)}, f32[1024,768]{1,0:T(8,128)}, f32[8,768]{1,0:T(8,128)}, f32[4,1,768]{2,1,0:T(1,128)}, bf16[16,48,3072]{2,1,0:T(8,128)(2,1)}, /*index=5*/bf16[16,48,3072]{2,1,0:T(8,128)(2,1)}) custom-call(s32[12]{0:T(128)} %pad_add_fusion.meta_ref, f32[1024,768]{1,0:T(8,128)} %input_gradient.2.refs_0_, ...), custom_call_target="tpu_custom_call" | custom-call | flops 309237645312 | bytes 50331648 | tf_op jit(solution)/shard_map/ffn_backward/pallas_call | solution.py:775
  373.8 2.1 collective-permute-start.30
  378.0 8.9 %out_backward.3 = (bf16[1024,768]{1,0:T(8,128)(2,1)}, bf16[16,48,384]{2,1,0:T(8,128)(2,1)}, bf16[16,48,384]{2,1,0:T(8,128)(2,1)}) custom-call(s32[12]{0:T(128)} %pad_add_fusion.meta_ref, bf16[1024,768]{1,0:T(8,128)(2,1)} %get-tuple-element.176.refs_0_, bf16[1024,768]{1,0:T(8,128)(2,1)} %get-tuple-element.135.refs_0_.refs_1_, ...), custom_call_target="tpu_custom_call" | custom-call | flops 38654705664 | bytes 7077888 | tf_op jit(solution)/shard_map/out_backward/pallas_call | solution.py:775
  387.0 1.9 add_bitcast_fusion.5
  392.8 2.3 collective-permute-start.34
  395.8 6.7 %collective-permute-start.33 = (bf16[48,1536]{1,0:T(8,128)(2,1)}, bf16[48,1536]{1,0:T(8,128)(2,1)}, u32[]{:S(2)}, u32[]{:S(2)}) collective-permute-start(bf16[48,1536]{1,0:T(8,128)(2,1)} %pad_maximum_fusion.19), channel_id=1, source_target_pairs={{0,16},{2,18},{4,20},{6,22},{8,24},{10,26},{12,28},{14,30},{16,0},... | collective-permute-start | bytes 442376 | tf_op jit(solution)/shard_map/ppermute | solution.py:78
  403.2 22.5 %attention_backward.3 = (bf16[3,1024,768]{2,1,0:T(8,128)(2,1)}, f32[8,768]{1,0:T(8,128)}) custom-call(s32[12]{0:T(128)} %pad_add_fusion.meta_ref, bf16[3,1024,768]{2,1,0:T(8,128)(2,1)} %qkv_forward.2.refs_0_, bf16[1024,768]{1,0:T(8,128)(2,1)} %get-tuple-element.135.refs_0_.refs_1_, bf16[1024,768]{1,0:T(8,128)(2,1)} %get-tuple-element.182.refs_2_, ...), custom_call_target="tpu_custom_call" | custom-call | flops 257698037760 | bytes 12582912 | tf_op jit(solution)/shard_map/attention_backward/pallas_call | solution.py:775
  427.8 4.5 add_convert_fusion.1
  434.2 8.9 %qkv_grad.3 = (bf16[16,48,1152]{2,1,0:T(8,128)(2,1)}, bf16[16,48,1152]{2,1,0:T(8,128)(2,1)}) custom-call(s32[12]{0:T(128)} %pad_add_fusion.meta_ref, bf16[1024,768]{1,0:T(8,128)(2,1)} %constant_dynamic-slice_fusion.2.refs_0_.refs_1_, bf16[3,1024,768]{2,1,0:T(8,128)(2,1)} %get-tuple-element.190.refs_1_.refs_0_, ...), custom_call_target="tpu_custom_call" | custom-call | flops 57982058496 | bytes 9830400 | tf_op jit(solution)/shard_map/qkv_grad/pallas_call | solution.py:775
  445.0 11.8 %input_gradient.3 = (f32[1024,768]{1,0:T(8,128)}, bf16[1024,768]{1,0:T(8,128)(2,1)}) custom-call(s32[12]{0:T(128)} %pad_add_fusion.meta_ref, bf16[3,1024,768]{2,1,0:T(8,128)(2,1)} %get-tuple-element.190.refs_1_.refs_0_, f32[1024,768]{1,0:T(8,128)} %get-tuple-element.191.refs_1_, bf16[8,48,768]{2,1,0:T(8,128)(2,1)} %copy-done.38, ...), custom_call_target="tpu_custom_call" | custom-call | flops 57982058496 | bytes 14548992 | tf_op jit(solution)/shard_map/input_gradient/pallas_call | solution.py:775
  458.7 2.0 collective-permute-start.48
  460.9 2.2 collective-permute-start.50
  463.4 5.8 %collective-permute-done.49 = f32[2,9216]{1,0:T(2,128)S(1)} collective-permute-done((f32[2,9216]{1,0:T(2,128)S(1)}, f32[2,9216]{1,0:T(2,128)S(1)}, u32[]{:S(2)}, u32[]{:S(2)}) %collective-permute-start.49) | collective-permute-done | bytes 73760 | tf_op jit(solution)/shard_map/ppermute | solution.py:78
  469.5 1.9 add_convert_fusion.3
  472.6 2.2 collective-permute-start.55
  475.0 12.3 %collective-permute-done.53 = bf16[4,48,1536]{2,1,0:T(8,128)(2,1)S(1)} collective-permute-done((bf16[4,48,1536]{2,1,0:T(8,128)(2,1)S(1)}, bf16[4,48,1536]{2,1,0:T(8,128)(2,1)S(1)}, u32[]{:S(2)}, u32[]{:S(2)}) %collective-permute-start.53) | collective-permute-done | bytes 589856 | tf_op jit(solution)/shard_map/ppermute | solution.py:78
  490.2 2.3 fusion.7
  495.4 2.2 collective-permute-start.57
  497.6 10.1 %collective-permute-done.37 = bf16[8,48,768]{2,1,0:T(8,128)(2,1)S(1)} collective-permute-done((bf16[8,48,768]{2,1,0:T(8,128)(2,1)S(1)}, bf16[8,48,768]{2,1,0:T(8,128)(2,1)S(1)}, u32[]{:S(2)}, u32[]{:S(2)}) %collective-permute-start.37) | collective-permute-done | bytes 589856 | tf_op jit(solution)/shard_map/ppermute | solution.py:78
  511.7 6.2 %collective-permute-done.51 = f32[2,9216]{1,0:T(2,128)S(1)} collective-permute-done((f32[2,9216]{1,0:T(2,128)S(1)}, f32[2,9216]{1,0:T(2,128)S(1)}, u32[]{:S(2)}, u32[]{:S(2)}) %collective-permute-start.51) | collective-permute-done | bytes 73760 | tf_op jit(solution)/shard_map/ppermute | solution.py:78
  520.7 5.9 %collective-permute-done.58 = bf16[48,3072]{1,0:T(8,128)(2,1)S(1)} collective-permute-done((bf16[48,3072]{1,0:T(8,128)(2,1)S(1)}, bf16[48,3072]{1,0:T(8,128)(2,1)S(1)}, u32[]{:S(2)}, u32[]{:S(2)}) %collective-permute-start.58) | collective-permute-done | bytes 294944 | tf_op jit(solution)/shard_map/ppermute | solution.py:78
  527.0 5.1 collective-permute-start.42
  532.3 2.5 collective-permute-start.44
  538.7 6.2 %collective-permute-done.43 = bf16[48,1536]{1,0:T(8,128)(2,1)} collective-permute-done((bf16[48,1536]{1,0:T(8,128)(2,1)S(1)}, bf16[48,1536]{1,0:T(8,128)(2,1)}, u32[]{:S(2)}, u32[]{:S(2)}) %collective-permute-start.43) | collective-permute-done | bytes 147488 | tf_op jit(solution)/shard_map/ppermute | solution.py:78
  547.6 5.2 collective-permute-done.39
  553.0 3.1 maximum_select_fusion
  (318 shorter events, 98.0 us)
Async XLA Ops:
  7.2 110.9 %all-gather.3.cloned.1.call-start = ((), (), s32[]{:S(2)}) async-start(), calls=%async_computation.1 | async-start | bytes 9732096 | tf_op jit(solution)/shard_map/all_gather | solution.py:150
  9.3 194.2 %all-gather.5.cloned.1.call-start = ((), (), s32[]{:S(2)}) async-start(), calls=%async_computation.2 | async-start | bytes 9732096 | tf_op jit(solution)/shard_map/all_gather | solution.py:150
  12.2 20.7 %collective-permute-start.1 = (bf16[1,48,1536]{2,1,0:T(8,128)(2,1)}, bf16[1,48,1536]{2,1,0:T(8,128)(2,1)}, u32[]{:S(2)}, u32[]{:S(2)}) collective-permute-start(bf16[1,48,1536]{2,1,0:T(8,128)(2,1)} %maximum_bitcast_fusion.2), channel_id=1, source_target_pairs={{0,8},{2,10},{4,12},{6,14},{8,0},{10,2},{12,4},{14,6},{16,24},{18,... | collective-permute-start | bytes 442376 | tf_op jit(solution)/shard_map/ppermute | solution.py:78
  15.2 19.3 %collective-permute-start.2 = (bf16[1,48,1536]{2,1,0:T(8,128)(2,1)}, bf16[1,48,1536]{2,1,0:T(8,128)(2,1)}, u32[]{:S(2)}, u32[]{:S(2)}) collective-permute-start(bf16[1,48,1536]{2,1,0:T(8,128)(2,1)} %maximum_bitcast_fusion.2), channel_id=1, source_target_pairs={{0,16},{2,18},{4,20},{6,22},{8,24},{10,26},{12,28},{14,30},{16,0},... | collective-permute-start | bytes 442376 | tf_op jit(solution)/shard_map/ppermute | solution.py:78
  17.8 18.3 %collective-permute-start.3 = (bf16[1,48,1536]{2,1,0:T(8,128)(2,1)}, bf16[1,48,1536]{2,1,0:T(8,128)(2,1)}, u32[]{:S(2)}, u32[]{:S(2)}) collective-permute-start(bf16[1,48,1536]{2,1,0:T(8,128)(2,1)} %maximum_bitcast_fusion.2), channel_id=1, source_target_pairs={{0,24},{2,26},{4,28},{6,30},{8,16},{10,18},{12,20},{14,22},{16,8},... | collective-permute-start | bytes 442376 | tf_op jit(solution)/shard_map/ppermute | solution.py:78
  20.4 11.7 %collective-permute-start = (f32[2,2304]{1,0:T(2,128)}, f32[2,2304]{1,0:T(2,128)}, u32[]{:S(2)}, u32[]{:S(2)}) collective-permute-start(f32[2,2304]{1,0:T(2,128)} %constant_dynamic-update-slice_fusion), channel_id=1, source_target_pairs={{0,1},{1,0},{2,3},{3,2},{4,5},{5,4},{6,7},{7,6},{8,9},{9,8},{10,11... | collective-permute-start | bytes 55304 | tf_op jit(solution)/shard_map/ppermute | solution.py:78
  22.9 533.2 %reduce-scatter.2.cloned.1.call-start = ((), (), s32[]{:S(2)}) async-start(), calls=%async_computation.3 | async-start | bytes 9732096 | tf_op jit(solution)/shard_map/reduce_scatter | solution.py:235
  39.1 12.5 %collective-permute-start.4 = (bf16[4,48,768]{2,1,0:T(8,128)(2,1)S(1)}, bf16[4,48,768]{2,1,0:T(8,128)(2,1)S(1)}, u32[]{:S(2)}, u32[]{:S(2)}) collective-permute-start(bf16[4,48,768]{2,1,0:T(8,128)(2,1)S(1)} %pad_maximum_fusion.5), channel_id=1, source_target_pairs={{0,4},{2,6},{4,0},{6,2},{8,12},{10,14},{12,8},{14,10},{16,20},{18,... | collective-permute-start | bytes 884744 | tf_op jit(solution)/shard_map/ppermute | solution.py:78
  48.8 19.0 %collective-permute-start.9 = (bf16[8,48,768]{2,1,0:T(8,128)(2,1)}, bf16[8,48,768]{2,1,0:T(8,128)(2,1)S(1)}, u32[]{:S(2)}, u32[]{:S(2)}) collective-permute-start(bf16[8,48,768]{2,1,0:T(8,128)(2,1)} %constant_dynamic-update-slice_fusion.7.refs_10_.refs_4_.refs_2_), channel_id=1, source_target_pairs={{0,4},{2,6},{4,0},{6,2},{8,12},{10,14},{12,8},{14,10},{16,20},{18,... | collective-permute-start | bytes 1769480 | tf_op jit(solution)/shard_map/ppermute | solution.py:78
  51.6 16.3 %collective-permute-start.5 = (bf16[8,48,768]{2,1,0:T(8,128)(2,1)S(1)}, bf16[8,48,768]{2,1,0:T(8,128)(2,1)S(1)}, u32[]{:S(2)}, u32[]{:S(2)}) collective-permute-start(bf16[8,48,768]{2,1,0:T(8,128)(2,1)S(1)} %constant_dynamic-update-slice_fusion.2.refs_2_.refs_6_), channel_id=1, source_target_pairs={{0,1},{1,0},{2,3},{3,2},{4,5},{5,4},{6,7},{7,6},{8,9},{9,8},{10,11... | collective-permute-start | bytes 1769480 | tf_op jit(solution)/shard_map/ppermute | solution.py:78
  53.1 18.8 %collective-permute-start.10 = (bf16[8,48,768]{2,1,0:T(8,128)(2,1)}, bf16[8,48,768]{2,1,0:T(8,128)(2,1)S(1)}, u32[]{:S(2)}, u32[]{:S(2)}) collective-permute-start(bf16[8,48,768]{2,1,0:T(8,128)(2,1)} %constant_dynamic-update-slice_fusion.7.refs_10_.refs_4_.refs_2_), channel_id=1, source_target_pairs={{0,2},{2,0},{4,6},{6,4},{8,10},{10,8},{12,14},{14,12},{16,18},{18,... | collective-permute-start | bytes 1769480 | tf_op jit(solution)/shard_map/ppermute | solution.py:78
  53.2 20.7 %collective-permute-start.6 = (bf16[8,48,768]{2,1,0:T(8,128)(2,1)S(1)}, bf16[8,48,768]{2,1,0:T(8,128)(2,1)S(1)}, u32[]{:S(2)}, u32[]{:S(2)}) collective-permute-start(bf16[8,48,768]{2,1,0:T(8,128)(2,1)S(1)} %constant_dynamic-update-slice_fusion.2.refs_2_.refs_6_), channel_id=1, source_target_pairs={{0,2},{2,0},{4,6},{6,4},{8,10},{10,8},{12,14},{14,12},{16,18},{18,... | collective-permute-start | bytes 1769480 | tf_op jit(solution)/shard_map/ppermute | solution.py:78
  69.8 14.0 %collective-permute-start.12 = (bf16[1,48,1536]{2,1,0:T(8,128)(2,1)S(1)}, bf16[1,48,1536]{2,1,0:T(8,128)(2,1)S(1)}, u32[]{:S(2)}, u32[]{:S(2)}) collective-permute-start(bf16[1,48,1536]{2,1,0:T(8,128)(2,1)S(1)} %maximum_bitcast_fusion.3), channel_id=1, source_target_pairs={{0,8},{2,10},{4,12},{6,14},{8,0},{10,2},{12,4},{14,6},{16,24},{18,... | collective-permute-start | bytes 442376 | tf_op jit(solution)/shard_map/ppermute | solution.py:78
  71.9 20.7 %collective-permute-start.13 = (bf16[1,48,1536]{2,1,0:T(8,128)(2,1)S(1)}, bf16[1,48,1536]{2,1,0:T(8,128)(2,1)S(1)}, u32[]{:S(2)}, u32[]{:S(2)}) collective-permute-start(bf16[1,48,1536]{2,1,0:T(8,128)(2,1)S(1)} %maximum_bitcast_fusion.3), channel_id=1, source_target_pairs={{0,16},{2,18},{4,20},{6,22},{8,24},{10,26},{12,28},{14,30},{16,0},... | collective-permute-start | bytes 442376 | tf_op jit(solution)/shard_map/ppermute | solution.py:78
  73.9 18.7 %collective-permute-start.14 = (bf16[1,48,1536]{2,1,0:T(8,128)(2,1)S(1)}, bf16[1,48,1536]{2,1,0:T(8,128)(2,1)S(1)}, u32[]{:S(2)}, u32[]{:S(2)}) collective-permute-start(bf16[1,48,1536]{2,1,0:T(8,128)(2,1)S(1)} %maximum_bitcast_fusion.3), channel_id=1, source_target_pairs={{0,24},{2,26},{4,28},{6,30},{8,16},{10,18},{12,20},{14,22},{16,8},... | collective-permute-start | bytes 442376 | tf_op jit(solution)/shard_map/ppermute | solution.py:78
  94.7 19.1 %collective-permute-start.19 = (bf16[4,48,768]{2,1,0:T(8,128)(2,1)S(1)}, bf16[4,48,768]{2,1,0:T(8,128)(2,1)S(1)}, u32[]{:S(2)}, u32[]{:S(2)}) collective-permute-start(bf16[4,48,768]{2,1,0:T(8,128)(2,1)S(1)} %pad_maximum_fusion.9), channel_id=1, source_target_pairs={{0,1},{1,0},{2,3},{3,2},{4,5},{5,4},{6,7},{7,6},{8,9},{9,8},{10,11... | collective-permute-start | bytes 884744 | tf_op jit(solution)/shard_map/ppermute | solution.py:78
  94.8 20.3 %collective-permute-start.15 = (bf16[4,48,768]{2,1,0:T(8,128)(2,1)S(1)}, bf16[4,48,768]{2,1,0:T(8,128)(2,1)S(1)}, u32[]{:S(2)}, u32[]{:S(2)}) collective-permute-start(bf16[4,48,768]{2,1,0:T(8,128)(2,1)S(1)} %pad_maximum_fusion.8), channel_id=1, source_target_pairs={{0,4},{2,6},{4,0},{6,2},{8,12},{10,14},{12,8},{14,10},{16,20},{18,... | collective-permute-start | bytes 884744 | tf_op jit(solution)/shard_map/ppermute | solution.py:78
  114.6 34.4 %collective-permute-start.20 = (bf16[8,48,768]{2,1,0:T(8,128)(2,1)}, bf16[8,48,768]{2,1,0:T(8,128)(2,1)}, u32[]{:S(2)}, u32[]{:S(2)}) collective-permute-start(bf16[8,48,768]{2,1,0:T(8,128)(2,1)} %constant_dynamic-update-slice_fusion.17.refs_10_.refs_4_.refs_2_), channel_id=1, source_target_pairs={{0,4},{2,6},{4,0},{6,2},{8,12},{10,14},{12,8},{14,10},{16,20},{18,... | collective-permute-start | bytes 1769480 | tf_op jit(solution)/shard_map/ppermute | solution.py:78
  115.2 36.3 %collective-permute-start.21 = (bf16[8,48,768]{2,1,0:T(8,128)(2,1)}, bf16[8,48,768]{2,1,0:T(8,128)(2,1)}, u32[]{:S(2)}, u32[]{:S(2)}) collective-permute-start(bf16[8,48,768]{2,1,0:T(8,128)(2,1)} %constant_dynamic-update-slice_fusion.17.refs_10_.refs_4_.refs_2_), channel_id=1, source_target_pairs={{0,2},{2,0},{4,6},{6,4},{8,10},{10,8},{12,14},{14,12},{16,18},{18,... | collective-permute-start | bytes 1769480 | tf_op jit(solution)/shard_map/ppermute | solution.py:78
  115.9 33.4 %collective-permute-start.16 = (bf16[8,48,768]{2,1,0:T(8,128)(2,1)}, bf16[8,48,768]{2,1,0:T(8,128)(2,1)}, u32[]{:S(2)}, u32[]{:S(2)}) collective-permute-start(bf16[8,48,768]{2,1,0:T(8,128)(2,1)} %constant_dynamic-update-slice_fusion.12.refs_2_.refs_6_), channel_id=1, source_target_pairs={{0,1},{1,0},{2,3},{3,2},{4,5},{5,4},{6,7},{7,6},{8,9},{9,8},{10,11... | collective-permute-start | bytes 1769480 | tf_op jit(solution)/shard_map/ppermute | solution.py:78
  117.9 33.6 %collective-permute-start.17 = (bf16[8,48,768]{2,1,0:T(8,128)(2,1)}, bf16[8,48,768]{2,1,0:T(8,128)(2,1)}, u32[]{:S(2)}, u32[]{:S(2)}) collective-permute-start(bf16[8,48,768]{2,1,0:T(8,128)(2,1)} %constant_dynamic-update-slice_fusion.12.refs_2_.refs_6_), channel_id=1, source_target_pairs={{0,2},{2,0},{4,6},{6,4},{8,10},{10,8},{12,14},{14,12},{16,18},{18,... | collective-permute-start | bytes 1769480 | tf_op jit(solution)/shard_map/ppermute | solution.py:78
  178.9 55.9 %collective-permute-start.23 = (bf16[1024,768]{1,0:T(8,128)(2,1)S(1)}, bf16[1024,768]{1,0:T(8,128)(2,1)}, u32[]{:S(2)}, u32[]{:S(2)}) collective-permute-start(bf16[1024,768]{1,0:T(8,128)(2,1)S(1)} %copy-done.8), channel_id=1, source_target_pairs={{0,1},{1,0},{2,3},{3,2},{4,5},{5,4},{6,7},{7,6},{8,9},{9,8},{10,11... | collective-permute-start | bytes 4718600 | tf_op jit(solution)/shard_map/ppermute | solution.py:78
  234.0 35.8 %collective-permute-start.24 = (bf16[1024,768]{1,0:T(8,128)(2,1)}, bf16[1024,768]{1,0:T(8,128)(2,1)}, u32[]{:S(2)}, u32[]{:S(2)}) collective-permute-start(bf16[1024,768]{1,0:T(8,128)(2,1)} %get-tuple-element.151), channel_id=1, source_target_pairs={{0,1},{1,0},{2,3},{3,2},{4,5},{5,4},{6,7},{7,6},{8,9},{9,8},{10,11... | collective-permute-start | bytes 4718600 | tf_op jit(solution)/shard_map/ppermute | solution.py:78
  310.0 21.0 %collective-permute-start.26 = (bf16[16,48,1152]{2,1,0:T(8,128)(2,1)}, bf16[16,48,1152]{2,1,0:T(8,128)(2,1)S(1)}, u32[]{:S(2)}, u32[]{:S(2)}) collective-permute-start(bf16[16,48,1152]{2,1,0:T(8,128)(2,1)} %get-tuple-element.175), channel_id=1, source_target_pairs={{0,2},{2,0},{4,6},{6,4},{8,10},{10,8},{12,14},{14,12},{16,18},{18,... | collective-permute-start | bytes 5308424 | tf_op jit(solution)/shard_map/ppermute | solution.py:78
  310.1 19.8 %collective-permute-start.25 = (bf16[16,48,384]{2,1,0:T(8,128)(2,1)}, bf16[16,48,384]{2,1,0:T(8,128)(2,1)}, u32[]{:S(2)}, u32[]{:S(2)}) collective-permute-start(bf16[16,48,384]{2,1,0:T(8,128)(2,1)} %get-tuple-element.174), channel_id=1, source_target_pairs={{0,2},{2,0},{4,6},{6,4},{8,10},{10,8},{12,14},{14,12},{16,18},{18,... | collective-permute-start | bytes 1769480 | tf_op jit(solution)/shard_map/ppermute | solution.py:78
  332.2 40.5 %collective-permute-start.28 = (bf16[8,48,768]{2,1,0:T(8,128)(2,1)}, bf16[8,48,768]{2,1,0:T(8,128)(2,1)}, u32[]{:S(2)}, u32[]{:S(2)}) collective-permute-start(bf16[8,48,768]{2,1,0:T(8,128)(2,1)} %add_convert_fusion.5), channel_id=1, source_target_pairs={{0,4},{2,6},{4,0},{6,2},{8,12},{10,14},{12,8},{14,10},{16,20},{18,... | collective-permute-start | bytes 1769480 | tf_op jit(solution)/shard_map/ppermute | solution.py:78
  334.4 41.5 %collective-permute-start.27 = (bf16[8,48,768]{2,1,0:T(8,128)(2,1)}, bf16[8,48,768]{2,1,0:T(8,128)(2,1)}, u32[]{:S(2)}, u32[]{:S(2)}) collective-permute-start(bf16[8,48,768]{2,1,0:T(8,128)(2,1)} %pad_maximum_fusion), channel_id=1, source_target_pairs={{0,1},{1,0},{2,3},{3,2},{4,5},{5,4},{6,7},{7,6},{8,9},{9,8},{10,11... | collective-permute-start | bytes 1769480 | tf_op jit(solution)/shard_map/ppermute | solution.py:78
  371.3 31.9 %collective-permute-start.31 = (bf16[16,48,3072]{2,1,0:T(8,128)(2,1)}, bf16[16,48,3072]{2,1,0:T(8,128)(2,1)}, u32[]{:S(2)}, u32[]{:S(2)}) collective-permute-start(bf16[16,48,3072]{2,1,0:T(8,128)(2,1)} %get-tuple-element.189), channel_id=1, source_target_pairs={{0,2},{2,0},{4,6},{6,4},{8,10},{10,8},{12,14},{14,12},{16,18},{18,... | collective-permute-start | bytes 14155784 | tf_op jit(solution)/shard_map/ppermute | solution.py:78
  373.8 13.1 %collective-permute-start.30 = (bf16[4,48,768]{2,1,0:T(8,128)(2,1)S(1)}, bf16[4,48,768]{2,1,0:T(8,128)(2,1)S(1)}, u32[]{:S(2)}, u32[]{:S(2)}) collective-permute-start(bf16[4,48,768]{2,1,0:T(8,128)(2,1)S(1)} %add_convert_fusion.9), channel_id=1, source_target_pairs={{0,1},{1,0},{2,3},{3,2},{4,5},{5,4},{6,7},{7,6},{8,9},{9,8},{10,11... | collective-permute-start | bytes 884744 | tf_op jit(solution)/shard_map/ppermute | solution.py:78
  392.8 39.5 %collective-permute-start.34 = (bf16[48,1536]{1,0:T(8,128)(2,1)}, bf16[48,1536]{1,0:T(8,128)(2,1)}, u32[]{:S(2)}, u32[]{:S(2)}) collective-permute-start(bf16[48,1536]{1,0:T(8,128)(2,1)} %pad_maximum_fusion.20), channel_id=1, source_target_pairs={{0,24},{2,26},{4,28},{6,30},{8,16},{10,18},{12,20},{14,22},{16,8},... | collective-permute-start | bytes 442376 | tf_op jit(solution)/shard_map/ppermute | solution.py:78
  395.8 37.8 %collective-permute-start.33 = (bf16[48,1536]{1,0:T(8,128)(2,1)}, bf16[48,1536]{1,0:T(8,128)(2,1)}, u32[]{:S(2)}, u32[]{:S(2)}) collective-permute-start(bf16[48,1536]{1,0:T(8,128)(2,1)} %pad_maximum_fusion.19), channel_id=1, source_target_pairs={{0,16},{2,18},{4,20},{6,22},{8,24},{10,26},{12,28},{14,30},{16,0},... | collective-permute-start | bytes 442376 | tf_op jit(solution)/shard_map/ppermute | solution.py:78
  403.2 31.0 %collective-permute-start.32 = (bf16[48,1536]{1,0:T(8,128)(2,1)}, bf16[48,1536]{1,0:T(8,128)(2,1)}, u32[]{:S(2)}, u32[]{:S(2)}) collective-permute-start(bf16[48,1536]{1,0:T(8,128)(2,1)} %pad_maximum_fusion.18), channel_id=1, source_target_pairs={{0,8},{2,10},{4,12},{6,14},{8,0},{10,2},{12,4},{14,6},{16,24},{18,... | collective-permute-start | bytes 442376 | tf_op jit(solution)/shard_map/ppermute | solution.py:78
  427.2 30.3 %collective-permute-start.45 = (f32[2,9216]{1,0:T(2,128)}, f32[2,9216]{1,0:T(2,128)}, u32[]{:S(2)}, u32[]{:S(2)}) collective-permute-start(f32[2,9216]{1,0:T(2,128)} %get-tuple-element.231), channel_id=1, source_target_pairs={{0,2},{2,0},{4,6},{6,4},{8,10},{10,8},{12,14},{14,12},{16,18},{18,... | collective-permute-start | bytes 221192 | tf_op jit(solution)/shard_map/ppermute | solution.py:78
  427.2 30.3 %collective-permute-start.46 = (f32[2,9216]{1,0:T(2,128)}, f32[2,9216]{1,0:T(2,128)}, u32[]{:S(2)}, u32[]{:S(2)}) collective-permute-start(f32[2,9216]{1,0:T(2,128)} %get-tuple-element.231), channel_id=1, source_target_pairs={{0,4},{2,6},{4,0},{6,2},{8,12},{10,14},{12,8},{14,10},{16,20},{18,... | collective-permute-start | bytes 221192 | tf_op jit(solution)/shard_map/ppermute | solution.py:78
  432.3 25.2 %collective-permute-start.47 = (f32[2,9216]{1,0:T(2,128)}, f32[2,9216]{1,0:T(2,128)}, u32[]{:S(2)}, u32[]{:S(2)}) collective-permute-start(f32[2,9216]{1,0:T(2,128)} %get-tuple-element.231), channel_id=1, source_target_pairs={{0,6},{2,4},{4,2},{6,0},{8,14},{10,12},{12,10},{14,8},{16,22},{18,... | collective-permute-start | bytes 221192 | tf_op jit(solution)/shard_map/ppermute | solution.py:78
  433.6 35.8 %collective-permute-start.54 = (bf16[8,48,1536]{2,1,0:T(8,128)(2,1)}, bf16[8,48,1536]{2,1,0:T(8,128)(2,1)S(1)}, u32[]{:S(2)}, u32[]{:S(2)}) collective-permute-start(bf16[8,48,1536]{2,1,0:T(8,128)(2,1)} %get-tuple-element.247), channel_id=1, source_target_pairs={{0,4},{2,6},{4,0},{6,2},{8,12},{10,14},{12,8},{14,10},{16,20},{18,... | collective-permute-start | bytes 3538952 | tf_op jit(solution)/shard_map/ppermute | solution.py:78
  434.2 35.2 %collective-permute-start.52 = (bf16[8,48,1536]{2,1,0:T(8,128)(2,1)}, bf16[8,48,1536]{2,1,0:T(8,128)(2,1)}, u32[]{:S(2)}, u32[]{:S(2)}) collective-permute-start(bf16[8,48,1536]{2,1,0:T(8,128)(2,1)} %get-tuple-element.243), channel_id=1, source_target_pairs={{0,1},{1,0},{2,3},{3,2},{4,5},{5,4},{6,7},{7,6},{8,9},{9,8},{10,11... | collective-permute-start | bytes 3538952 | tf_op jit(solution)/shard_map/ppermute | solution.py:78
  469.2 24.1 %collective-permute-start.36 = (bf16[16,48,1152]{2,1,0:T(8,128)(2,1)S(1)}, bf16[16,48,1152]{2,1,0:T(8,128)(2,1)S(1)}, u32[]{:S(2)}, u32[]{:S(2)}) collective-permute-start(bf16[16,48,1152]{2,1,0:T(8,128)(2,1)S(1)} %copy-done.40), channel_id=1, source_target_pairs={{0,2},{2,0},{4,6},{6,4},{8,10},{10,8},{12,14},{14,12},{16,18},{18,... | collective-permute-start | bytes 5308424 | tf_op jit(solution)/shard_map/ppermute | solution.py:78
  471.4 15.8 %collective-permute-start.53 = (bf16[4,48,1536]{2,1,0:T(8,128)(2,1)S(1)}, bf16[4,48,1536]{2,1,0:T(8,128)(2,1)S(1)}, u32[]{:S(2)}, u32[]{:S(2)}) collective-permute-start(bf16[4,48,1536]{2,1,0:T(8,128)(2,1)S(1)} %get-tuple-element.245), channel_id=1, source_target_pairs={{0,4},{2,6},{4,0},{6,2},{8,12},{10,14},{12,8},{14,10},{16,20},{18,... | collective-permute-start | bytes 1769480 | tf_op jit(solution)/shard_map/ppermute | solution.py:78
  472.6 15.9 %collective-permute-start.55 = (bf16[4,48,1536]{2,1,0:T(8,128)(2,1)S(1)}, bf16[4,48,1536]{2,1,0:T(8,128)(2,1)S(1)}, u32[]{:S(2)}, u32[]{:S(2)}) collective-permute-start(bf16[4,48,1536]{2,1,0:T(8,128)(2,1)S(1)} %get-tuple-element.249), channel_id=1, source_target_pairs={{0,1},{1,0},{2,3},{3,2},{4,5},{5,4},{6,7},{7,6},{8,9},{9,8},{10,11... | collective-permute-start | bytes 1769480 | tf_op jit(solution)/shard_map/ppermute | solution.py:78
  492.4 28.2 %collective-permute-start.56 = (bf16[48,3072]{1,0:T(8,128)(2,1)S(1)}, bf16[48,3072]{1,0:T(8,128)(2,1)S(1)}, u32[]{:S(2)}, u32[]{:S(2)}) collective-permute-start(bf16[48,3072]{1,0:T(8,128)(2,1)S(1)} %pad_maximum_fusion.15), channel_id=1, source_target_pairs={{0,8},{2,10},{4,12},{6,14},{8,0},{10,2},{12,4},{14,6},{16,24},{18,... | collective-permute-start | bytes 884744 | tf_op jit(solution)/shard_map/ppermute | solution.py:78
  493.4 14.3 %collective-permute-start.37 = (bf16[8,48,768]{2,1,0:T(8,128)(2,1)S(1)}, bf16[8,48,768]{2,1,0:T(8,128)(2,1)S(1)}, u32[]{:S(2)}, u32[]{:S(2)}) collective-permute-start(bf16[8,48,768]{2,1,0:T(8,128)(2,1)S(1)} %pad_maximum_fusion.1), channel_id=1, source_target_pairs={{0,1},{1,0},{2,3},{3,2},{4,5},{5,4},{6,7},{7,6},{8,9},{9,8},{10,11... | collective-permute-start | bytes 1769480 | tf_op jit(solution)/shard_map/ppermute | solution.py:78
  494.7 14.8 %collective-permute-start.38 = (bf16[8,48,768]{2,1,0:T(8,128)(2,1)S(1)}, bf16[8,48,768]{2,1,0:T(8,128)(2,1)S(1)}, u32[]{:S(2)}, u32[]{:S(2)}) collective-permute-start(bf16[8,48,768]{2,1,0:T(8,128)(2,1)S(1)} %add_convert_fusion.4), channel_id=1, source_target_pairs={{0,4},{2,6},{4,0},{6,2},{8,12},{10,14},{12,8},{14,10},{16,20},{18,... | collective-permute-start | bytes 1769480 | tf_op jit(solution)/shard_map/ppermute | solution.py:78
  495.4 25.3 %collective-permute-start.57 = (bf16[48,3072]{1,0:T(8,128)(2,1)S(1)}, bf16[48,3072]{1,0:T(8,128)(2,1)S(1)}, u32[]{:S(2)}, u32[]{:S(2)}) collective-permute-start(bf16[48,3072]{1,0:T(8,128)(2,1)S(1)} %pad_maximum_fusion.16), channel_id=1, source_target_pairs={{0,16},{2,18},{4,20},{6,22},{8,24},{10,26},{12,28},{14,30},{16,0},... | collective-permute-start | bytes 884744 | tf_op jit(solution)/shard_map/ppermute | solution.py:78
  519.4 33.4 %collective-permute-start.39 = (bf16[1024,768]{1,0:T(8,128)(2,1)}, bf16[1024,768]{1,0:T(8,128)(2,1)S(1)}, u32[]{:S(2)}, u32[]{:S(2)}) collective-permute-start(bf16[1024,768]{1,0:T(8,128)(2,1)} %get-tuple-element.209), channel_id=1, source_target_pairs={{0,1},{1,0},{2,3},{3,2},{4,5},{5,4},{6,7},{7,6},{8,9},{9,8},{10,11... | collective-permute-start | bytes 4718600 | tf_op jit(solution)/shard_map/ppermute | solution.py:78
  527.0 11.8 %collective-permute-start.42 = (bf16[48,1536]{1,0:T(8,128)(2,1)S(1)}, bf16[48,1536]{1,0:T(8,128)(2,1)S(1)}, u32[]{:S(2)}, u32[]{:S(2)}) collective-permute-start(bf16[48,1536]{1,0:T(8,128)(2,1)S(1)} %pad_maximum_fusion.21), channel_id=1, source_target_pairs={{0,8},{2,10},{4,12},{6,14},{8,0},{10,2},{12,4},{14,6},{16,24},{18,... | collective-permute-start | bytes 442376 | tf_op jit(solution)/shard_map/ppermute | solution.py:78
  532.1 12.8 %collective-permute-start.43 = (bf16[48,1536]{1,0:T(8,128)(2,1)S(1)}, bf16[48,1536]{1,0:T(8,128)(2,1)}, u32[]{:S(2)}, u32[]{:S(2)}) collective-permute-start(bf16[48,1536]{1,0:T(8,128)(2,1)S(1)} %pad_maximum_fusion.22), channel_id=1, source_target_pairs={{0,16},{2,18},{4,20},{6,22},{8,24},{10,26},{12,28},{14,30},{16,0},... | collective-permute-start | bytes 442376 | tf_op jit(solution)/shard_map/ppermute | solution.py:78
  532.3 12.7 %collective-permute-start.44 = (bf16[48,1536]{1,0:T(8,128)(2,1)S(1)}, bf16[48,1536]{1,0:T(8,128)(2,1)}, u32[]{:S(2)}, u32[]{:S(2)}) collective-permute-start(bf16[48,1536]{1,0:T(8,128)(2,1)S(1)} %pad_maximum_fusion.23), channel_id=1, source_target_pairs={{0,24},{2,26},{4,28},{6,30},{8,16},{10,18},{12,20},{14,22},{16,8},... | collective-permute-start | bytes 442376 | tf_op jit(solution)/shard_map/ppermute | solution.py:78
  (62 other events, 669.2 us)
Sparse Core Ops, SparseCore 0:
  11.5 103.8 all-gather.2
  118.9 84.5 all-gather.4
  310.7 140.3 reduce-scatter.1
